TPU v7x, 32 devices: a whole 2x2x4 slice. The times are simulated.
32 devices in a mesh: wide: 8 (over z, y), narrow: 4 (over x, core).
Axes of the slice: x: 2, y: 2, z: 4, core: 2. Of those that a mesh axis runs over, the one named last changes fastest.
Arguments:
- inputs: bfloat16 [8192, 1024], P('wide', 'narrow'), may hold values from -6 to 6
- segments: int32 [8, 1024], P('wide'), may hold values from 0 to 2, never falling along the last dimension, each value on 1 to 512 neighbouring positions
- attn_gain: bfloat16 [1024], P('wide'), may hold values from 0.5 to 1.5
- qkv_weight: bfloat16 [1024, 3, 1024], P('wide', None, 'narrow'), may hold values from -0.1875 to 0.1875
- out_weight: bfloat16 [1024, 1024], P('narrow', 'wide'), may hold values from -1.5 to 1.5
- memory_gain: bfloat16 [1024], P('wide'), may hold values from 0.5 to 1.5
- query_weight: bfloat16 [1024, 8, 256], P('wide', 'narrow'), may hold values from -0.1875 to 0.1875
- sub_keys: bfloat16 [8, 256, 256], P('narrow', 'wide'), may hold values from -0.5 to 0.5
- gate_weight: bfloat16 [1024, 1024], P('wide', 'narrow'), may hold values from -0.1875 to 0.1875
- memory_values: bfloat16 [65536, 1024], P('wide', 'narrow'), may hold values from -6 to 6
- memory_out: bfloat16 [1024, 1024], P('narrow', 'wide'), may hold values from -0.375 to 0.375
- picks: int32 [8192, 128], P('wide'), may hold values from 0 to 65535, as said below
- cotangent: bfloat16 [8192, 1024], P('wide', 'narrow'), may hold values from -6 to 6
Outputs:
- outputs: bfloat16 [8192, 1024], P('wide', 'narrow')
- input_grad: float32 [8192, 1024], P('wide', 'narrow')
- attn_gain_grad: float32 [1024], P('wide')
- qkv_grad: float32 [1024, 3, 1024], P('wide', None, 'narrow')
- out_grad: float32 [1024, 1024], P('narrow', 'wide')
- memory_gain_grad: float32 [1024], P('wide')
- query_grad: float32 [1024, 8, 256], P('wide', 'narrow')
- sub_keys_grad: float32 [8, 256, 256], P('narrow', 'wide')
- gate_grad: float32 [1024, 1024], P('wide', 'narrow')
- values_grad: float32 [65536, 1024], P('wide', 'narrow')
- memory_out_grad: float32 [1024, 1024], P('narrow', 'wide')
Inputs may be any that keep to these rules, and one draw needn't show every extreme that they name: `segments`: segment numbers never fall along a sequence; every document spans 1 to 512 positions. The 128 rows of one token are all different; columns k * 32 to (k + 1) * 32 - 1 are the picks of memory head k.
All inputs are finite; a program needn't handle non-finite values.
Results may differ from a plain program's by a relative error of at most 0.023.
Values may be sent and summed in bfloat16 or wider, within the bound.
No kernel may reach another device: no remote copies, remote signals or barrier semaphores. Data moves between devices by JAX's collectives and lax.ppermute only.
A program may use at most 320 MiB of HBM per device.

v0:
```python
import jax
import jax.numpy as jnp
from jax import lax
from jax.sharding import PartitionSpec as P

HD = 64
PKH = 4
NKEYS = 256
TOPK = 32
PICKS = 128


EPSILON = 1e-06
HIGHEST = lax.Precision.HIGHEST
MASKED = -1e30


def norm_rows(activations, gain_row):
    factor = lax.rsqrt(jnp.mean(activations * activations, axis=-1, keepdims=True) + EPSILON)
    return (factor, activations * factor * gain_row)


def norm_back(activations, factor, gain_row, upstream):
    inner_sum = jnp.mean(gain_row * upstream * activations, axis=-1, keepdims=True)
    through = factor * gain_row * upstream - activations * (factor * factor * factor) * inner_sum
    return (through, jnp.sum(upstream * activations * factor, axis=0))


def masked_scores(query_block, key_rows, segment_block, segment_row, offset):
    block_rows = query_block.shape[0]
    positions = jnp.arange(key_rows.shape[0], dtype=jnp.int32)
    scores = jnp.einsum("qhd,khd->hqk", query_block, key_rows, preferred_element_type=jnp.float32)
    scores = scores * query_block.shape[2] ** (-0.5)
    allowed = (positions[None, :] <= (offset + positions[:block_rows])[:, None]) & (
        segment_block[:, None] == segment_row[None, :]
    )
    return jnp.where(allowed[None], scores, MASKED)


def attend_forward(queries, key_rows, value_rows, segment_row):
    length = queries.shape[0]
    block_rows = min(512, length)

    def one_block(number):
        offset = number * block_rows
        query_block = lax.dynamic_slice_in_dim(queries, offset, block_rows, 0)
        segment_block = lax.dynamic_slice_in_dim(segment_row, offset, block_rows, 0)
        scores = masked_scores(query_block, key_rows, segment_block, segment_row, offset)
        row_peak = jnp.max(scores, axis=-1, keepdims=True)
        raised = jnp.exp(scores - row_peak)
        totals = jnp.sum(raised, axis=-1, keepdims=True)
        attention = (raised / totals).astype(jnp.bfloat16)
        mixture = jnp.einsum(
            "hqk,khd->qhd", attention, value_rows, preferred_element_type=jnp.float32
        )
        return (mixture.astype(jnp.bfloat16), (row_peak + jnp.log(totals))[:, :, 0])

    outputs, logsum = lax.map(one_block, jnp.arange(length // block_rows, dtype=jnp.int32))
    head_width = queries.shape[1] * queries.shape[2]
    logsum = jnp.transpose(logsum, (1, 0, 2)).reshape(queries.shape[1], length)
    return (outputs.reshape(length, head_width), logsum)


def attend_backward(queries, key_rows, value_rows, segment_row, logsum, heads_grad):
    length = queries.shape[0]
    block_rows = min(512, length)
    factor = queries.shape[2] ** (-0.5)

    def one_block(running, number):
        key_sum, value_sum = running
        offset = number * block_rows
        query_block = lax.dynamic_slice_in_dim(queries, offset, block_rows, 0)
        segment_block = lax.dynamic_slice_in_dim(segment_row, offset, block_rows, 0)
        grad_block = lax.dynamic_slice_in_dim(heads_grad, offset, block_rows, 0)
        logsum_block = lax.dynamic_slice_in_dim(logsum, offset, block_rows, 1)
        scores = masked_scores(query_block, key_rows, segment_block, segment_row, offset)
        attention = jnp.exp(scores - logsum_block[:, :, None])
        prob_grad = jnp.einsum(
            "qhd,khd->hqk", grad_block, value_rows, preferred_element_type=jnp.float32
        )
        centre = jnp.sum(attention * prob_grad, axis=-1, keepdims=True)
        score_grad = (attention * (prob_grad - centre)).astype(jnp.bfloat16)
        query_grad = (
            jnp.einsum("hqk,khd->qhd", score_grad, key_rows, preferred_element_type=jnp.float32)
            * factor
        )
        key_sum = (
            key_sum
            + jnp.einsum(
                "hqk,qhd->khd", score_grad, query_block, preferred_element_type=jnp.float32
            )
            * factor
        )
        value_sum = value_sum + jnp.einsum(
            "hqk,qhd->khd",
            attention.astype(jnp.bfloat16),
            grad_block,
            preferred_element_type=jnp.float32,
        )
        return ((key_sum, value_sum), query_grad)

    empty_sum = jnp.zeros(key_rows.shape, jnp.float32)
    carried, query_parts = lax.scan(
        one_block, (empty_sum, empty_sum), jnp.arange(length // block_rows, dtype=jnp.int32)
    )
    return (query_parts.reshape(queries.shape), carried[0], carried[1])


def token_blocks(function, arrays):
    total_rows = arrays[0].shape[0]
    block_rows = min(256, total_rows)
    block_count = total_rows // block_rows
    stacked = tuple(
        (member.reshape((block_count, block_rows) + member.shape[1:]) for member in arrays)
    )
    result = lax.map(function, stacked)
    return result.reshape((block_count * block_rows,) + result.shape[2:])


def pick_table(row_numbers, pick_values, table_rows):
    groups = table_rows // NKEYS
    upper = row_numbers // NKEYS
    lower = row_numbers % NKEYS
    first = (upper[:, :, None] == jnp.arange(groups, dtype=jnp.int32)[None, None, :]).astype(
        jnp.bfloat16
    )
    second = (lower[:, :, None] == jnp.arange(NKEYS, dtype=jnp.int32)[None, None, :]).astype(
        jnp.bfloat16
    )
    first = first * pick_values[:, :, None]
    table = jnp.einsum("tpa,tpb->tab", first, second, preferred_element_type=jnp.float32)
    return table.astype(jnp.bfloat16).reshape(row_numbers.shape[0], table_rows)


def weighted_rows(row_numbers, pick_values, portion):
    table_rows = portion.shape[0]

    def one_block(bundle):
        table = pick_table(bundle[0], bundle[1], table_rows)
        return jnp.dot(table, portion, preferred_element_type=jnp.float32)

    return token_blocks(one_block, (row_numbers, pick_values))


def picked_products(row_numbers, grad_rows, portion):
    table_rows = portion.shape[0]

    def one_block(bundle):
        local_row = bundle[0]
        inside = (local_row >= 0) & (local_row < table_rows)
        products = lax.dot_general(
            bundle[1], portion, (((1,), (1,)), ((), ())), preferred_element_type=jnp.float32
        )
        chosen = jnp.take_along_axis(products, jnp.clip(local_row, 0, table_rows - 1), axis=1)
        return jnp.where(inside, chosen, 0.0)

    return token_blocks(one_block, (row_numbers, grad_rows))


def row_grads(row_numbers, pick_values, grad_rows, amount):
    total_rows = row_numbers.shape[0]
    block_rows = min(256, total_rows)
    block_count = total_rows // block_rows
    width = grad_rows.shape[1]
    stacked = (
        row_numbers.reshape(block_count, block_rows, -1),
        pick_values.reshape(block_count, block_rows, -1),
        grad_rows.reshape(block_count, block_rows, width),
    )

    def one_block(running, bundle):
        table = pick_table(bundle[0], bundle[1], amount)
        summed = lax.dot_general(
            table, bundle[2], (((0,), (0,)), ((), ())), preferred_element_type=jnp.float32
        )
        return (running + summed, None)

    result, unused = lax.scan(one_block, jnp.zeros((amount, width), jnp.float32), stacked)
    return result


def per_device(
    inputs,
    segments,
    attn_gain,
    qkv_weight,
    out_weight,
    memory_gain,
    query_weight,
    sub_keys,
    gate_weight,
    memory_values,
    memory_out,
    picks,
    cotangent,
):
    gathered = (
        lax.all_gather(attn_gain, "wide", axis=0, tiled=True),
        lax.all_gather(qkv_weight, "wide", axis=0, tiled=True),
        lax.all_gather(out_weight, "wide", axis=1, tiled=True),
        lax.all_gather(memory_gain, "wide", axis=0, tiled=True),
        lax.all_gather(query_weight, "wide", axis=0, tiled=True),
        lax.all_gather(sub_keys, "wide", axis=1, tiled=True),
        lax.all_gather(gate_weight, "wide", axis=0, tiled=True),
        lax.all_gather(memory_out, "wide", axis=1, tiled=True),
    )
    gain_one = gathered[0].astype(jnp.float32)
    qkv_full = gathered[1]
    out_full = gathered[2]
    gain_two = gathered[3].astype(jnp.float32)
    query_full = gathered[4]
    keys_full = gathered[5]
    gate_full = gathered[6]
    mixer_full = gathered[7]
    length = inputs.shape[0]
    width = inputs.shape[1]
    column = lax.axis_index("narrow")
    shard_rows = memory_values.shape[0]
    rows_one = lax.all_gather(inputs, "narrow", axis=1, tiled=True).astype(jnp.float32)
    factor_one, normed = norm_rows(rows_one, gain_one)
    normed = normed.astype(jnp.bfloat16)
    mixture = jnp.einsum(
        "td,djc->tjc", normed, qkv_full, preferred_element_type=jnp.float32
    ).astype(jnp.bfloat16)
    head_count = width // HD
    queries = mixture[:, 0].reshape(length, head_count, HD)
    key_rows = mixture[:, 1].reshape(length, head_count, HD)
    value_rows = mixture[:, 2].reshape(length, head_count, HD)
    segment_row = segments[0]
    head_rows, logsum = attend_forward(queries, key_rows, value_rows, segment_row)
    branch_part = jnp.dot(head_rows, out_full, preferred_element_type=jnp.float32)
    hidden = rows_one + lax.psum(branch_part, "narrow")
    factor_two, second = norm_rows(hidden, gain_two)
    second = second.astype(jnp.bfloat16)
    gate_value = jnp.dot(second, gate_full, preferred_element_type=jnp.float32)
    memory_query = jnp.einsum(
        "td,due->tue", second, query_full, preferred_element_type=jnp.float32
    ).astype(jnp.bfloat16)
    unit_count = memory_query.shape[1]
    grouped = picks.reshape(length, PKH, TOPK)
    key_range = jnp.arange(NKEYS, dtype=jnp.int32)
    head_numbers = []
    key_tables = []
    unit_parts = []
    for unit_slot in range(unit_count):
        unit_number = column * unit_count + unit_slot
        head_number = unit_number // 2
        head_picks = lax.dynamic_index_in_dim(grouped, head_number, axis=1, keepdims=False)
        key_number = jnp.where(unit_number % 2 == 0, head_picks // NKEYS, head_picks % NKEYS)
        key_table = (key_number[:, :, None] == key_range[None, None, :]).astype(jnp.float32)
        key_scores = jnp.einsum(
            "te,ke->tk",
            memory_query[:, unit_slot],
            keys_full[unit_slot],
            preferred_element_type=jnp.float32,
        )
        unit_parts.append(jnp.einsum("tk,tjk->tj", key_scores, key_table, precision=HIGHEST))
        head_numbers.append(head_number)
        key_tables.append(key_table)
    all_parts = lax.all_gather(jnp.stack(unit_parts, axis=1), "narrow", axis=1, tiled=True)
    mem_scores = jnp.sum(all_parts.reshape(length, PKH, 2, TOPK), axis=2)
    score_peak = jnp.max(mem_scores, axis=-1, keepdims=True)
    raised = jnp.exp(mem_scores - score_peak)
    mem_probs = raised / jnp.sum(raised, axis=-1, keepdims=True)
    pick_weights = mem_probs.astype(jnp.bfloat16).reshape(length, PICKS)
    memory = weighted_rows(
        picks, pick_weights, lax.all_gather(memory_values, "wide", axis=0, tiled=True)
    )
    gate_act = jax.nn.silu(gate_value)
    product = (gate_act * memory).astype(jnp.bfloat16)
    mixer_part = jnp.dot(product, mixer_full, preferred_element_type=jnp.float32)
    mixer_sum = lax.psum_scatter(
        mixer_part.astype(jnp.bfloat16), "narrow", scatter_dimension=1, tiled=True
    ).astype(jnp.float32)
    own_hidden = lax.dynamic_slice_in_dim(hidden, column * width, width, 1)
    outputs = (own_hidden + mixer_sum).astype(jnp.bfloat16)
    upstream = lax.all_gather(cotangent, "narrow", axis=1, tiled=True)
    product_grad = lax.dot_general(
        upstream, mixer_full, (((1,), (1,)), ((), ())), preferred_element_type=jnp.float32
    )
    mixer_grad = lax.dot_general(
        product, upstream, (((0,), (0,)), ((), ())), preferred_element_type=jnp.float32
    )
    memory_grad = (product_grad * gate_act).astype(jnp.bfloat16)
    sigmoid = jax.nn.sigmoid(gate_value)
    gate_rows_grad = (
        product_grad * memory * sigmoid * (1.0 + gate_value * (1.0 - sigmoid))
    ).astype(jnp.bfloat16)
    pick_part = picked_products(
        picks, memory_grad, lax.all_gather(memory_values, "wide", axis=0, tiled=True)
    )
    values_grad = lax.psum_scatter(
        row_grads(picks, pick_weights, memory_grad, lax.axis_size("wide") * shard_rows).astype(
            jnp.bfloat16
        ),
        "wide",
        scatter_dimension=0,
        tiled=True,
    ).astype(jnp.float32)
    pick_grad = lax.psum(pick_part, "narrow").reshape(length, PKH, TOPK)
    centre = jnp.sum(mem_probs * pick_grad, axis=-1, keepdims=True)
    score_grad = (mem_probs * (pick_grad - centre)).astype(jnp.bfloat16)
    query_grads = []
    key_grads = []
    for unit_slot in range(unit_count):
        head_grad = lax.dynamic_index_in_dim(
            score_grad, head_numbers[unit_slot], axis=1, keepdims=False
        ).astype(jnp.float32)
        spread = jnp.einsum("tj,tjk->tk", head_grad, key_tables[unit_slot], precision=HIGHEST)
        query_grads.append(
            jnp.dot(spread, keys_full[unit_slot].astype(jnp.float32), precision=HIGHEST)
        )
        key_grads.append(
            lax.dot_general(
                spread,
                memory_query[:, unit_slot].astype(jnp.float32),
                (((0,), (0,)), ((), ())),
                precision=HIGHEST,
            )
        )
    memory_query_grad = jnp.stack(query_grads, axis=1).astype(jnp.bfloat16)
    key_grad = jnp.stack(key_grads, axis=0)
    query_weight_grad = jnp.einsum(
        "td,tue->due", second, memory_query_grad, preferred_element_type=jnp.float32
    )
    gate_weight_grad = lax.dot_general(
        second, gate_rows_grad, (((0,), (0,)), ((), ())), preferred_element_type=jnp.float32
    )
    second_part = lax.dot_general(
        gate_rows_grad, gate_full, (((1,), (1,)), ((), ())), preferred_element_type=jnp.float32
    )
    second_part = second_part + jnp.einsum(
        "tue,due->td", memory_query_grad, query_full, preferred_element_type=jnp.float32
    )
    second_grad = lax.psum(second_part, "narrow")
    through_two, gain_two_part = norm_back(hidden, factor_two, gain_two, second_grad)
    hidden_grad = upstream.astype(jnp.float32) + through_two
    branch_grad = hidden_grad.astype(jnp.bfloat16)
    out_weight_grad = lax.dot_general(
        head_rows, branch_grad, (((0,), (0,)), ((), ())), preferred_element_type=jnp.float32
    )
    heads_grad = lax.dot_general(
        branch_grad, out_full, (((1,), (1,)), ((), ())), preferred_element_type=jnp.float32
    )
    heads_grad = heads_grad.astype(jnp.bfloat16).reshape(length, head_count, HD)
    query_back, key_back, value_back = attend_backward(
        queries, key_rows, value_rows, segment_row, logsum, heads_grad
    )
    mixed_grad = jnp.stack(
        [
            query_back.reshape(length, width),
            key_back.reshape(length, width),
            value_back.reshape(length, width),
        ],
        axis=1,
    ).astype(jnp.bfloat16)
    qkv_weight_grad = jnp.einsum(
        "td,tjc->djc", normed, mixed_grad, preferred_element_type=jnp.float32
    )
    normed_part = jnp.einsum(
        "tjc,djc->td", mixed_grad, qkv_full, preferred_element_type=jnp.float32
    )
    normed_grad = lax.psum(normed_part.astype(jnp.bfloat16), "narrow").astype(jnp.float32)
    through_one, gain_one_part = norm_back(rows_one, factor_one, gain_one, normed_grad)
    input_full = hidden_grad + through_one
    input_grad = lax.dynamic_slice_in_dim(input_full, column * width, width, 1)
    summed = (
        lax.psum_scatter(
            gain_one_part.astype(jnp.bfloat16), "wide", scatter_dimension=0, tiled=True
        ).astype(jnp.float32),
        lax.psum_scatter(
            qkv_weight_grad.astype(jnp.bfloat16), "wide", scatter_dimension=0, tiled=True
        ).astype(jnp.float32),
        lax.psum_scatter(
            out_weight_grad.astype(jnp.bfloat16), "wide", scatter_dimension=1, tiled=True
        ).astype(jnp.float32),
        lax.psum_scatter(
            gain_two_part.astype(jnp.bfloat16), "wide", scatter_dimension=0, tiled=True
        ).astype(jnp.float32),
        lax.psum_scatter(
            query_weight_grad.astype(jnp.bfloat16), "wide", scatter_dimension=0, tiled=True
        ).astype(jnp.float32),
        lax.psum_scatter(
            key_grad.astype(jnp.bfloat16), "wide", scatter_dimension=1, tiled=True
        ).astype(jnp.float32),
        lax.psum_scatter(
            gate_weight_grad.astype(jnp.bfloat16), "wide", scatter_dimension=0, tiled=True
        ).astype(jnp.float32),
        lax.psum_scatter(
            mixer_grad.astype(jnp.bfloat16), "wide", scatter_dimension=1, tiled=True
        ).astype(jnp.float32),
    )
    return (
        outputs,
        input_grad,
        summed[0],
        summed[1],
        summed[2],
        summed[3],
        summed[4],
        summed[5],
        summed[6],
        values_grad,
        summed[7],
    )


def solution(mesh):
    return jax.shard_map(
        per_device,
        mesh=mesh,
        in_specs=(
            P("wide", "narrow"),
            P("wide", None),
            P("wide"),
            P("wide", None, "narrow"),
            P("narrow", "wide"),
            P("wide"),
            P("wide", "narrow", None),
            P("narrow", "wide", None),
            P("wide", "narrow"),
            P("wide", "narrow"),
            P("narrow", "wide"),
            P("wide", None),
            P("wide", "narrow"),
        ),
        out_specs=(
            P("wide", "narrow"),
            P("wide", "narrow"),
            P("wide"),
            P("wide", None, "narrow"),
            P("narrow", "wide"),
            P("wide"),
            P("wide", "narrow", None),
            P("narrow", "wide", None),
            P("wide", "narrow"),
            P("wide", "narrow"),
            P("narrow", "wide"),
        ),
        check_vma=False,
    )
```

profile of v0, /device:TPU:0, one launch (start us, length us, event | category | flops | bytes accessed | tf_op | source)
XLA Modules:
  0.0 4177.5 jit_solution(5307876388544344446)
XLA Ops:
  9.8 22.3 all-gather
  32.1 28.6 all_gather.40
  63.5 20.9 all-gather.11.cloned.1.call-done
  84.4 4.0 convolution_convert_fusion.2
  88.5 17.9 while.62
  112.3 17.6 all-gather.1
  130.8 31.1 all_gather.44
  161.9 32.6 all-reduce.8.cloned.1.call-done
  194.6 3.5 multiply_reduce_fusion.3
  201.8 36.0 all-gather.13.cloned.1.call-done
  242.2 21.1 fusion.80
  264.5 20.2 fusion.82
  287.1 75.0 %all_gather.42 = bf16[1024,256]{1,0:T(8,128)(2,1)S(1)} all-gather(bf16[128,256]{1,0:T(8,128)(2,1)S(1)} %copy-done.62), channel_id=1, replica_groups=mesh['wide'=8,'narrow'=4] {'wide'}, dimensions={0}, use_global_device_ids=true | all-gather | bytes 589824 | tf_op jit(solution)/shard_map/all_gather | solution.py:204
  362.1 40.0 all_gather.47
  408.2 543.9 %all-gather.17.cloned.1.call-done = bf16[65536,256]{1,0:T(8,128)(2,1)} async-done(((bf16[8192,256]{1,0:T(8,128)(2,1)}), bf16[65536,256]{1,0:T(8,128)(2,1)}) %all-gather.17.cloned.1.call-update) | async-done | bytes 33554448 | tf_op jit(solution)/shard_map/all_gather | solution.py:267
  952.1 290.2 %while.63 = (s32[]{:T(128)}, f32[4,256,256]{2,1,0:T(8,128)}, s32[4,256,128]{2,1,0:T(8,128)S(1)}, bf16[4,256,128]{2,1,0:T(8,128)(2,1)S(1)}, bf16[65536,256]{1,0:T(8,128)(2,1)}, /*index=5*/s32[]{:T(128)}) while((s32[]{:T(128)}, f32[4,256,256]{2,1,0:T(8,128)}, s32[4,256,128]{2,1,0:T(8,128)S(1)}, bf16[4,256,128]{2,1,0:T(8,128)(2,1)S(1)}, ...), condition=%wide.region_11.12_spmd, body=%wide.region_10.11_spmd.sunk | while | flops 12927664128 | bytes 169082976 | solution.py:116
  952.3 17.2 fusion.238
  969.5 31.0 copy.149
  1000.5 24.2 fusion.239
  1024.9 17.2 fusion.238
  1042.1 31.0 copy.149
  1073.1 24.2 fusion.239
  1097.4 17.2 fusion.238
  1114.7 31.0 copy.149
  1145.6 24.2 fusion.239
  1170.0 17.2 fusion.238
  1187.2 31.0 copy.149
  1218.2 24.2 fusion.239
  1242.4 4.3 multiply_convert_fusion.2
  1246.7 1732.3 %while.64 = (s32[]{:T(128)}, f32[4,256,128]{1,0,2:T(4,128)S(1)}, s32[4,256,128]{2,1,0:T(8,128)S(1)}, bf16[4,256,256]{2,1,0:T(8,128)(2,1)S(1)}, bf16[65536,256]{1,0:T(8,128)(2,1)}, /*index=5*/s32[]{:T(128)}, s32[]{:T(128)}) while((s32[]{:T(128)}, f32[4,256,128]{1,0,2:T(4,128)S(1)}, s32[4,256,128]{2,1,0:T(8,128)S(1)}, ...), condition=%wide.region_14.15_spmd, body=%wide.region_13.14_spmd.sunk | while | flops 8590622720 | bytes 102498384 | solution.py:116
  1246.8 33.7 fusion.242
  1280.4 397.4 %gather_fusion = f32[32768]{0:T(1024)S(1)} fusion(f32[256,65536]{1,0:T(8,128)} %fusion.242, s32[32768]{0:T(1024)S(1)} %fusion.243), kind=kCustom, calls=%fused_computation.clone.1 | custom fusion | bytes 524288 | tf_op jit(solution)/shard_map/while/body/eval_jaxpr/jit(take_along_axis)/gather | solution.py:154
  1680.0 33.6 fusion.242
  1713.6 397.0 %gather_fusion = f32[32768]{0:T(1024)S(1)} fusion(f32[256,65536]{1,0:T(8,128)} %fusion.242, s32[32768]{0:T(1024)S(1)} %fusion.243), kind=kCustom, calls=%fused_computation.clone.1 | custom fusion | bytes 524288 | tf_op jit(solution)/shard_map/while/body/eval_jaxpr/jit(take_along_axis)/gather | solution.py:154
  2112.7 33.6 fusion.242
  2146.3 397.8 %gather_fusion = f32[32768]{0:T(1024)S(1)} fusion(f32[256,65536]{1,0:T(8,128)} %fusion.242, s32[32768]{0:T(1024)S(1)} %fusion.243), kind=kCustom, calls=%fused_computation.clone.1 | custom fusion | bytes 524288 | tf_op jit(solution)/shard_map/while/body/eval_jaxpr/jit(take_along_axis)/gather | solution.py:154
  2546.2 33.6 fusion.242
  2579.8 397.2 %gather_fusion = f32[32768]{0:T(1024)S(1)} fusion(f32[256,65536]{1,0:T(8,128)} %fusion.242, s32[32768]{0:T(1024)S(1)} %fusion.243), kind=kCustom, calls=%fused_computation.clone.1 | custom fusion | bytes 524288 | tf_op jit(solution)/shard_map/while/body/eval_jaxpr/jit(take_along_axis)/gather | solution.py:154
  2983.4 29.1 all-reduce.10.cloned.1.call-done
  3014.6 9.8 fusion.81
  3026.6 9.8 fusion.79
  3059.3 68.5 %all-reduce.12.cloned.1.call-done = f32[1024,1024]{1,0:T(8,128)} async-done(((f32[1024,1024]{1,0:T(8,128)}), f32[1024,1024]{1,0:T(8,128)}) %all-reduce.12.cloned.1.call-update) | async-done | bytes 4194320 | tf_op jit(solution)/shard_map/psum | solution.py:335
  3127.8 5.2 multiply_reduce_fusion.1
  3143.5 27.5 while.65
  3177.1 4.7 bitcast_convert_fusion
  3184.2 4.7 convolution_convert_fusion.1
  3188.9 399.2 %while.66 = (s32[]{:T(128)}, f32[65536,256]{1,0:T(8,128)}, s32[4,256,128]{2,1,0:T(8,128)S(1)}, bf16[4,256,128]{2,1,0:T(8,128)(2,1)}, bf16[4,256,256]{2,1,0:T(8,128)(2,1)}, /*index=5*/s32[]{:T(128)}, s32[]{:T(128)}) while((s32[]{:T(128)}, f32[65536,256]{1,0:T(8,128)}, s32[4,256,128]{2,1,0:T(8,128)S(1)}, ...), condition=%wide.region_34.35_spmd.clone, body=%wide.region_33.34_spmd.clone.sunk | while | flops 12961218560 | bytes 269615200 | solution.py:178
  3189.9 17.1 fusion.262
  3207.1 31.0 copy.151
  3238.0 33.9 convolution_add_fusion.2
  3273.0 17.1 fusion.262
  3290.1 31.0 copy.151
  3321.1 56.0 %convolution_add_fusion.2 = f32[65536,256]{1,0:T(8,128)} fusion(bf16[256,65536]{1,0:T(8,128)(2,1)} %bitcast.356, f32[65536,256]{1,0:T(8,128)} %get-tuple-element.902, pred[]{:T(512)S(6)} %compare.59, bf16[4,256,256]{2,1,0:T(8,128)(2,1)} %get-tuple-element.912, s32[]{:T(128)S(6)} %copy.196), kind=kOutput, calls=%fused_computation.84.clone.2 | convolution fusion | flops 8623489024 | bytes 167903232 | tf_op jit(solution)/shard_map/while/body/eval_jaxpr/dot_general | solution.py:173
  3378.2 17.1 fusion.262
  3395.3 31.0 copy.151
  3426.3 56.5 %convolution_add_fusion.2 = f32[65536,256]{1,0:T(8,128)} fusion(bf16[256,65536]{1,0:T(8,128)(2,1)} %bitcast.356, f32[65536,256]{1,0:T(8,128)} %get-tuple-element.902, pred[]{:T(512)S(6)} %compare.59, bf16[4,256,256]{2,1,0:T(8,128)(2,1)} %get-tuple-element.912, s32[]{:T(128)S(6)} %copy.196), kind=kOutput, calls=%fused_computation.84.clone.2 | convolution fusion | flops 8623489024 | bytes 167903232 | tf_op jit(solution)/shard_map/while/body/eval_jaxpr/dot_general | solution.py:173
  3483.8 17.1 fusion.262
  3500.9 31.0 copy.151
  3531.9 56.2 %convolution_add_fusion.2 = f32[65536,256]{1,0:T(8,128)} fusion(bf16[256,65536]{1,0:T(8,128)(2,1)} %bitcast.356, f32[65536,256]{1,0:T(8,128)} %get-tuple-element.902, pred[]{:T(512)S(6)} %compare.59, bf16[4,256,256]{2,1,0:T(8,128)(2,1)} %get-tuple-element.912, s32[]{:T(128)S(6)} %copy.196), kind=kOutput, calls=%fused_computation.84.clone.2 | convolution fusion | flops 8623489024 | bytes 167903232 | tf_op jit(solution)/shard_map/while/body/eval_jaxpr/dot_general | solution.py:173
  3588.1 32.5 convert_element_type.191
  3633.0 4.2 convert_element_type.177
  3638.9 22.3 all-reduce.2
  3669.2 495.0 %reduce-scatter.23.cloned.1.call-done = bf16[8192,256]{1,0:T(8,128)(2,1)} async-done(((bf16[65536,256]{1,0:T(8,128)(2,1)}), bf16[8192,256]{1,0:T(8,128)(2,1)}) %reduce-scatter.23.cloned.1.call-update) | async-done | bytes 4194320 | tf_op jit(solution)/shard_map/reduce_scatter | solution.py:292
  4164.2 6.2 convert_element_type.192
  (370 shorter events, 156.3 us)
Async XLA Ops:
  7.2 53.5 %all-gather.9.cloned.1.call-start = ((), (), s32[]{:S(2)}) async-start(), calls=%async_computation.8 | async-start | bytes 2621440 | tf_op jit(solution)/shard_map/all_gather | solution.py:219
  7.9 76.5 %all-gather.11.cloned.1.call-start = ((), (), s32[]{:S(2)}) async-start(), calls=%async_computation.9 | async-start | bytes 1769472 | tf_op jit(solution)/shard_map/all_gather | solution.py:199
  9.7 184.8 %all-reduce.8.cloned.1.call-start = ((), (), s32[]{:S(2)}) async-start(), calls=%async_computation.10 | async-start | bytes 8388608 | tf_op jit(solution)/shard_map/psum | solution.py:232
  32.1 52.3 %copy-start.68 = (f32[8,1,128]{2,1,0:T(1,128)}, f32[8,1,128]{2,1,0:T(1,128)S(1)}, u32[]{:S(2)}) copy-start(f32[8,1,128]{2,1,0:T(1,128)S(1)} %convert_element_type.195) | copy-start | bytes 12292
  60.7 46.4 %copy-start.20 = (bf16[256,1024]{1,0:T(8,128)(2,1)}, bf16[256,1024]{1,0:T(8,128)(2,1)S(1)}, u32[]{:S(2)}) copy-start(bf16[256,1024]{1,0:T(8,128)(2,1)S(1)} %all_gather.40) | copy-start | bytes 1572868
  63.5 20.9 copy-start.64
  110.7 19.3 copy-start.7
  110.7 20.1 copy-start.67
  110.7 127.1 %all-gather.13.cloned.1.call-start = ((), (), s32[]{:S(2)}) async-start(), calls=%async_computation.11 | async-start | bytes 1179648 | tf_op jit(solution)/shard_map/all_gather | solution.py:202
  112.3 293.2 %all-gather.15.cloned.1.call-start = ((), (), s32[]{:S(2)}) async-start(), calls=%async_computation.12 | async-start | bytes 1310720 | tf_op jit(solution)/shard_map/all_gather | solution.py:260
  129.9 68.8 %copy-start.60 = (f32[8,1,128]{2,1,0:T(1,128)}, f32[8,1,128]{2,1,0:T(1,128)S(1)}, u32[]{:S(2)}) copy-start(f32[8,1,128]{2,1,0:T(1,128)S(1)} %convert_element_type.196) | copy-start | bytes 12292
  130.6 133.8 %copy-start.50 = (s32[1024,32]{1,0:T(8,128)}, s32[1024,32]{1,0:T(8,128)S(1)}, u32[]{:S(2)}) copy-start(s32[1024,32]{1,0:T(8,128)S(1)} %copy.80) | copy-start | bytes 393220
  130.8 111.4 %copy-start.48 = (s32[1024,32]{1,0:T(8,128)}, s32[1024,32]{1,0:T(8,128)S(1)}, u32[]{:S(2)}) copy-start(s32[1024,32]{1,0:T(8,128)S(1)} %copy.81) | copy-start | bytes 393220
  161.9 79.3 %copy-start.27 = (bf16[2,256,256]{2,1,0:T(8,128)(2,1)}, bf16[2,256,256]{2,1,0:T(8,128)(2,1)S(1)}, u32[]{:S(2)}) copy-start(bf16[2,256,256]{2,1,0:T(8,128)(2,1)S(1)} %all_gather.44) | copy-start | bytes 786436
  198.7 42.2 %copy-start.58 = (f32[1024]{0:T(1024)}, f32[1024]{0:T(1024)S(1)}, u32[]{:S(2)}) copy-start(f32[1024]{0:T(1024)S(1)} %get-tuple-element.526) | copy-start | bytes 12292
  284.7 77.5 %copy-start.63 = (bf16[256,128]{1,0:T(8,128)(2,1)S(1)}, bf16[256,128]{1,0:T(8,128)(2,1)}, u32[]{:S(2)}) copy-start(bf16[256,128]{1,0:T(8,128)(2,1)} %param.33) | copy-start | bytes 196612
  285.7 666.4 %all-gather.17.cloned.1.call-start = ((), (), s32[]{:S(2)}) async-start(), calls=%async_computation.13 | async-start | bytes 37748736 | tf_op jit(solution)/shard_map/all_gather | solution.py:267
  286.3 956.1 %all-gather.19.cloned.1.call-start = ((), (), s32[]{:S(2)}) async-start(), calls=%async_computation.15 | async-start | bytes 2621440 | tf_op jit(solution)/shard_map/all_gather | solution.py:277
  287.0 2725.4 %all-reduce.10.cloned.1.call-start = ((), (), s32[]{:S(2)}) async-start(), calls=%async_computation.16 | async-start | bytes 1048576 | tf_op jit(solution)/shard_map/psum | solution.py:300
  362.1 40.0 copy-start.29
  952.1 290.2 %copy-start.36 = (bf16[256,1024]{1,0:T(8,128)(2,1)S(1)}, bf16[256,1024]{1,0:T(8,128)(2,1)}, u32[]{:S(2)}) copy-start(bf16[256,1024]{1,0:T(8,128)(2,1)} %all_gather.47) | copy-start | bytes 1572868
  1242.3 4.3 copy-start.26
  1242.4 4.3 copy-start.52
  1246.7 1734.0 %copy-start.30 = (bf16[1024,256]{1,0:T(8,128)(2,1)S(1)}, bf16[1024,256]{1,0:T(8,128)(2,1)}, u32[]{:S(2)}) copy-start(bf16[1024,256]{1,0:T(8,128)(2,1)} %copy-done.29) | copy-start | bytes 1572868
  1246.7 1734.0 %copy-start.44 = (bf16[1024,256]{1,0:T(8,128)(2,1)S(1)}, bf16[1024,256]{1,0:T(8,128)(2,1)}, u32[]{:S(2)}) copy-start(bf16[1024,256]{1,0:T(8,128)(2,1)} %get-tuple-element.514) | copy-start | bytes 1572868
  2979.0 35.2 copy-start.8
  2979.0 35.2 copy-start.25
  2980.2 34.5 copy-start.51
  2980.2 147.6 %all-reduce.12.cloned.1.call-start = ((), (), s32[]{:S(2)}) async-start(), calls=%async_computation.17 | async-start | bytes 8388608 | tf_op jit(solution)/shard_map/psum | solution.py:335
  3014.6 10.9 copy-start.28
  3014.6 11.9 copy-start.49
  3026.1 11.9 copy-start.31
  3026.5 12.3 copy-start.14
  3026.6 12.3 copy-start.39
  3042.1 6.5 copy-start.17
  3042.2 582.9 %reduce-scatter.19.cloned.1.call-start = ((), (), s32[]{:S(2)}) async-start(), calls=%async_computation.21 | async-start | bytes 294912 | tf_op jit(solution)/shard_map/reduce_scatter | solution.py:383
  3048.6 577.9 %reduce-scatter.27.cloned.1.call-start = ((), (), s32[]{:S(2)}) async-start(), calls=%async_computation.25 | async-start | bytes 589824
  3051.2 5.7 copy-start.32
  3051.2 5.7 copy-start.34
  3051.2 5.7 copy-start.35
  3053.4 574.7 %reduce-scatter.21.cloned.1.call-start = ((), (), s32[]{:S(2)}) async-start(), calls=%async_computation.22 | async-start | bytes 589824 | tf_op jit(solution)/shard_map/reduce_scatter | solution.py:386
  3056.8 71.0 %copy-start.59 = (f32[1024]{0:T(1024)S(1)}, f32[1024]{0:T(1024)}, u32[]{:S(2)}) copy-start(f32[1024]{0:T(1024)} %copy-done.58) | copy-start | bytes 12292
  3056.8 71.0 %copy-start.61 = (f32[8,1,128]{2,1,0:T(1,128)S(1)}, f32[8,1,128]{2,1,0:T(1,128)}, u32[]{:S(2)}) copy-start(f32[8,1,128]{2,1,0:T(1,128)} %copy-done.60) | copy-start | bytes 12292
  3056.8 572.8 %reduce-scatter.17.cloned.1.call-start = ((), (), s32[]{:S(2)}) async-start(), calls=%async_computation.20 | async-start | bytes 1179648 | tf_op jit(solution)/shard_map/reduce_scatter | solution.py:380
  3059.2 572.2 %reduce-scatter.25.cloned.1.call-start = ((), (), s32[]{:S(2)}) async-start(), calls=%async_computation.24 | async-start | bytes 589824
  3059.3 73.8 %copy-start.71 = (f32[1024]{0:T(1024)S(1)}, f32[1024]{0:T(1024)}, u32[]{:S(2)}) copy-start(f32[1024]{0:T(1024)} %get-tuple-element.525) | copy-start | bytes 12292
  3127.8 5.2 copy-start.3
  3127.8 5.9 copy-start.15
  3133.8 4.6 copy-start.19
  3139.1 4.4 copy-start.1
  3139.1 4.4 copy-start.6
  3139.1 4.4 copy-start.13
  3139.1 4.4 copy-start.43
  3139.1 4.4 copy-start.57
  3143.3 489.8 %all-reduce.14.cloned.1.call-start = ((), (), s32[]{:S(2)}) async-start(), calls=%async_computation.18 | async-start | bytes 4194304 | tf_op jit(solution)/shard_map/psum | solution.py:363
  3177.1 4.8 copy-start.37
  3177.1 4.8 copy-start.38
  3181.8 483.3 %reduce-scatter.13.cloned.1.call-start = ((), (), s32[]{:S(2)}) async-start(), calls=%async_computation.14 | async-start | bytes 2621440 | tf_op jit(solution)/shard_map/reduce_scatter | solution.py:272
  3184.1 483.4 %reduce-scatter.15.cloned.1.call-start = ((), (), s32[]{:S(2)}) async-start(), calls=%async_computation.19 | async-start | bytes 1769472 | tf_op jit(solution)/shard_map/reduce_scatter | solution.py:371
  3184.1 4.7 copy-start.9
  3188.8 975.4 %reduce-scatter.23.cloned.1.call-start = ((), (), s32[]{:S(2)}) async-start(), calls=%async_computation.23 | async-start | bytes 37748736 | tf_op jit(solution)/shard_map/reduce_scatter | solution.py:292
  3625.1 12.1 copy-start.66
  3633.0 5.9 copy-start.73
  3633.0 28.8 copy-start.72
  (34 other events, 68.0 us)
Sparse Core Ops, SparseCore 0:
  9.6 25.5 all-gather.8
  37.7 46.6 all-gather.10
  110.8 83.6 all-reduce.7
  197.4 40.3 all-gather.12
  285.8 15.4 all-gather.14
  302.8 649.3 all-gather.16
  953.8 22.2 all-gather.18
  2980.3 32.1 all-reduce.9
  3042.3 85.4 all-reduce.11
  3131.6 61.4 reduce-scatter.18
  3196.4 60.8 reduce-scatter.26
  3260.9 60.9 reduce-scatter.20
  3325.3 62.4 reduce-scatter.16
  3391.4 60.9 reduce-scatter.24
  3454.6 50.3 all-reduce.13
  3507.5 31.4 reduce-scatter.12
  3542.3 65.4 reduce-scatter.14
  3620.8 543.3 reduce-scatter.22
where the time goes:
time: 4240 us; the launch traced here: 4180 us
  local copies, waits for them, and re-layouts  1880 us (44%)
  waiting for transfers between devices  1230 us (29%)
  matrix products  714 us (17%)
  blocking collectives  237 us (6%)
  other arithmetic  96.4 us (2%)
    gather x4, local copies, waits for them, and re-layouts, one_block(): jnp.take_along_axis(products, jnp.clip(local_row, 0, table_rows - 1), axi...  1590 us
    all_gather x1, waiting for transfers between devices, per_device(): lax.all_gather(memory_values, 'wide', axis=0, tiled=True)  544 us
    reduce_scatter x1, waiting for transfers between devices, per_device(): lax.psum_scatter(row_grads(picks, pick_weights, memory_grad, lax.axis_siz...  495 us
    while x24, local copies, waits for them, and re-layouts  248 us
    dot_general x4, matrix products, one_block(): lax.dot_general(table, bundle[2], (((0,), (0,)), ((), ())), preferred_ele...  203 us
    dot_general x8, matrix products, pick_table(): jnp.einsum('tpa,tpb->tab', first, second, preferred_element_type=jnp.floa...  137 us
    dot_general x4, matrix products, one_block(): lax.dot_general(bundle[1], portion, (((1,), (1,)), ((), ())), preferred_e...  134 us
    dot_general x4, matrix products, one_block(): return jnp.dot(table, portion, preferred_element_type=jnp.float32)  96.7 us
  transfers between devices with their start and end apart: 18, of which 7 were waited for; matrix products, arithmetic and copies ran while one was open for 20% of the time, Pallas kernels for 0%

commit v1 on v0

v1 whole, which is shorter than its diff:
```python
import functools

import jax
import jax.numpy as jnp
from jax import lax
from jax.experimental import pallas as pl
from jax.experimental.pallas import tpu as pltpu
from jax.sharding import PartitionSpec as P

HD = 64
PKH = 4
NKEYS = 256
TOPK = 32
PICKS = 128
LANES = 128


EPSILON = 1e-06
MASKED = -1e30
BF16 = jnp.bfloat16
F32 = jnp.float32
NT = (((1,), (1,)), ((), ()))
TN = (((0,), (0,)), ((), ()))


def norm_rows(activations, gain_row):
    factor = lax.rsqrt(jnp.mean(activations * activations, axis=-1, keepdims=True) + EPSILON)
    return (factor, activations * factor * gain_row)


def norm_back(activations, factor, gain_row, upstream):
    inner_sum = jnp.mean(gain_row * upstream * activations, axis=-1, keepdims=True)
    through = factor * gain_row * upstream - activations * (factor * factor * factor) * inner_sum
    return (through, jnp.sum(upstream * activations * factor, axis=0))


def masked_scores(query_block, key_rows, segment_block, segment_row, offset):
    block_rows = query_block.shape[0]
    positions = jnp.arange(key_rows.shape[0], dtype=jnp.int32)
    scores = jnp.einsum("qhd,khd->hqk", query_block, key_rows, preferred_element_type=jnp.float32)
    scores = scores * query_block.shape[2] ** (-0.5)
    allowed = (positions[None, :] <= (offset + positions[:block_rows])[:, None]) & (
        segment_block[:, None] == segment_row[None, :]
    )
    return jnp.where(allowed[None], scores, MASKED)


def attend_forward(queries, key_rows, value_rows, segment_row):
    length = queries.shape[0]
    block_rows = min(512, length)

    def one_block(number):
        offset = number * block_rows
        query_block = lax.dynamic_slice_in_dim(queries, offset, block_rows, 0)
        segment_block = lax.dynamic_slice_in_dim(segment_row, offset, block_rows, 0)
        scores = masked_scores(query_block, key_rows, segment_block, segment_row, offset)
        row_peak = jnp.max(scores, axis=-1, keepdims=True)
        raised = jnp.exp(scores - row_peak)
        totals = jnp.sum(raised, axis=-1, keepdims=True)
        attention = (raised / totals).astype(jnp.bfloat16)
        mixture = jnp.einsum(
            "hqk,khd->qhd", attention, value_rows, preferred_element_type=jnp.float32
        )
        return (mixture.astype(jnp.bfloat16), (row_peak + jnp.log(totals))[:, :, 0])

    outputs, logsum = lax.map(one_block, jnp.arange(length // block_rows, dtype=jnp.int32))
    head_width = queries.shape[1] * queries.shape[2]
    logsum = jnp.transpose(logsum, (1, 0, 2)).reshape(queries.shape[1], length)
    return (outputs.reshape(length, head_width), logsum)


def attend_backward(queries, key_rows, value_rows, segment_row, logsum, heads_grad):
    length = queries.shape[0]
    block_rows = min(512, length)
    factor = queries.shape[2] ** (-0.5)

    def one_block(running, number):
        key_sum, value_sum = running
        offset = number * block_rows
        query_block = lax.dynamic_slice_in_dim(queries, offset, block_rows, 0)
        segment_block = lax.dynamic_slice_in_dim(segment_row, offset, block_rows, 0)
        grad_block = lax.dynamic_slice_in_dim(heads_grad, offset, block_rows, 0)
        logsum_block = lax.dynamic_slice_in_dim(logsum, offset, block_rows, 1)
        scores = masked_scores(query_block, key_rows, segment_block, segment_row, offset)
        attention = jnp.exp(scores - logsum_block[:, :, None])
        prob_grad = jnp.einsum(
            "qhd,khd->hqk", grad_block, value_rows, preferred_element_type=jnp.float32
        )
        centre = jnp.sum(attention * prob_grad, axis=-1, keepdims=True)
        score_grad = (attention * (prob_grad - centre)).astype(jnp.bfloat16)
        query_grad = (
            jnp.einsum("hqk,khd->qhd", score_grad, key_rows, preferred_element_type=jnp.float32)
            * factor
        )
        key_sum = (
            key_sum
            + jnp.einsum(
                "hqk,qhd->khd", score_grad, query_block, preferred_element_type=jnp.float32
            )
            * factor
        )
        value_sum = value_sum + jnp.einsum(
            "hqk,qhd->khd",
            attention.astype(jnp.bfloat16),
            grad_block,
            preferred_element_type=jnp.float32,
        )
        return ((key_sum, value_sum), query_grad)

    empty_sum = jnp.zeros(key_rows.shape, jnp.float32)
    carried, query_parts = lax.scan(
        one_block, (empty_sum, empty_sum), jnp.arange(length // block_rows, dtype=jnp.int32)
    )
    return (query_parts.reshape(queries.shape), carried[0], carried[1])


def params(mib):
    return pltpu.CompilerParams(vmem_limit_bytes=mib << 20)


def picked_body(base_ref, picks_ref, grad_ref, table_ref, out_ref, *, chunk):
    local = picks_ref[...] - base_ref[0]
    upper = local >> 7
    lower = local & (LANES - 1)
    grads = grad_ref[...]
    total = jnp.zeros(local.shape, F32)
    for start in range(0, table_ref.shape[0], chunk):
        products = lax.dot_general(
            grads, table_ref[pl.ds(start, chunk), :], NT, preferred_element_type=F32
        )
        for lane in range(0, chunk, LANES):
            found = jnp.take_along_axis(products[:, lane : lane + LANES], lower, axis=1)
            total = jnp.where(upper == (start + lane) // LANES, found, total)
    out_ref[...] = total


def picked_products(base, picks, grads, table, rows=256, chunk=1024):
    amount, width = grads.shape
    total = table.shape[0]
    return pl.pallas_call(
        functools.partial(picked_body, chunk=chunk),
        grid=(amount // rows,),
        in_specs=[
            pl.BlockSpec(memory_space=pltpu.SMEM),
            pl.BlockSpec((rows, PICKS), lambda i: (i, 0)),
            pl.BlockSpec((rows, width), lambda i: (i, 0)),
            pl.BlockSpec((total, width), lambda i: (0, 0)),
        ],
        out_specs=pl.BlockSpec((rows, PICKS), lambda i: (i, 0)),
        out_shape=jax.ShapeDtypeStruct((amount, PICKS), F32),
        compiler_params=params(48),
        cost_estimate=pl.CostEstimate(
            flops=8 * amount * total * width, bytes_accessed=amount * width * 4, transcendentals=0
        ),
        name="picked_products",
    )(base, picks, grads, table)


def bag_body(
    base_ref, picks_ref, weight_ref, table_ref, out_ref, keep_ref, held, upper, lower, weights,
    *, chunk, unroll
):
    rows = picks_ref.shape[0]
    groups = table_ref.shape[0] // LANES
    local = picks_ref[...] - base_ref[0]
    upper[...] = (local >> 7).astype(F32)
    lower[...] = (local & (LANES - 1)).astype(F32)
    weights[...] = weight_ref[...].astype(F32)
    group_ids = lax.broadcasted_iota(jnp.int32, (groups, LANES), 0).astype(F32).astype(BF16)
    lane_ids = lax.broadcasted_iota(jnp.int32, (LANES, LANES), 0).astype(F32).astype(BF16)
    zero = jnp.zeros((), BF16)
    one = jnp.ones((), BF16)

    def spread_row(ref, token, count):
        row = jnp.broadcast_to(ref[pl.ds(token, 1), :], (16, LANES)).astype(BF16)
        return jnp.concatenate([row] * (count // 16), axis=0)

    def some_tokens(step, carried):
        for slot in range(unroll):
            token = step * unroll + slot
            first = jnp.where(
                group_ids == spread_row(upper, token, groups),
                spread_row(weights, token, groups),
                zero,
            )
            second = jnp.where(lane_ids == spread_row(lower, token, LANES), one, zero)
            held[pl.ds(token, groups, stride=rows), :] = lax.dot_general(
                first, second, NT, preferred_element_type=F32
            )
        return carried

    lax.fori_loop(0, rows // unroll, some_tokens, 0)
    total = jnp.zeros(out_ref.shape, F32)
    for start in range(0, table_ref.shape[0], chunk):
        parts = [
            held[pl.ds(group * rows, rows), :].astype(BF16)
            for group in range(start // LANES, (start + chunk) // LANES)
        ]
        block = jnp.concatenate(parts, axis=1)
        keep_ref[:, pl.ds(start, chunk)] = block
        total = total + jnp.dot(
            block, table_ref[pl.ds(start, chunk), :], preferred_element_type=F32
        )
    out_ref[...] = total.astype(out_ref.dtype)


def bag_sums(base, picks, weights, table, rows=256, chunk=1024, unroll=32):
    amount = picks.shape[0]
    total, width = table.shape
    return pl.pallas_call(
        functools.partial(bag_body, chunk=chunk, unroll=unroll),
        grid=(amount // rows,),
        in_specs=[
            pl.BlockSpec(memory_space=pltpu.SMEM),
            pl.BlockSpec((rows, PICKS), lambda i: (i, 0)),
            pl.BlockSpec((rows, PICKS), lambda i: (i, 0)),
            pl.BlockSpec((total, width), lambda i: (0, 0)),
        ],
        out_specs=[
            pl.BlockSpec((rows, width), lambda i: (i, 0)),
            pl.BlockSpec((rows, total), lambda i: (i, 0)),
        ],
        out_shape=[
            jax.ShapeDtypeStruct((amount, width), BF16),
            jax.ShapeDtypeStruct((amount, total), BF16),
        ],
        scratch_shapes=[pltpu.VMEM((total // LANES * rows, LANES), F32)]
        + [pltpu.VMEM((rows, LANES), F32)] * 3,
        compiler_params=params(56),
        cost_estimate=pl.CostEstimate(
            flops=12 * amount * total * width, bytes_accessed=amount * total * 2, transcendentals=0
        ),
        name="bag_sums",
    )(base, picks, weights, table)


def unit_indices(picks, number):
    return jnp.where(number % 2 == 0, picks >> 8, picks & (NKEYS - 1))


def scores_body(column_ref, picks_ref, query_ref, keys_ref, out_ref, *, units):
    picks = picks_ref[...]
    lanes = lax.broadcasted_iota(jnp.int32, picks.shape, 1)
    total = jnp.zeros(picks.shape, F32)
    for unit in range(units):
        number = column_ref[0] * units + unit
        index = unit_indices(picks, number)
        scores = lax.dot_general(
            query_ref[:, unit * NKEYS : (unit + 1) * NKEYS],
            keys_ref[unit],
            NT,
            preferred_element_type=F32,
        )
        lower = index & (LANES - 1)
        low_part = jnp.take_along_axis(scores[:, :LANES], lower, axis=1)
        high_part = jnp.take_along_axis(scores[:, LANES:], lower, axis=1)
        found = jnp.where(index < LANES, low_part, high_part)
        total = total + jnp.where(lanes // TOPK == number // 2, found, 0.0)
    out_ref[...] = total


def pick_scores(column, picks, queries, keys, rows=256):
    amount = picks.shape[0]
    units = keys.shape[0]
    return pl.pallas_call(
        functools.partial(scores_body, units=units),
        grid=(amount // rows,),
        in_specs=[
            pl.BlockSpec(memory_space=pltpu.SMEM),
            pl.BlockSpec((rows, PICKS), lambda i: (i, 0)),
            pl.BlockSpec((rows, units * NKEYS), lambda i: (i, 0)),
            pl.BlockSpec(keys.shape, lambda i: (0, 0, 0)),
        ],
        out_specs=pl.BlockSpec((rows, PICKS), lambda i: (i, 0)),
        out_shape=jax.ShapeDtypeStruct((amount, PICKS), F32),
        compiler_params=params(32),
        name="pick_scores",
    )(column, picks, queries, keys)


def spread_body(
    column_ref, picks_ref, grad_ref, query_ref, keys_ref, out_ref, sum_ref, held_index, held_grad,
    *, units
):
    rows = picks_ref.shape[0]
    held_grad[...] = grad_ref[...].astype(F32).T

    @pl.when(pl.program_id(0) == 0)
    def clear():
        sum_ref[...] = jnp.zeros_like(sum_ref)

    key_ids = lax.broadcasted_iota(jnp.int32, (NKEYS, rows), 0)
    for unit in range(units):
        number = column_ref[0] * units + unit
        first = (number // 2) * TOPK
        held_index[...] = unit_indices(picks_ref[...], number).T
        table = jnp.zeros((NKEYS, rows), F32)
        for slot in range(TOPK):
            index = held_index[pl.ds(first + slot, 1), :]
            grad = held_grad[pl.ds(first + slot, 1), :]
            table = table + jnp.where(key_ids == index, grad, 0.0)
        table = table.astype(BF16)
        span = slice(unit * NKEYS, (unit + 1) * NKEYS)
        out_ref[:, span] = lax.dot_general(
            table, keys_ref[unit], TN, preferred_element_type=F32
        ).astype(BF16)
        sum_ref[unit] += jnp.dot(table, query_ref[:, span], preferred_element_type=F32)


def spread_grads(column, picks, grads, queries, keys, rows=128):
    amount = picks.shape[0]
    units = keys.shape[0]
    return pl.pallas_call(
        functools.partial(spread_body, units=units),
        grid=(amount // rows,),
        in_specs=[
            pl.BlockSpec(memory_space=pltpu.SMEM),
            pl.BlockSpec((rows, PICKS), lambda i: (i, 0)),
            pl.BlockSpec((rows, PICKS), lambda i: (i, 0)),
            pl.BlockSpec((rows, units * NKEYS), lambda i: (i, 0)),
            pl.BlockSpec(keys.shape, lambda i: (0, 0, 0)),
        ],
        out_specs=[
            pl.BlockSpec((rows, units * NKEYS), lambda i: (i, 0)),
            pl.BlockSpec(keys.shape, lambda i: (0, 0, 0)),
        ],
        out_shape=[
            jax.ShapeDtypeStruct((amount, units * NKEYS), BF16),
            jax.ShapeDtypeStruct(keys.shape, F32),
        ],
        scratch_shapes=[pltpu.VMEM((PICKS, rows), jnp.int32), pltpu.VMEM((PICKS, rows), F32)],
        compiler_params=params(32),
        name="spread_grads",
    )(column, picks, grads, queries, keys)


def gather_wide(block):
    return lax.all_gather(block, "wide")


def sum_wide(block):
    return lax.psum_scatter(block, "wide", scatter_dimension=0)


def rows_last(blocks):
    parts, rows, columns = blocks.shape
    return jnp.transpose(blocks, (1, 0, 2)).reshape(rows, parts * columns)


def columns_first(block, parts):
    rows = block.shape[0]
    return jnp.transpose(block.reshape(rows, parts, -1), (1, 0, 2))


def per_device(
    inputs,
    segments,
    attn_gain,
    qkv_weight,
    out_weight,
    memory_gain,
    query_weight,
    sub_keys,
    gate_weight,
    memory_values,
    memory_out,
    picks,
    cotangent,
):
    length, width = inputs.shape
    shards = lax.axis_size("wide")
    column = lax.axis_index("narrow")
    column_ref = column.astype(jnp.int32).reshape(1)
    shard_rows = memory_values.shape[0]
    base = (lax.axis_index("wide") * shard_rows).astype(jnp.int32).reshape(1)
    units = sub_keys.shape[0]
    model = qkv_weight.shape[0] * shards

    rows_one = lax.all_gather(inputs, "narrow", axis=1, tiled=True).astype(F32)
    gains = gather_wide(jnp.stack([attn_gain, memory_gain])).astype(F32)
    gain_one = gains[:, 0].reshape(model)
    gain_two = gains[:, 1].reshape(model)
    qkv_full = gather_wide(qkv_weight).reshape(model, 3, width)
    out_full = rows_last(gather_wide(out_weight))
    query_full = gather_wide(query_weight.reshape(-1, units * NKEYS)).reshape(model, units * NKEYS)
    gate_full = gather_wide(gate_weight).reshape(model, width)
    keys_full = jnp.transpose(gather_wide(sub_keys), (1, 0, 2, 3)).reshape(units, NKEYS, NKEYS)
    mixer_full = rows_last(gather_wide(memory_out))
    upstream = lax.all_gather(cotangent, "narrow", axis=1, tiled=True)
    all_picks = gather_wide(picks).reshape(shards * length, PICKS)

    factor_one, normed = norm_rows(rows_one, gain_one)
    normed = normed.astype(BF16)
    mixture = jnp.einsum("td,djc->tjc", normed, qkv_full, preferred_element_type=F32).astype(BF16)
    head_count = width // HD
    queries = mixture[:, 0].reshape(length, head_count, HD)
    key_rows = mixture[:, 1].reshape(length, head_count, HD)
    value_rows = mixture[:, 2].reshape(length, head_count, HD)
    segment_row = segments[0]
    head_rows, logsum = attend_forward(queries, key_rows, value_rows, segment_row)
    branch_part = jnp.dot(head_rows, out_full, preferred_element_type=F32).astype(BF16)
    hidden = rows_one + lax.psum(branch_part, "narrow").astype(F32)
    factor_two, second = norm_rows(hidden, gain_two)
    second = second.astype(BF16)

    gate_value = jnp.dot(second, gate_full, preferred_element_type=F32)
    gate_act = jax.nn.silu(gate_value)
    product_grad = lax.dot_general(upstream, mixer_full, NT, preferred_element_type=F32)
    memory_grad = (product_grad * gate_act).astype(BF16)
    all_grads = gather_wide(memory_grad).reshape(shards * length, width)

    memory_query = jnp.dot(second, query_full, preferred_element_type=F32).astype(BF16)
    own_scores = pick_scores(column_ref, picks, memory_query, keys_full)
    mem_scores = lax.psum(own_scores, "narrow").reshape(length, PKH, TOPK)
    score_peak = jnp.max(mem_scores, axis=-1, keepdims=True)
    raised = jnp.exp(mem_scores - score_peak)
    mem_probs = raised / jnp.sum(raised, axis=-1, keepdims=True)
    pick_weights = mem_probs.astype(BF16).reshape(length, PICKS)
    all_weights = gather_wide(pick_weights).reshape(shards * length, PICKS)

    pick_part = picked_products(base, all_picks, all_grads, memory_values).astype(BF16)
    memory_part, tables = bag_sums(base, all_picks, all_weights, memory_values)
    pick_own = sum_wide(pick_part.reshape(shards, length, PICKS)).astype(F32)
    memory = sum_wide(memory_part.reshape(shards, length, width)).astype(F32)
    values_grad = lax.dot_general(tables, all_grads, TN, preferred_element_type=F32)

    product = (gate_act * memory).astype(BF16)
    mixer_part = jnp.dot(product, mixer_full, preferred_element_type=F32)
    mixer_sum = lax.psum_scatter(
        mixer_part.astype(BF16), "narrow", scatter_dimension=1, tiled=True
    ).astype(F32)
    own_hidden = lax.dynamic_slice_in_dim(hidden, column * width, width, 1)
    outputs = (own_hidden + mixer_sum).astype(BF16)
    mixer_grad = lax.dot_general(product, upstream, TN, preferred_element_type=F32)
    sigmoid = jax.nn.sigmoid(gate_value)
    gate_rows_grad = (
        product_grad * memory * sigmoid * (1.0 + gate_value * (1.0 - sigmoid))
    ).astype(BF16)

    pick_own, mem_probs = lax.optimization_barrier((pick_own, mem_probs))
    pick_grad = lax.psum(pick_own, "narrow").reshape(length, PKH, TOPK)
    centre = jnp.sum(mem_probs * pick_grad, axis=-1, keepdims=True)
    score_grad = (mem_probs * (pick_grad - centre)).astype(BF16).reshape(length, PICKS)
    memory_query_grad, key_grad = spread_grads(
        column_ref, picks, score_grad, memory_query, keys_full
    )
    query_weight_grad = lax.dot_general(second, memory_query_grad, TN, preferred_element_type=F32)
    gate_weight_grad = lax.dot_general(second, gate_rows_grad, TN, preferred_element_type=F32)
    second_part = lax.dot_general(gate_rows_grad, gate_full, NT, preferred_element_type=F32)
    second_part = second_part + lax.dot_general(
        memory_query_grad, query_full, NT, preferred_element_type=F32
    )
    second_grad = lax.psum(second_part.astype(BF16), "narrow").astype(F32)
    through_two, gain_two_part = norm_back(hidden, factor_two, gain_two, second_grad)
    hidden_grad = upstream.astype(F32) + through_two
    branch_grad = hidden_grad.astype(BF16)
    out_weight_grad = lax.dot_general(head_rows, branch_grad, TN, preferred_element_type=F32)
    heads_grad = lax.dot_general(branch_grad, out_full, NT, preferred_element_type=F32)
    heads_grad = heads_grad.astype(BF16).reshape(length, head_count, HD)
    query_back, key_back, value_back = attend_backward(
        queries, key_rows, value_rows, segment_row, logsum, heads_grad
    )
    mixed_grad = jnp.stack(
        [
            query_back.reshape(length, width),
            key_back.reshape(length, width),
            value_back.reshape(length, width),
        ],
        axis=1,
    ).astype(BF16)
    qkv_weight_grad = jnp.einsum("td,tjc->djc", normed, mixed_grad, preferred_element_type=F32)
    normed_part = jnp.einsum("tjc,djc->td", mixed_grad, qkv_full, preferred_element_type=F32)
    normed_grad = lax.psum(normed_part.astype(BF16), "narrow").astype(F32)
    through_one, gain_one_part = norm_back(rows_one, factor_one, gain_one, normed_grad)
    input_full = hidden_grad + through_one
    input_grad = lax.dynamic_slice_in_dim(input_full, column * width, width, 1)

    gain_sums = sum_wide(
        jnp.stack([gain_one_part, gain_two_part], axis=1).astype(BF16).reshape(shards, -1, 2)
    ).astype(F32)
    qkv_sum = sum_wide(qkv_weight_grad.astype(BF16).reshape(shards, -1, 3, width)).astype(F32)
    out_sum = sum_wide(columns_first(out_weight_grad.astype(BF16), shards)).astype(F32)
    query_sum = sum_wide(query_weight_grad.astype(BF16).reshape(shards, -1, units, NKEYS))
    key_sum = sum_wide(
        jnp.transpose(key_grad.astype(BF16).reshape(units, shards, -1, NKEYS), (1, 0, 2, 3))
    ).astype(F32)
    gate_sum = sum_wide(gate_weight_grad.astype(BF16).reshape(shards, -1, width)).astype(F32)
    mixer_grad_sum = sum_wide(columns_first(mixer_grad.astype(BF16), shards)).astype(F32)
    return (
        outputs,
        input_grad,
        gain_sums[:, 0],
        qkv_sum,
        out_sum,
        gain_sums[:, 1],
        query_sum.astype(F32),
        key_sum,
        gate_sum,
        values_grad,
        mixer_grad_sum,
    )


def solution(mesh):
    return jax.shard_map(
        per_device,
        mesh=mesh,
        in_specs=(
            P("wide", "narrow"),
            P("wide", None),
            P("wide"),
            P("wide", None, "narrow"),
            P("narrow", "wide"),
            P("wide"),
            P("wide", "narrow", None),
            P("narrow", "wide", None),
            P("wide", "narrow"),
            P("wide", "narrow"),
            P("narrow", "wide"),
            P("wide", None),
            P("wide", "narrow"),
        ),
        out_specs=(
            P("wide", "narrow"),
            P("wide", "narrow"),
            P("wide"),
            P("wide", None, "narrow"),
            P("narrow", "wide"),
            P("wide"),
            P("wide", "narrow", None),
            P("narrow", "wide", None),
            P("wide", "narrow"),
            P("wide", "narrow"),
            P("narrow", "wide"),
        ),
        check_vma=False,
    )
```

time: 4240 us -> 1720 us (0.41); the launches traced: 4180 us -> 1720 us
  local copies, waits for them, and re-layouts: 1880 us -> 36.2 us
  matrix products: 714 us -> 145 us
  Pallas kernels: 0 us -> 520 us
  waiting for transfers between devices: 1230 us -> 763 us
  blocking collectives: 237 us -> 170 us
    gather x4 -> x0, local copies, waits for them, and re-layouts: 1590 us -> none  [one_block(): jnp.take_along_axis(products, jnp.clip(local_row, 0, table_rows - 1), axi...]
    dot_general x45 -> x16, matrix products: 685 us -> 100 us  [the longest x1 53.1 us: per_device(): lax.dot_general(tables, all_grads, TN, preferred_element_type=F32)]
    pallas_call x0 -> x4, Pallas kernels: none -> 520 us  [the longest x1 315 us: bag_sums(): pl.pallas_call(functools.partial(bag_body, chunk=chunk, unroll=unroll), g...]
    all_gather x5 -> x6, waiting for transfers between devices: 601 us -> 248 us  [the longest x5 248 us: gather_wide(): return lax.all_gather(block, 'wide')]
    while x25 -> x20, local copies, waits for them, and re-layouts: 248 us -> 0.4 us
    reduce_scatter x6 -> x9, waiting for transfers between devices: 495 us -> 342 us  [the longest x8 311 us: sum_wide(): return lax.psum_scatter(block, 'wide', scatter_dimension=0)]
    all_gather x6 -> x5, blocking collectives: 215 us -> 151 us  [gather_wide(): return lax.all_gather(block, 'wide')]
    psum x4 -> x5, waiting for transfers between devices: 130 us -> 170 us  [the longest x1 51.3 us: per_device(): normed_grad = lax.psum(normed_part.astype(BF16), 'narrow').astype(F32)]
  transfers between devices with their start and end apart: 18 -> 21, of which waited for: 7 -> 18; matrix products, arithmetic and copies ran while one was open for 20% -> 11% of each run, Pallas kernels for 0% -> 18%
where the time goes in v1:
time: 1720 us
  waiting for transfers between devices  763 us (44%)
  Pallas kernels  520 us (30%)
  blocking collectives  170 us (10%)
  matrix products  145 us (8%)
  other arithmetic  61 us (4%)
  local copies, waits for them, and re-layouts  36.2 us (2%)
    pallas_call x1, Pallas kernels, bag_sums(): pl.pallas_call(functools.partial(bag_body, chunk=chunk, unroll=unroll), g...  315 us
    reduce_scatter x8, waiting for transfers between devices, sum_wide(): return lax.psum_scatter(block, 'wide', scatter_dimension=0)  311 us
    all_gather x5, waiting for transfers between devices, gather_wide(): return lax.all_gather(block, 'wide')  248 us
    pallas_call x1, Pallas kernels, picked_products(): pl.pallas_call(functools.partial(picked_body, chunk=chunk), grid=(amount...  191 us
    all_gather x5, blocking collectives, gather_wide(): return lax.all_gather(block, 'wide')  151 us
    dot_general x1, matrix products, per_device(): lax.dot_general(tables, all_grads, TN, preferred_element_type=F32)  53.1 us
    psum x1, waiting for transfers between devices, per_device(): normed_grad = lax.psum(normed_part.astype(BF16), 'narrow').astype(F32)  51.3 us
    psum x1, waiting for transfers between devices, per_device(): second_grad = lax.psum(second_part.astype(BF16), 'narrow').astype(F32)  39.9 us
  transfers between devices with their start and end apart: 21, of which 18 were waited for; matrix products, arithmetic and copies ran while one was open for 11% of the time, Pallas kernels for 18%

profile of v1, /device:TPU:0, one launch (start us, length us, event | category | flops | bytes accessed | tf_op | source)
XLA Modules:
  0.0 1715.4 jit_solution(15581792421057084327)
XLA Ops:
  9.8 33.3 %all-gather.2 = bf16[2048,128]{1,0:T(8,128)(2,1)S(1)} all-gather(bf16[256,128]{1,0:T(8,128)(2,1)} %param.21), channel_id=4, replica_groups=mesh['wide'=8,'narrow'=4] {'wide'}, dimensions={0}, use_global_device_ids=true | all-gather | bytes 589824 | tf_op jit(solution)/shard_map/all_gather | solution.py:338
  44.0 20.5 %all-gather.9 = bf16[8,2,128]{2,1,0:T(2,128)(2,1)S(1)} all-gather(bf16[1,2,128]{2,1,0:T(2,128)(2,1)S(1)} %maximum_bitcast_fusion), channel_id=2, replica_groups=mesh['wide'=8,'narrow'=4] {'wide'}, dimensions={0}, use_global_device_ids=true | all-gather | bytes 4608 | tf_op jit(solution)/shard_map/all_gather | solution.py:338
  67.3 15.7 all-gather.24.cloned.1.call-done
  83.1 4.0 convolution_convert_fusion.3
  87.2 17.9 %while.27 = (s32[]{:T(128)}, bf16[2,512,4,64]{1,3,2,0:T(8,128)(2,1)S(1)}, f32[2,4,512]{2,1,0:T(4,128)S(1)}, s32[2]{0:T(128)S(1)}, s32[1024]{0:T(1024)S(1)}, /*in...) while((s32[]{:T(128)}, ...), condition=%wide.region_4.5_spmd, body=%wide.region_1.4_spmd.sunk | while | flops 563739136 | bytes 28922060 | solution.py:66
  90.8 2.3 fusion.138
  93.1 3.0 fusion.139
  99.7 2.3 fusion.138
  102.1 3.0 fusion.139
  113.8 31.0 %all-gather.5 = bf16[16,32,256]{2,1,0:T(8,128)(2,1)S(1)} all-gather(bf16[2,32,256]{2,1,0:T(8,128)(2,1)S(1)} %copy-done.58), channel_id=7, replica_groups=mesh['wide'=8,'narrow'=4] {'wide'}, dimensions={0}, use_global_device_ids=true | all-gather | bytes 294912 | tf_op jit(solution)/shard_map/all_gather | solution.py:338
  144.8 17.8 %all-reduce.7.cloned.1.call-done = bf16[1024,1024]{1,0:T(8,128)(2,1)} async-done(((bf16[1024,1024]{1,0:T(8,128)(2,1)}), bf16[1024,1024]{1,0:T(8,128)(2,1)}) %all-reduce.7.cloned.1.call-update) | async-done | bytes 2097168 | tf_op jit(solution)/shard_map/psum | solution.py:402
  162.7 2.5 multiply_reduce_fusion.1
  167.9 37.8 %all-gather.20.cloned.1.call-done = bf16[8,128,512]{2,1,0:T(8,128)(2,1)} async-done(((bf16[1,128,512]{2,1,0:T(8,128)(2,1)}), bf16[8,128,512]{2,1,0:T(8,128)(2,1)}) %all-gather.20.cloned.1.call-update) | async-done | bytes 1048592 | tf_op jit(solution)/shard_map/all_gather | solution.py:338
  205.7 3.2 convolution_convert_fusion.5.query_ref
  208.9 3.1 pick_scores.1
  213.6 31.5 %all-reduce.9.cloned.1.call-done = f32[1024,128]{1,0:T(8,128)} async-done(((f32[1024,128]{1,0:T(8,128)}), f32[1024,128]{1,0:T(8,128)}) %all-reduce.9.cloned.1.call-update) | async-done | bytes 524304 | tf_op jit(solution)/shard_map/psum | solution.py:414
  249.4 71.4 %all-gather.26.cloned.1.call-done.picks_ref = s32[8192,128]{1,0:T(8,128)} async-done(((s32[1024,128]{1,0:T(8,128)}), s32[8192,128]{1,0:T(8,128)}) %all-gather.26.cloned.1.call-update) | async-done | bytes 4194320 | tf_op jit(solution)/shard_map/all_gather | solution.py:338
  320.7 50.5 %all-gather.28.cloned.1.call-done.weight_ref = bf16[8192,128]{1,0:T(8,128)(2,1)} async-done(((bf16[1024,128]{1,0:T(8,128)(2,1)}), bf16[8192,128]{1,0:T(8,128)(2,1)}) %all-gather.28.cloned.1.call-update) | async-done | bytes 2097168 | tf_op jit(solution)/shard_map/all_gather | solution.py:338
  371.2 314.6 %bag_sums.1 = (bf16[8192,256]{1,0:T(8,128)(2,1)}, bf16[8192,8192]{1,0:T(8,128)(2,1)}) custom-call(s32[1]{0:T(128)} %bitcast.18.base_ref, s32[8192,128]{1,0:T(8,128)} %all-gather.26.cloned.1.call-done.picks_ref, bf16[8192,128]{1,0:T(8,128)(2,1)} %all-gather.28.cloned.1.call-done.weight_ref, bf16[8192,256]{1,0:T(8,128)(2,1)} %table_ref.3), custom_call_target="tpu_custom_call" | custom-call | flops 206158430208 | bytes 134217728 | tf_op jit(solution)/shard_map/bag_sums/pallas_call | solution.py:210
  686.7 33.1 %all-gather.7 = bf16[2048,128]{1,0:T(8,128)(2,1)S(1)} all-gather(bf16[256,128]{1,0:T(8,128)(2,1)S(1)} %copy-done.54), channel_id=9, replica_groups=mesh['wide'=8,'narrow'=4] {'wide'}, dimensions={0}, use_global_device_ids=true | all-gather | bytes 589824 | tf_op jit(solution)/shard_map/all_gather | solution.py:338
  720.9 32.6 %all-gather.3 = bf16[1024,256]{1,0:T(8,128)(2,1)S(1)} all-gather(bf16[128,256]{1,0:T(8,128)(2,1)S(1)} %copy-done.55), channel_id=5, replica_groups=mesh['wide'=8,'narrow'=4] {'wide'}, dimensions={0}, use_global_device_ids=true | all-gather | bytes 589824 | tf_op jit(solution)/shard_map/all_gather | solution.py:338
  755.2 28.3 %reduce-scatter.10.cloned.1.call-done = bf16[1,1024,256]{2,1,0:T(8,128)(2,1)} async-done(((bf16[8,1024,256]{2,1,0:T(8,128)(2,1)}), bf16[1,1024,256]{2,1,0:T(8,128)(2,1)}) %reduce-scatter.10.cloned.1.call-update) | async-done | bytes 524304 | tf_op jit(solution)/shard_map/reduce_scatter | solution.py:342
  783.5 4.0 multiply_convert_fusion.2
  787.9 72.8 %all-gather.30.cloned.1.call-done.grad_ref = bf16[8192,256]{1,0:T(8,128)(2,1)} async-done(((bf16[1024,256]{1,0:T(8,128)(2,1)}), bf16[8192,256]{1,0:T(8,128)(2,1)}) %all-gather.30.cloned.1.call-update) | async-done | bytes 4194320 | tf_op jit(solution)/shard_map/all_gather | solution.py:338
  860.7 190.6 %picked_products.1 = f32[8192,128]{1,0:T(8,128)S(1)} custom-call(s32[1]{0:T(128)} %bitcast.18.base_ref, s32[8192,128]{1,0:T(8,128)} %all-gather.26.cloned.1.call-done.picks_ref, bf16[8192,256]{1,0:T(8,128)(2,1)} %all-gather.30.cloned.1.call-done.grad_ref, bf16[8192,256]{1,0:T(8,128)(2,1)} %table_ref.3), custom_call_target="tpu_custom_call" | custom-call | flops 137438953472 | bytes 8388608 | tf_op jit(solution)/shard_map/picked_products/pallas_call | solution.py:140
  1051.6 2.6 copy.81
  1054.4 66.0 %reduce-scatter.14.cloned.1.call-done = bf16[1,1024,128]{1,2,0:T(8,128)(2,1)} async-done(((bf16[8,1024,128]{1,2,0:T(8,128)(2,1)}), bf16[1,1024,128]{1,2,0:T(8,128)(2,1)}) %reduce-scatter.14.cloned.1.call-update) | async-done | bytes 262160 | tf_op jit(solution)/shard_map/reduce_scatter | solution.py:342
  1122.3 2.8 fusion.81
  1125.0 29.7 %all-reduce.11.cloned.1.call-done = f32[1024,4,32]{0,2,1:T(8,128)} async-done(((f32[1024,4,32]{0,2,1:T(8,128)}), f32[1024,4,32]{0,2,1:T(8,128)}) %all-reduce.11.cloned.1.call-update) | async-done | bytes 524304 | tf_op jit(solution)/shard_map/psum | solution.py:441
  1156.3 11.9 spread_grads.1
  1169.0 5.3 add_convert_fusion
  1174.4 2.6 convolution_convert_fusion.7
  1177.1 2.9 fusion.54
  1181.9 3.8 convolution_convert_fusion
  1185.9 39.9 %all-reduce.13.cloned.1.call-done = bf16[1024,1024]{1,0:T(8,128)(2,1)} async-done(((bf16[1024,1024]{1,0:T(8,128)(2,1)}), bf16[1024,1024]{1,0:T(8,128)(2,1)}) %all-reduce.13.cloned.1.call-update) | async-done | bytes 2097168 | tf_op jit(solution)/shard_map/psum | solution.py:453
  1225.9 4.6 fusion.51
  1230.5 3.2 fusion.47
  1237.3 46.9 %while.28 = (s32[]{:T(128)}, f32[1024,4,64]{0,2,1:T(8,128)S(1)}, f32[1024,4,64]{0,2,1:T(8,128)}, bf16[2,512,4,64]{1,3,2,0:T(8,128)(2,1)}, s32[2]{0:T(128)S(1)}, ...) while((s32[]{:T(128)}, f32[1024,4,64]{0,2,1:T(8,128)S(1)}, ...), condition=%wide.region_19.20_spmd.clone, body=%wide.region_17.19_spmd.clone.sunk | while | flops 1376647680 | bytes 145830800 | solution.py:111
  1241.5 3.2 multiply_reduce_fusion.4
  1244.9 3.7 multiply_convert_fusion.4
  1248.6 3.4 fusion.151
  1252.0 4.7 fusion.153
  1256.7 3.6 fusion.152
  1264.5 3.2 multiply_reduce_fusion.4
  1267.8 3.7 multiply_convert_fusion.4
  1271.5 3.4 fusion.151
  1274.9 4.6 fusion.153
  1279.6 4.6 fusion.152
  1290.8 5.1 bitcast_convert_fusion
  1300.9 3.0 fusion.53
  1305.6 2.4 convert_element_type.166
  1309.5 46.0 %reduce-scatter.26.cloned.1.call-done = bf16[1,256,128]{2,1,0:T(8,128)(2,1)} async-done(((bf16[8,256,128]{2,1,0:T(8,128)(2,1)}), bf16[1,256,128]{2,1,0:T(8,128)(2,1)}) %reduce-scatter.26.cloned.1.call-update) | async-done | bytes 65552 | tf_op jit(solution)/shard_map/reduce_scatter | solution.py:342
  1357.1 3.1 convolution_convert_fusion.2
  1361.5 53.1 %fusion.82 = f32[8192,256]{1,0:T(8,128)} fusion(bf16[8192,8192]{1,0:T(8,128)(2,1)} %get-tuple-element.139, bf16[8192,256]{1,0:T(8,128)(2,1)} %all-gather.30.cloned.1.call-done.grad_ref), kind=kOutput, calls=%fused_computation.145 | convolution fusion | flops 34359738368 | bytes 146800640 | tf_op jit(solution)/shard_map/dot_general | solution.py:425
  1414.7 5.3 reduce-scatter.22.cloned.1.call-done
  1421.3 31.6 %reduce-scatter.12.cloned.1.call-done = bf16[1024,256]{1,0:T(8,128)(2,1)} async-done(((bf16[1024,1024]{1,0:T(8,128)(2,1)}), bf16[1024,256]{1,0:T(8,128)(2,1)}) %reduce-scatter.12.cloned.1.call-update) | async-done | bytes 524304 | tf_op jit(solution)/shard_map/reduce_scatter | solution.py:429
  1455.2 51.3 %all-reduce.15.cloned.1.call-done = bf16[1024,1024]{1,0:T(8,128)(2,1)} async-done(((bf16[1024,1024]{1,0:T(8,128)(2,1)}), bf16[1024,1024]{1,0:T(8,128)(2,1)}) %all-reduce.15.cloned.1.call-update) | async-done | bytes 2097168 | tf_op jit(solution)/shard_map/psum | solution.py:473
  1506.6 3.2 fusion.45
  1509.9 64.7 %reduce-scatter.20.cloned.1.call-done = bf16[1,128,2,256]{3,1,2,0:T(8,128)(2,1)} async-done(((bf16[8,128,2,256]{3,1,2,0:T(8,128)(2,1)}), bf16[1,128,2,256]{3,1,2,0:T(8,128)(2,1)}) %reduce-scatter.20.cloned.1.call-update) | async-done | bytes 131088 | tf_op jit(solution)/shard_map/reduce_scatter | solution.py:342
  1576.4 4.1 convert_element_type.194
  1580.5 19.5 %all-reduce = bf16[8,128,2]{1,2,0:T(2,128)(2,1)S(1)} all-reduce(bf16[8,128,2]{1,2,0:T(2,128)(2,1)S(1)} %copy.88), channel_id=14, replica_groups=mesh['wide'=8,'narrow'=4] {'wide'}, use_global_device_ids=true, to_apply=%region_24.25.clone | all-reduce | flops 2048 | bytes 8192
  1601.1 37.5 %reduce-scatter.18.cloned.1.call-done = bf16[1,256,128]{2,1,0:T(8,128)(2,1)} async-done(((bf16[8,256,128]{2,1,0:T(8,128)(2,1)}), bf16[1,256,128]{2,1,0:T(8,128)(2,1)}) %reduce-scatter.18.cloned.1.call-update) | async-done | bytes 65552 | tf_op jit(solution)/shard_map/reduce_scatter | solution.py:342
  1640.2 3.3 dynamic-slice_add_fusion
  1643.5 62.9 %reduce-scatter.16.cloned.1.call-done = bf16[1,128,3,256]{3,1,2,0:T(8,128)(2,1)} async-done(((bf16[8,128,3,256]{3,1,2,0:T(8,128)(2,1)}), bf16[1,128,3,256]{3,1,2,0:T(8,128)(2,1)}) %reduce-scatter.16.cloned.1.call-update) | async-done | bytes 196624 | tf_op jit(solution)/shard_map/reduce_scatter | solution.py:342
  (280 shorter events, 78.5 us)
Async XLA Ops:
  7.2 57.4 %all-gather.18.cloned.1.call-start = ((), (), s32[]{:S(2)}) async-start(), calls=%async_computation.9 | async-start | bytes 2621440 | tf_op jit(solution)/shard_map/all_gather | solution.py:379
  7.9 75.2 %all-gather.24.cloned.1.call-start = ((), (), s32[]{:S(2)}) async-start(), calls=%async_computation.26 | async-start | bytes 1769472 | tf_op jit(solution)/shard_map/all_gather | solution.py:338
  9.7 152.9 %all-reduce.7.cloned.1.call-start = ((), (), s32[]{:S(2)}) async-start(), calls=%async_computation.10 | async-start | bytes 4194304 | tf_op jit(solution)/shard_map/psum | solution.py:402
  43.3 66.8 %copy-start.29 = (bf16[256,8,128]{0,2,1:T(8,128)(2,1)}, bf16[256,8,128]{0,2,1:T(8,128)(2,1)S(1)}, u32[]{:S(2)}) copy-start(bf16[256,8,128]{0,2,1:T(8,128)(2,1)S(1)} %copy.75) | copy-start | bytes 1572868
  64.6 22.5 %copy-start.59 = (f32[8,1,128]{2,1,0:T(1,128)}, f32[8,1,128]{2,1,0:T(1,128)S(1)}, u32[]{:S(2)}) copy-start(f32[8,1,128]{2,1,0:T(1,128)S(1)} %get-tuple-element.251) | copy-start | bytes 12292
  64.6 101.2 %copy-start.52 = (f32[8,1,128]{2,1,0:T(1,128)}, f32[8,1,128]{2,1,0:T(1,128)S(1)}, u32[]{:S(2)}) copy-start(f32[8,1,128]{2,1,0:T(1,128)S(1)} %get-tuple-element.252) | copy-start | bytes 12292
  67.3 19.7 %copy-start.56 = (f32[1024]{0:T(1024)}, f32[1024]{0:T(1024)S(1)}, u32[]{:S(2)}) copy-start(f32[1024]{0:T(1024)S(1)} %get-tuple-element.248) | copy-start | bytes 12292
  83.1 4.1 copy-start.36
  108.1 36.7 %copy-start.10 = (bf16[1024,4,64]{0,2,1:T(8,128)(2,1)}, bf16[1024,4,64]{0,2,1:T(8,128)(2,1)S(1)}, u32[]{:S(2)}) copy-start(bf16[1024,4,64]{0,2,1:T(8,128)(2,1)S(1)} %get-tuple-element.501) | copy-start | bytes 1572868
  108.1 4.9 copy-start.47
  108.1 5.7 copy-start.58
  108.1 54.5 %copy-start.12 = (bf16[1024,1024]{1,0:T(8,128)(2,1)S(1)}, bf16[1024,1024]{1,0:T(8,128)(2,1)}, u32[]{:S(2)}) copy-start(bf16[1024,1024]{1,0:T(8,128)(2,1)} %all-gather.18.cloned.1.call-done) | copy-start | bytes 6291460
  112.9 92.8 %all-gather.20.cloned.1.call-start = ((), (), s32[]{:S(2)}) async-start(), calls=%async_computation.11 | async-start | bytes 1179648 | tf_op jit(solution)/shard_map/all_gather | solution.py:338
  113.8 131.3 %all-reduce.9.cloned.1.call-start = ((), (), s32[]{:S(2)}) async-start(), calls=%async_computation.12 | async-start | bytes 1048576 | tf_op jit(solution)/shard_map/psum | solution.py:414
  144.8 64.0 %copy-start.4 = (bf16[8,2,32,256]{3,2,0,1:T(8,128)(2,1)}, bf16[8,2,32,256]{3,2,0,1:T(8,128)(2,1)S(1)}, u32[]{:S(2)}) copy-start(bf16[8,2,32,256]{3,2,0,1:T(8,128)(2,1)S(1)} %copy.76) | copy-start | bytes 786436
  165.8 43.1 %copy-start.50 = (f32[1024]{0:T(1024)}, f32[1024]{0:T(1024)S(1)}, u32[]{:S(2)}) copy-start(f32[1024]{0:T(1024)S(1)} %get-tuple-element.250) | copy-start | bytes 12292
  213.0 107.7 %all-gather.26.cloned.1.call-start = ((), (), s32[]{:S(2)}) async-start(), calls=%async_computation.27 | async-start | bytes 4718592 | tf_op jit(solution)/shard_map/all_gather | solution.py:338
  213.6 157.7 %all-gather.28.cloned.1.call-start = ((), (), s32[]{:S(2)}) async-start(), calls=%async_computation.28 | async-start | bytes 2359296 | tf_op jit(solution)/shard_map/all_gather | solution.py:338
  246.4 439.4 %copy-start.23 = (f32[1024,128]{0,1:T(8,128)}, f32[1024,128]{0,1:T(8,128)S(1)}, u32[]{:S(2)}) copy-start(f32[1024,128]{0,1:T(8,128)S(1)} %copy.77) | copy-start | bytes 1572868
  246.5 439.4 %copy-start.43 = (f32[1024,4]{0,1:T(4,128)}, f32[1024,4]{0,1:T(4,128)S(1)}, u32[]{:S(2)}) copy-start(f32[1024,4]{0,1:T(4,128)S(1)} %bitcast_reduce_fusion) | copy-start | bytes 49156
  248.6 506.6 %all-gather.22.cloned.1.call-start = ((), (), s32[]{:S(2)}) async-start(), calls=%async_computation.15 | async-start | bytes 2621440 | tf_op jit(solution)/shard_map/all_gather | solution.py:389
  249.3 534.1 %reduce-scatter.10.cloned.1.call-start = ((), (), s32[]{:S(2)}) async-start(), calls=%async_computation.13 | async-start | bytes 4718592 | tf_op jit(solution)/shard_map/reduce_scatter | solution.py:342
  685.9 35.0 %copy-start.55 = (bf16[128,256]{1,0:T(8,128)(2,1)S(1)}, bf16[128,256]{1,0:T(8,128)(2,1)}, u32[]{:S(2)}) copy-start(bf16[128,256]{1,0:T(8,128)(2,1)} %param.25) | copy-start | bytes 196612
  685.9 67.6 %copy-start.33 = (bf16[1024,1024]{1,0:T(8,128)(2,1)S(1)}, bf16[1024,1024]{1,0:T(8,128)(2,1)}, u32[]{:S(2)}) copy-start(bf16[1024,1024]{1,0:T(8,128)(2,1)} %multiply_convert_fusion.1) | copy-start | bytes 6291460
  685.9 174.8 %all-gather.30.cloned.1.call-start = ((), (), s32[]{:S(2)}) async-start(), calls=%async_computation.29 | async-start | bytes 4718592 | tf_op jit(solution)/shard_map/all_gather | solution.py:338
  720.9 62.6 %copy-start.40 = (bf16[256,8,128]{0,2,1:T(8,128)(2,1)S(1)}, bf16[256,8,128]{0,2,1:T(8,128)(2,1)}, u32[]{:S(2)}) copy-start(bf16[256,8,128]{0,2,1:T(8,128)(2,1)} %copy.80) | copy-start | bytes 1572868
  787.5 332.9 %reduce-scatter.14.cloned.1.call-start = ((), (), s32[]{:S(2)}) async-start(), calls=%async_computation.16 | async-start | bytes 2359296 | tf_op jit(solution)/shard_map/reduce_scatter | solution.py:342
  1054.2 68.1 %copy-start.39 = (bf16[1024,256]{1,0:T(8,128)(2,1)S(1)}, bf16[1024,256]{1,0:T(8,128)(2,1)}, u32[]{:S(2)}) copy-start(bf16[1024,256]{1,0:T(8,128)(2,1)} %get-tuple-element.243) | copy-start | bytes 1572868
  1054.2 100.6 %all-reduce.11.cloned.1.call-start = ((), (), s32[]{:S(2)}) async-start(), calls=%async_computation.17 | async-start | bytes 1048576 | tf_op jit(solution)/shard_map/psum | solution.py:441
  1054.4 101.9 %copy-start.1 = (s32[1024,128]{1,0:T(8,128)S(1)}, s32[1024,128]{1,0:T(8,128)}, u32[]{:S(2)}) copy-start(s32[1024,128]{1,0:T(8,128)} %picks_ref.3) | copy-start | bytes 1572868
  1054.4 101.9 %copy-start.3 = (bf16[1024,512]{1,0:T(8,128)(2,1)S(1)}, bf16[1024,512]{1,0:T(8,128)(2,1)}, u32[]{:S(2)}) copy-start(bf16[1024,512]{1,0:T(8,128)(2,1)} %copy-done.2) | copy-start | bytes 3145732
  1054.4 101.9 %copy-start.5 = (bf16[8,2,32,256]{3,2,0,1:T(8,128)(2,1)S(1)}, bf16[8,2,32,256]{3,2,0,1:T(8,128)(2,1)}, u32[]{:S(2)}) copy-start(bf16[8,2,32,256]{3,2,0,1:T(8,128)(2,1)} %copy-done.4) | copy-start | bytes 786436
  1122.2 103.6 %all-reduce.13.cloned.1.call-start = ((), (), s32[]{:S(2)}) async-start(), calls=%async_computation.18 | async-start | bytes 4194304 | tf_op jit(solution)/shard_map/psum | solution.py:453
  1169.0 5.4 copy-start.34
  1174.3 133.7 %reduce-scatter.24.cloned.1.call-start = ((), (), s32[]{:S(2)}) async-start(), calls=%async_computation.24 | async-start | bytes 589824 | tf_op jit(solution)/shard_map/reduce_scatter | solution.py:342
  1177.0 4.0 copy-start.7
  1177.0 178.5 %reduce-scatter.26.cloned.1.call-start = ((), (), s32[]{:S(2)}) async-start(), calls=%async_computation.25 | async-start | bytes 589824 | tf_op jit(solution)/shard_map/reduce_scatter | solution.py:342
  1180.9 239.0 %reduce-scatter.22.cloned.1.call-start = ((), (), s32[]{:S(2)}) async-start(), calls=%async_computation.23 | async-start | bytes 294912 | tf_op jit(solution)/shard_map/reduce_scatter | solution.py:342
  1181.8 271.2 %reduce-scatter.12.cloned.1.call-start = ((), (), s32[]{:S(2)}) async-start(), calls=%async_computation.14 | async-start | bytes 2621440 | tf_op jit(solution)/shard_map/reduce_scatter | solution.py:429
  1181.9 44.0 %copy-start.13 = (bf16[1024,1024]{1,0:T(8,128)(2,1)S(1)}, bf16[1024,1024]{1,0:T(8,128)(2,1)}, u32[]{:S(2)}) copy-start(bf16[1024,1024]{1,0:T(8,128)(2,1)} %all-gather.18.cloned.1.call-done) | copy-start | bytes 6291460
  1181.9 44.0 %copy-start.51 = (f32[1024]{0:T(1024)S(1)}, f32[1024]{0:T(1024)}, u32[]{:S(2)}) copy-start(f32[1024]{0:T(1024)} %copy-done.50) | copy-start | bytes 12292
  1181.9 44.0 %copy-start.53 = (f32[8,1,128]{2,1,0:T(1,128)S(1)}, f32[8,1,128]{2,1,0:T(1,128)}, u32[]{:S(2)}) copy-start(f32[8,1,128]{2,1,0:T(1,128)} %copy-done.52) | copy-start | bytes 12292
  1185.7 44.8 %copy-start.61 = (f32[1024]{0:T(1024)S(1)}, f32[1024]{0:T(1024)}, u32[]{:S(2)}) copy-start(f32[1024]{0:T(1024)} %get-tuple-element.249) | copy-start | bytes 12292
  1185.7 320.9 %all-reduce.15.cloned.1.call-start = ((), (), s32[]{:S(2)}) async-start(), calls=%async_computation.19 | async-start | bytes 4194304 | tf_op jit(solution)/shard_map/psum | solution.py:473
  1225.8 4.7 copy-start.19
  1225.9 4.7 copy-start.22
  1225.9 4.7 copy-start.31
  1230.5 5.2 copy-start.30
  1248.6 8.1 copy-start.9
  1252.0 4.7 copy-start.26
  1271.5 8.0 copy-start.9
  1274.9 4.7 copy-start.26
  1290.8 5.2 copy-start.35
  1296.0 278.6 %reduce-scatter.20.cloned.1.call-start = ((), (), s32[]{:S(2)}) async-start(), calls=%async_computation.22 | async-start | bytes 1179648 | tf_op jit(solution)/shard_map/reduce_scatter | solution.py:342
  1300.8 4.1 copy-start.60
  1300.8 4.2 copy-start.64
  1300.8 4.8 copy-start.14
  1300.8 337.8 %reduce-scatter.18.cloned.1.call-start = ((), (), s32[]{:S(2)}) async-start(), calls=%async_computation.21 | async-start | bytes 589824 | tf_op jit(solution)/shard_map/reduce_scatter | solution.py:342
  1303.9 53.1 %copy-start.38 = (bf16[1024,1,256]{2,0,1:T(8,128)(2,1)S(1)}, bf16[1024,1,256]{2,0,1:T(8,128)(2,1)}, u32[]{:S(2)}) copy-start(bf16[1024,1,256]{2,0,1:T(8,128)(2,1)} %reshape.355) | copy-start | bytes 1572868
  1304.0 53.1 %copy-start.41 = (bf16[1024,1,256]{2,0,1:T(8,128)(2,1)S(1)}, bf16[1024,1,256]{2,0,1:T(8,128)(2,1)}, u32[]{:S(2)}) copy-start(bf16[1024,1,256]{2,0,1:T(8,128)(2,1)} %copy.85) | copy-start | bytes 1572868
  1304.0 53.1 %copy-start.57 = (f32[1024]{0:T(1024)S(1)}, f32[1024]{0:T(1024)}, u32[]{:S(2)}) copy-start(f32[1024]{0:T(1024)} %copy-done.56) | copy-start | bytes 12292
  1304.9 401.6 %reduce-scatter.16.cloned.1.call-start = ((), (), s32[]{:S(2)}) async-start(), calls=%async_computation.20 | async-start | bytes 1769472 | tf_op jit(solution)/shard_map/reduce_scatter | solution.py:342
  1414.7 95.2 %copy-start.63 = (bf16[1024]{0:T(1024)(128)(2,1)S(1)}, bf16[1024]{0:T(1024)(128)(2,1)}, u32[]{:S(2)}) copy-start(bf16[1024]{0:T(1024)(128)(2,1)} %get-tuple-element.190) | copy-start | bytes 6148
  1509.8 130.4 %copy-start.62 = (f32[1024]{0:T(1024)S(1)}, f32[1024]{0:T(1024)}, u32[]{:S(2)}) copy-start(f32[1024]{0:T(1024)} %get-tuple-element.247) | copy-start | bytes 12292
  (27 other events, 59.3 us)
Sparse Core Ops, SparseCore 0:
  9.6 25.5 all-gather.17
  37.7 45.2 all-gather.23
  113.1 49.5 all-reduce.6
  165.4 40.2 all-gather.19
  213.1 31.9 all-reduce.8
  247.3 73.3 all-gather.25
  323.7 47.5 all-gather.27
  372.9 21.3 all-gather.21
  686.1 97.3 reduce-scatter.9
  787.6 73.1 all-gather.29
  1054.3 66.0 reduce-scatter.13
  1122.6 32.0 all-reduce.10
  1174.4 51.3 all-reduce.12
  1229.4 62.0 reduce-scatter.23
  1294.7 60.8 reduce-scatter.25
  1359.7 60.2 reduce-scatter.21
  1422.5 30.4 reduce-scatter.11
  1455.2 51.3 all-reduce.14
  1510.9 63.5 reduce-scatter.19
  1577.7 60.9 reduce-scatter.17
  1642.5 63.9 reduce-scatter.15

commit v2 on v1

--- a/solution.py
+++ b/solution.py
@@ -334,6 +334,39 @@
     )(column, picks, grads, queries, keys)
 
 
+def swap_narrow(block, bit):
+    size = lax.axis_size("narrow")
+    return lax.ppermute(block, "narrow", [(i, i ^ bit) for i in range(size)])
+
+
+def swap_wide(block, bit):
+    size = lax.axis_size("wide")
+    return lax.ppermute(block, "wide", [(i, i ^ bit) for i in range(size)])
+
+
+def gather_by_swaps(block, axis, bits):
+    size = lax.axis_size(axis)
+    me = lax.axis_index(axis)
+    held = {0: block}
+    for bit in bits:
+        moved = {}
+        for offset, part in held.items():
+            moved[offset ^ bit] = lax.ppermute(part, axis, [(i, i ^ bit) for i in range(size)])
+        held.update(moved)
+    stacked = jnp.stack([held[offset] for offset in range(size)])
+    return [lax.dynamic_index_in_dim(stacked, me ^ number, 0, False) for number in range(size)]
+
+
+def bits_down(size):
+    return [1 << level for level in reversed(range(size.bit_length() - 1))]
+
+
+def gather_narrow(block):
+    return jnp.concatenate(
+        gather_by_swaps(block, "narrow", bits_down(lax.axis_size("narrow"))), axis=1
+    )
+
+
 def gather_wide(block):
     return lax.all_gather(block, "wide")
 
@@ -342,14 +375,31 @@
     return lax.psum_scatter(block, "wide", scatter_dimension=0)
 
 
-def rows_last(blocks):
-    parts, rows, columns = blocks.shape
-    return jnp.transpose(blocks, (1, 0, 2)).reshape(rows, parts * columns)
-
-
-def columns_first(block, parts):
-    rows = block.shape[0]
-    return jnp.transpose(block.reshape(rows, parts, -1), (1, 0, 2))
+def lane_blocks(block):
+    return jnp.concatenate(
+        [block[..., start : start + LANES] for start in range(0, block.shape[-1], LANES)], axis=-2
+    )
+
+
+def join_lanes(blocks, rows):
+    count = blocks.shape[-2] // rows
+    return jnp.concatenate(
+        [blocks[..., part * rows : (part + 1) * rows, :] for part in range(count)], axis=-1
+    )
+
+
+def pack(blocks):
+    return jnp.concatenate([lane_blocks(block) for block in blocks], axis=-2)
+
+
+def unpack(packed, shapes):
+    result = []
+    start = 0
+    for rows, columns in shapes:
+        stop = start + rows * columns // LANES
+        result.append(join_lanes(packed[..., start:stop, :], rows))
+        start = stop
+    return result
 
 
 def per_device(
@@ -374,130 +424,188 @@
     shard_rows = memory_values.shape[0]
     base = (lax.axis_index("wide") * shard_rows).astype(jnp.int32).reshape(1)
     units = sub_keys.shape[0]
-    model = qkv_weight.shape[0] * shards
-
-    rows_one = lax.all_gather(inputs, "narrow", axis=1, tiled=True).astype(F32)
-    gains = gather_wide(jnp.stack([attn_gain, memory_gain])).astype(F32)
+    part = qkv_weight.shape[0]
+    model = part * shards
+    key_part = sub_keys.shape[1]
+
+    rows_one = gather_narrow(inputs).astype(F32)
+    first_shapes = [(3 * part, width), (2 * part // LANES, LANES)]
+    first_pack = pack(
+        [
+            jnp.transpose(qkv_weight, (1, 0, 2)).reshape(3 * part, width),
+            jnp.concatenate([attn_gain, memory_gain]).reshape(-1, LANES),
+        ]
+    )
+    qkv_parts, gains = unpack(gather_wide(first_pack), first_shapes)
+    qkv_full = [
+        qkv_parts[:, j * part : (j + 1) * part].reshape(model, width) for j in range(3)
+    ]
+    gains = gains.reshape(shards, 2, part).astype(F32)
     gain_one = gains[:, 0].reshape(model)
     gain_two = gains[:, 1].reshape(model)
-    qkv_full = gather_wide(qkv_weight).reshape(model, 3, width)
-    out_full = rows_last(gather_wide(out_weight))
-    query_full = gather_wide(query_weight.reshape(-1, units * NKEYS)).reshape(model, units * NKEYS)
-    gate_full = gather_wide(gate_weight).reshape(model, width)
-    keys_full = jnp.transpose(gather_wide(sub_keys), (1, 0, 2, 3)).reshape(units, NKEYS, NKEYS)
-    mixer_full = rows_last(gather_wide(memory_out))
-    upstream = lax.all_gather(cotangent, "narrow", axis=1, tiled=True)
-    all_picks = gather_wide(picks).reshape(shards * length, PICKS)
+    second_shapes = [
+        (part, width),
+        (part, width),
+        (part, width),
+        (part, units * NKEYS),
+        (units * key_part, NKEYS),
+    ]
+    second_pack = pack(
+        [
+            out_weight.T,
+            memory_out.T,
+            gate_weight,
+            query_weight.reshape(part, units * NKEYS),
+            sub_keys.reshape(units * key_part, NKEYS),
+        ]
+    )
+    second_pack, first_pack = lax.optimization_barrier((second_pack, first_pack))
+    out_turned, mixer_turned, gate_full, query_full, keys_full = unpack(
+        gather_wide(second_pack), second_shapes
+    )
+    out_turned = out_turned.reshape(model, width)
+    mixer_turned = mixer_turned.reshape(model, width)
+    gate_full = gate_full.reshape(model, width)
+    query_full = query_full.reshape(model, units * NKEYS)
+    keys_full = jnp.transpose(
+        keys_full.reshape(shards, units, key_part, NKEYS), (1, 0, 2, 3)
+    ).reshape(units, NKEYS, NKEYS)
+    out_all = gather_narrow(out_turned)
+    upstream = gather_narrow(cotangent)
+    all_picks = jnp.concatenate(
+        gather_by_swaps(picks.astype(jnp.uint16), "wide", bits_down(shards)[::-1]), axis=0
+    ).astype(jnp.int32)
 
     factor_one, normed = norm_rows(rows_one, gain_one)
     normed = normed.astype(BF16)
-    mixture = jnp.einsum("td,djc->tjc", normed, qkv_full, preferred_element_type=F32).astype(BF16)
+    mixture = [
+        jnp.dot(normed, qkv_full[j], preferred_element_type=F32).astype(BF16) for j in range(3)
+    ]
     head_count = width // HD
-    queries = mixture[:, 0].reshape(length, head_count, HD)
-    key_rows = mixture[:, 1].reshape(length, head_count, HD)
-    value_rows = mixture[:, 2].reshape(length, head_count, HD)
+    queries, key_rows, value_rows = [
+        member.reshape(length, head_count, HD) for member in mixture
+    ]
     segment_row = segments[0]
     head_rows, logsum = attend_forward(queries, key_rows, value_rows, segment_row)
-    branch_part = jnp.dot(head_rows, out_full, preferred_element_type=F32).astype(BF16)
-    hidden = rows_one + lax.psum(branch_part, "narrow").astype(F32)
+    head_all = gather_narrow(head_rows)
+    hidden = rows_one + lax.dot_general(head_all, out_all, NT, preferred_element_type=F32)
     factor_two, second = norm_rows(hidden, gain_two)
     second = second.astype(BF16)
 
     gate_value = jnp.dot(second, gate_full, preferred_element_type=F32)
     gate_act = jax.nn.silu(gate_value)
-    product_grad = lax.dot_general(upstream, mixer_full, NT, preferred_element_type=F32)
+    product_grad = jnp.dot(upstream, mixer_turned, preferred_element_type=F32)
     memory_grad = (product_grad * gate_act).astype(BF16)
     all_grads = gather_wide(memory_grad).reshape(shards * length, width)
 
     memory_query = jnp.dot(second, query_full, preferred_element_type=F32).astype(BF16)
     own_scores = pick_scores(column_ref, picks, memory_query, keys_full)
-    mem_scores = lax.psum(own_scores, "narrow").reshape(length, PKH, TOPK)
+    for bit in bits_down(lax.axis_size("narrow")):
+        own_scores = own_scores + swap_narrow(own_scores, bit)
+    mem_scores = own_scores.reshape(length, PKH, TOPK)
     score_peak = jnp.max(mem_scores, axis=-1, keepdims=True)
     raised = jnp.exp(mem_scores - score_peak)
     mem_probs = raised / jnp.sum(raised, axis=-1, keepdims=True)
     pick_weights = mem_probs.astype(BF16).reshape(length, PICKS)
+    pick_weights, memory_grad = lax.optimization_barrier((pick_weights, memory_grad))
     all_weights = gather_wide(pick_weights).reshape(shards * length, PICKS)
 
     pick_part = picked_products(base, all_picks, all_grads, memory_values).astype(BF16)
+    all_weights, pick_part = lax.optimization_barrier((all_weights, pick_part))
     memory_part, tables = bag_sums(base, all_picks, all_weights, memory_values)
     pick_own = sum_wide(pick_part.reshape(shards, length, PICKS)).astype(F32)
+    memory_part, pick_own = lax.optimization_barrier((memory_part, pick_own))
     memory = sum_wide(memory_part.reshape(shards, length, width)).astype(F32)
+    tables, pick_own = lax.optimization_barrier((tables, pick_own))
     values_grad = lax.dot_general(tables, all_grads, TN, preferred_element_type=F32)
 
+    for bit in bits_down(lax.axis_size("narrow")):
+        pick_own = pick_own + swap_narrow(pick_own, bit)
+    pick_grad = pick_own.reshape(length, PKH, TOPK)
+    centre = jnp.sum(mem_probs * pick_grad, axis=-1, keepdims=True)
+    score_grad = (mem_probs * (pick_grad - centre)).astype(BF16).reshape(length, PICKS)
+    memory_query_grad, key_grad = spread_grads(
+        column_ref, picks, score_grad, memory_query, keys_full
+    )
+
     product = (gate_act * memory).astype(BF16)
-    mixer_part = jnp.dot(product, mixer_full, preferred_element_type=F32)
-    mixer_sum = lax.psum_scatter(
-        mixer_part.astype(BF16), "narrow", scatter_dimension=1, tiled=True
-    ).astype(F32)
-    own_hidden = lax.dynamic_slice_in_dim(hidden, column * width, width, 1)
-    outputs = (own_hidden + mixer_sum).astype(BF16)
-    mixer_grad = lax.dot_general(product, upstream, TN, preferred_element_type=F32)
     sigmoid = jax.nn.sigmoid(gate_value)
     gate_rows_grad = (
         product_grad * memory * sigmoid * (1.0 + gate_value * (1.0 - sigmoid))
     ).astype(BF16)
-
-    pick_own, mem_probs = lax.optimization_barrier((pick_own, mem_probs))
-    pick_grad = lax.psum(pick_own, "narrow").reshape(length, PKH, TOPK)
-    centre = jnp.sum(mem_probs * pick_grad, axis=-1, keepdims=True)
-    score_grad = (mem_probs * (pick_grad - centre)).astype(BF16).reshape(length, PICKS)
-    memory_query_grad, key_grad = spread_grads(
-        column_ref, picks, score_grad, memory_query, keys_full
-    )
-    query_weight_grad = lax.dot_general(second, memory_query_grad, TN, preferred_element_type=F32)
-    gate_weight_grad = lax.dot_general(second, gate_rows_grad, TN, preferred_element_type=F32)
     second_part = lax.dot_general(gate_rows_grad, gate_full, NT, preferred_element_type=F32)
     second_part = second_part + lax.dot_general(
         memory_query_grad, query_full, NT, preferred_element_type=F32
     )
     second_grad = lax.psum(second_part.astype(BF16), "narrow").astype(F32)
+
+    mixer_part = lax.dot_general(product, mixer_turned, NT, preferred_element_type=F32)
+    mixer_part = mixer_part.astype(BF16)
+    mixer_part, second_grad = lax.optimization_barrier((mixer_part, second_grad))
+    mixer_sum = lax.psum_scatter(mixer_part, "narrow", scatter_dimension=1, tiled=True).astype(F32)
+    own_hidden = lax.dynamic_slice_in_dim(hidden, column * width, width, 1)
+    outputs = (own_hidden + mixer_sum).astype(BF16)
+
     through_two, gain_two_part = norm_back(hidden, factor_two, gain_two, second_grad)
     hidden_grad = upstream.astype(F32) + through_two
     branch_grad = hidden_grad.astype(BF16)
-    out_weight_grad = lax.dot_general(head_rows, branch_grad, TN, preferred_element_type=F32)
-    heads_grad = lax.dot_general(branch_grad, out_full, NT, preferred_element_type=F32)
+    heads_grad = jnp.dot(branch_grad, out_turned, preferred_element_type=F32)
     heads_grad = heads_grad.astype(BF16).reshape(length, head_count, HD)
+
+    mixer_grad = lax.dot_general(upstream, product, TN, preferred_element_type=F32)
+    query_grad = lax.dot_general(second, memory_query_grad, TN, preferred_element_type=F32)
+    gate_grad = lax.dot_general(second, gate_rows_grad, TN, preferred_element_type=F32)
+    key_grad = jnp.transpose(
+        key_grad.astype(BF16).reshape(units, shards, key_part, NKEYS), (1, 0, 2, 3)
+    ).reshape(shards, units * key_part, NKEYS)
+
+    def by_shard(block):
+        return block.astype(BF16).reshape(shards, part, block.shape[1])
+
+    early_pack = pack([by_shard(mixer_grad), by_shard(gate_grad), by_shard(query_grad), key_grad])
+    early_pack, heads_grad = lax.optimization_barrier((early_pack, heads_grad))
+    early_sums = sum_wide(early_pack).astype(F32)
+    mixer_sums, gate_sums, query_sums, key_sums = unpack(early_sums, second_shapes[1:])
+
     query_back, key_back, value_back = attend_backward(
         queries, key_rows, value_rows, segment_row, logsum, heads_grad
     )
-    mixed_grad = jnp.stack(
-        [
-            query_back.reshape(length, width),
-            key_back.reshape(length, width),
-            value_back.reshape(length, width),
-        ],
-        axis=1,
+    mixed_grad = [
+        member.reshape(length, width).astype(BF16)
+        for member in (query_back, key_back, value_back)
+    ]
+    normed_part = sum(
+        lax.dot_general(mixed_grad[j], qkv_full[j], NT, preferred_element_type=F32)
+        for j in range(3)
     ).astype(BF16)
-    qkv_weight_grad = jnp.einsum("td,tjc->djc", normed, mixed_grad, preferred_element_type=F32)
-    normed_part = jnp.einsum("tjc,djc->td", mixed_grad, qkv_full, preferred_element_type=F32)
-    normed_grad = lax.psum(normed_part.astype(BF16), "narrow").astype(F32)
+    normed_grad = lax.psum(normed_part, "narrow").astype(F32)
+    out_grad = lax.dot_general(branch_grad, head_rows, TN, preferred_element_type=F32)
+    qkv_grad = [
+        lax.dot_general(normed, mixed_grad[j], TN, preferred_element_type=F32) for j in range(3)
+    ]
     through_one, gain_one_part = norm_back(rows_one, factor_one, gain_one, normed_grad)
     input_full = hidden_grad + through_one
     input_grad = lax.dynamic_slice_in_dim(input_full, column * width, width, 1)
-
-    gain_sums = sum_wide(
-        jnp.stack([gain_one_part, gain_two_part], axis=1).astype(BF16).reshape(shards, -1, 2)
-    ).astype(F32)
-    qkv_sum = sum_wide(qkv_weight_grad.astype(BF16).reshape(shards, -1, 3, width)).astype(F32)
-    out_sum = sum_wide(columns_first(out_weight_grad.astype(BF16), shards)).astype(F32)
-    query_sum = sum_wide(query_weight_grad.astype(BF16).reshape(shards, -1, units, NKEYS))
-    key_sum = sum_wide(
-        jnp.transpose(key_grad.astype(BF16).reshape(units, shards, -1, NKEYS), (1, 0, 2, 3))
-    ).astype(F32)
-    gate_sum = sum_wide(gate_weight_grad.astype(BF16).reshape(shards, -1, width)).astype(F32)
-    mixer_grad_sum = sum_wide(columns_first(mixer_grad.astype(BF16), shards)).astype(F32)
+    gain_parts = jnp.concatenate(
+        [gain_one_part.reshape(shards, 1, part), gain_two_part.reshape(shards, 1, part)], axis=1
+    ).astype(BF16).reshape(shards, -1, LANES)
+    late_pack = pack([by_shard(block) for block in qkv_grad] + [by_shard(out_grad), gain_parts])
+    late_sums = sum_wide(late_pack).astype(F32)
+    late_shapes = [(part, width)] * 4 + [(2 * part // LANES, LANES)]
+    query_sum, key_sum, value_sum, out_sum, gain_sums = unpack(late_sums, late_shapes)
+    gain_sums = gain_sums.reshape(2, part)
     return (
         outputs,
         input_grad,
-        gain_sums[:, 0],
-        qkv_sum,
-        out_sum,
-        gain_sums[:, 1],
-        query_sum.astype(F32),
-        key_sum,
-        gate_sum,
+        gain_sums[0],
+        jnp.stack([query_sum, key_sum, value_sum], axis=1),
+        out_sum.T,
+        gain_sums[1],
+        query_sums.reshape(part, units, NKEYS),
+        key_sums.reshape(units, key_part, NKEYS),
+        gate_sums,
         values_grad,
-        mixer_grad_sum,
+        mixer_sums.T,
     )
 
 

time: 1720 us -> 1220 us (0.71)
  waiting for transfers between devices: 763 us -> 356 us
  blocking collectives: 170 us -> 0 us
  local copies, waits for them, and re-layouts: 36.2 us -> 101 us
    all_gather x5 -> x4, waiting for transfers between devices: 248 us -> 66.9 us  [gather_wide(): return lax.all_gather(block, 'wide')]
    reduce_scatter x8 -> x4, waiting for transfers between devices: 311 us -> 141 us  [sum_wide(): return lax.psum_scatter(block, 'wide', scatter_dimension=0)]
    all_gather x5 -> x0, blocking collectives: 151 us -> none  [gather_wide(): return lax.all_gather(block, 'wide')]
    psum x4 -> x1, waiting for transfers between devices: 130 us -> 24.3 us  [per_device(): normed_grad = lax.psum(normed_part, 'narrow').astype(F32)]
    ppermute x0 -> x23, waiting for transfers between devices: none -> 91 us  [the longest x19 73.4 us: gather_by_swaps(): lax.ppermute(part, axis, [(i, i ^ bit) for i in range(size)])]
    reduce_scatter x1, waiting for transfers between devices: 31.6 us -> 0.01 us  [per_device(): lax.psum_scatter(mixer_part, 'narrow', scatter_dimension=1, tiled=True)]
    unnamed x124 -> x231, local copies, waits for them, and re-layouts: 12.4 us -> 43.6 us
    unnamed x1 -> x0, blocking collectives: 19.5 us -> none
  transfers between devices with their start and end apart: 21 -> 34, of which waited for: 18 -> 19; matrix products, arithmetic and copies ran while one was open for 11% -> 17% of each run, Pallas kernels for 18% -> 43%
where the time goes in v2:
time: 1220 us; the launch traced here: 1210 us
  Pallas kernels  520 us (43%)
  waiting for transfers between devices  356 us (29%)
  matrix products  131 us (11%)
  local copies, waits for them, and re-layouts  101 us (8%)
  other arithmetic  68.6 us (6%)
  starting transfers between devices  16.1 us (1%)
  between operations  15.7 us (1%)
    pallas_call x1, Pallas kernels, bag_sums(): pl.pallas_call(functools.partial(bag_body, chunk=chunk, unroll=unroll), g...  315 us
    pallas_call x1, Pallas kernels, picked_products(): pl.pallas_call(functools.partial(picked_body, chunk=chunk), grid=(amount...  191 us
    reduce_scatter x4, waiting for transfers between devices, sum_wide(): return lax.psum_scatter(block, 'wide', scatter_dimension=0)  141 us
    ppermute x19, waiting for transfers between devices, gather_by_swaps(): lax.ppermute(part, axis, [(i, i ^ bit) for i in range(size)])  73.4 us
    all_gather x4, waiting for transfers between devices, gather_wide(): return lax.all_gather(block, 'wide')  66.9 us
    dot_general x1, matrix products, per_device(): lax.dot_general(tables, all_grads, TN, preferred_element_type=F32)  53.8 us
    unnamed x231, local copies, waits for them, and re-layouts  43.6 us
    psum x1, waiting for transfers between devices, per_device(): second_grad = lax.psum(second_part.astype(BF16), 'narrow').astype(F32)  31.1 us
  transfers between devices with their start and end apart: 34, of which 19 were waited for; matrix products, arithmetic and copies ran while one was open for 17% of the time, Pallas kernels for 43%

profile of v2, /device:TPU:0, one launch (start us, length us, event | category | flops | bytes accessed | tf_op | source)
XLA Modules:
  0.0 1211.9 jit_solution(2546557460224735637)
XLA Ops:
  9.6 3.0 collective-permute-start.1
  13.6 12.0 collective-permute-done.1
  33.9 23.8 %all-gather.16.cloned.1.call-done = bf16[8,770,128]{2,1,0:T(8,128)(2,1)} async-done(((bf16[1,770,128]{2,1,0:T(8,128)(2,1)}), bf16[8,770,128]{2,1,0:T(8,128)(2,1)}) %all-gather.16.cloned.1.call-update) | async-done | bytes 1576976 | tf_op jit(solution)/shard_map/all_gather | solution.py:371
  58.6 4.3 fusion.42
  65.7 18.9 %while.27 = (s32[]{:T(128)}, bf16[2,512,4,64]{1,3,2,0:T(8,128)(2,1)}, f32[2,4,512]{2,1,0:T(4,128)S(1)}, s32[2]{0:T(128)S(1)}, s32[1024]{0:T(1024)S(1)}, /*index=...) while((s32[]{:T(128)}, ...), condition=%wide.region_4.5_spmd, body=%wide.region_1.4_spmd.sunk | while | flops 563739136 | bytes 28922568 | solution.py:66
  69.3 2.3 fusion.178
  71.6 3.6 fusion.179
  78.7 2.3 fusion.178
  81.1 3.6 fusion.179
  90.3 26.6 %all-gather.10.cloned.1.call-done = bf16[11264,128]{0,1:T(8,128)(2,1)} async-done(((bf16[1408,128]{0,1:T(8,128)(2,1)}), bf16[11264,128]{0,1:T(8,128)(2,1)}) %all-gather.10.cloned.1.call-update) | async-done | bytes 2883600 | tf_op jit(solution)/shard_map/all_gather | solution.py:371
  116.9 4.7 copy.130
  121.7 3.0 fusion.88
  131.1 2.2 copy.136
  133.3 2.0 copy.137
  135.4 2.1 copy.138
  143.2 2.4 multiply_reduce_fusion.3
  154.9 5.7 collective-permute-done.9
  164.0 13.0 %collective-permute-done.10 = u16[1024,128]{1,0:T(8,128)(2,1)} collective-permute-done((u16[1024,128]{1,0:T(8,128)(2,1)}, u16[1024,128]{1,0:T(8,128)(2,1)}, u32[]{:S(2)}, u32[]{:S(2)}) %collective-permute-start.10) | collective-permute-done | bytes 262176 | tf_op jit(solution)/shard_map/ppermute | solution.py:354
  178.0 14.0 %collective-permute-done.11 = u16[1024,128]{1,0:T(8,128)(2,1)S(1)} collective-permute-done((u16[1024,128]{1,0:T(8,128)(2,1)}, u16[1024,128]{1,0:T(8,128)(2,1)S(1)}, u32[]{:S(2)}, u32[]{:S(2)}) %collective-permute-start.11) | collective-permute-done | bytes 262176 | tf_op jit(solution)/shard_map/ppermute | solution.py:354
  194.2 14.8 %collective-permute-done.13 = u16[1024,128]{1,0:T(8,128)(2,1)S(1)} collective-permute-done((u16[1024,128]{1,0:T(8,128)(2,1)}, u16[1024,128]{1,0:T(8,128)(2,1)S(1)}, u32[]{:S(2)}, u32[]{:S(2)}) %collective-permute-start.13) | collective-permute-done | bytes 262176 | tf_op jit(solution)/shard_map/ppermute | solution.py:354
  209.1 5.5 collective-permute-done.14
  217.3 2.7 pick_scores.1
  220.1 8.2 collective-permute-done.15
  228.6 2.9 collective-permute-done.16
  232.2 2.3 convert_element_type.169.picks_ref
  236.9 16.5 %all-gather.14.cloned.1.call-done.grad_ref = bf16[8192,256]{1,0:T(8,128)(2,1)} async-done(((bf16[1024,256]{1,0:T(8,128)(2,1)}), bf16[8192,256]{1,0:T(8,128)(2,1)}) %all-gather.14.cloned.1.call-update) | async-done | bytes 4194320 | tf_op jit(solution)/shard_map/all_gather | solution.py:371
  253.4 190.6 %picked_products.1 = f32[8192,128]{1,0:T(8,128)S(1)} custom-call(s32[1]{0:T(128)} %bitcast.49.base_ref, s32[8192,128]{1,0:T(8,128)} %convert_element_type.169.picks_ref, bf16[8192,256]{1,0:T(8,128)(2,1)} %all-gather.14.cloned.1.call-done.grad_ref, bf16[8192,256]{1,0:T(8,128)(2,1)} %table_ref.3), custom_call_target="tpu_custom_call" | custom-call | flops 137438953472 | bytes 8388608 | tf_op jit(solution)/shard_map/picked_products/pallas_call | solution.py:140
  445.6 314.6 %bag_sums.1 = (bf16[8192,256]{1,0:T(8,128)(2,1)}, bf16[8192,8192]{1,0:T(8,128)(2,1)}) custom-call(s32[1]{0:T(128)} %bitcast.49.base_ref, s32[8192,128]{1,0:T(8,128)} %convert_element_type.169.picks_ref, bf16[8192,128]{1,0:T(8,128)(2,1)} %all-gather.12.cloned.1.call-done.weight_ref, bf16[8192,256]{1,0:T(8,128)(2,1)} %table_ref.3), custom_call_target="tpu_custom_call" | custom-call | flops 206158430208 | bytes 134217728 | tf_op jit(solution)/shard_map/bag_sums/pallas_call | solution.py:210
  762.8 12.5 %collective-permute-done.21 = f32[1024,128]{1,0:T(8,128)S(1)} collective-permute-done((f32[1024,128]{1,0:T(8,128)S(1)}, f32[1024,128]{1,0:T(8,128)S(1)}, u32[]{:S(2)}, u32[]{:S(2)}) %collective-permute-start.21) | collective-permute-done | bytes 524320 | tf_op jit(solution)/shard_map/ppermute | solution.py:339
  776.2 2.2 collective-permute-done.22
  778.4 2.1 add.201
  780.5 2.1 copy.140
  782.5 2.1 fusion.39
  784.7 2.0 copy.141
  788.3 12.0 spread_grads.1
  811.2 37.0 %reduce-scatter.8.cloned.1.call-done = bf16[1,1024,256]{2,1,0:T(8,128)(2,1)} async-done(((bf16[8,1024,256]{2,1,0:T(8,128)(2,1)}), bf16[1,1024,256]{2,1,0:T(8,128)(2,1)}) %reduce-scatter.8.cloned.1.call-update) | async-done | bytes 524304 | tf_op jit(solution)/shard_map/reduce_scatter | solution.py:375
  853.1 2.6 add_convert_fusion.1
  867.8 4.6 concatenate.89
  872.4 3.4 convolution_convert_fusion
  875.9 31.1 %all-reduce.3.cloned.1.call-done = bf16[1024,1024]{0,1:T(8,128)(2,1)} async-done(((bf16[1024,1024]{0,1:T(8,128)(2,1)}), bf16[1024,1024]{0,1:T(8,128)(2,1)}) %all-reduce.3.cloned.1.call-update) | async-done | bytes 2097168 | tf_op jit(solution)/shard_map/psum | solution.py:540
  907.0 2.2 convert_element_type.183
  911.0 4.7 subtract_add_fusion
  915.7 2.0 copy-done.12
  919.4 44.9 %while.28 = (s32[]{:T(128)}, f32[1024,4,64]{0,2,1:T(8,128)S(1)}, f32[1024,4,64]{0,2,1:T(8,128)}, bf16[2,512,4,64]{1,3,2,0:T(8,128)(2,1)}, s32[2]{0:T(128)S(1)}, ...) while((s32[]{:T(128)}, f32[1024,4,64]{0,2,1:T(8,128)S(1)}, ...), condition=%wide.region_16.17_spmd.clone, body=%wide.region_14.16_spmd.clone.sunk | while | flops 1376647680 | bytes 143733616 | solution.py:111
  923.0 3.2 multiply_reduce_fusion.6
  926.3 3.7 multiply_convert_fusion.5
  930.0 3.3 fusion.191
  933.3 4.7 fusion.193
  938.0 3.6 fusion.192
  944.7 3.2 multiply_reduce_fusion.6
  948.1 3.7 multiply_convert_fusion.5
  951.8 3.3 fusion.191
  955.1 4.7 fusion.193
  959.7 4.6 fusion.192
  973.4 2.6 fusion.87
  982.8 2.4 convolution_convert_fusion.4
  987.0 2.4 convolution_convert_fusion.5
  991.3 2.3 convolution_convert_fusion.6
  999.1 24.3 %all-reduce.5.cloned.1.call-done = bf16[1024,1024]{0,1:T(8,128)(2,1)} async-done(((bf16[1024,1024]{0,1:T(8,128)(2,1)}), bf16[1024,1024]{0,1:T(8,128)(2,1)}) %all-reduce.5.cloned.1.call-update) | async-done | bytes 2097168 | tf_op jit(solution)/shard_map/psum | solution.py:581
  1023.4 4.6 fusion.45
  1028.2 4.9 concatenate.90
  1033.1 53.8 %fusion.108 = f32[8192,256]{1,0:T(8,128)} fusion(bf16[8192,8192]{1,0:T(8,128)(2,1)} %get-tuple-element.159, bf16[8192,256]{1,0:T(8,128)(2,1)} %all-gather.14.cloned.1.call-done.grad_ref), kind=kOutput, calls=%fused_computation.237 | convolution fusion | flops 34359738368 | bytes 146800640 | tf_op jit(solution)/shard_map/dot_general | solution.py:520
  1093.3 36.7 %reduce-scatter.14.cloned.1.call-done = bf16[1,1152,128]{1,2,0:T(8,128)(2,1)} async-done(((bf16[8,1152,128]{1,2,0:T(8,128)(2,1)}), bf16[1,1152,128]{1,2,0:T(8,128)(2,1)}) %reduce-scatter.14.cloned.1.call-update) | async-done | bytes 294928 | tf_op jit(solution)/shard_map/reduce_scatter | solution.py:375
  1134.1 67.6 %reduce-scatter.12.cloned.1.call-done = bf16[1,1026,128]{1,2,0:T(8,128)(2,1)} async-done(((bf16[8,1026,128]{1,2,0:T(8,128)(2,1)}), bf16[1,1026,128]{1,2,0:T(8,128)(2,1)}) %reduce-scatter.12.cloned.1.call-update) | async-done | bytes 262672 | tf_op jit(solution)/shard_map/reduce_scatter | solution.py:375
  (454 shorter events, 142.0 us)
Async XLA Ops:
  7.2 50.5 %all-gather.16.cloned.1.call-start = ((), (), s32[]{:S(2)}) async-start(), calls=%async_computation.15 | async-start | bytes 1787904 | tf_op jit(solution)/shard_map/all_gather | solution.py:371
  9.6 107.4 %all-gather.10.cloned.1.call-start = ((), (), s32[]{:S(2)}) async-start(), calls=%async_computation.12 | async-start | bytes 3244032 | tf_op jit(solution)/shard_map/all_gather | solution.py:371
  9.6 16.0 %collective-permute-start.1 = (bf16[1024,256]{1,0:T(8,128)(2,1)}, bf16[1024,256]{1,0:T(8,128)(2,1)S(1)}, u32[]{:S(2)}, u32[]{:S(2)}) collective-permute-start(bf16[1024,256]{1,0:T(8,128)(2,1)} %param.17), channel_id=1, source_target_pairs={{0,2},{1,3},{2,0},{3,1},{4,6},{5,7},{6,4},{7,5},{8,10},{9,11},{10,... | collective-permute-start | bytes 1572872 | tf_op jit(solution)/shard_map/ppermute | solution.py:354
  12.6 17.8 %collective-permute-start = (bf16[1024,256]{1,0:T(8,128)(2,1)}, bf16[1024,256]{1,0:T(8,128)(2,1)S(1)}, u32[]{:S(2)}, u32[]{:S(2)}) collective-permute-start(bf16[1024,256]{1,0:T(8,128)(2,1)} %param.17), channel_id=1, source_target_pairs={{0,1},{1,0},{2,3},{3,2},{4,5},{5,4},{6,7},{7,6},{8,9},{9,8},{10,11... | collective-permute-start | bytes 1572872 | tf_op jit(solution)/shard_map/ppermute | solution.py:354
  12.6 77.1 %collective-permute-start.19 = (bf16[1024,256]{1,0:T(8,128)(2,1)}, bf16[1024,256]{1,0:T(8,128)(2,1)}, u32[]{:S(2)}, u32[]{:S(2)}) collective-permute-start(bf16[1024,256]{1,0:T(8,128)(2,1)} %param.29), channel_id=1, source_target_pairs={{0,2},{1,3},{2,0},{3,1},{4,6},{5,7},{6,4},{7,5},{8,10},{9,11},{10,... | collective-permute-start | bytes 1572872 | tf_op jit(solution)/shard_map/ppermute | solution.py:354
  25.6 4.8 collective-permute-start.2
  30.3 223.1 %all-gather.14.cloned.1.call-start = ((), (), s32[]{:S(2)}) async-start(), calls=%async_computation.14 | async-start | bytes 4718592 | tf_op jit(solution)/shard_map/all_gather | solution.py:371
  32.1 111.0 %copy-start.18 = (bf16[1,1024,256]{1,2,0:T(8,128)(2,1)}, bf16[1,1024,256]{1,2,0:T(8,128)(2,1)S(1)}, u32[]{:S(2)}) copy-start(bf16[1,1024,256]{1,2,0:T(8,128)(2,1)S(1)} %copy.120) | copy-start | bytes 1572868
  32.3 110.8 %copy-start.20 = (bf16[1,1024,256]{1,2,0:T(8,128)(2,1)}, bf16[1,1024,256]{1,2,0:T(8,128)(2,1)S(1)}, u32[]{:S(2)}) copy-start(bf16[1,1024,256]{1,2,0:T(8,128)(2,1)S(1)} %copy.121) | copy-start | bytes 1572868
  32.6 110.6 %copy-start.22 = (bf16[1,1024,256]{1,2,0:T(8,128)(2,1)}, bf16[1,1024,256]{1,2,0:T(8,128)(2,1)S(1)}, u32[]{:S(2)}) copy-start(bf16[1,1024,256]{1,2,0:T(8,128)(2,1)S(1)} %copy.122) | copy-start | bytes 1572868
  32.8 30.3 %copy-start.24 = (bf16[1,1024,256]{1,2,0:T(8,128)(2,1)}, bf16[1,1024,256]{1,2,0:T(8,128)(2,1)S(1)}, u32[]{:S(2)}) copy-start(bf16[1,1024,256]{1,2,0:T(8,128)(2,1)S(1)} %copy.119) | copy-start | bytes 1572868
  33.9 29.4 %copy-start.94 = (f32[1024]{0:T(1024)}, f32[1024]{0:T(1024)S(1)}, u32[]{:S(2)}) copy-start(f32[1024]{0:T(1024)S(1)} %get-tuple-element.372) | copy-start | bytes 12292
  58.5 87.7 %copy-start.90 = (f32[8,1,128]{2,1,0:T(1,128)}, f32[8,1,128]{2,1,0:T(1,128)S(1)}, u32[]{:S(2)}) copy-start(f32[8,1,128]{2,1,0:T(1,128)S(1)} %get-tuple-element.369) | copy-start | bytes 12292
  84.6 37.0 %copy-start.86 = (f32[2,4,512]{2,1,0:T(4,128)}, f32[2,4,512]{2,1,0:T(4,128)S(1)}, u32[]{:S(2)}) copy-start(f32[2,4,512]{2,1,0:T(4,128)S(1)} %get-tuple-element.152) | copy-start | bytes 49156
  84.6 40.0 %copy-start.7 = (bf16[1024,4,64]{0,2,1:T(8,128)(2,1)}, bf16[1024,4,64]{0,2,1:T(8,128)(2,1)S(1)}, u32[]{:S(2)}) copy-start(bf16[1024,4,64]{0,2,1:T(8,128)(2,1)S(1)} %get-tuple-element.616) | copy-start | bytes 1572868
  84.6 40.0 %copy-start.14 = (bf16[1024,4,64]{0,2,1:T(8,128)(2,1)}, bf16[1024,4,64]{0,2,1:T(8,128)(2,1)S(1)}, u32[]{:S(2)}) copy-start(bf16[1024,4,64]{0,2,1:T(8,128)(2,1)S(1)} %get-tuple-element.617) | copy-start | bytes 1572868
  84.6 40.0 %copy-start.16 = (bf16[1024,4,64]{0,2,1:T(8,128)(2,1)}, bf16[1024,4,64]{0,2,1:T(8,128)(2,1)S(1)}, u32[]{:S(2)}) copy-start(bf16[1024,4,64]{0,2,1:T(8,128)(2,1)S(1)} %get-tuple-element.618) | copy-start | bytes 1572868
  88.3 38.0 %collective-permute-start.4 = (bf16[1024,256]{0,1:T(8,128)(2,1)}, bf16[1024,256]{0,1:T(8,128)(2,1)}, u32[]{:S(2)}, u32[]{:S(2)}) collective-permute-start(bf16[1024,256]{0,1:T(8,128)(2,1)} %bitcast.149), channel_id=1, source_target_pairs={{0,2},{1,3},{2,0},{3,1},{4,6},{5,7},{6,4},{7,5},{8,10},{9,11},{10,... | collective-permute-start | bytes 1572872 | tf_op jit(solution)/shard_map/ppermute | solution.py:354
  89.8 37.0 %collective-permute-start.18 = (bf16[1024,256]{1,0:T(8,128)(2,1)}, bf16[1024,256]{1,0:T(8,128)(2,1)}, u32[]{:S(2)}, u32[]{:S(2)}) collective-permute-start(bf16[1024,256]{1,0:T(8,128)(2,1)} %param.29), channel_id=1, source_target_pairs={{0,1},{1,0},{2,3},{3,2},{4,5},{5,4},{6,7},{7,6},{8,9},{9,8},{10,11... | collective-permute-start | bytes 1572872 | tf_op jit(solution)/shard_map/ppermute | solution.py:354
  89.8 37.0 %collective-permute-start.20 = (bf16[1024,256]{1,0:T(8,128)(2,1)}, bf16[1024,256]{1,0:T(8,128)(2,1)}, u32[]{:S(2)}, u32[]{:S(2)}) collective-permute-start(bf16[1024,256]{1,0:T(8,128)(2,1)} %collective-permute-done.19), channel_id=1, source_target_pairs={{0,1},{1,0},{2,3},{3,2},{4,5},{5,4},{6,7},{7,6},{8,9},{9,8},{10,11... | collective-permute-start | bytes 1572872 | tf_op jit(solution)/shard_map/ppermute | solution.py:354
  124.7 13.9 %collective-permute-start.7 = (bf16[1024,256]{1,0:T(8,128)(2,1)S(1)}, bf16[1024,256]{1,0:T(8,128)(2,1)}, u32[]{:S(2)}, u32[]{:S(2)}) collective-permute-start(bf16[1024,256]{1,0:T(8,128)(2,1)S(1)} %bitcast.346), channel_id=1, source_target_pairs={{0,2},{1,3},{2,0},{3,1},{4,6},{5,7},{6,4},{7,5},{8,10},{9,11},{10,... | collective-permute-start | bytes 1572872 | tf_op jit(solution)/shard_map/ppermute | solution.py:354
  126.3 12.8 %collective-permute-start.3 = (bf16[1024,256]{0,1:T(8,128)(2,1)}, bf16[1024,256]{0,1:T(8,128)(2,1)}, u32[]{:S(2)}, u32[]{:S(2)}) collective-permute-start(bf16[1024,256]{0,1:T(8,128)(2,1)} %bitcast.149), channel_id=1, source_target_pairs={{0,1},{1,0},{2,3},{3,2},{4,5},{5,4},{6,7},{7,6},{8,9},{9,8},{10,11... | collective-permute-start | bytes 1572872 | tf_op jit(solution)/shard_map/ppermute | solution.py:354
  126.3 12.8 %collective-permute-start.5 = (bf16[1024,256]{0,1:T(8,128)(2,1)}, bf16[1024,256]{0,1:T(8,128)(2,1)}, u32[]{:S(2)}, u32[]{:S(2)}) collective-permute-start(bf16[1024,256]{0,1:T(8,128)(2,1)} %collective-permute-done.4), channel_id=1, source_target_pairs={{0,1},{1,0},{2,3},{3,2},{4,5},{5,4},{6,7},{7,6},{8,9},{9,8},{10,11... | collective-permute-start | bytes 1572872 | tf_op jit(solution)/shard_map/ppermute | solution.py:354
  138.6 2.8 collective-permute-start.6
  138.6 2.9 collective-permute-start.8
  151.1 64.7 %copy-start.76 = (bf16[8,128,128]{2,1,0:T(8,128)(2,1)S(1)}, bf16[8,128,128]{2,1,0:T(8,128)(2,1)}, u32[]{:S(2)}) copy-start(bf16[8,128,128]{2,1,0:T(8,128)(2,1)} %get-tuple-element.289) | copy-start | bytes 786436
  151.1 64.7 %copy-start.77 = (bf16[8,128,128]{2,1,0:T(8,128)(2,1)S(1)}, bf16[8,128,128]{2,1,0:T(8,128)(2,1)}, u32[]{:S(2)}) copy-start(bf16[8,128,128]{2,1,0:T(8,128)(2,1)} %get-tuple-element.290) | copy-start | bytes 786436
  151.1 64.7 %copy-start.78 = (bf16[8,128,128]{2,1,0:T(8,128)(2,1)S(1)}, bf16[8,128,128]{2,1,0:T(8,128)(2,1)}, u32[]{:S(2)}) copy-start(bf16[8,128,128]{2,1,0:T(8,128)(2,1)} %get-tuple-element.291) | copy-start | bytes 786436
  151.1 294.4 %all-gather.12.cloned.1.call-start = ((), (), s32[]{:S(2)}) async-start(), calls=%async_computation.13 | async-start | bytes 2359296 | tf_op jit(solution)/shard_map/all_gather | solution.py:371
  152.0 8.6 collective-permute-start.9
  152.5 24.5 %collective-permute-start.10 = (u16[1024,128]{1,0:T(8,128)(2,1)}, u16[1024,128]{1,0:T(8,128)(2,1)}, u32[]{:S(2)}, u32[]{:S(2)}) collective-permute-start(u16[1024,128]{1,0:T(8,128)(2,1)} %get-tuple-element.281), channel_id=1, source_target_pairs={{0,8},{4,12},{8,0},{12,4},{16,24},{20,28},{24,16},{28,20},{1,9},{5... | collective-permute-start | bytes 786440 | tf_op jit(solution)/shard_map/ppermute | solution.py:354
  154.0 39.1 %collective-permute-start.12 = (u16[1024,128]{1,0:T(8,128)(2,1)}, u16[1024,128]{1,0:T(8,128)(2,1)}, u32[]{:S(2)}, u32[]{:S(2)}) collective-permute-start(u16[1024,128]{1,0:T(8,128)(2,1)} %get-tuple-element.281), channel_id=1, source_target_pairs={{0,16},{4,20},{8,24},{12,28},{16,0},{20,4},{24,8},{28,12},{1,17},{... | collective-permute-start | bytes 786440 | tf_op jit(solution)/shard_map/ppermute | solution.py:354
  154.9 60.9 %copy-start.79 = (bf16[8,128,128]{2,1,0:T(8,128)(2,1)S(1)}, bf16[8,128,128]{2,1,0:T(8,128)(2,1)}, u32[]{:S(2)}) copy-start(bf16[8,128,128]{2,1,0:T(8,128)(2,1)} %get-tuple-element.292) | copy-start | bytes 786436
  154.9 61.1 %copy-start.57 = (bf16[1024,1024]{0,1:T(8,128)(2,1)S(1)}, bf16[1024,1024]{0,1:T(8,128)(2,1)}, u32[]{:S(2)}) copy-start(bf16[1024,1024]{0,1:T(8,128)(2,1)} %copy-done.56) | copy-start | bytes 6291460
  160.6 31.5 %collective-permute-start.11 = (u16[1024,128]{1,0:T(8,128)(2,1)}, u16[1024,128]{1,0:T(8,128)(2,1)S(1)}, u32[]{:S(2)}, u32[]{:S(2)}) collective-permute-start(u16[1024,128]{1,0:T(8,128)(2,1)} %collective-permute-done.9), channel_id=1, source_target_pairs={{0,8},{4,12},{8,0},{12,4},{16,24},{20,28},{24,16},{28,20},{1,9},{5... | collective-permute-start | bytes 786440 | tf_op jit(solution)/shard_map/ppermute | solution.py:354
  162.0 47.0 %collective-permute-start.13 = (u16[1024,128]{1,0:T(8,128)(2,1)}, u16[1024,128]{1,0:T(8,128)(2,1)S(1)}, u32[]{:S(2)}, u32[]{:S(2)}) collective-permute-start(u16[1024,128]{1,0:T(8,128)(2,1)} %collective-permute-done.9), channel_id=1, source_target_pairs={{0,16},{4,20},{8,24},{12,28},{16,0},{20,4},{24,8},{28,12},{1,17},{... | collective-permute-start | bytes 786440 | tf_op jit(solution)/shard_map/ppermute | solution.py:354
  177.0 37.6 %collective-permute-start.14 = (u16[1024,128]{1,0:T(8,128)(2,1)}, u16[1024,128]{1,0:T(8,128)(2,1)S(1)}, u32[]{:S(2)}, u32[]{:S(2)}) collective-permute-start(u16[1024,128]{1,0:T(8,128)(2,1)} %collective-permute-done.10), channel_id=1, source_target_pairs={{0,16},{4,20},{8,24},{12,28},{16,0},{20,4},{24,8},{28,12},{1,17},{... | collective-permute-start | bytes 786440 | tf_op jit(solution)/shard_map/ppermute | solution.py:354
  192.1 36.2 %collective-permute-start.15 = (u16[1024,128]{1,0:T(8,128)(2,1)S(1)}, u16[1024,128]{1,0:T(8,128)(2,1)S(1)}, u32[]{:S(2)}, u32[]{:S(2)}) collective-permute-start(u16[1024,128]{1,0:T(8,128)(2,1)S(1)} %collective-permute-done.11), channel_id=1, source_target_pairs={{0,16},{4,20},{8,24},{12,28},{16,0},{20,4},{24,8},{28,12},{1,17},{... | collective-permute-start | bytes 786440 | tf_op jit(solution)/shard_map/ppermute | solution.py:354
  220.0 11.5 collective-permute-start.16
  231.6 2.8 collective-permute-start.17
  234.5 209.5 %copy-start.28 = (f32[1024,128]{1,0:T(8,128)}, f32[1024,128]{1,0:T(8,128)S(1)}, u32[]{:S(2)}) copy-start(f32[1024,128]{1,0:T(8,128)S(1)} %add.198) | copy-start | bytes 1572868
  234.8 209.2 %copy-start.84 = (f32[1024,4]{0,1:T(4,128)}, f32[1024,4]{0,1:T(4,128)S(1)}, u32[]{:S(2)}) copy-start(f32[1024,4]{0,1:T(4,128)S(1)} %bitcast_reduce_fusion) | copy-start | bytes 49156
  235.7 208.3 %copy-start.32 = (f32[1024,128]{1,0:T(8,128)}, f32[1024,128]{1,0:T(8,128)S(1)}, u32[]{:S(2)}) copy-start(f32[1024,128]{1,0:T(8,128)S(1)} %copy.134) | copy-start | bytes 1572868
  236.0 208.0 %copy-start.34 = (f32[1024,128]{1,0:T(8,128)}, f32[1024,128]{1,0:T(8,128)S(1)}, u32[]{:S(2)}) copy-start(f32[1024,128]{1,0:T(8,128)S(1)} %copy.133) | copy-start | bytes 1572868
  236.9 523.4 %reduce-scatter.6.cloned.1.call-start = ((), (), s32[]{:S(2)}) async-start(), calls=%async_computation.5 | async-start | bytes 2359296 | tf_op jit(solution)/shard_map/reduce_scatter | solution.py:375
  445.6 402.6 %reduce-scatter.8.cloned.1.call-start = ((), (), s32[]{:S(2)}) async-start(), calls=%async_computation.6 | async-start | bytes 4718592 | tf_op jit(solution)/shard_map/reduce_scatter | solution.py:375
  761.3 25.4 %copy-start.29 = (f32[1024,128]{1,0:T(8,128)S(1)}, f32[1024,128]{1,0:T(8,128)}, u32[]{:S(2)}) copy-start(f32[1024,128]{1,0:T(8,128)} %copy-done.28) | copy-start | bytes 1572868
  761.3 145.7 %all-reduce.3.cloned.1.call-start = ((), (), s32[]{:S(2)}) async-start(), calls=%async_computation.7 | async-start | bytes 4194304 | tf_op jit(solution)/shard_map/psum | solution.py:540
  761.4 13.9 %collective-permute-start.21 = (f32[1024,128]{1,0:T(8,128)S(1)}, f32[1024,128]{1,0:T(8,128)S(1)}, u32[]{:S(2)}, u32[]{:S(2)}) collective-permute-start(f32[1024,128]{1,0:T(8,128)S(1)} %bitcast_convert_fusion), channel_id=1, source_target_pairs={{0,2},{1,3},{2,0},{3,1},{4,6},{5,7},{6,4},{7,5},{8,10},{9,11},{10,... | collective-permute-start | bytes 1572872 | tf_op jit(solution)/shard_map/ppermute | solution.py:339
  776.2 2.3 collective-permute-start.22
  801.6 46.6 %copy-start.66 = (f32[1024,256]{1,0:T(8,128)S(1)}, f32[1024,256]{1,0:T(8,128)}, u32[]{:S(2)}) copy-start(f32[1024,256]{1,0:T(8,128)} %copy-done.65) | copy-start | bytes 3145732
  802.8 47.2 %copy-start.63 = (bf16[8,128,256]{2,1,0:T(8,128)(2,1)S(1)}, bf16[8,128,256]{2,1,0:T(8,128)(2,1)}, u32[]{:S(2)}) copy-start(bf16[8,128,256]{2,1,0:T(8,128)(2,1)} %copy-done.62) | copy-start | bytes 1572868
  855.7 167.7 %all-reduce.5.cloned.1.call-start = ((), (), s32[]{:S(2)}) async-start(), calls=%async_computation.9 | async-start | bytes 4194304 | tf_op jit(solution)/shard_map/psum | solution.py:581
  875.8 33.4 %copy-start.89 = (f32[1024]{0:T(1024)S(1)}, f32[1024]{0:T(1024)}, u32[]{:S(2)}) copy-start(f32[1024]{0:T(1024)} %copy-done.88) | copy-start | bytes 12292
  875.9 33.4 %copy-start.91 = (f32[8,1,128]{2,1,0:T(1,128)S(1)}, f32[8,1,128]{2,1,0:T(1,128)}, u32[]{:S(2)}) copy-start(f32[8,1,128]{2,1,0:T(1,128)} %copy-done.90) | copy-start | bytes 12292
  971.8 119.0 %reduce-scatter.10.cloned.1.call-start = ((), (), s32[]{:S(2)}) async-start(), calls=%async_computation.8 | async-start | bytes 2621440 | tf_op jit(solution)/shard_map/reduce_scatter | solution.py:545
  972.5 157.5 %reduce-scatter.14.cloned.1.call-start = ((), (), s32[]{:S(2)}) async-start(), calls=%async_computation.11 | async-start | bytes 2654208 | tf_op jit(solution)/shard_map/reduce_scatter | solution.py:375
  973.1 228.7 %reduce-scatter.12.cloned.1.call-start = ((), (), s32[]{:S(2)}) async-start(), calls=%async_computation.10 | async-start | bytes 2654208 | tf_op jit(solution)/shard_map/reduce_scatter | solution.py:375
  991.3 32.1 %copy-start.95 = (f32[1024]{0:T(1024)S(1)}, f32[1024]{0:T(1024)}, u32[]{:S(2)}) copy-start(f32[1024]{0:T(1024)} %copy-done.94) | copy-start | bytes 12292
  993.6 34.6 %copy-start.67 = (bf16[8,128,128]{1,2,0:T(8,128)(2,1)S(1)}, bf16[8,128,128]{1,2,0:T(8,128)(2,1)}, u32[]{:S(2)}) copy-start(bf16[8,128,128]{1,2,0:T(8,128)(2,1)} %copy.198) | copy-start | bytes 786436
  993.6 34.6 %copy-start.68 = (bf16[8,128,128]{1,2,0:T(8,128)(2,1)S(1)}, bf16[8,128,128]{1,2,0:T(8,128)(2,1)}, u32[]{:S(2)}) copy-start(bf16[8,128,128]{1,2,0:T(8,128)(2,1)} %copy.195) | copy-start | bytes 786436
  993.6 34.6 %copy-start.69 = (bf16[8,128,128]{1,2,0:T(8,128)(2,1)S(1)}, bf16[8,128,128]{1,2,0:T(8,128)(2,1)}, u32[]{:S(2)}) copy-start(bf16[8,128,128]{1,2,0:T(8,128)(2,1)} %copy.196) | copy-start | bytes 786436
  993.7 34.6 %copy-start.70 = (bf16[8,128,128]{1,2,0:T(8,128)(2,1)S(1)}, bf16[8,128,128]{1,2,0:T(8,128)(2,1)}, u32[]{:S(2)}) copy-start(bf16[8,128,128]{1,2,0:T(8,128)(2,1)} %copy.193) | copy-start | bytes 786436
  1033.1 53.8 %copy-start.27 = (bf16[1024,1024]{0,1:T(8,128)(2,1)S(1)}, bf16[1024,1024]{0,1:T(8,128)(2,1)}, u32[]{:S(2)}) copy-start(bf16[1024,1024]{0,1:T(8,128)(2,1)} %all-reduce.5.cloned.1.call-done) | copy-start | bytes 6291460
  (74 other events, 363.7 us)
Sparse Core Ops, SparseCore 0:
  10.8 46.8 all-gather.15
  60.4 56.4 all-gather.9
  151.2 102.1 all-gather.13
  256.0 48.1 all-gather.11
  445.7 66.6 reduce-scatter.5
  761.4 86.7 reduce-scatter.7
  855.8 51.1 all-reduce.2
  971.9 51.4 all-reduce.4
  1026.1 31.4 reduce-scatter.9
  1060.9 69.0 reduce-scatter.13
  1133.5 68.2 reduce-scatter.11

commit v3 on v2

--- a/solution.py
+++ b/solution.py
@@ -26,12 +26,6 @@
 def norm_rows(activations, gain_row):
     factor = lax.rsqrt(jnp.mean(activations * activations, axis=-1, keepdims=True) + EPSILON)
     return (factor, activations * factor * gain_row)
-
-
-def norm_back(activations, factor, gain_row, upstream):
-    inner_sum = jnp.mean(gain_row * upstream * activations, axis=-1, keepdims=True)
-    through = factor * gain_row * upstream - activations * (factor * factor * factor) * inner_sum
-    return (through, jnp.sum(upstream * activations * factor, axis=0))
 
 
 def masked_scores(query_block, key_rows, segment_block, segment_row, offset):
@@ -114,97 +108,135 @@
     return (query_parts.reshape(queries.shape), carried[0], carried[1])
 
 
+SLOTS = 32
+
+
 def params(mib):
     return pltpu.CompilerParams(vmem_limit_bytes=mib << 20)
 
 
-def picked_body(base_ref, picks_ref, grad_ref, table_ref, out_ref, *, chunk):
-    local = picks_ref[...] - base_ref[0]
-    upper = local >> 7
-    lower = local & (LANES - 1)
-    grads = grad_ref[...]
-    total = jnp.zeros(local.shape, F32)
-    for start in range(0, table_ref.shape[0], chunk):
-        products = lax.dot_general(
-            grads, table_ref[pl.ds(start, chunk), :], NT, preferred_element_type=F32
-        )
-        for lane in range(0, chunk, LANES):
-            found = jnp.take_along_axis(products[:, lane : lane + LANES], lower, axis=1)
-            total = jnp.where(upper == (start + lane) // LANES, found, total)
-    out_ref[...] = total
-
-
-def picked_products(base, picks, grads, table, rows=256, chunk=1024):
-    amount, width = grads.shape
-    total = table.shape[0]
-    return pl.pallas_call(
-        functools.partial(picked_body, chunk=chunk),
-        grid=(amount // rows,),
-        in_specs=[
-            pl.BlockSpec(memory_space=pltpu.SMEM),
-            pl.BlockSpec((rows, PICKS), lambda i: (i, 0)),
-            pl.BlockSpec((rows, width), lambda i: (i, 0)),
-            pl.BlockSpec((total, width), lambda i: (0, 0)),
-        ],
-        out_specs=pl.BlockSpec((rows, PICKS), lambda i: (i, 0)),
-        out_shape=jax.ShapeDtypeStruct((amount, PICKS), F32),
-        compiler_params=params(48),
-        cost_estimate=pl.CostEstimate(
-            flops=8 * amount * total * width, bytes_accessed=amount * width * 4, transcendentals=0
-        ),
-        name="picked_products",
-    )(base, picks, grads, table)
+def lane_numbers(shape):
+    return lax.broadcasted_iota(jnp.int32, shape, len(shape) - 1)
+
+
+def count_local(local, total):
+    inside = (local >= 0) & (local < total)
+    square = (LANES, LANES)
+    upto = lax.broadcasted_iota(jnp.int32, square, 0) <= lax.broadcasted_iota(jnp.int32, square, 1)
+    return jnp.dot(
+        jnp.where(inside, 1.0, 0.0).astype(BF16),
+        jnp.where(upto, 1.0, 0.0).astype(BF16),
+        preferred_element_type=F32,
+    )
+
+
+def rounds_of(counts):
+    most = jnp.max(counts[:, LANES - 1 :]).astype(jnp.int32)
+    return (most + (SLOTS - 1)) // SLOTS
+
+
+def compact(counts, members, start):
+    target = ((lane_numbers(counts.shape) & (SLOTS - 1)) + (start + 1)).astype(F32)
+    place = jnp.zeros(counts.shape, jnp.int32)
+    step = LANES // 2
+    while step:
+        seen = jnp.take_along_axis(counts, place + (step - 1), axis=1)
+        place = jnp.where(seen < target, place + step, place)
+        step //= 2
+    valid = target <= counts[:, LANES - 1 :]
+    return valid, [jnp.take_along_axis(member, place, axis=1) for member in members]
+
+
+def group_masks():
+    own = lax.broadcasted_iota(jnp.int32, (8, LANES), 0)
+    lane = lane_numbers((8, LANES)) // SLOTS
+    per = LANES // SLOTS
+    return [own == lane + per * block for block in range(8 // per)]
+
+
+def lane_table(low, masks):
+    ids = lax.broadcasted_iota(jnp.int32, (NKEYS, LANES), 0).astype(F32).astype(BF16)
+    parts = []
+    for mask in masks:
+        row = jnp.sum(jnp.where(mask, low, 0.0), axis=0, keepdims=True)
+        row = jnp.broadcast_to(row, (16, LANES)).astype(BF16)
+        row = jnp.concatenate([row] * (NKEYS // 16), axis=0)
+        parts.append(jnp.where(ids == row, jnp.ones((), BF16), jnp.zeros((), BF16)))
+    return jnp.concatenate(parts, axis=1)
 
 
 def bag_body(
-    base_ref, picks_ref, weight_ref, table_ref, out_ref, keep_ref, held, upper, lower, weights,
-    *, chunk, unroll
+    base_ref, picks_ref, weight_ref, table_ref, out_ref, keep_ref, counts, locals_, high, low,
+    weights, *, chunk, unroll
 ):
     rows = picks_ref.shape[0]
-    groups = table_ref.shape[0] // LANES
+    total = table_ref.shape[0]
+    groups = total // NKEYS
     local = picks_ref[...] - base_ref[0]
-    upper[...] = (local >> 7).astype(F32)
-    lower[...] = (local & (LANES - 1)).astype(F32)
-    weights[...] = weight_ref[...].astype(F32)
-    group_ids = lax.broadcasted_iota(jnp.int32, (groups, LANES), 0).astype(F32).astype(BF16)
-    lane_ids = lax.broadcasted_iota(jnp.int32, (LANES, LANES), 0).astype(F32).astype(BF16)
-    zero = jnp.zeros((), BF16)
-    one = jnp.ones((), BF16)
-
-    def spread_row(ref, token, count):
-        row = jnp.broadcast_to(ref[pl.ds(token, 1), :], (16, LANES)).astype(BF16)
-        return jnp.concatenate([row] * (count // 16), axis=0)
-
-    def some_tokens(step, carried):
-        for slot in range(unroll):
-            token = step * unroll + slot
-            first = jnp.where(
-                group_ids == spread_row(upper, token, groups),
-                spread_row(weights, token, groups),
-                zero,
-            )
-            second = jnp.where(lane_ids == spread_row(lower, token, LANES), one, zero)
-            held[pl.ds(token, groups, stride=rows), :] = lax.dot_general(
-                first, second, NT, preferred_element_type=F32
-            )
+    counts[...] = count_local(local, total)
+    locals_[...] = local
+    masks = group_masks()
+
+    def eight(token):
+        span = pl.ds(token, 8)
+        own_high = high[span, :]
+        weight = weights[span, :]
+        weight = jnp.concatenate([weight, weight], axis=0).astype(BF16)
+        zero = jnp.zeros((), BF16)
+        parts = []
+        for mask in masks:
+            own = jnp.where(mask, own_high, -1.0)
+            pair = jnp.concatenate([own, own - 1.0], axis=0).astype(BF16)
+            rows_of = [
+                jnp.where(pair == jnp.array(group, BF16), weight, zero)
+                for group in range(0, groups, 2)
+            ]
+            parts.append(jnp.concatenate(rows_of, axis=0))
+        return lax.dot_general(
+            jnp.concatenate(parts, axis=1),
+            lane_table(low[span, :], masks),
+            NT,
+            preferred_element_type=F32,
+        )
+
+    def one_round(number, first):
+        members = [locals_[...], weight_ref[...].astype(F32)]
+        valid, (found, weight) = compact(counts[...], members, number * SLOTS)
+        high[...] = jnp.where(valid, found >> 8, -1).astype(F32)
+        low[...] = (found & (NKEYS - 1)).astype(F32)
+        weights[...] = weight
+
+        def some_tokens(step, carried):
+            for slot in range(unroll):
+                token = pl.multiple_of((step * unroll + slot) * 16, 16)
+                top = eight(token)
+                bottom = eight(token + 8)
+                for group in range(groups):
+                    part = slice(group * 8, group * 8 + 8)
+                    block = jnp.concatenate([top[part], bottom[part]], axis=0).astype(BF16)
+                    span = (pl.ds(token, 16), slice(group * NKEYS, (group + 1) * NKEYS))
+                    keep_ref[span] = block if first else keep_ref[span] + block
+            return carried
+
+        lax.fori_loop(0, rows // (16 * unroll), some_tokens, 0)
+
+    def more(number, carried):
+        one_round(number, False)
         return carried
 
-    lax.fori_loop(0, rows // unroll, some_tokens, 0)
-    total = jnp.zeros(out_ref.shape, F32)
-    for start in range(0, table_ref.shape[0], chunk):
-        parts = [
-            held[pl.ds(group * rows, rows), :].astype(BF16)
-            for group in range(start // LANES, (start + chunk) // LANES)
-        ]
-        block = jnp.concatenate(parts, axis=1)
-        keep_ref[:, pl.ds(start, chunk)] = block
-        total = total + jnp.dot(
-            block, table_ref[pl.ds(start, chunk), :], preferred_element_type=F32
-        )
-    out_ref[...] = total.astype(out_ref.dtype)
-
-
-def bag_sums(base, picks, weights, table, rows=256, chunk=1024, unroll=32):
+    one_round(0, True)
+    lax.fori_loop(1, rounds_of(counts[...]), more, 0)
+    result = jnp.zeros(out_ref.shape, F32)
+    for start in range(0, total, chunk):
+        result = result + jnp.dot(
+            keep_ref[:, pl.ds(start, chunk)],
+            table_ref[pl.ds(start, chunk), :],
+            preferred_element_type=F32,
+        )
+    out_ref[...] = result.astype(out_ref.dtype)
+
+
+def bag_sums(base, picks, weights, table, rows=256, chunk=1024, unroll=8):
     amount = picks.shape[0]
     total, width = table.shape
     return pl.pallas_call(
@@ -224,14 +256,111 @@
             jax.ShapeDtypeStruct((amount, width), BF16),
             jax.ShapeDtypeStruct((amount, total), BF16),
         ],
-        scratch_shapes=[pltpu.VMEM((total // LANES * rows, LANES), F32)]
-        + [pltpu.VMEM((rows, LANES), F32)] * 3,
+        scratch_shapes=[
+            pltpu.VMEM((rows, LANES), F32),
+            pltpu.VMEM((rows, LANES), jnp.int32),
+            pltpu.VMEM((rows, LANES), F32),
+            pltpu.VMEM((rows, LANES), F32),
+            pltpu.VMEM((rows, LANES), F32),
+        ],
         compiler_params=params(56),
         cost_estimate=pl.CostEstimate(
-            flops=12 * amount * total * width, bytes_accessed=amount * total * 2, transcendentals=0
+            flops=9 * amount * total * width, bytes_accessed=amount * total * 2, transcendentals=0
         ),
         name="bag_sums",
     )(base, picks, weights, table)
+
+
+def picked_body(
+    base_ref, picks_ref, grad_ref, table_ref, out_ref, counts, locals_, high, low, found_at, held,
+    *, unroll
+):
+    rows = picks_ref.shape[0]
+    total = table_ref.shape[1]
+    groups = total // NKEYS
+    local = picks_ref[...] - base_ref[0]
+    counts[...] = count_local(local, total)
+    locals_[...] = local
+    masks = group_masks()
+    grads = grad_ref[...]
+    for group in range(groups):
+        held[group] = jnp.dot(
+            grads,
+            table_ref[:, group * NKEYS : (group + 1) * NKEYS],
+            preferred_element_type=F32,
+        )
+
+    def eight(token):
+        span = pl.ds(token, 8)
+        left = jnp.concatenate([held[group, span, :] for group in range(groups)], axis=0)
+        seen = jnp.dot(
+            left.astype(BF16), lane_table(low[span, :], masks), preferred_element_type=F32
+        )
+        own_high = high[span, :]
+        result = jnp.zeros((8, LANES), F32)
+        for block, mask in enumerate(masks):
+            own = jnp.where(mask, own_high, -1.0)
+            for group in range(groups):
+                part = seen[group * 8 : group * 8 + 8, block * LANES : (block + 1) * LANES]
+                result = jnp.where(own == float(group), part, result)
+        found_at[span, :] = result
+
+    def one_round(number, first):
+        valid, (found,) = compact(counts[...], [locals_[...]], number * SLOTS)
+        high[...] = jnp.where(valid, found >> 8, -1).astype(F32)
+        low[...] = (found & (NKEYS - 1)).astype(F32)
+
+        def some_tokens(step, carried):
+            for slot in range(unroll):
+                eight(pl.multiple_of((step * unroll + slot) * 8, 8))
+            return carried
+
+        lax.fori_loop(0, rows // (8 * unroll), some_tokens, 0)
+        slot = counts[...].astype(jnp.int32) - (1 + number * SLOTS)
+        inside = (locals_[...] >= 0) & (locals_[...] < total)
+        here = (slot >= 0) & (slot < SLOTS) & inside
+        token = lax.broadcasted_iota(jnp.int32, slot.shape, 0) & (LANES // SLOTS - 1)
+        lane = token * SLOTS + jnp.clip(slot, 0, SLOTS - 1)
+        value = jnp.take_along_axis(found_at[...], lane, axis=1)
+        before = jnp.zeros(value.shape, F32) if first else out_ref[...].astype(F32)
+        out_ref[...] = jnp.where(here, value, before).astype(out_ref.dtype)
+
+    def more(number, carried):
+        one_round(number, False)
+        return carried
+
+    one_round(0, True)
+    lax.fori_loop(1, rounds_of(counts[...]), more, 0)
+
+
+def picked_products(base, picks, grads, table, rows=256, unroll=16):
+    amount, width = grads.shape
+    total = table.shape[1]
+    return pl.pallas_call(
+        functools.partial(picked_body, unroll=unroll),
+        grid=(amount // rows,),
+        in_specs=[
+            pl.BlockSpec(memory_space=pltpu.SMEM),
+            pl.BlockSpec((rows, PICKS), lambda i: (i, 0)),
+            pl.BlockSpec((rows, width), lambda i: (i, 0)),
+            pl.BlockSpec((width, total), lambda i: (0, 0)),
+        ],
+        out_specs=pl.BlockSpec((rows, PICKS), lambda i: (i, 0)),
+        out_shape=jax.ShapeDtypeStruct((amount, PICKS), BF16),
+        scratch_shapes=[
+            pltpu.VMEM((rows, LANES), F32),
+            pltpu.VMEM((rows, LANES), jnp.int32),
+            pltpu.VMEM((rows, LANES), F32),
+            pltpu.VMEM((rows, LANES), F32),
+            pltpu.VMEM((rows, LANES), F32),
+            pltpu.VMEM((total // NKEYS, rows, NKEYS), F32),
+        ],
+        compiler_params=params(56),
+        cost_estimate=pl.CostEstimate(
+            flops=7 * amount * total * width, bytes_accessed=amount * width * 4, transcendentals=0
+        ),
+        name="picked_products",
+    )(base, picks, grads, table)
 
 
 def unit_indices(picks, number):
@@ -339,11 +468,6 @@
     return lax.ppermute(block, "narrow", [(i, i ^ bit) for i in range(size)])
 
 
-def swap_wide(block, bit):
-    size = lax.axis_size("wide")
-    return lax.ppermute(block, "wide", [(i, i ^ bit) for i in range(size)])
-
-
 def gather_by_swaps(block, axis, bits):
     size = lax.axis_size(axis)
     me = lax.axis_index(axis)
@@ -355,6 +479,33 @@
         held.update(moved)
     stacked = jnp.stack([held[offset] for offset in range(size)])
     return [lax.dynamic_index_in_dim(stacked, me ^ number, 0, False) for number in range(size)]
+
+
+def sum_by_swaps(block, axis):
+    for bit in bits_down(lax.axis_size(axis)):
+        block = block + lax.ppermute(
+            block, axis, [(i, i ^ bit) for i in range(lax.axis_size(axis))]
+        )
+    return block
+
+
+def scatter_narrow(block):
+    size = lax.axis_size("narrow")
+    me = lax.axis_index("narrow")
+    width = block.shape[1] // size
+    parts = jnp.stack([block[:, n * width : (n + 1) * width] for n in range(size)])
+    held = [lax.dynamic_index_in_dim(parts, me ^ offset, 0, False) for offset in range(size)]
+    for bit in bits_down(size)[::-1]:
+        arrived = {
+            offset: swap_narrow(held[offset ^ bit].astype(BF16), bit)
+            for offset in range(size)
+            if not offset & (2 * bit - 1)
+        }
+        held = {
+            offset: held[offset].astype(F32) + value.astype(F32)
+            for offset, value in arrived.items()
+        }
+    return held[0]
 
 
 def bits_down(size):
@@ -429,14 +580,15 @@
     key_part = sub_keys.shape[1]
 
     rows_one = gather_narrow(inputs).astype(F32)
-    first_shapes = [(3 * part, width), (2 * part // LANES, LANES)]
+    first_shapes = [(3 * part, width), (part, width), (2 * part // LANES, LANES)]
     first_pack = pack(
         [
             jnp.transpose(qkv_weight, (1, 0, 2)).reshape(3 * part, width),
+            out_weight.T,
             jnp.concatenate([attn_gain, memory_gain]).reshape(-1, LANES),
         ]
     )
-    qkv_parts, gains = unpack(gather_wide(first_pack), first_shapes)
+    qkv_parts, out_turned, gains = unpack(gather_wide(first_pack), first_shapes)
     qkv_full = [
         qkv_parts[:, j * part : (j + 1) * part].reshape(model, width) for j in range(3)
     ]
@@ -446,13 +598,11 @@
     second_shapes = [
         (part, width),
         (part, width),
-        (part, width),
         (part, units * NKEYS),
         (units * key_part, NKEYS),
     ]
     second_pack = pack(
         [
-            out_weight.T,
             memory_out.T,
             gate_weight,
             query_weight.reshape(part, units * NKEYS),
@@ -460,7 +610,7 @@
         ]
     )
     second_pack, first_pack = lax.optimization_barrier((second_pack, first_pack))
-    out_turned, mixer_turned, gate_full, query_full, keys_full = unpack(
+    mixer_turned, gate_full, query_full, keys_full = unpack(
         gather_wide(second_pack), second_shapes
     )
     out_turned = out_turned.reshape(model, width)
@@ -500,9 +650,7 @@
 
     memory_query = jnp.dot(second, query_full, preferred_element_type=F32).astype(BF16)
     own_scores = pick_scores(column_ref, picks, memory_query, keys_full)
-    for bit in bits_down(lax.axis_size("narrow")):
-        own_scores = own_scores + swap_narrow(own_scores, bit)
-    mem_scores = own_scores.reshape(length, PKH, TOPK)
+    mem_scores = sum_by_swaps(own_scores, "narrow").reshape(length, PKH, TOPK)
     score_peak = jnp.max(mem_scores, axis=-1, keepdims=True)
     raised = jnp.exp(mem_scores - score_peak)
     mem_probs = raised / jnp.sum(raised, axis=-1, keepdims=True)
@@ -510,7 +658,7 @@
     pick_weights, memory_grad = lax.optimization_barrier((pick_weights, memory_grad))
     all_weights = gather_wide(pick_weights).reshape(shards * length, PICKS)
 
-    pick_part = picked_products(base, all_picks, all_grads, memory_values).astype(BF16)
+    pick_part = picked_products(base, all_picks, all_grads, memory_values.T)
     all_weights, pick_part = lax.optimization_barrier((all_weights, pick_part))
     memory_part, tables = bag_sums(base, all_picks, all_weights, memory_values)
     pick_own = sum_wide(pick_part.reshape(shards, length, PICKS)).astype(F32)
@@ -519,9 +667,7 @@
     tables, pick_own = lax.optimization_barrier((tables, pick_own))
     values_grad = lax.dot_general(tables, all_grads, TN, preferred_element_type=F32)
 
-    for bit in bits_down(lax.axis_size("narrow")):
-        pick_own = pick_own + swap_narrow(pick_own, bit)
-    pick_grad = pick_own.reshape(length, PKH, TOPK)
+    pick_grad = sum_by_swaps(pick_own, "narrow").reshape(length, PKH, TOPK)
     centre = jnp.sum(mem_probs * pick_grad, axis=-1, keepdims=True)
     score_grad = (mem_probs * (pick_grad - centre)).astype(BF16).reshape(length, PICKS)
     memory_query_grad, key_grad = spread_grads(
@@ -537,18 +683,29 @@
     second_part = second_part + lax.dot_general(
         memory_query_grad, query_full, NT, preferred_element_type=F32
     )
-    second_grad = lax.psum(second_part.astype(BF16), "narrow").astype(F32)
+    turned = second_part * gain_two
+    inner_part = jnp.sum(turned * hidden, axis=-1)
+    gain_two_part = jnp.sum(second_part * hidden * factor_two, axis=0)
+    tiny = sum_by_swaps(jnp.concatenate([inner_part, gain_two_part]), "narrow")
+    inner_two = tiny[:length, None] / model
+    gain_two_part = tiny[length:]
+    own_second_grad = scatter_narrow(second_part)
+
+    def own_columns(block):
+        return lax.dynamic_slice_in_dim(block, column * width, width, block.ndim - 1)
+
+    own_hidden = own_columns(hidden)
+    own_hidden_grad = (
+        cotangent.astype(F32)
+        + factor_two * own_columns(gain_two) * own_second_grad
+        - own_hidden * (factor_two * factor_two * factor_two) * inner_two
+    )
+    branch_grad = gather_narrow(own_hidden_grad.astype(BF16))
 
     mixer_part = lax.dot_general(product, mixer_turned, NT, preferred_element_type=F32)
-    mixer_part = mixer_part.astype(BF16)
-    mixer_part, second_grad = lax.optimization_barrier((mixer_part, second_grad))
-    mixer_sum = lax.psum_scatter(mixer_part, "narrow", scatter_dimension=1, tiled=True).astype(F32)
-    own_hidden = lax.dynamic_slice_in_dim(hidden, column * width, width, 1)
-    outputs = (own_hidden + mixer_sum).astype(BF16)
-
-    through_two, gain_two_part = norm_back(hidden, factor_two, gain_two, second_grad)
-    hidden_grad = upstream.astype(F32) + through_two
-    branch_grad = hidden_grad.astype(BF16)
+    mixer_part, branch_grad = lax.optimization_barrier((mixer_part, branch_grad))
+    outputs = (own_hidden + scatter_narrow(mixer_part)).astype(BF16)
+
     heads_grad = jnp.dot(branch_grad, out_turned, preferred_element_type=F32)
     heads_grad = heads_grad.astype(BF16).reshape(length, head_count, HD)
 
@@ -565,7 +722,7 @@
     early_pack = pack([by_shard(mixer_grad), by_shard(gate_grad), by_shard(query_grad), key_grad])
     early_pack, heads_grad = lax.optimization_barrier((early_pack, heads_grad))
     early_sums = sum_wide(early_pack).astype(F32)
-    mixer_sums, gate_sums, query_sums, key_sums = unpack(early_sums, second_shapes[1:])
+    mixer_sums, gate_sums, query_sums, key_sums = unpack(early_sums, second_shapes)
 
     query_back, key_back, value_back = attend_backward(
         queries, key_rows, value_rows, segment_row, logsum, heads_grad
@@ -577,15 +734,22 @@
     normed_part = sum(
         lax.dot_general(mixed_grad[j], qkv_full[j], NT, preferred_element_type=F32)
         for j in range(3)
-    ).astype(BF16)
-    normed_grad = lax.psum(normed_part, "narrow").astype(F32)
+    )
     out_grad = lax.dot_general(branch_grad, head_rows, TN, preferred_element_type=F32)
     qkv_grad = [
         lax.dot_general(normed, mixed_grad[j], TN, preferred_element_type=F32) for j in range(3)
     ]
-    through_one, gain_one_part = norm_back(rows_one, factor_one, gain_one, normed_grad)
-    input_full = hidden_grad + through_one
-    input_grad = lax.dynamic_slice_in_dim(input_full, column * width, width, 1)
+    inner_part = jnp.sum(normed_part * gain_one * rows_one, axis=-1)
+    gain_one_part = jnp.sum(normed_part * rows_one * factor_one, axis=0)
+    tiny = sum_by_swaps(jnp.concatenate([inner_part, gain_one_part]), "narrow")
+    inner_one = tiny[:length, None] / model
+    gain_one_part = tiny[length:]
+    own_normed_grad = scatter_narrow(normed_part)
+    input_grad = (
+        own_hidden_grad
+        + factor_one * own_columns(gain_one) * own_normed_grad
+        - inputs.astype(F32) * (factor_one * factor_one * factor_one) * inner_one
+    )
     gain_parts = jnp.concatenate(
         [gain_one_part.reshape(shards, 1, part), gain_two_part.reshape(shards, 1, part)], axis=1
     ).astype(BF16).reshape(shards, -1, LANES)

time: 1220 us -> 844 us (0.69)
  Pallas kernels: 520 us -> 242 us
  waiting for transfers between devices: 356 us -> 250 us
    pallas_call x1, Pallas kernels: 315 us -> 128 us  [bag_sums(): pl.pallas_call(functools.partial(bag_body, chunk=chunk, unroll=unroll), g...]
    pallas_call x1, Pallas kernels: 191 us -> 99.9 us  [picked_products(): pl.pallas_call(functools.partial(picked_body, unroll=unroll), grid=(amoun...]
    psum x2 -> x0, waiting for transfers between devices: 55.4 us -> none  [the longest x1 31.1 us: per_device(): second_grad = lax.psum(second_part.astype(BF16), 'narrow').astype(F32)]
    reduce_scatter x4, waiting for transfers between devices: 141 us -> 87 us  [sum_wide(): return lax.psum_scatter(block, 'wide', scatter_dimension=0)]
    ppermute x0 -> x8, waiting for transfers between devices: none -> 18.4 us  [sum_by_swaps(): lax.ppermute(block, axis, [(i, i ^ bit) for i in range(lax.axis_size(axis...]
    all_gather x4, waiting for transfers between devices: 66.9 us -> 54.3 us  [gather_wide(): return lax.all_gather(block, 'wide')]
    unnamed x231 -> x245, local copies, waits for them, and re-layouts: 43.6 us -> 50.2 us
    ppermute x19 -> x22, waiting for transfers between devices: 73.4 us -> 69.5 us  [gather_by_swaps(): lax.ppermute(part, axis, [(i, i ^ bit) for i in range(size)])]
  transfers between devices with their start and end apart: 34 -> 47, of which waited for: 19 -> 20; matrix products, arithmetic and copies ran while one was open for 17% -> 23% of each run, Pallas kernels for 43% -> 29%
where the time goes in v3:
time: 844 us; the launch traced here: 839 us
  waiting for transfers between devices  250 us (30%)
  Pallas kernels  242 us (29%)
  matrix products  132 us (16%)
  local copies, waits for them, and re-layouts  105 us (12%)
  other arithmetic  65.5 us (8%)
  starting transfers between devices  24.5 us (3%)
  between operations  16.3 us (2%)
    pallas_call x1, Pallas kernels, bag_sums(): pl.pallas_call(functools.partial(bag_body, chunk=chunk, unroll=unroll), g...  128 us
    pallas_call x1, Pallas kernels, picked_products(): pl.pallas_call(functools.partial(picked_body, unroll=unroll), grid=(amoun...  99.9 us
    reduce_scatter x4, waiting for transfers between devices, sum_wide(): return lax.psum_scatter(block, 'wide', scatter_dimension=0)  87 us
    ppermute x22, waiting for transfers between devices, gather_by_swaps(): lax.ppermute(part, axis, [(i, i ^ bit) for i in range(size)])  69.5 us
    all_gather x4, waiting for transfers between devices, gather_wide(): return lax.all_gather(block, 'wide')  54.3 us
    dot_general x1, matrix products, per_device(): lax.dot_general(tables, all_grads, TN, preferred_element_type=F32)  53.1 us
    unnamed x245, local copies, waits for them, and re-layouts  50.2 us
    ppermute x9, waiting for transfers between devices, swap_narrow(): return lax.ppermute(block, 'narrow', [(i, i ^ bit) for i in range(size)])  20.9 us
  transfers between devices with their start and end apart: 47, of which 20 were waited for; matrix products, arithmetic and copies ran while one was open for 23% of the time, Pallas kernels for 29%

profile of v3, /device:TPU:0, one launch (start us, length us, event | category | flops | bytes accessed | tf_op | source)
XLA Modules:
  0.0 839.0 jit_solution(7201757860772972986)
XLA Ops:
  11.5 3.0 collective-permute-start.1
  15.0 12.4 %collective-permute-done.1 = bf16[1024,256]{1,0:T(8,128)(2,1)S(1)} collective-permute-done((bf16[1024,256]{1,0:T(8,128)(2,1)}, bf16[1024,256]{1,0:T(8,128)(2,1)S(1)}, u32[]{:S(2)}, u32[]{:S(2)}) %collective-permute-start.1) | collective-permute-done | bytes 524320 | tf_op jit(solution)/shard_map/ppermute | solution.py:478
  32.2 5.7 collective-permute-done.19
  41.4 22.5 %all-gather.16.cloned.1.call-done = bf16[8,1026,128]{2,1,0:T(8,128)(2,1)} async-done(((bf16[1,1026,128]{2,1,0:T(8,128)(2,1)}), bf16[8,1026,128]{2,1,0:T(8,128)(2,1)}) %all-gather.16.cloned.1.call-update) | async-done | bytes 2101264 | tf_op jit(solution)/shard_map/all_gather | solution.py:522
  64.8 4.9 fusion.42
  72.8 18.9 %while.27 = (s32[]{:T(128)}, bf16[2,512,4,64]{1,3,2,0:T(8,128)(2,1)}, f32[2,4,512]{2,1,0:T(4,128)S(1)}, s32[2]{0:T(128)S(1)}, s32[1024]{0:T(1024)S(1)}, /*index=...) while((s32[]{:T(128)}, ...), condition=%wide.region_4.5_spmd, body=%wide.region_1.4_spmd.sunk | while | flops 563739136 | bytes 28922568 | solution.py:60
  76.3 2.3 fusion.202
  78.7 3.6 fusion.203
  85.8 2.3 fusion.202
  88.1 3.6 fusion.203
  91.7 2.1 copy.128
  102.6 14.9 %all-gather.10.cloned.1.call-done = bf16[9216,128]{0,1:T(8,128)(2,1)} async-done(((bf16[1152,128]{0,1:T(8,128)(2,1)}), bf16[9216,128]{0,1:T(8,128)(2,1)}) %all-gather.10.cloned.1.call-update) | async-done | bytes 2359312 | tf_op jit(solution)/shard_map/all_gather | solution.py:522
  117.5 3.2 copy.135
  126.6 2.4 multiply_reduce_fusion.3
  138.9 6.4 copy.140
  149.7 9.5 %collective-permute-done.10 = u16[1024,128]{1,0:T(8,128)(2,1)} collective-permute-done((u16[1024,128]{1,0:T(8,128)(2,1)}, u16[1024,128]{1,0:T(8,128)(2,1)}, u32[]{:S(2)}, u32[]{:S(2)}) %collective-permute-start.10) | collective-permute-done | bytes 262176 | tf_op jit(solution)/shard_map/ppermute | solution.py:478
  161.0 15.2 %collective-permute-done.11 = u16[1024,128]{1,0:T(8,128)(2,1)S(1)} collective-permute-done((u16[1024,128]{1,0:T(8,128)(2,1)}, u16[1024,128]{1,0:T(8,128)(2,1)S(1)}, u32[]{:S(2)}, u32[]{:S(2)}) %collective-permute-start.11) | collective-permute-done | bytes 262176 | tf_op jit(solution)/shard_map/ppermute | solution.py:478
  179.6 13.3 %collective-permute-done.13 = u16[1024,128]{1,0:T(8,128)(2,1)S(1)} collective-permute-done((u16[1024,128]{1,0:T(8,128)(2,1)}, u16[1024,128]{1,0:T(8,128)(2,1)S(1)}, u32[]{:S(2)}, u32[]{:S(2)}) %collective-permute-start.13) | collective-permute-done | bytes 262176 | tf_op jit(solution)/shard_map/ppermute | solution.py:478
  193.7 4.9 collective-permute-done.14
  200.9 2.3 pick_scores.1
  204.8 7.3 collective-permute-done.15
  212.4 2.8 collective-permute-done.16
  215.8 2.3 convert_element_type.223.picks_ref
  220.6 17.0 %all-gather.14.cloned.1.call-done.grad_ref = bf16[8192,256]{1,0:T(8,128)(2,1)} async-done(((bf16[1024,256]{1,0:T(8,128)(2,1)}), bf16[8192,256]{1,0:T(8,128)(2,1)}) %all-gather.14.cloned.1.call-update) | async-done | bytes 4194320 | tf_op jit(solution)/shard_map/all_gather | solution.py:522
  237.6 99.9 %picked_products.1 = bf16[8192,128]{1,0:T(8,128)(2,1)} custom-call(s32[1]{0:T(128)} %bitcast.49.base_ref, s32[8192,128]{1,0:T(8,128)} %convert_element_type.223.picks_ref, bf16[8192,256]{1,0:T(8,128)(2,1)} %all-gather.14.cloned.1.call-done.grad_ref, bf16[256,8192]{1,0:T(8,128)(2,1)} %bitcast.437), custom_call_target="tpu_custom_call" | custom-call | flops 120259084288 | bytes 8388608 | tf_op jit(solution)/shard_map/picked_products/pallas_call | solution.py:339
  337.6 128.0 %bag_sums.1 = (bf16[8192,256]{1,0:T(8,128)(2,1)}, bf16[8192,8192]{1,0:T(8,128)(2,1)}) custom-call(s32[1]{0:T(128)} %bitcast.49.base_ref, s32[8192,128]{1,0:T(8,128)} %convert_element_type.223.picks_ref, bf16[8192,128]{1,0:T(8,128)(2,1)} %all-gather.12.cloned.1.call-done.weight_ref, bf16[8192,256]{1,0:T(8,128)(2,1)} %table_ref.1), custom_call_target="tpu_custom_call" | custom-call | flops 154618822656 | bytes 134217728 | tf_op jit(solution)/shard_map/bag_sums/pallas_call | solution.py:242
  468.3 12.3 %collective-permute-done.21 = f32[1024,128]{1,0:T(8,128)S(1)} collective-permute-done((f32[1024,128]{1,0:T(8,128)S(1)}, f32[1024,128]{1,0:T(8,128)S(1)}, u32[]{:S(2)}, u32[]{:S(2)}) %collective-permute-start.21) | collective-permute-done | bytes 524320 | tf_op jit(solution)/shard_map/ppermute | solution.py:486
  483.7 2.1 add.252
  485.8 2.1 copy.142
  487.9 2.2 fusion.39
  490.0 2.0 copy.143
  493.7 12.3 %spread_grads.1 = (bf16[1024,512]{1,0:T(8,128)(2,1)S(1)}, f32[2,256,256]{2,1,0:T(8,128)S(1)}) custom-call(s32[1]{0:T(128)} %bitcast.66.column_ref, s32[1024,128]{1,0:T(8,128)S(1)} %copy-done, bf16[1024,128]{1,0:T(8,128)(2,1)S(1)} %multiply_convert_fusion.3.grad_ref, bf16[1024,512]{1,0:T(8,128)(2,1)S(1)} %copy-done.2, bf16[2,256,256]{2,1,0:T(8,128)(2,1)S(1)} %bitcast.412), custom_call_target="tpu_custom_call" | custom-call | tf_op jit(solution)/shard_map/spread_grads/pallas_call | solution.py:442
  508.4 45.6 %reduce-scatter.7.cloned.1.call-done = bf16[1,1024,256]{2,1,0:T(8,128)(2,1)} async-done(((bf16[8,1024,256]{2,1,0:T(8,128)(2,1)}), bf16[1,1024,256]{2,1,0:T(8,128)(2,1)}) %reduce-scatter.7.cloned.1.call-update) | async-done | bytes 524304 | tf_op jit(solution)/shard_map/reduce_scatter | solution.py:526
  579.1 11.2 %collective-permute-done.25 = bf16[1024,256]{0,1:T(8,128)(2,1)S(1)} collective-permute-done((bf16[1024,256]{0,1:T(8,128)(2,1)S(1)}, bf16[1024,256]{0,1:T(8,128)(2,1)S(1)}, u32[]{:S(2)}, u32[]{:S(2)}) %collective-permute-start.25) | collective-permute-done | bytes 524320 | tf_op jit(solution)/shard_map/ppermute | solution.py:468
  590.3 3.2 fusion.109
  594.2 2.5 convolution_convert_fusion.8
  601.2 4.4 concatenate.100
  606.4 4.0 fusion.107
  612.4 2.6 convolution_convert_fusion.6
  615.0 2.7 convolution_convert_fusion.2
  617.8 45.0 %while.28 = (s32[]{:T(128)}, f32[1024,4,64]{0,2,1:T(8,128)S(1)}, f32[1024,4,64]{0,2,1:T(8,128)}, bf16[2,512,4,64]{1,3,2,0:T(8,128)(2,1)}, s32[2]{0:T(128)S(1)}, ...) while((s32[]{:T(128)}, f32[1024,4,64]{0,2,1:T(8,128)S(1)}, ...), condition=%wide.region_15.16_spmd.clone, body=%wide.region_13.15_spmd.clone.sunk | while | flops 1376647680 | bytes 143733616 | solution.py:105
  621.0 3.2 multiply_reduce_fusion.6
  624.4 3.8 multiply_convert_fusion.5
  628.1 3.3 fusion.215
  631.4 4.7 fusion.217
  636.1 3.6 fusion.216
  642.9 3.2 multiply_reduce_fusion.6
  646.2 3.8 multiply_convert_fusion.5
  650.0 3.3 fusion.215
  653.3 4.6 fusion.217
  658.0 4.6 fusion.216
  662.9 2.4 convolution_convert_fusion.4
  672.3 4.9 fusion.43
  678.6 2.2 collective-permute-done.37
  682.7 4.3 concatenate.102
  687.4 2.5 slice_bitcast_fusion.3
  694.0 5.6 copy.144
  699.5 2.5 slice_bitcast_fusion.7
  706.4 2.2 fusion.69
  709.8 53.1 %fusion.130 = f32[8192,256]{1,0:T(8,128)} fusion(bf16[8192,8192]{1,0:T(8,128)(2,1)} %get-tuple-element.159, bf16[8192,256]{1,0:T(8,128)(2,1)} %all-gather.14.cloned.1.call-done.grad_ref), kind=kOutput, calls=%fused_computation.291 | convolution fusion | flops 34359738368 | bytes 146800640 | tf_op jit(solution)/shard_map/dot_general | solution.py:668
  762.9 2.2 fusion.74
  770.0 9.7 %collective-permute-done.33 = bf16[1024,256]{0,1:T(8,128)(2,1)} collective-permute-done((bf16[1024,256]{0,1:T(8,128)(2,1)}, bf16[1024,256]{0,1:T(8,128)(2,1)}, u32[]{:S(2)}, u32[]{:S(2)}) %collective-permute-start.33) | collective-permute-done | bytes 524320 | tf_op jit(solution)/shard_map/ppermute | solution.py:468
  779.7 2.2 fusion.77
  786.4 41.4 %reduce-scatter.11.cloned.1.call-done = bf16[1,1152,128]{1,2,0:T(8,128)(2,1)} async-done(((bf16[8,1152,128]{1,2,0:T(8,128)(2,1)}), bf16[1,1152,128]{1,2,0:T(8,128)(2,1)}) %reduce-scatter.11.cloned.1.call-update) | async-done | bytes 294928 | tf_op jit(solution)/shard_map/reduce_scatter | solution.py:526
  (504 shorter events, 145.8 us)
Async XLA Ops:
  7.2 56.7 %all-gather.16.cloned.1.call-start = ((), (), s32[]{:S(2)}) async-start(), calls=%async_computation.11 | async-start | bytes 2377728 | tf_op jit(solution)/shard_map/all_gather | solution.py:522
  11.4 106.1 %all-gather.10.cloned.1.call-start = ((), (), s32[]{:S(2)}) async-start(), calls=%async_computation.8 | async-start | bytes 2654208 | tf_op jit(solution)/shard_map/all_gather | solution.py:522
  11.5 16.0 %collective-permute-start.1 = (bf16[1024,256]{1,0:T(8,128)(2,1)}, bf16[1024,256]{1,0:T(8,128)(2,1)S(1)}, u32[]{:S(2)}, u32[]{:S(2)}) collective-permute-start(bf16[1024,256]{1,0:T(8,128)(2,1)} %param.17), channel_id=1, source_target_pairs={{0,2},{1,3},{2,0},{3,1},{4,6},{5,7},{6,4},{7,5},{8,10},{9,11},{10,... | collective-permute-start | bytes 1572872 | tf_op jit(solution)/shard_map/ppermute | solution.py:478
  14.5 23.5 %collective-permute-start = (bf16[1024,256]{1,0:T(8,128)(2,1)}, bf16[1024,256]{1,0:T(8,128)(2,1)S(1)}, u32[]{:S(2)}, u32[]{:S(2)}) collective-permute-start(bf16[1024,256]{1,0:T(8,128)(2,1)} %param.17), channel_id=1, source_target_pairs={{0,1},{1,0},{2,3},{3,2},{4,5},{5,4},{6,7},{7,6},{8,9},{9,8},{10,11... | collective-permute-start | bytes 1572872 | tf_op jit(solution)/shard_map/ppermute | solution.py:478
  14.5 23.5 %collective-permute-start.19 = (bf16[1024,256]{1,0:T(8,128)(2,1)}, bf16[1024,256]{1,0:T(8,128)(2,1)}, u32[]{:S(2)}, u32[]{:S(2)}) collective-permute-start(bf16[1024,256]{1,0:T(8,128)(2,1)} %param.29), channel_id=1, source_target_pairs={{0,2},{1,3},{2,0},{3,1},{4,6},{5,7},{6,4},{7,5},{8,10},{9,11},{10,... | collective-permute-start | bytes 1572872 | tf_op jit(solution)/shard_map/ppermute | solution.py:478
  14.6 84.0 %collective-permute-start.18 = (bf16[1024,256]{1,0:T(8,128)(2,1)}, bf16[1024,256]{1,0:T(8,128)(2,1)}, u32[]{:S(2)}, u32[]{:S(2)}) collective-permute-start(bf16[1024,256]{1,0:T(8,128)(2,1)} %param.29), channel_id=1, source_target_pairs={{0,1},{1,0},{2,3},{3,2},{4,5},{5,4},{6,7},{7,6},{8,9},{9,8},{10,11... | collective-permute-start | bytes 1572872 | tf_op jit(solution)/shard_map/ppermute | solution.py:478
  27.4 10.5 %collective-permute-start.2 = (bf16[1024,256]{1,0:T(8,128)(2,1)S(1)}, bf16[1024,256]{1,0:T(8,128)(2,1)S(1)}, u32[]{:S(2)}, u32[]{:S(2)}) collective-permute-start(bf16[1024,256]{1,0:T(8,128)(2,1)S(1)} %collective-permute-done.1), channel_id=1, source_target_pairs={{0,1},{1,0},{2,3},{3,2},{4,5},{5,4},{6,7},{7,6},{8,9},{9,8},{10,11... | collective-permute-start | bytes 1572872 | tf_op jit(solution)/shard_map/ppermute | solution.py:478
  32.1 205.4 %all-gather.14.cloned.1.call-start = ((), (), s32[]{:S(2)}) async-start(), calls=%async_computation.10 | async-start | bytes 4718592 | tf_op jit(solution)/shard_map/all_gather | solution.py:522
  38.0 60.7 %collective-permute-start.20 = (bf16[1024,256]{1,0:T(8,128)(2,1)}, bf16[1024,256]{1,0:T(8,128)(2,1)}, u32[]{:S(2)}, u32[]{:S(2)}) collective-permute-start(bf16[1024,256]{1,0:T(8,128)(2,1)} %collective-permute-done.19), channel_id=1, source_target_pairs={{0,1},{1,0},{2,3},{3,2},{4,5},{5,4},{6,7},{7,6},{8,9},{9,8},{10,11... | collective-permute-start | bytes 1572872 | tf_op jit(solution)/shard_map/ppermute | solution.py:478
  39.6 86.9 %copy-start.26 = (bf16[1,1024,256]{1,2,0:T(8,128)(2,1)}, bf16[1,1024,256]{1,2,0:T(8,128)(2,1)S(1)}, u32[]{:S(2)}) copy-start(bf16[1,1024,256]{1,2,0:T(8,128)(2,1)S(1)} %copy.124) | copy-start | bytes 1572868
  39.9 29.8 %copy-start.28 = (bf16[1,1024,256]{1,2,0:T(8,128)(2,1)}, bf16[1,1024,256]{1,2,0:T(8,128)(2,1)S(1)}, u32[]{:S(2)}) copy-start(bf16[1,1024,256]{1,2,0:T(8,128)(2,1)S(1)} %copy.125) | copy-start | bytes 1572868
  40.1 29.7 %copy-start.31 = (bf16[1,1024,256]{1,2,0:T(8,128)(2,1)}, bf16[1,1024,256]{1,2,0:T(8,128)(2,1)S(1)}, u32[]{:S(2)}) copy-start(bf16[1,1024,256]{1,2,0:T(8,128)(2,1)S(1)} %copy.126) | copy-start | bytes 1572868
  64.8 64.8 %copy-start.95 = (f32[8,1,128]{2,1,0:T(1,128)}, f32[8,1,128]{2,1,0:T(1,128)S(1)}, u32[]{:S(2)}) copy-start(f32[8,1,128]{2,1,0:T(1,128)S(1)} %get-tuple-element.389) | copy-start | bytes 12292
  94.7 26.0 %collective-permute-start.4 = (bf16[1024,256]{0,1:T(8,128)(2,1)}, bf16[1024,256]{0,1:T(8,128)(2,1)}, u32[]{:S(2)}, u32[]{:S(2)}) collective-permute-start(bf16[1024,256]{0,1:T(8,128)(2,1)} %bitcast.182), channel_id=1, source_target_pairs={{0,2},{1,3},{2,0},{3,1},{4,6},{5,7},{6,4},{7,5},{8,10},{9,11},{10,... | collective-permute-start | bytes 1572872 | tf_op jit(solution)/shard_map/ppermute | solution.py:478
  98.1 23.8 %collective-permute-start.7 = (bf16[1024,256]{1,0:T(8,128)(2,1)}, bf16[1024,256]{1,0:T(8,128)(2,1)}, u32[]{:S(2)}, u32[]{:S(2)}) collective-permute-start(bf16[1024,256]{1,0:T(8,128)(2,1)} %bitcast.35), channel_id=1, source_target_pairs={{0,2},{1,3},{2,0},{3,1},{4,6},{5,7},{6,4},{7,5},{8,10},{9,11},{10,... | collective-permute-start | bytes 1572872 | tf_op jit(solution)/shard_map/ppermute | solution.py:478
  101.7 20.9 %collective-permute-start.3 = (bf16[1024,256]{0,1:T(8,128)(2,1)}, bf16[1024,256]{0,1:T(8,128)(2,1)}, u32[]{:S(2)}, u32[]{:S(2)}) collective-permute-start(bf16[1024,256]{0,1:T(8,128)(2,1)} %bitcast.182), channel_id=1, source_target_pairs={{0,1},{1,0},{2,3},{3,2},{4,5},{5,4},{6,7},{7,6},{8,9},{9,8},{10,11... | collective-permute-start | bytes 1572872 | tf_op jit(solution)/shard_map/ppermute | solution.py:478
  102.1 22.5 %collective-permute-start.6 = (bf16[1024,256]{1,0:T(8,128)(2,1)}, bf16[1024,256]{1,0:T(8,128)(2,1)}, u32[]{:S(2)}, u32[]{:S(2)}) collective-permute-start(bf16[1024,256]{1,0:T(8,128)(2,1)} %bitcast.35), channel_id=1, source_target_pairs={{0,1},{1,0},{2,3},{3,2},{4,5},{5,4},{6,7},{7,6},{8,9},{9,8},{10,11... | collective-permute-start | bytes 1572872 | tf_op jit(solution)/shard_map/ppermute | solution.py:478
  120.7 2.2 collective-permute-start.5
  121.9 2.7 collective-permute-start.8
  135.0 202.5 %all-gather.12.cloned.1.call-start = ((), (), s32[]{:S(2)}) async-start(), calls=%async_computation.9 | async-start | bytes 2359296 | tf_op jit(solution)/shard_map/all_gather | solution.py:522
  136.0 9.4 %collective-permute-start.9 = (u16[1024,128]{1,0:T(8,128)(2,1)}, u16[1024,128]{1,0:T(8,128)(2,1)}, u32[]{:S(2)}, u32[]{:S(2)}) collective-permute-start(u16[1024,128]{1,0:T(8,128)(2,1)} %get-tuple-element.283), channel_id=1, source_target_pairs={{0,4},{4,0},{8,12},{12,8},{16,20},{20,16},{24,28},{28,24},{1,5},{5... | collective-permute-start | bytes 786440 | tf_op jit(solution)/shard_map/ppermute | solution.py:478
  136.5 22.7 %collective-permute-start.10 = (u16[1024,128]{1,0:T(8,128)(2,1)}, u16[1024,128]{1,0:T(8,128)(2,1)}, u32[]{:S(2)}, u32[]{:S(2)}) collective-permute-start(u16[1024,128]{1,0:T(8,128)(2,1)} %get-tuple-element.283), channel_id=1, source_target_pairs={{0,8},{4,12},{8,0},{12,4},{16,24},{20,28},{24,16},{28,20},{1,9},{5... | collective-permute-start | bytes 786440 | tf_op jit(solution)/shard_map/ppermute | solution.py:478
  138.0 39.9 %collective-permute-start.12 = (u16[1024,128]{1,0:T(8,128)(2,1)}, u16[1024,128]{1,0:T(8,128)(2,1)}, u32[]{:S(2)}, u32[]{:S(2)}) collective-permute-start(u16[1024,128]{1,0:T(8,128)(2,1)} %get-tuple-element.283), channel_id=1, source_target_pairs={{0,16},{4,20},{8,24},{12,28},{16,0},{20,4},{24,8},{28,12},{1,17},{... | collective-permute-start | bytes 786440 | tf_op jit(solution)/shard_map/ppermute | solution.py:478
  145.3 54.0 %copy-start.69 = (bf16[8,128,128]{2,1,0:T(8,128)(2,1)S(1)}, bf16[8,128,128]{2,1,0:T(8,128)(2,1)}, u32[]{:S(2)}) copy-start(bf16[8,128,128]{2,1,0:T(8,128)(2,1)} %get-tuple-element.309) | copy-start | bytes 786436
  145.3 54.1 %copy-start.70 = (bf16[8,128,128]{2,1,0:T(8,128)(2,1)S(1)}, bf16[8,128,128]{2,1,0:T(8,128)(2,1)}, u32[]{:S(2)}) copy-start(bf16[8,128,128]{2,1,0:T(8,128)(2,1)} %get-tuple-element.310) | copy-start | bytes 786436
  145.3 54.1 %copy-start.71 = (bf16[8,128,128]{2,1,0:T(8,128)(2,1)S(1)}, bf16[8,128,128]{2,1,0:T(8,128)(2,1)}, u32[]{:S(2)}) copy-start(bf16[8,128,128]{2,1,0:T(8,128)(2,1)} %get-tuple-element.311) | copy-start | bytes 786436
  145.3 54.1 %copy-start.72 = (bf16[8,128,128]{2,1,0:T(8,128)(2,1)S(1)}, bf16[8,128,128]{2,1,0:T(8,128)(2,1)}, u32[]{:S(2)}) copy-start(bf16[8,128,128]{2,1,0:T(8,128)(2,1)} %get-tuple-element.312) | copy-start | bytes 786436
  145.3 54.2 %copy-start.50 = (bf16[1024,1024]{0,1:T(8,128)(2,1)S(1)}, bf16[1024,1024]{0,1:T(8,128)(2,1)}, u32[]{:S(2)}) copy-start(bf16[1024,1024]{0,1:T(8,128)(2,1)} %copy-done.49) | copy-start | bytes 6291460
  145.4 30.8 %collective-permute-start.11 = (u16[1024,128]{1,0:T(8,128)(2,1)}, u16[1024,128]{1,0:T(8,128)(2,1)S(1)}, u32[]{:S(2)}, u32[]{:S(2)}) collective-permute-start(u16[1024,128]{1,0:T(8,128)(2,1)} %collective-permute-done.9), channel_id=1, source_target_pairs={{0,8},{4,12},{8,0},{12,4},{16,24},{20,28},{24,16},{28,20},{1,9},{5... | collective-permute-start | bytes 786440 | tf_op jit(solution)/shard_map/ppermute | solution.py:478
  146.9 46.0 %collective-permute-start.13 = (u16[1024,128]{1,0:T(8,128)(2,1)}, u16[1024,128]{1,0:T(8,128)(2,1)S(1)}, u32[]{:S(2)}, u32[]{:S(2)}) collective-permute-start(u16[1024,128]{1,0:T(8,128)(2,1)} %collective-permute-done.9), channel_id=1, source_target_pairs={{0,16},{4,20},{8,24},{12,28},{16,0},{20,4},{24,8},{28,12},{1,17},{... | collective-permute-start | bytes 786440 | tf_op jit(solution)/shard_map/ppermute | solution.py:478
  159.2 39.3 %collective-permute-start.14 = (u16[1024,128]{1,0:T(8,128)(2,1)}, u16[1024,128]{1,0:T(8,128)(2,1)S(1)}, u32[]{:S(2)}, u32[]{:S(2)}) collective-permute-start(u16[1024,128]{1,0:T(8,128)(2,1)} %collective-permute-done.10), channel_id=1, source_target_pairs={{0,16},{4,20},{8,24},{12,28},{16,0},{20,4},{24,8},{28,12},{1,17},{... | collective-permute-start | bytes 786440 | tf_op jit(solution)/shard_map/ppermute | solution.py:478
  176.2 35.9 %collective-permute-start.15 = (u16[1024,128]{1,0:T(8,128)(2,1)S(1)}, u16[1024,128]{1,0:T(8,128)(2,1)S(1)}, u32[]{:S(2)}, u32[]{:S(2)}) collective-permute-start(u16[1024,128]{1,0:T(8,128)(2,1)S(1)} %collective-permute-done.11), channel_id=1, source_target_pairs={{0,16},{4,20},{8,24},{12,28},{16,0},{20,4},{24,8},{28,12},{1,17},{... | collective-permute-start | bytes 786440 | tf_op jit(solution)/shard_map/ppermute | solution.py:478
  203.2 12.0 %collective-permute-start.16 = (f32[1024,128]{1,0:T(8,128)S(1)}, f32[1024,128]{1,0:T(8,128)S(1)}, u32[]{:S(2)}, u32[]{:S(2)}) collective-permute-start(f32[1024,128]{1,0:T(8,128)S(1)} %pick_scores.1), channel_id=1, source_target_pairs={{0,2},{1,3},{2,0},{3,1},{4,6},{5,7},{6,4},{7,5},{8,10},{9,11},{10,... | collective-permute-start | bytes 1572872 | tf_op jit(solution)/shard_map/ppermute | solution.py:486
  215.3 2.8 collective-permute-start.17
  218.2 119.3 %copy-start.19 = (f32[1024,128]{1,0:T(8,128)}, f32[1024,128]{1,0:T(8,128)S(1)}, u32[]{:S(2)}) copy-start(f32[1024,128]{1,0:T(8,128)S(1)} %add.249) | copy-start | bytes 1572868
  218.4 119.0 %copy-start.87 = (f32[1024,4]{0,1:T(4,128)}, f32[1024,4]{0,1:T(4,128)S(1)}, u32[]{:S(2)}) copy-start(f32[1024,4]{0,1:T(4,128)S(1)} %bitcast_reduce_fusion) | copy-start | bytes 49156
  219.4 118.1 %copy-start.21 = (f32[1024,128]{1,0:T(8,128)}, f32[1024,128]{1,0:T(8,128)S(1)}, u32[]{:S(2)}) copy-start(f32[1024,128]{1,0:T(8,128)S(1)} %copy.139) | copy-start | bytes 1572868
  219.7 117.8 %copy-start.23 = (f32[1024,128]{1,0:T(8,128)}, f32[1024,128]{1,0:T(8,128)S(1)}, u32[]{:S(2)}) copy-start(f32[1024,128]{1,0:T(8,128)S(1)} %copy.138) | copy-start | bytes 1572868
  220.6 245.0 %reduce-scatter.5.cloned.1.call-start = ((), (), s32[]{:S(2)}) async-start(), calls=%async_computation.4 | async-start | bytes 2359296 | tf_op jit(solution)/shard_map/reduce_scatter | solution.py:526
  337.6 216.4 %reduce-scatter.7.cloned.1.call-start = ((), (), s32[]{:S(2)}) async-start(), calls=%async_computation.5 | async-start | bytes 4718592 | tf_op jit(solution)/shard_map/reduce_scatter | solution.py:526
  466.7 316.3 %reduce-scatter.9.cloned.1.call-start = ((), (), s32[]{:S(2)}) async-start(), calls=%async_computation.6 | async-start | bytes 2654208 | tf_op jit(solution)/shard_map/reduce_scatter | solution.py:526
  466.8 13.8 %collective-permute-start.21 = (f32[1024,128]{1,0:T(8,128)S(1)}, f32[1024,128]{1,0:T(8,128)S(1)}, u32[]{:S(2)}, u32[]{:S(2)}) collective-permute-start(f32[1024,128]{1,0:T(8,128)S(1)} %bitcast_convert_fusion), channel_id=1, source_target_pairs={{0,2},{1,3},{2,0},{3,1},{4,6},{5,7},{6,4},{7,5},{8,10},{9,11},{10,... | collective-permute-start | bytes 1572872 | tf_op jit(solution)/shard_map/ppermute | solution.py:486
  481.4 2.3 collective-permute-start.22
  506.0 48.0 %copy-start.61 = (f32[1024,256]{1,0:T(8,128)S(1)}, f32[1024,256]{1,0:T(8,128)}, u32[]{:S(2)}) copy-start(f32[1024,256]{1,0:T(8,128)} %copy-done.60) | copy-start | bytes 3145732
  507.3 48.5 %copy-start.58 = (bf16[8,128,256]{2,1,0:T(8,128)(2,1)S(1)}, bf16[8,128,256]{2,1,0:T(8,128)(2,1)}, u32[]{:S(2)}) copy-start(bf16[8,128,256]{2,1,0:T(8,128)(2,1)} %copy-done.57) | copy-start | bytes 1572868
  564.4 10.7 %collective-permute-start.24 = (bf16[1024,256]{0,1:T(8,128)(2,1)}, bf16[1024,256]{0,1:T(8,128)(2,1)}, u32[]{:S(2)}, u32[]{:S(2)}) collective-permute-start(bf16[1024,256]{0,1:T(8,128)(2,1)} %get-tuple-element.301), channel_id=1, source_target_pairs={{0,1},{1,0},{2,3},{3,2},{4,5},{5,4},{6,7},{7,6},{8,9},{9,8},{10,11... | collective-permute-start | bytes 1572872 | tf_op jit(solution)/shard_map/ppermute | solution.py:468
  572.3 6.8 collective-permute-start.23
  572.8 4.4 collective-permute-start.26
  576.6 13.7 %collective-permute-start.25 = (bf16[1024,256]{0,1:T(8,128)(2,1)S(1)}, bf16[1024,256]{0,1:T(8,128)(2,1)S(1)}, u32[]{:S(2)}, u32[]{:S(2)}) collective-permute-start(bf16[1024,256]{0,1:T(8,128)(2,1)S(1)} %fusion.78), channel_id=1, source_target_pairs={{0,2},{1,3},{2,0},{3,1},{4,6},{5,7},{6,4},{7,5},{8,10},{9,11},{10,... | collective-permute-start | bytes 1572872 | tf_op jit(solution)/shard_map/ppermute | solution.py:468
  577.2 1.8 collective-permute-start.27
  593.5 12.9 %collective-permute-start.29 = (bf16[1024,256]{0,1:T(8,128)(2,1)S(1)}, bf16[1024,256]{0,1:T(8,128)(2,1)}, u32[]{:S(2)}, u32[]{:S(2)}) collective-permute-start(bf16[1024,256]{0,1:T(8,128)(2,1)S(1)} %get-tuple-element.280), channel_id=1, source_target_pairs={{0,2},{1,3},{2,0},{3,1},{4,6},{5,7},{6,4},{7,5},{8,10},{9,11},{10,... | collective-permute-start | bytes 1572872 | tf_op jit(solution)/shard_map/ppermute | solution.py:478
  605.7 5.0 collective-permute-start.28
  606.4 4.3 collective-permute-start.30
  677.2 3.7 collective-permute-start.37
  680.8 1.6 collective-permute-start.38
  687.1 140.7 %reduce-scatter.11.cloned.1.call-start = ((), (), s32[]{:S(2)}) async-start(), calls=%async_computation.7 | async-start | bytes 2654208 | tf_op jit(solution)/shard_map/reduce_scatter | solution.py:526
  693.5 12.9 %collective-permute-start.35 = (bf16[1024,256]{0,1:T(8,128)(2,1)S(1)}, bf16[1024,256]{0,1:T(8,128)(2,1)S(1)}, u32[]{:S(2)}, u32[]{:S(2)}) collective-permute-start(bf16[1024,256]{0,1:T(8,128)(2,1)S(1)} %get-tuple-element.289), channel_id=1, source_target_pairs={{0,1},{1,0},{2,3},{3,2},{4,5},{5,4},{6,7},{7,6},{8,9},{9,8},{10,11... | collective-permute-start | bytes 1572872 | tf_op jit(solution)/shard_map/ppermute | solution.py:468
  694.0 72.1 %collective-permute-start.34 = (bf16[1024,256]{0,1:T(8,128)(2,1)}, bf16[1024,256]{0,1:T(8,128)(2,1)S(1)}, u32[]{:S(2)}, u32[]{:S(2)}) collective-permute-start(bf16[1024,256]{0,1:T(8,128)(2,1)} %get-tuple-element.288), channel_id=1, source_target_pairs={{0,1},{1,0},{2,3},{3,2},{4,5},{5,4},{6,7},{7,6},{8,9},{9,8},{10,11... | collective-permute-start | bytes 1572872 | tf_op jit(solution)/shard_map/ppermute | solution.py:468
  705.8 57.1 %collective-permute-start.32 = (bf16[1024,256]{0,1:T(8,128)(2,1)}, bf16[1024,256]{0,1:T(8,128)(2,1)S(1)}, u32[]{:S(2)}, u32[]{:S(2)}) collective-permute-start(bf16[1024,256]{0,1:T(8,128)(2,1)} %get-tuple-element.295), channel_id=1, source_target_pairs={{0,1},{1,0},{2,3},{3,2},{4,5},{5,4},{6,7},{7,6},{8,9},{9,8},{10,11... | collective-permute-start | bytes 1572872 | tf_op jit(solution)/shard_map/ppermute | solution.py:468
  708.6 58.3 %copy-start.39 = (f32[1024,256]{0,1:T(8,128)S(1)}, f32[1024,256]{0,1:T(8,128)}, u32[]{:S(2)}) copy-start(f32[1024,256]{0,1:T(8,128)} %get-tuple-element.281) | copy-start | bytes 3145732
  708.6 58.3 %copy-start.101 = (f32[1024]{0:T(1024)S(1)}, f32[1024]{0:T(1024)}, u32[]{:S(2)}) copy-start(f32[1024]{0:T(1024)} %get-tuple-element.391) | copy-start | bytes 12292
  708.6 57.5 %collective-permute-start.36 = (bf16[1024,256]{0,1:T(8,128)(2,1)}, bf16[1024,256]{0,1:T(8,128)(2,1)S(1)}, u32[]{:S(2)}, u32[]{:S(2)}) collective-permute-start(bf16[1024,256]{0,1:T(8,128)(2,1)} %fusion.69), channel_id=1, source_target_pairs={{0,2},{1,3},{2,0},{3,1},{4,6},{5,7},{6,4},{7,5},{8,10},{9,11},{10,... | collective-permute-start | bytes 1572872 | tf_op jit(solution)/shard_map/ppermute | solution.py:468
  762.9 7.2 collective-permute-start.31
  765.0 14.6 %collective-permute-start.33 = (bf16[1024,256]{0,1:T(8,128)(2,1)}, bf16[1024,256]{0,1:T(8,128)(2,1)}, u32[]{:S(2)}, u32[]{:S(2)}) collective-permute-start(bf16[1024,256]{0,1:T(8,128)(2,1)} %fusion.74), channel_id=1, source_target_pairs={{0,2},{1,3},{2,0},{3,1},{4,6},{5,7},{6,4},{7,5},{8,10},{9,11},{10,... | collective-permute-start | bytes 1572872 | tf_op jit(solution)/shard_map/ppermute | solution.py:468
  (90 other events, 596.2 us)
Sparse Core Ops, SparseCore 0:
  11.5 52.2 all-gather.15
  66.7 50.7 all-gather.9
  135.2 102.3 all-gather.13
  240.1 48.5 all-gather.11
  337.7 67.1 reduce-scatter.4
  466.8 87.1 reduce-scatter.6
  687.2 68.6 reduce-scatter.8
  759.7 68.0 reduce-scatter.10

commit v4 on v3

--- a/solution.py
+++ b/solution.py
@@ -12,7 +12,10 @@
 NKEYS = 256
 TOPK = 32
 PICKS = 128
+DOCS = 3
+DOC_MOST = 512
 LANES = 128
+PARTS = 2
 
 
 EPSILON = 1e-06
@@ -28,84 +31,126 @@
     return (factor, activations * factor * gain_row)
 
 
-def masked_scores(query_block, key_rows, segment_block, segment_row, offset):
-    block_rows = query_block.shape[0]
-    positions = jnp.arange(key_rows.shape[0], dtype=jnp.int32)
-    scores = jnp.einsum("qhd,khd->hqk", query_block, key_rows, preferred_element_type=jnp.float32)
-    scores = scores * query_block.shape[2] ** (-0.5)
-    allowed = (positions[None, :] <= (offset + positions[:block_rows])[:, None]) & (
-        segment_block[:, None] == segment_row[None, :]
-    )
-    return jnp.where(allowed[None], scores, MASKED)
-
-
-def attend_forward(queries, key_rows, value_rows, segment_row):
-    length = queries.shape[0]
-    block_rows = min(512, length)
-
-    def one_block(number):
-        offset = number * block_rows
-        query_block = lax.dynamic_slice_in_dim(queries, offset, block_rows, 0)
-        segment_block = lax.dynamic_slice_in_dim(segment_row, offset, block_rows, 0)
-        scores = masked_scores(query_block, key_rows, segment_block, segment_row, offset)
-        row_peak = jnp.max(scores, axis=-1, keepdims=True)
-        raised = jnp.exp(scores - row_peak)
-        totals = jnp.sum(raised, axis=-1, keepdims=True)
-        attention = (raised / totals).astype(jnp.bfloat16)
-        mixture = jnp.einsum(
-            "hqk,khd->qhd", attention, value_rows, preferred_element_type=jnp.float32
-        )
-        return (mixture.astype(jnp.bfloat16), (row_peak + jnp.log(totals))[:, :, 0])
-
-    outputs, logsum = lax.map(one_block, jnp.arange(length // block_rows, dtype=jnp.int32))
-    head_width = queries.shape[1] * queries.shape[2]
-    logsum = jnp.transpose(logsum, (1, 0, 2)).reshape(queries.shape[1], length)
-    return (outputs.reshape(length, head_width), logsum)
-
-
-def attend_backward(queries, key_rows, value_rows, segment_row, logsum, heads_grad):
-    length = queries.shape[0]
-    block_rows = min(512, length)
-    factor = queries.shape[2] ** (-0.5)
-
-    def one_block(running, number):
-        key_sum, value_sum = running
-        offset = number * block_rows
-        query_block = lax.dynamic_slice_in_dim(queries, offset, block_rows, 0)
-        segment_block = lax.dynamic_slice_in_dim(segment_row, offset, block_rows, 0)
-        grad_block = lax.dynamic_slice_in_dim(heads_grad, offset, block_rows, 0)
-        logsum_block = lax.dynamic_slice_in_dim(logsum, offset, block_rows, 1)
-        scores = masked_scores(query_block, key_rows, segment_block, segment_row, offset)
-        attention = jnp.exp(scores - logsum_block[:, :, None])
-        prob_grad = jnp.einsum(
-            "qhd,khd->hqk", grad_block, value_rows, preferred_element_type=jnp.float32
-        )
-        centre = jnp.sum(attention * prob_grad, axis=-1, keepdims=True)
-        score_grad = (attention * (prob_grad - centre)).astype(jnp.bfloat16)
-        query_grad = (
-            jnp.einsum("hqk,khd->qhd", score_grad, key_rows, preferred_element_type=jnp.float32)
-            * factor
-        )
-        key_sum = (
-            key_sum
-            + jnp.einsum(
-                "hqk,qhd->khd", score_grad, query_block, preferred_element_type=jnp.float32
+def document_starts(segment_row):
+    starts = jnp.zeros(segment_row.shape, jnp.int32)
+    for number in range(1, DOCS):
+        before = jnp.sum((segment_row == number - 1).astype(jnp.int32))
+        starts = starts + jnp.where(segment_row >= number, before, 0)
+    return starts
+
+
+def key_window(block, rows):
+    first = max(0, (block * rows - (DOC_MOST - 1)) // rows * rows)
+    return first, (block + 1) * rows
+
+
+def head_lanes(shape, head, axis):
+    return lax.broadcasted_iota(jnp.int32, shape, axis) // HD == head
+
+
+def turned_probs(keys, queries, starts, first, offset):
+    scores = lax.dot_general(keys, queries, NT, preferred_element_type=F32) * HD ** (-0.5)
+    key_ids = lax.broadcasted_iota(jnp.int32, scores.shape, 0) + first
+    query_ids = lax.broadcasted_iota(jnp.int32, scores.shape, 1) + offset
+    allowed = (key_ids >= starts) & (key_ids <= query_ids)
+    scores = jnp.where(allowed, scores, MASKED)
+    raised = jnp.exp(scores - jnp.max(scores, axis=0, keepdims=True))
+    return raised * (1.0 / jnp.sum(raised, axis=0, keepdims=True))
+
+
+def attend_body(start_ref, query_ref, key_ref, value_ref, out_ref, *, rows):
+    length = query_ref.shape[0]
+    values_turned = value_ref[...].T
+    for block in range(length // rows):
+        first, last = key_window(block, rows)
+        span = slice(block * rows, last)
+        queries = query_ref[span, :]
+        mixture = jnp.zeros((LANES, rows), F32)
+        for head in range(LANES // HD):
+            own = jnp.where(head_lanes(queries.shape, head, 1), queries, jnp.zeros((), BF16))
+            probs = turned_probs(
+                key_ref[first:last, :], own, start_ref[:, span], first, block * rows
             )
-            * factor
-        )
-        value_sum = value_sum + jnp.einsum(
-            "hqk,qhd->khd",
-            attention.astype(jnp.bfloat16),
-            grad_block,
-            preferred_element_type=jnp.float32,
-        )
-        return ((key_sum, value_sum), query_grad)
-
-    empty_sum = jnp.zeros(key_rows.shape, jnp.float32)
-    carried, query_parts = lax.scan(
-        one_block, (empty_sum, empty_sum), jnp.arange(length // block_rows, dtype=jnp.int32)
-    )
-    return (query_parts.reshape(queries.shape), carried[0], carried[1])
+            part = jnp.dot(
+                values_turned[:, first:last], probs.astype(BF16), preferred_element_type=F32
+            )
+            mixture = jnp.where(head_lanes(part.shape, head, 0), part, mixture)
+        out_ref[span, :] = mixture.T.astype(BF16)
+
+
+def attend_forward(starts, queries, key_rows, value_rows, rows=256):
+    length, width = queries.shape
+    column = pl.BlockSpec((length, LANES), lambda i: (0, i))
+    return pl.pallas_call(
+        functools.partial(attend_body, rows=rows),
+        grid=(width // LANES,),
+        in_specs=[pl.BlockSpec((1, length), lambda i: (0, 0)), column, column, column],
+        out_specs=column,
+        out_shape=jax.ShapeDtypeStruct((length, width), BF16),
+        compiler_params=params(32),
+        cost_estimate=pl.CostEstimate(
+            flops=16 * length * length * width, bytes_accessed=8 * length * width, transcendentals=0
+        ),
+        name="attend_forward",
+    )(starts, queries, key_rows, value_rows)
+
+
+def attend_back_body(
+    start_ref, query_ref, key_ref, value_ref, grad_ref, dq_ref, dk_ref, dv_ref, key_sum, value_sum,
+    *, rows
+):
+    length = query_ref.shape[0]
+    keys_turned = key_ref[...].T
+    key_sum[...] = jnp.zeros_like(key_sum)
+    value_sum[...] = jnp.zeros_like(value_sum)
+    zero = jnp.zeros((), BF16)
+    factor = HD ** (-0.5)
+    for block in range(length // rows):
+        first, last = key_window(block, rows)
+        span = slice(block * rows, last)
+        window = slice(first, last)
+        queries = query_ref[span, :]
+        grads = grad_ref[span, :]
+        query_sum = jnp.zeros((LANES, rows), F32)
+        for head in range(LANES // HD):
+            mask = head_lanes(queries.shape, head, 1)
+            own = jnp.where(mask, queries, zero)
+            own_grads = jnp.where(mask, grads, zero)
+            probs = turned_probs(key_ref[window, :], own, start_ref[:, span], first, block * rows)
+            prob_grad = lax.dot_general(
+                value_ref[window, :], own_grads, NT, preferred_element_type=F32
+            )
+            centre = jnp.sum(probs * prob_grad, axis=0, keepdims=True)
+            score_grad = (probs * (prob_grad - centre)).astype(BF16)
+            part = jnp.dot(keys_turned[:, window], score_grad, preferred_element_type=F32)
+            query_sum = jnp.where(head_lanes(part.shape, head, 0), part, query_sum)
+            key_sum[window, :] += jnp.dot(score_grad, own, preferred_element_type=F32)
+            value_sum[window, :] += jnp.dot(
+                probs.astype(BF16), own_grads, preferred_element_type=F32
+            )
+        dq_ref[span, :] = (query_sum.T * factor).astype(BF16)
+    dk_ref[...] = (key_sum[...] * factor).astype(BF16)
+    dv_ref[...] = value_sum[...].astype(BF16)
+
+
+def attend_backward(starts, queries, key_rows, value_rows, heads_grad, rows=256):
+    length, width = queries.shape
+    column = pl.BlockSpec((length, LANES), lambda i: (0, i))
+    return pl.pallas_call(
+        functools.partial(attend_back_body, rows=rows),
+        grid=(width // LANES,),
+        in_specs=[pl.BlockSpec((1, length), lambda i: (0, 0))] + [column] * 4,
+        out_specs=[column] * 3,
+        out_shape=[jax.ShapeDtypeStruct((length, width), BF16)] * 3,
+        scratch_shapes=[pltpu.VMEM((length, LANES), F32)] * 2,
+        compiler_params=params(40),
+        cost_estimate=pl.CostEstimate(
+            flops=40 * length * length * width,
+            bytes_accessed=14 * length * width,
+            transcendentals=0,
+        ),
+        name="attend_backward",
+    )(starts, queries, key_rows, value_rows, heads_grad)
 
 
 SLOTS = 32
@@ -166,9 +211,10 @@
 
 
 def bag_body(
-    base_ref, picks_ref, weight_ref, table_ref, out_ref, keep_ref, counts, locals_, high, low,
-    weights, *, chunk, unroll
+    base_ref, picks_ref, weight_ref, table_ref, before_ref, out_ref, keep_ref, counts, locals_,
+    high, low, weights, *, chunk, unroll
 ):
+    del before_ref
     rows = picks_ref.shape[0]
     total = table_ref.shape[0]
     groups = total // NKEYS
@@ -236,26 +282,32 @@
     out_ref[...] = result.astype(out_ref.dtype)
 
 
-def bag_sums(base, picks, weights, table, rows=256, chunk=1024, unroll=8):
+def bag_sums(base, picks, weights, table, before, part, parts, shards, rows=256, chunk=1024,
+             unroll=8):
     amount = picks.shape[0]
     total, width = table.shape
+    whole = amount // shards // rows
+    count = whole // parts
+
+    def place(i):
+        return (i // count * whole + part * count + i % count, 0)
+
+    kept = jax.ShapeDtypeStruct((amount, total), BF16)
     return pl.pallas_call(
         functools.partial(bag_body, chunk=chunk, unroll=unroll),
-        grid=(amount // rows,),
+        grid=(shards * count,),
         in_specs=[
             pl.BlockSpec(memory_space=pltpu.SMEM),
-            pl.BlockSpec((rows, PICKS), lambda i: (i, 0)),
-            pl.BlockSpec((rows, PICKS), lambda i: (i, 0)),
+            pl.BlockSpec((rows, PICKS), place),
+            pl.BlockSpec((rows, PICKS), place),
             pl.BlockSpec((total, width), lambda i: (0, 0)),
+            pl.BlockSpec(memory_space=pl.ANY),
         ],
         out_specs=[
             pl.BlockSpec((rows, width), lambda i: (i, 0)),
-            pl.BlockSpec((rows, total), lambda i: (i, 0)),
+            pl.BlockSpec((rows, total), place),
         ],
-        out_shape=[
-            jax.ShapeDtypeStruct((amount, width), BF16),
-            jax.ShapeDtypeStruct((amount, total), BF16),
-        ],
+        out_shape=[jax.ShapeDtypeStruct((amount // parts, width), BF16), kept],
         scratch_shapes=[
             pltpu.VMEM((rows, LANES), F32),
             pltpu.VMEM((rows, LANES), jnp.int32),
@@ -263,12 +315,15 @@
             pltpu.VMEM((rows, LANES), F32),
             pltpu.VMEM((rows, LANES), F32),
         ],
+        input_output_aliases={} if before is None else {4: 1},
         compiler_params=params(56),
         cost_estimate=pl.CostEstimate(
-            flops=9 * amount * total * width, bytes_accessed=amount * total * 2, transcendentals=0
+            flops=9 * amount * total * width // parts,
+            bytes_accessed=amount * total * 2 // parts,
+            transcendentals=0,
         ),
         name="bag_sums",
-    )(base, picks, weights, table)
+    )(base, picks, weights, table, base if before is None else before)
 
 
 def picked_body(
@@ -468,17 +523,24 @@
     return lax.ppermute(block, "narrow", [(i, i ^ bit) for i in range(size)])
 
 
+def swap_all(held, axis, bit):
+    pairs = [(i, i ^ bit) for i in range(lax.axis_size(axis))]
+    moved = {offset ^ bit: lax.ppermute(part, axis, pairs) for offset, part in held.items()}
+    return {**held, **moved}
+
+
+def in_order(held, axis):
+    me = lax.axis_index(axis)
+    size = lax.axis_size(axis)
+    stacked = jnp.stack([held[offset] for offset in range(size)])
+    return [lax.dynamic_index_in_dim(stacked, me ^ number, 0, False) for number in range(size)]
+
+
 def gather_by_swaps(block, axis, bits):
-    size = lax.axis_size(axis)
-    me = lax.axis_index(axis)
     held = {0: block}
     for bit in bits:
-        moved = {}
-        for offset, part in held.items():
-            moved[offset ^ bit] = lax.ppermute(part, axis, [(i, i ^ bit) for i in range(size)])
-        held.update(moved)
-    stacked = jnp.stack([held[offset] for offset in range(size)])
-    return [lax.dynamic_index_in_dim(stacked, me ^ number, 0, False) for number in range(size)]
+        held = swap_all(held, axis, bit)
+    return in_order(held, axis)
 
 
 def sum_by_swaps(block, axis):
@@ -622,25 +684,28 @@
     ).reshape(units, NKEYS, NKEYS)
     out_all = gather_narrow(out_turned)
     upstream = gather_narrow(cotangent)
-    all_picks = jnp.concatenate(
-        gather_by_swaps(picks.astype(jnp.uint16), "wide", bits_down(shards)[::-1]), axis=0
-    ).astype(jnp.int32)
+    moving = {0: picks.astype(jnp.uint16)}
+    bits = bits_down(shards)
+    moving = swap_all(moving, "wide", bits[0])
+    rows_one, moving = lax.optimization_barrier((rows_one, moving))
+    for bit in bits[1:-1]:
+        moving = swap_all(moving, "wide", bit)
 
     factor_one, normed = norm_rows(rows_one, gain_one)
     normed = normed.astype(BF16)
-    mixture = [
+    normed, moving = lax.optimization_barrier((normed, moving))
+    moving = swap_all(moving, "wide", bits[-1])
+    queries, key_rows, value_rows = [
         jnp.dot(normed, qkv_full[j], preferred_element_type=F32).astype(BF16) for j in range(3)
     ]
-    head_count = width // HD
-    queries, key_rows, value_rows = [
-        member.reshape(length, head_count, HD) for member in mixture
-    ]
-    segment_row = segments[0]
-    head_rows, logsum = attend_forward(queries, key_rows, value_rows, segment_row)
+    starts = document_starts(segments)
+    head_rows = attend_forward(starts, queries, key_rows, value_rows)
     head_all = gather_narrow(head_rows)
     hidden = rows_one + lax.dot_general(head_all, out_all, NT, preferred_element_type=F32)
     factor_two, second = norm_rows(hidden, gain_two)
     second = second.astype(BF16)
+    second, moving = lax.optimization_barrier((second, moving))
+    all_picks = jnp.concatenate(in_order(moving, "wide"), axis=0).astype(jnp.int32)
 
     gate_value = jnp.dot(second, gate_full, preferred_element_type=F32)
     gate_act = jax.nn.silu(gate_value)
@@ -660,12 +725,18 @@
 
     pick_part = picked_products(base, all_picks, all_grads, memory_values.T)
     all_weights, pick_part = lax.optimization_barrier((all_weights, pick_part))
-    memory_part, tables = bag_sums(base, all_picks, all_weights, memory_values)
     pick_own = sum_wide(pick_part.reshape(shards, length, PICKS)).astype(F32)
-    memory_part, pick_own = lax.optimization_barrier((memory_part, pick_own))
-    memory = sum_wide(memory_part.reshape(shards, length, width)).astype(F32)
-    tables, pick_own = lax.optimization_barrier((tables, pick_own))
+    tables = None
+    memory_parts = []
+    for number in range(PARTS):
+        part_sums, tables = bag_sums(
+            base, all_picks, all_weights, memory_values, tables, number, PARTS, shards
+        )
+        part_sums, pick_own = lax.optimization_barrier((part_sums, pick_own))
+        memory_parts.append(sum_wide(part_sums.reshape(shards, length // PARTS, width)))
     values_grad = lax.dot_general(tables, all_grads, TN, preferred_element_type=F32)
+    memory_parts, values_grad = lax.optimization_barrier((memory_parts, values_grad))
+    memory = jnp.concatenate(memory_parts, axis=0).astype(F32)
 
     pick_grad = sum_by_swaps(pick_own, "narrow").reshape(length, PKH, TOPK)
     centre = jnp.sum(mem_probs * pick_grad, axis=-1, keepdims=True)
@@ -707,7 +778,7 @@
     outputs = (own_hidden + scatter_narrow(mixer_part)).astype(BF16)
 
     heads_grad = jnp.dot(branch_grad, out_turned, preferred_element_type=F32)
-    heads_grad = heads_grad.astype(BF16).reshape(length, head_count, HD)
+    heads_grad = heads_grad.astype(BF16)
 
     mixer_grad = lax.dot_general(upstream, product, TN, preferred_element_type=F32)
     query_grad = lax.dot_general(second, memory_query_grad, TN, preferred_element_type=F32)
@@ -719,18 +790,7 @@
     def by_shard(block):
         return block.astype(BF16).reshape(shards, part, block.shape[1])
 
-    early_pack = pack([by_shard(mixer_grad), by_shard(gate_grad), by_shard(query_grad), key_grad])
-    early_pack, heads_grad = lax.optimization_barrier((early_pack, heads_grad))
-    early_sums = sum_wide(early_pack).astype(F32)
-    mixer_sums, gate_sums, query_sums, key_sums = unpack(early_sums, second_shapes)
-
-    query_back, key_back, value_back = attend_backward(
-        queries, key_rows, value_rows, segment_row, logsum, heads_grad
-    )
-    mixed_grad = [
-        member.reshape(length, width).astype(BF16)
-        for member in (query_back, key_back, value_back)
-    ]
+    mixed_grad = attend_backward(starts, queries, key_rows, value_rows, heads_grad)
     normed_part = sum(
         lax.dot_general(mixed_grad[j], qkv_full[j], NT, preferred_element_type=F32)
         for j in range(3)
@@ -753,10 +813,16 @@
     gain_parts = jnp.concatenate(
         [gain_one_part.reshape(shards, 1, part), gain_two_part.reshape(shards, 1, part)], axis=1
     ).astype(BF16).reshape(shards, -1, LANES)
-    late_pack = pack([by_shard(block) for block in qkv_grad] + [by_shard(out_grad), gain_parts])
-    late_sums = sum_wide(late_pack).astype(F32)
-    late_shapes = [(part, width)] * 4 + [(2 * part // LANES, LANES)]
-    query_sum, key_sum, value_sum, out_sum, gain_sums = unpack(late_sums, late_shapes)
+    all_grads_pack = pack(
+        [by_shard(block) for block in qkv_grad + [out_grad, mixer_grad, gate_grad, query_grad]]
+        + [key_grad, gain_parts]
+    )
+    sums = sum_wide(all_grads_pack).astype(F32)
+    sum_shapes = [(part, width)] * 4 + second_shapes + [(2 * part // LANES, LANES)]
+    (
+        query_sum, key_sum, value_sum, out_sum, mixer_sums, gate_sums, query_sums, key_sums,
+        gain_sums,
+    ) = unpack(sums, sum_shapes)
     gain_sums = gain_sums.reshape(2, part)
     return (
         outputs,

time: 844 us -> 774 us (0.917)
  matrix products: 132 us -> 79.9 us
  Pallas kernels: 242 us -> 270 us
  other arithmetic: 65.5 us -> 39.5 us
  waiting for transfers between devices: 250 us -> 230 us
    all_gather x4, waiting for transfers between devices: 54.3 us -> 100 us  [gather_wide(): return lax.all_gather(block, 'wide')]
    dot_general x14 -> x0, matrix products: 43.5 us -> none  [the longest x2 9.29 us: one_block(): jnp.einsum('hqk,khd->qhd', score_grad, key_rows, preferred_element_type=j...]
    ppermute x22, waiting for transfers between devices: 69.5 us -> 30.6 us  [swap_all(): lax.ppermute(part, axis, pairs)]
    reduce_scatter x4, waiting for transfers between devices: 87 us -> 50.2 us  [sum_wide(): return lax.psum_scatter(block, 'wide', scatter_dimension=0)]
    pallas_call x0 -> x2, Pallas kernels: none -> 22.2 us  [the longest x1 12.3 us: attend_backward(): pl.pallas_call(functools.partial(attend_back_body, rows=rows), grid=(widt...]
    unnamed x245 -> x276, local copies, waits for them, and re-layouts: 50.2 us -> 60.8 us
    ppermute x9, waiting for transfers between devices: 20.9 us -> 30.8 us  [swap_narrow(): return lax.ppermute(block, 'narrow', [(i, i ^ bit) for i in range(size)])]
    pallas_call x1 -> x2, Pallas kernels: 128 us -> 134 us  [bag_sums(): pl.pallas_call(functools.partial(bag_body, chunk=chunk, unroll=unroll), g...]
  transfers between devices with their start and end apart: 47 -> 47, of which waited for: 20 -> 17; matrix products, arithmetic and copies ran while one was open for 23% -> 21% of each run, Pallas kernels for 29% -> 34%
where the time goes in v4:
time: 774 us; the launch traced here: 767 us
  Pallas kernels  270 us (35%)
  waiting for transfers between devices  230 us (30%)
  local copies, waits for them, and re-layouts  103 us (13%)
  matrix products  79.9 us (10%)
  other arithmetic  39.5 us (5%)
  starting transfers between devices  27 us (3%)
  between operations  16.5 us (2%)
    pallas_call x2, Pallas kernels, bag_sums(): pl.pallas_call(functools.partial(bag_body, chunk=chunk, unroll=unroll), g...  134 us
    all_gather x4, waiting for transfers between devices, gather_wide(): return lax.all_gather(block, 'wide')  100 us
    pallas_call x1, Pallas kernels, picked_products(): pl.pallas_call(functools.partial(picked_body, unroll=unroll), grid=(amoun...  99.7 us
    unnamed x276, local copies, waits for them, and re-layouts  60.8 us
    dot_general x1, matrix products, per_device(): lax.dot_general(tables, all_grads, TN, preferred_element_type=F32)  53.8 us
    reduce_scatter x4, waiting for transfers between devices, sum_wide(): return lax.psum_scatter(block, 'wide', scatter_dimension=0)  50.2 us
    ppermute x9, waiting for transfers between devices, swap_narrow(): return lax.ppermute(block, 'narrow', [(i, i ^ bit) for i in range(size)])  30.8 us
    ppermute x22, waiting for transfers between devices, swap_all(): lax.ppermute(part, axis, pairs)  30.6 us
  transfers between devices with their start and end apart: 47, of which 17 were waited for; matrix products, arithmetic and copies ran while one was open for 21% of the time, Pallas kernels for 34%

profile of v4, /device:TPU:0, one launch (start us, length us, event | category | flops | bytes accessed | tf_op | source)
XLA Modules:
  0.0 766.7 jit_solution(17469261785084735280)
XLA Ops:
  11.6 3.0 collective-permute-start.1
  15.1 1.8 convert_element_type.179
  16.9 2.8 collective-permute-start.3
  22.0 5.5 collective-permute-done.1
  30.4 7.6 collective-permute-done.19
  43.8 28.3 %all-gather.16.cloned.1.call-done = bf16[8,1026,128]{2,1,0:T(8,128)(2,1)} async-done(((bf16[1,1026,128]{2,1,0:T(8,128)(2,1)}), bf16[8,1026,128]{2,1,0:T(8,128)(2,1)}) %all-gather.16.cloned.1.call-update) | async-done | bytes 2101264 | tf_op jit(solution)/shard_map/all_gather | solution.py:584
  73.2 1.7 collective-permute-start.10
  75.7 2.8 multiply_convert_fusion.1
  82.0 10.0 %attend_forward.1 = bf16[1024,256]{1,0:T(8,128)(2,1)S(1)} custom-call(s32[1,1024]{1,0:T(1,128)S(1)} %fusion.54.start_ref, bf16[1024,256]{1,0:T(8,128)(2,1)S(1)} %convolution_convert_fusion.11.query_ref, bf16[1024,256]{1,0:T(8,128)(2,1)S(1)} %convolution_convert_fusion.10.key_ref, bf16[1024,256]{1,0:T(8,128)(2,1)S(1)} %convolution_convert_fusion.9.value_ref), custom_call_target="tpu_custom_call" | custom-call | flops 4294967296 | bytes 2097152 | tf_op jit(solution)/shard_map/attend_forward/pallas_call | solution.py:84
  92.4 1.6 pad_maximum_fusion.6
  95.9 1.7 collective-permute-start.12
  97.6 31.1 %all-gather.10.cloned.1.call-done = bf16[9216,128]{0,1:T(8,128)(2,1)} async-done(((bf16[1152,128]{0,1:T(8,128)(2,1)}), bf16[9216,128]{0,1:T(8,128)(2,1)}) %all-gather.10.cloned.1.call-update) | async-done | bytes 2359312 | tf_op jit(solution)/shard_map/all_gather | solution.py:584
  128.7 3.1 copy.131
  134.3 1.5 collective-permute-start.14
  135.7 1.5 pad_maximum_fusion.5
  138.7 1.5 pad_maximum_fusion.4
  140.4 2.0 copy-done.17
  142.4 2.4 multiply_reduce_fusion.4
  146.8 1.9 collective-permute-done.14
  148.7 4.7 collective-permute-done.15
  155.0 1.9 multiply_convert_fusion.2
  157.0 6.7 copy.136
  164.0 1.8 copy-done.39
  167.2 2.3 pick_scores.1
  169.5 1.6 collective-permute-start.16
  174.9 7.7 %collective-permute-done.16 = f32[1024,128]{1,0:T(8,128)S(1)} collective-permute-done((f32[1024,128]{1,0:T(8,128)S(1)}, f32[1024,128]{1,0:T(8,128)S(1)}, u32[]{:S(2)}, u32[]{:S(2)}) %collective-permute-start.16) | collective-permute-done | bytes 524320 | tf_op jit(solution)/shard_map/ppermute | solution.py:548
  183.2 2.3 convert_element_type.188.picks_ref
  188.0 40.9 %all-gather.14.cloned.1.call-done.grad_ref = bf16[8192,256]{1,0:T(8,128)(2,1)} async-done(((bf16[1024,256]{1,0:T(8,128)(2,1)}), bf16[8192,256]{1,0:T(8,128)(2,1)}) %all-gather.14.cloned.1.call-update) | async-done | bytes 4194320 | tf_op jit(solution)/shard_map/all_gather | solution.py:584
  229.0 99.7 %picked_products.1 = bf16[8192,128]{1,0:T(8,128)(2,1)} custom-call(s32[1]{0:T(128)} %bitcast.41.base_ref.before_ref, s32[8192,128]{1,0:T(8,128)} %convert_element_type.188.picks_ref, bf16[8192,256]{1,0:T(8,128)(2,1)} %all-gather.14.cloned.1.call-done.grad_ref, bf16[256,8192]{1,0:T(8,128)(2,1)} %bitcast.329), custom_call_target="tpu_custom_call" | custom-call | flops 120259084288 | bytes 8388608 | tf_op jit(solution)/shard_map/picked_products/pallas_call | solution.py:394
  328.8 67.1 %bag_sums.2 = (bf16[4096,256]{1,0:T(8,128)(2,1)}, bf16[8192,8192]{1,0:T(8,128)(2,1)}) custom-call(s32[1]{0:T(128)} %bitcast.41.base_ref.before_ref, s32[8192,128]{1,0:T(8,128)} %convert_element_type.188.picks_ref, bf16[8192,128]{1,0:T(8,128)(2,1)} %all-gather.12.cloned.1.call-done.weight_ref, bf16[8192,256]{1,0:T(8,128)(2,1)} %table_ref.3, ...), custom_call_target="tpu_custom_call" | custom-call | flops 77309411328 | bytes 67108864 | tf_op jit(solution)/shard_map/bag_sums/pallas_call | solution.py:296
  397.0 67.0 %bag_sums.3 = (bf16[4096,256]{1,0:T(8,128)(2,1)}, bf16[8192,8192]{1,0:T(8,128)(2,1)}) custom-call(s32[1]{0:T(128)} %bitcast.41.base_ref.before_ref, s32[8192,128]{1,0:T(8,128)} %convert_element_type.188.picks_ref, bf16[8192,128]{1,0:T(8,128)(2,1)} %all-gather.12.cloned.1.call-done.weight_ref, ...), custom_call_target="tpu_custom_call", output_to_operand_aliasing={{1}: (4, {})} | custom-call | flops 77309411328 | bytes 67108864 | tf_op jit(solution)/shard_map/bag_sums/pallas_call | solution.py:296
  464.0 1.4 collective-permute-start.21
  466.6 9.9 %collective-permute-done.21 = f32[1024,128]{1,0:T(8,128)S(1)} collective-permute-done((f32[1024,128]{1,0:T(8,128)S(1)}, f32[1024,128]{1,0:T(8,128)S(1)}, u32[]{:S(2)}, u32[]{:S(2)}) %collective-permute-start.21) | collective-permute-done | bytes 524320 | tf_op jit(solution)/shard_map/ppermute | solution.py:548
  476.6 53.8 %fusion.88 = f32[8192,256]{1,0:T(8,128)} fusion(bf16[8192,8192]{1,0:T(8,128)(2,1)} %get-tuple-element.77, bf16[8192,256]{1,0:T(8,128)(2,1)} %all-gather.14.cloned.1.call-done.grad_ref), kind=kOutput, calls=%fused_computation.244 | convolution fusion | flops 34359738368 | bytes 146800640 | tf_op jit(solution)/shard_map/dot_general | solution.py:737
  532.5 2.2 copy.139
  534.8 1.5 multiply_convert_fusion.3.grad_ref
  536.3 12.0 %spread_grads.1 = (bf16[1024,512]{1,0:T(8,128)(2,1)S(1)}, f32[2,256,256]{2,1,0:T(8,128)S(1)}) custom-call(s32[1]{0:T(128)} %bitcast.58.column_ref, s32[1024,128]{1,0:T(8,128)S(1)} %copy-done.1, bf16[1024,128]{1,0:T(8,128)(2,1)S(1)} %multiply_convert_fusion.3.grad_ref, bf16[1024,512]{1,0:T(8,128)(2,1)S(1)} %copy-done.3, bf16[2,256,256]{2,1,0:T(8,128)(2,1)S(1)} %bitcast.323), custom_call_target="tpu_custom_call" | custom-call | tf_op jit(solution)/shard_map/spread_grads/pallas_call | solution.py:497
  554.4 2.1 fusion.24
  559.0 1.7 multiply_reduce_fusion.3
  560.7 1.6 collective-permute-start.26
  570.2 11.6 %collective-permute-done.25 = bf16[1024,256]{0,1:T(8,128)(2,1)} collective-permute-done((bf16[1024,256]{0,1:T(8,128)(2,1)S(1)}, bf16[1024,256]{0,1:T(8,128)(2,1)}, u32[]{:S(2)}, u32[]{:S(2)}) %collective-permute-start.25) | collective-permute-done | bytes 524320 | tf_op jit(solution)/shard_map/ppermute | solution.py:523
  581.9 2.5 fusion.68
  587.6 10.0 %collective-permute-done.29 = bf16[1024,256]{0,1:T(8,128)(2,1)} collective-permute-done((bf16[1024,256]{0,1:T(8,128)(2,1)S(1)}, bf16[1024,256]{0,1:T(8,128)(2,1)}, u32[]{:S(2)}, u32[]{:S(2)}) %collective-permute-start.29) | collective-permute-done | bytes 524320 | tf_op jit(solution)/shard_map/ppermute | solution.py:528
  597.7 4.0 fusion.66
  602.6 1.5 pad_maximum_fusion.8
  606.7 12.3 %attend_backward.1 = (bf16[1024,256]{1,0:T(8,128)(2,1)S(1)}, bf16[1024,256]{1,0:T(8,128)(2,1)S(1)}, bf16[1024,256]{1,0:T(8,128)(2,1)S(1)}) custom-call(s32[1,1024]{1,0:T(1,128)S(1)} %copy-done.9, bf16[1024,256]{1,0:T(8,128)(2,1)S(1)} %copy-done.11, bf16[1024,256]{1,0:T(8,128)(2,1)S(1)} %copy-done.13, bf16[1024,256]{1,0:T(8,128)(2,1)S(1)} %copy-done.15, ...), custom_call_target="tpu_custom_call" | custom-call | flops 10737418240 | bytes 3670016 | tf_op jit(solution)/shard_map/attend_backward/pallas_call | solution.py:139
  624.9 1.4 copy-done.18
  626.4 3.1 multiply_reduce_fusion.1
  635.1 1.9 copy.181
  637.0 1.8 copy.182
  638.8 1.8 copy.183
  640.6 1.8 copy.184
  642.4 1.8 copy.185
  644.2 1.8 copy.186
  646.0 1.8 copy.187
  648.7 8.3 %concatenate.102 = bf16[8,2178,128]{1,2,0:T(8,128)(2,1)} concatenate(bf16[8,128,128]{1,2,0:T(8,128)(2,1)} %copy.180, bf16[8,128,128]{1,2,0:T(8,128)(2,1)} %copy.181, bf16[8,128,128]{1,2,0:T(8,128)(2,1)} %copy.182, bf16[8,128,128]{1,2,0:T(8,128)(2,1)} %copy.183, bf16[8,128,128]{1,2,0:T(8,128)(2,1)} %copy.184, bf16[8,128,128]{1,2,0:T(8,128)(2,1)} %copy.185, ...), dimensions={1} | concatenate | bytes 8921088 | tf_op jit(solution)/shard_map/concatenate | solution.py:605
  657.0 5.4 copy.140
  662.4 2.6 slice_bitcast_fusion.7
  667.2 1.6 copy-done.21
  676.2 11.5 %collective-permute-done.33 = bf16[1024,256]{0,1:T(8,128)(2,1)} collective-permute-done((bf16[1024,256]{0,1:T(8,128)(2,1)}, bf16[1024,256]{0,1:T(8,128)(2,1)}, u32[]{:S(2)}, u32[]{:S(2)}) %collective-permute-start.33) | collective-permute-done | bytes 524320 | tf_op jit(solution)/shard_map/ppermute | solution.py:523
  687.8 2.2 fusion.33
  690.9 7.5 collective-permute-done.36
  699.3 1.9 fusion.29
  702.5 50.2 %reduce-scatter.11.cloned.1.call-done = bf16[1,2178,128]{1,2,0:T(8,128)(2,1)} async-done(((bf16[8,2178,128]{1,2,0:T(8,128)(2,1)}), bf16[1,2178,128]{1,2,0:T(8,128)(2,1)}) %reduce-scatter.11.cloned.1.call-update) | async-done | bytes 557584 | tf_op jit(solution)/shard_map/reduce_scatter | solution.py:588
  (466 shorter events, 98.3 us)
Async XLA Ops:
  7.2 30.9 %copy-start.46 = (bf16[1024,256]{1,0:T(8,128)(2,1)S(1)}, bf16[1024,256]{1,0:T(8,128)(2,1)}, u32[]{:S(2)}) copy-start(bf16[1024,256]{1,0:T(8,128)(2,1)} %param.13) | copy-start | bytes 1572868
  7.2 14.6 %copy-start.111 = (bf16[2,32,256]{2,1,0:T(8,128)(2,1)S(1)}, bf16[2,32,256]{2,1,0:T(8,128)(2,1)}, u32[]{:S(2)}) copy-start(bf16[2,32,256]{2,1,0:T(8,128)(2,1)} %param.20) | copy-start | bytes 98308
  7.2 20.3 %copy-start.104 = (bf16[256,128]{1,0:T(8,128)(2,1)S(1)}, bf16[256,128]{1,0:T(8,128)(2,1)}, u32[]{:S(2)}) copy-start(bf16[256,128]{1,0:T(8,128)(2,1)} %param.23) | copy-start | bytes 196612
  7.2 21.3 %copy-start.113 = (s32[1,1024]{1,0:T(1,128)S(1)}, s32[1,1024]{1,0:T(1,128)}, u32[]{:S(2)}) copy-start(s32[1,1024]{1,0:T(1,128)} %param.14) | copy-start | bytes 12292
  7.2 64.9 %all-gather.16.cloned.1.call-start = ((), (), s32[]{:S(2)}) async-start(), calls=%async_computation.11 | async-start | bytes 2377728 | tf_op jit(solution)/shard_map/all_gather | solution.py:584
  11.5 117.2 %all-gather.10.cloned.1.call-start = ((), (), s32[]{:S(2)}) async-start(), calls=%async_computation.8 | async-start | bytes 2654208 | tf_op jit(solution)/shard_map/all_gather | solution.py:584
  11.6 16.0 %collective-permute-start.1 = (bf16[1024,256]{1,0:T(8,128)(2,1)}, bf16[1024,256]{1,0:T(8,128)(2,1)S(1)}, u32[]{:S(2)}, u32[]{:S(2)}) collective-permute-start(bf16[1024,256]{1,0:T(8,128)(2,1)} %param.13), channel_id=1, source_target_pairs={{0,2},{1,3},{2,0},{3,1},{4,6},{5,7},{6,4},{7,5},{8,10},{9,11},{10,... | collective-permute-start | bytes 1572872 | tf_op jit(solution)/shard_map/ppermute | solution.py:528
  14.6 23.5 %collective-permute-start = (bf16[1024,256]{1,0:T(8,128)(2,1)}, bf16[1024,256]{1,0:T(8,128)(2,1)S(1)}, u32[]{:S(2)}, u32[]{:S(2)}) collective-permute-start(bf16[1024,256]{1,0:T(8,128)(2,1)} %param.13), channel_id=1, source_target_pairs={{0,1},{1,0},{2,3},{3,2},{4,5},{5,4},{6,7},{7,6},{8,9},{9,8},{10,11... | collective-permute-start | bytes 1572872 | tf_op jit(solution)/shard_map/ppermute | solution.py:528
  14.6 23.5 %collective-permute-start.19 = (bf16[1024,256]{1,0:T(8,128)(2,1)}, bf16[1024,256]{1,0:T(8,128)(2,1)}, u32[]{:S(2)}, u32[]{:S(2)}) collective-permute-start(bf16[1024,256]{1,0:T(8,128)(2,1)} %param.25), channel_id=1, source_target_pairs={{0,2},{1,3},{2,0},{3,1},{4,6},{5,7},{6,4},{7,5},{8,10},{9,11},{10,... | collective-permute-start | bytes 1572872 | tf_op jit(solution)/shard_map/ppermute | solution.py:528
  14.7 77.7 %collective-permute-start.18 = (bf16[1024,256]{1,0:T(8,128)(2,1)}, bf16[1024,256]{1,0:T(8,128)(2,1)}, u32[]{:S(2)}, u32[]{:S(2)}) collective-permute-start(bf16[1024,256]{1,0:T(8,128)(2,1)} %param.25), channel_id=1, source_target_pairs={{0,1},{1,0},{2,3},{3,2},{4,5},{5,4},{6,7},{7,6},{8,9},{9,8},{10,11... | collective-permute-start | bytes 1572872 | tf_op jit(solution)/shard_map/ppermute | solution.py:528
  16.9 23.9 %collective-permute-start.3 = (u16[1024,128]{1,0:T(8,128)(2,1)}, u16[1024,128]{1,0:T(8,128)(2,1)S(1)}, u32[]{:S(2)}, u32[]{:S(2)}) collective-permute-start(u16[1024,128]{1,0:T(8,128)(2,1)} %convert_element_type.179), channel_id=1, source_target_pairs={{0,16},{4,20},{8,24},{12,28},{16,0},{20,4},{24,8},{28,12},{1,17},{... | collective-permute-start | bytes 786440 | tf_op jit(solution)/shard_map/ppermute | solution.py:528
  27.5 10.5 %collective-permute-start.2 = (bf16[1024,256]{1,0:T(8,128)(2,1)S(1)}, bf16[1024,256]{1,0:T(8,128)(2,1)S(1)}, u32[]{:S(2)}, u32[]{:S(2)}) collective-permute-start(bf16[1024,256]{1,0:T(8,128)(2,1)S(1)} %collective-permute-done.1), channel_id=1, source_target_pairs={{0,1},{1,0},{2,3},{3,2},{4,5},{5,4},{6,7},{7,6},{8,9},{9,8},{10,11... | collective-permute-start | bytes 1572872 | tf_op jit(solution)/shard_map/ppermute | solution.py:528
  28.4 200.6 %all-gather.14.cloned.1.call-start = ((), (), s32[]{:S(2)}) async-start(), calls=%async_computation.10 | async-start | bytes 4718592 | tf_op jit(solution)/shard_map/all_gather | solution.py:584
  30.4 51.5 %copy-start.8 = (s32[1,1024]{1,0:T(1,128)}, s32[1,1024]{1,0:T(1,128)S(1)}, u32[]{:S(2)}) copy-start(s32[1,1024]{1,0:T(1,128)S(1)} %fusion.54.start_ref) | copy-start | bytes 12292
  38.1 54.4 %collective-permute-start.20 = (bf16[1024,256]{1,0:T(8,128)(2,1)}, bf16[1024,256]{1,0:T(8,128)(2,1)}, u32[]{:S(2)}, u32[]{:S(2)}) collective-permute-start(bf16[1024,256]{1,0:T(8,128)(2,1)} %collective-permute-done.19), channel_id=1, source_target_pairs={{0,1},{1,0},{2,3},{3,2},{4,5},{5,4},{6,7},{7,6},{8,9},{9,8},{10,11... | collective-permute-start | bytes 1572872 | tf_op jit(solution)/shard_map/ppermute | solution.py:528
  40.8 37.7 %copy-start.86 = (u16[1024,128]{1,0:T(8,128)(2,1)}, u16[1024,128]{1,0:T(8,128)(2,1)S(1)}, u32[]{:S(2)}) copy-start(u16[1024,128]{1,0:T(8,128)(2,1)S(1)} %collective-permute-done.3) | copy-start | bytes 786436
  40.8 37.7 %collective-permute-start.4 = (u16[1024,128]{1,0:T(8,128)(2,1)}, u16[1024,128]{1,0:T(8,128)(2,1)}, u32[]{:S(2)}, u32[]{:S(2)}) collective-permute-start(u16[1024,128]{1,0:T(8,128)(2,1)} %convert_element_type.179), channel_id=1, source_target_pairs={{0,8},{4,12},{8,0},{12,4},{16,24},{20,28},{24,16},{28,20},{1,9},{5... | collective-permute-start | bytes 786440 | tf_op jit(solution)/shard_map/ppermute | solution.py:528
  41.8 36.8 %collective-permute-start.5 = (u16[1024,128]{1,0:T(8,128)(2,1)S(1)}, u16[1024,128]{1,0:T(8,128)(2,1)S(1)}, u32[]{:S(2)}, u32[]{:S(2)}) collective-permute-start(u16[1024,128]{1,0:T(8,128)(2,1)S(1)} %collective-permute-done.3), channel_id=1, source_target_pairs={{0,8},{4,12},{8,0},{12,4},{16,24},{20,28},{24,16},{28,20},{1,9},{5... | collective-permute-start | bytes 786440 | tf_op jit(solution)/shard_map/ppermute | solution.py:528
  43.8 34.7 %copy-start.100 = (f32[1024]{0:T(1024)}, f32[1024]{0:T(1024)S(1)}, u32[]{:S(2)}) copy-start(f32[1024]{0:T(1024)S(1)} %get-tuple-element.236) | copy-start | bytes 12292
  73.2 62.5 %copy-start.48 = (bf16[8,128,256]{2,1,0:T(8,128)(2,1)}, bf16[8,128,256]{2,1,0:T(8,128)(2,1)S(1)}, u32[]{:S(2)}) copy-start(bf16[8,128,256]{2,1,0:T(8,128)(2,1)S(1)} %pad_maximum_fusion.12) | copy-start | bytes 1572868
  73.2 58.6 %collective-permute-start.10 = (bf16[1024,256]{1,0:T(8,128)(2,1)S(1)}, bf16[1024,256]{1,0:T(8,128)(2,1)}, u32[]{:S(2)}, u32[]{:S(2)}) collective-permute-start(bf16[1024,256]{1,0:T(8,128)(2,1)S(1)} %bitcast.343), channel_id=1, source_target_pairs={{0,2},{1,3},{2,0},{3,1},{4,6},{5,7},{6,4},{7,5},{8,10},{9,11},{10,... | collective-permute-start | bytes 1572872 | tf_op jit(solution)/shard_map/ppermute | solution.py:528
  75.7 69.7 %copy-start.109 = (f32[8,1,128]{2,1,0:T(1,128)}, f32[8,1,128]{2,1,0:T(1,128)S(1)}, u32[]{:S(2)}) copy-start(f32[8,1,128]{2,1,0:T(1,128)S(1)} %get-tuple-element.233) | copy-start | bytes 12292
  92.0 46.7 %copy-start.6 = (bf16[1024,256]{1,0:T(8,128)(2,1)}, bf16[1024,256]{1,0:T(8,128)(2,1)S(1)}, u32[]{:S(2)}) copy-start(bf16[1024,256]{1,0:T(8,128)(2,1)S(1)} %attend_forward.1) | copy-start | bytes 1572868
  92.0 41.0 %collective-permute-start.7 = (bf16[1024,256]{1,0:T(8,128)(2,1)S(1)}, bf16[1024,256]{1,0:T(8,128)(2,1)}, u32[]{:S(2)}, u32[]{:S(2)}) collective-permute-start(bf16[1024,256]{1,0:T(8,128)(2,1)S(1)} %attend_forward.1), channel_id=1, source_target_pairs={{0,2},{1,3},{2,0},{3,1},{4,6},{5,7},{6,4},{7,5},{8,10},{9,11},{10,... | collective-permute-start | bytes 1572872 | tf_op jit(solution)/shard_map/ppermute | solution.py:528
  95.4 38.2 %collective-permute-start.9 = (bf16[1024,256]{1,0:T(8,128)(2,1)S(1)}, bf16[1024,256]{1,0:T(8,128)(2,1)}, u32[]{:S(2)}, u32[]{:S(2)}) collective-permute-start(bf16[1024,256]{1,0:T(8,128)(2,1)S(1)} %bitcast.344), channel_id=1, source_target_pairs={{0,1},{1,0},{2,3},{3,2},{4,5},{5,4},{6,7},{7,6},{8,9},{9,8},{10,11... | collective-permute-start | bytes 1572872 | tf_op jit(solution)/shard_map/ppermute | solution.py:528
  95.4 42.0 %collective-permute-start.6 = (bf16[1024,256]{1,0:T(8,128)(2,1)S(1)}, bf16[1024,256]{1,0:T(8,128)(2,1)}, u32[]{:S(2)}, u32[]{:S(2)}) collective-permute-start(bf16[1024,256]{1,0:T(8,128)(2,1)S(1)} %attend_forward.1), channel_id=1, source_target_pairs={{0,1},{1,0},{2,3},{3,2},{4,5},{5,4},{6,7},{7,6},{8,9},{9,8},{10,11... | collective-permute-start | bytes 1572872 | tf_op jit(solution)/shard_map/ppermute | solution.py:528
  95.9 50.9 %collective-permute-start.12 = (u16[1024,128]{1,0:T(8,128)(2,1)}, u16[1024,128]{1,0:T(8,128)(2,1)}, u32[]{:S(2)}, u32[]{:S(2)}) collective-permute-start(u16[1024,128]{1,0:T(8,128)(2,1)} %convert_element_type.179), channel_id=1, source_target_pairs={{0,4},{4,0},{8,12},{12,8},{16,20},{20,16},{24,28},{28,24},{1,5},{5... | collective-permute-start | bytes 786440 | tf_op jit(solution)/shard_map/ppermute | solution.py:528
  131.8 2.4 collective-permute-start.11
  133.0 5.7 collective-permute-start.8
  133.5 20.7 %copy-start.74 = (bf16[8,128,256]{2,1,0:T(8,128)(2,1)}, bf16[8,128,256]{2,1,0:T(8,128)(2,1)S(1)}, u32[]{:S(2)}) copy-start(bf16[8,128,256]{2,1,0:T(8,128)(2,1)S(1)} %pad_maximum_fusion.14) | copy-start | bytes 1572868
  133.6 19.8 %copy-start.51 = (bf16[8,128,256]{2,1,0:T(8,128)(2,1)}, bf16[8,128,256]{2,1,0:T(8,128)(2,1)S(1)}, u32[]{:S(2)}) copy-start(bf16[8,128,256]{2,1,0:T(8,128)(2,1)S(1)} %pad_maximum_fusion.13) | copy-start | bytes 1572868
  133.6 13.2 %collective-permute-start.13 = (u16[1024,128]{1,0:T(8,128)(2,1)}, u16[1024,128]{1,0:T(8,128)(2,1)S(1)}, u32[]{:S(2)}, u32[]{:S(2)}) collective-permute-start(u16[1024,128]{1,0:T(8,128)(2,1)} %collective-permute-done.4), channel_id=1, source_target_pairs={{0,4},{4,0},{8,12},{12,8},{16,20},{20,16},{24,28},{28,24},{1,5},{5... | collective-permute-start | bytes 786440 | tf_op jit(solution)/shard_map/ppermute | solution.py:528
  134.3 14.4 %collective-permute-start.14 = (u16[1024,128]{1,0:T(8,128)(2,1)S(1)}, u16[1024,128]{1,0:T(8,128)(2,1)S(1)}, u32[]{:S(2)}, u32[]{:S(2)}) collective-permute-start(u16[1024,128]{1,0:T(8,128)(2,1)S(1)} %copy-done.87), channel_id=1, source_target_pairs={{0,4},{4,0},{8,12},{12,8},{16,20},{20,16},{24,28},{28,24},{1,5},{5... | collective-permute-start | bytes 786440 | tf_op jit(solution)/shard_map/ppermute | solution.py:528
  138.2 15.2 %collective-permute-start.15 = (u16[1024,128]{1,0:T(8,128)(2,1)S(1)}, u16[1024,128]{1,0:T(8,128)(2,1)S(1)}, u32[]{:S(2)}, u32[]{:S(2)}) collective-permute-start(u16[1024,128]{1,0:T(8,128)(2,1)S(1)} %copy-done.90), channel_id=1, source_target_pairs={{0,4},{4,0},{8,12},{12,8},{16,20},{20,16},{24,28},{28,24},{1,5},{5... | collective-permute-start | bytes 786440 | tf_op jit(solution)/shard_map/ppermute | solution.py:528
  156.9 171.8 %all-gather.12.cloned.1.call-start = ((), (), s32[]{:S(2)}) async-start(), calls=%async_computation.9 | async-start | bytes 2359296 | tf_op jit(solution)/shard_map/all_gather | solution.py:584
  169.5 13.1 %collective-permute-start.16 = (f32[1024,128]{1,0:T(8,128)S(1)}, f32[1024,128]{1,0:T(8,128)S(1)}, u32[]{:S(2)}, u32[]{:S(2)}) collective-permute-start(f32[1024,128]{1,0:T(8,128)S(1)} %pick_scores.1), channel_id=1, source_target_pairs={{0,2},{1,3},{2,0},{3,1},{4,6},{5,7},{6,4},{7,5},{8,10},{9,11},{10,... | collective-permute-start | bytes 1572872 | tf_op jit(solution)/shard_map/ppermute | solution.py:548
  182.7 2.8 collective-permute-start.17
  186.8 141.9 %copy-start.27 = (f32[1024,128]{1,0:T(8,128)}, f32[1024,128]{1,0:T(8,128)S(1)}, u32[]{:S(2)}) copy-start(f32[1024,128]{1,0:T(8,128)S(1)} %copy.135) | copy-start | bytes 1572868
  187.1 141.6 %copy-start.29 = (f32[1024,128]{1,0:T(8,128)}, f32[1024,128]{1,0:T(8,128)S(1)}, u32[]{:S(2)}) copy-start(f32[1024,128]{1,0:T(8,128)S(1)} %copy.134) | copy-start | bytes 1572868
  188.0 207.9 %reduce-scatter.5.cloned.1.call-start = ((), (), s32[]{:S(2)}) async-start(), calls=%async_computation.4 | async-start | bytes 2359296 | tf_op jit(solution)/shard_map/reduce_scatter | solution.py:588
  328.7 225.7 %reduce-scatter.7.cloned.1.call-start = ((), (), s32[]{:S(2)}) async-start(), calls=%async_computation.5 | async-start | bytes 2359296 | tf_op jit(solution)/shard_map/reduce_scatter | solution.py:588
  396.9 157.5 %reduce-scatter.9.cloned.1.call-start = ((), (), s32[]{:S(2)}) async-start(), calls=%async_computation.6 | async-start | bytes 2359296 | tf_op jit(solution)/shard_map/reduce_scatter | solution.py:588
  397.0 68.4 %copy-start.45 = (bf16[1024,256]{1,0:T(8,128)(2,1)S(1)}, bf16[1024,256]{1,0:T(8,128)(2,1)}, u32[]{:S(2)}) copy-start(bf16[1024,256]{1,0:T(8,128)(2,1)} %param.25) | copy-start | bytes 1572868
  397.0 69.4 %copy-start.110 = (f32[8,1,128]{2,1,0:T(1,128)S(1)}, f32[8,1,128]{2,1,0:T(1,128)}, u32[]{:S(2)}) copy-start(f32[8,1,128]{2,1,0:T(1,128)} %copy-done.109) | copy-start | bytes 12292
  464.0 12.5 %collective-permute-start.21 = (f32[1024,128]{1,0:T(8,128)S(1)}, f32[1024,128]{1,0:T(8,128)S(1)}, u32[]{:S(2)}, u32[]{:S(2)}) collective-permute-start(f32[1024,128]{1,0:T(8,128)S(1)} %bitcast_convert_fusion), channel_id=1, source_target_pairs={{0,2},{1,3},{2,0},{3,1},{4,6},{5,7},{6,4},{7,5},{8,10},{9,11},{10,... | collective-permute-start | bytes 1572872 | tf_op jit(solution)/shard_map/ppermute | solution.py:548
  466.5 286.2 %reduce-scatter.11.cloned.1.call-start = ((), (), s32[]{:S(2)}) async-start(), calls=%async_computation.7 | async-start | bytes 5308416 | tf_op jit(solution)/shard_map/reduce_scatter | solution.py:588
  476.5 53.9 %collective-permute-start.22 = (f32[1024,128]{1,0:T(8,128)S(1)}, f32[1024,128]{1,0:T(8,128)S(1)}, u32[]{:S(2)}, u32[]{:S(2)}) collective-permute-start(f32[1024,128]{1,0:T(8,128)S(1)} %add.206), channel_id=1, source_target_pairs={{0,1},{1,0},{2,3},{3,2},{4,5},{5,4},{6,7},{7,6},{8,9},{9,8},{10,11... | collective-permute-start | bytes 1572872 | tf_op jit(solution)/shard_map/ppermute | solution.py:548
  560.7 7.6 collective-permute-start.26
  563.7 3.9 collective-permute-start.24
  563.9 6.4 collective-permute-start.23
  567.8 14.1 %collective-permute-start.25 = (bf16[1024,256]{0,1:T(8,128)(2,1)S(1)}, bf16[1024,256]{0,1:T(8,128)(2,1)}, u32[]{:S(2)}, u32[]{:S(2)}) collective-permute-start(bf16[1024,256]{0,1:T(8,128)(2,1)S(1)} %fusion.34), channel_id=1, source_target_pairs={{0,2},{1,3},{2,0},{3,1},{4,6},{5,7},{6,4},{7,5},{8,10},{9,11},{10,... | collective-permute-start | bytes 1572872 | tf_op jit(solution)/shard_map/ppermute | solution.py:523
  568.4 1.9 collective-permute-start.27
  584.4 13.2 %collective-permute-start.29 = (bf16[1024,256]{0,1:T(8,128)(2,1)S(1)}, bf16[1024,256]{0,1:T(8,128)(2,1)}, u32[]{:S(2)}, u32[]{:S(2)}) collective-permute-start(bf16[1024,256]{0,1:T(8,128)(2,1)S(1)} %get-tuple-element.130), channel_id=1, source_target_pairs={{0,2},{1,3},{2,0},{3,1},{4,6},{5,7},{6,4},{7,5},{8,10},{9,11},{10,... | collective-permute-start | bytes 1572872 | tf_op jit(solution)/shard_map/ppermute | solution.py:528
  587.6 15.0 %collective-permute-start.28 = (bf16[1024,256]{0,1:T(8,128)(2,1)S(1)}, bf16[1024,256]{0,1:T(8,128)(2,1)S(1)}, u32[]{:S(2)}, u32[]{:S(2)}) collective-permute-start(bf16[1024,256]{0,1:T(8,128)(2,1)S(1)} %get-tuple-element.130), channel_id=1, source_target_pairs={{0,1},{1,0},{2,3},{3,2},{4,5},{5,4},{6,7},{7,6},{8,9},{9,8},{10,11... | collective-permute-start | bytes 1572872 | tf_op jit(solution)/shard_map/ppermute | solution.py:528
  597.6 5.0 collective-permute-start.30
  629.5 3.7 collective-permute-start.37
  633.2 14.6 %collective-permute-start.38 = (f32[2048]{0:T(1024)S(1)}, f32[2048]{0:T(1024)S(1)}, u32[]{:S(2)}, u32[]{:S(2)}) collective-permute-start(f32[2048]{0:T(1024)S(1)} %fusion.62), channel_id=1, source_target_pairs={{0,1},{1,0},{2,3},{3,2},{4,5},{5,4},{6,7},{7,6},{8,9},{9,8},{10,11... | collective-permute-start | bytes 24584 | tf_op jit(solution)/shard_map/ppermute | solution.py:548
  666.6 5.1 collective-permute-start.32
  671.1 2.8 collective-permute-start.35
  671.8 4.5 collective-permute-start.31
  672.7 15.0 %collective-permute-start.33 = (bf16[1024,256]{0,1:T(8,128)(2,1)}, bf16[1024,256]{0,1:T(8,128)(2,1)}, u32[]{:S(2)}, u32[]{:S(2)}) collective-permute-start(bf16[1024,256]{0,1:T(8,128)(2,1)} %fusion.30), channel_id=1, source_target_pairs={{0,2},{1,3},{2,0},{3,1},{4,6},{5,7},{6,4},{7,5},{8,10},{9,11},{10,... | collective-permute-start | bytes 1572872 | tf_op jit(solution)/shard_map/ppermute | solution.py:523
  673.9 17.0 %collective-permute-start.34 = (bf16[1024,256]{0,1:T(8,128)(2,1)}, bf16[1024,256]{0,1:T(8,128)(2,1)S(1)}, u32[]{:S(2)}, u32[]{:S(2)}) collective-permute-start(bf16[1024,256]{0,1:T(8,128)(2,1)} %get-tuple-element.132), channel_id=1, source_target_pairs={{0,1},{1,0},{2,3},{3,2},{4,5},{5,4},{6,7},{7,6},{8,9},{9,8},{10,11... | collective-permute-start | bytes 1572872 | tf_op jit(solution)/shard_map/ppermute | solution.py:523
  674.9 23.6 %collective-permute-start.36 = (bf16[1024,256]{0,1:T(8,128)(2,1)}, bf16[1024,256]{0,1:T(8,128)(2,1)S(1)}, u32[]{:S(2)}, u32[]{:S(2)}) collective-permute-start(bf16[1024,256]{0,1:T(8,128)(2,1)} %fusion.25), channel_id=1, source_target_pairs={{0,2},{1,3},{2,0},{3,1},{4,6},{5,7},{6,4},{7,5},{8,10},{9,11},{10,... | collective-permute-start | bytes 1572872 | tf_op jit(solution)/shard_map/ppermute | solution.py:523
  676.2 23.1 %copy-start.112 = (f32[1024]{0:T(1024)S(1)}, f32[1024]{0:T(1024)}, u32[]{:S(2)}) copy-start(f32[1024]{0:T(1024)} %get-tuple-element.235) | copy-start | bytes 12292
  (98 other events, 430.5 us)
Sparse Core Ops, SparseCore 0:
  11.6 60.3 all-gather.15
  74.9 53.7 all-gather.9
  157.0 71.8 all-gather.13
  231.5 47.5 all-gather.11
  328.8 66.2 reduce-scatter.4
  398.6 66.8 reduce-scatter.6
  469.0 66.8 reduce-scatter.8
  657.2 95.4 reduce-scatter.10

commit v5 on v4

--- a/solution.py
+++ b/solution.py
@@ -15,7 +15,8 @@
 DOCS = 3
 DOC_MOST = 512
 LANES = 128
-PARTS = 2
+GAIN_ROWS = 16
+COVER = 1
 
 
 EPSILON = 1e-06
@@ -145,7 +146,7 @@
         scratch_shapes=[pltpu.VMEM((length, LANES), F32)] * 2,
         compiler_params=params(40),
         cost_estimate=pl.CostEstimate(
-            flops=40 * length * length * width,
+            flops=COVER * length * length * width,
             bytes_accessed=14 * length * width,
             transcendentals=0,
         ),
@@ -180,7 +181,7 @@
     return (most + (SLOTS - 1)) // SLOTS
 
 
-def compact(counts, members, start):
+def search(counts, start):
     target = ((lane_numbers(counts.shape) & (SLOTS - 1)) + (start + 1)).astype(F32)
     place = jnp.zeros(counts.shape, jnp.int32)
     step = LANES // 2
@@ -188,8 +189,42 @@
         seen = jnp.take_along_axis(counts, place + (step - 1), axis=1)
         place = jnp.where(seen < target, place + step, place)
         step //= 2
-    valid = target <= counts[:, LANES - 1 :]
-    return valid, [jnp.take_along_axis(member, place, axis=1) for member in members]
+    return target <= counts[:, LANES - 1 :], place
+
+
+def place_of(counts, local, number):
+    valid, place = search(counts, number * SLOTS)
+    return place, jnp.where(valid, jnp.take_along_axis(local, place, axis=1), -1)
+
+
+def locate_body(base_ref, picks_ref, count_ref, place_ref, found_ref, *, total):
+    local = picks_ref[...] - base_ref[0]
+    counts = count_local(local, total)
+    valid, place = search(counts, 0)
+    count_ref[...] = counts
+    place_ref[...] = place
+    found_ref[...] = jnp.where(valid, jnp.take_along_axis(local, place, axis=1), -1)
+
+
+def locate(base, picks, total, rows=512):
+    block = pl.BlockSpec((rows, PICKS), lambda i: (i, 0))
+    amount = picks.shape[0]
+    return pl.pallas_call(
+        functools.partial(locate_body, total=total),
+        grid=(amount // rows,),
+        in_specs=[pl.BlockSpec(memory_space=pltpu.SMEM), block],
+        out_specs=[block] * 3,
+        out_shape=[
+            jax.ShapeDtypeStruct((amount, PICKS), F32),
+            jax.ShapeDtypeStruct((amount, PICKS), jnp.int32),
+            jax.ShapeDtypeStruct((amount, PICKS), jnp.int32),
+        ],
+        compiler_params=params(32),
+        cost_estimate=pl.CostEstimate(
+            flops=amount * PICKS * 20000, bytes_accessed=amount * PICKS * 16, transcendentals=0
+        ),
+        name="locate",
+    )(base, picks)
 
 
 def group_masks():
@@ -211,16 +246,12 @@
 
 
 def bag_body(
-    base_ref, picks_ref, weight_ref, table_ref, before_ref, out_ref, keep_ref, counts, locals_,
+    base_ref, picks_ref, count_ref, place_ref, found_ref, weight_ref, table_ref, out_ref, keep_ref,
     high, low, weights, *, chunk, unroll
 ):
-    del before_ref
     rows = picks_ref.shape[0]
     total = table_ref.shape[0]
     groups = total // NKEYS
-    local = picks_ref[...] - base_ref[0]
-    counts[...] = count_local(local, total)
-    locals_[...] = local
     masks = group_masks()
 
     def eight(token):
@@ -245,12 +276,10 @@
             preferred_element_type=F32,
         )
 
-    def one_round(number, first):
-        members = [locals_[...], weight_ref[...].astype(F32)]
-        valid, (found, weight) = compact(counts[...], members, number * SLOTS)
-        high[...] = jnp.where(valid, found >> 8, -1).astype(F32)
+    def one_round(place, found, first):
+        high[...] = (found >> 8).astype(F32)
         low[...] = (found & (NKEYS - 1)).astype(F32)
-        weights[...] = weight
+        weights[...] = jnp.take_along_axis(weight_ref[...].astype(F32), place, axis=1)
 
         def some_tokens(step, carried):
             for slot in range(unroll):
@@ -267,11 +296,12 @@
         lax.fori_loop(0, rows // (16 * unroll), some_tokens, 0)
 
     def more(number, carried):
-        one_round(number, False)
+        local = picks_ref[...] - base_ref[0]
+        one_round(*place_of(count_ref[...], local, number), False)
         return carried
 
-    one_round(0, True)
-    lax.fori_loop(1, rounds_of(counts[...]), more, 0)
+    one_round(place_ref[...], found_ref[...], True)
+    lax.fori_loop(1, rounds_of(count_ref[...]), more, 0)
     result = jnp.zeros(out_ref.shape, F32)
     for start in range(0, total, chunk):
         result = result + jnp.dot(
@@ -282,60 +312,40 @@
     out_ref[...] = result.astype(out_ref.dtype)
 
 
-def bag_sums(base, picks, weights, table, before, part, parts, shards, rows=256, chunk=1024,
-             unroll=8):
+def bag_sums(base, picks, located, weights, table, rows=256, chunk=1024, unroll=16):
     amount = picks.shape[0]
     total, width = table.shape
-    whole = amount // shards // rows
-    count = whole // parts
-
-    def place(i):
-        return (i // count * whole + part * count + i % count, 0)
-
-    kept = jax.ShapeDtypeStruct((amount, total), BF16)
+    block = pl.BlockSpec((rows, PICKS), lambda i: (i, 0))
     return pl.pallas_call(
         functools.partial(bag_body, chunk=chunk, unroll=unroll),
-        grid=(shards * count,),
-        in_specs=[
-            pl.BlockSpec(memory_space=pltpu.SMEM),
-            pl.BlockSpec((rows, PICKS), place),
-            pl.BlockSpec((rows, PICKS), place),
-            pl.BlockSpec((total, width), lambda i: (0, 0)),
-            pl.BlockSpec(memory_space=pl.ANY),
-        ],
+        grid=(amount // rows,),
+        in_specs=[pl.BlockSpec(memory_space=pltpu.SMEM)]
+        + [block] * 5
+        + [pl.BlockSpec((total, width), lambda i: (0, 0))],
         out_specs=[
             pl.BlockSpec((rows, width), lambda i: (i, 0)),
-            pl.BlockSpec((rows, total), place),
-        ],
-        out_shape=[jax.ShapeDtypeStruct((amount // parts, width), BF16), kept],
-        scratch_shapes=[
-            pltpu.VMEM((rows, LANES), F32),
-            pltpu.VMEM((rows, LANES), jnp.int32),
-            pltpu.VMEM((rows, LANES), F32),
-            pltpu.VMEM((rows, LANES), F32),
-            pltpu.VMEM((rows, LANES), F32),
-        ],
-        input_output_aliases={} if before is None else {4: 1},
+            pl.BlockSpec((rows, total), lambda i: (i, 0)),
+        ],
+        out_shape=[
+            jax.ShapeDtypeStruct((amount, width), BF16),
+            jax.ShapeDtypeStruct((amount, total), BF16),
+        ],
+        scratch_shapes=[pltpu.VMEM((rows, LANES), F32)] * 3,
         compiler_params=params(56),
         cost_estimate=pl.CostEstimate(
-            flops=9 * amount * total * width // parts,
-            bytes_accessed=amount * total * 2 // parts,
-            transcendentals=0,
+            flops=9 * amount * total * width, bytes_accessed=amount * total * 2, transcendentals=0
         ),
         name="bag_sums",
-    )(base, picks, weights, table, base if before is None else before)
+    )(base, picks, *located, weights, table)
 
 
 def picked_body(
-    base_ref, picks_ref, grad_ref, table_ref, out_ref, counts, locals_, high, low, found_at, held,
-    *, unroll
+    base_ref, picks_ref, count_ref, found_ref, grad_ref, table_ref, out_ref, high, low, found_at,
+    held, *, unroll
 ):
     rows = picks_ref.shape[0]
     total = table_ref.shape[1]
     groups = total // NKEYS
-    local = picks_ref[...] - base_ref[0]
-    counts[...] = count_local(local, total)
-    locals_[...] = local
     masks = group_masks()
     grads = grad_ref[...]
     for group in range(groups):
@@ -360,9 +370,8 @@
                 result = jnp.where(own == float(group), part, result)
         found_at[span, :] = result
 
-    def one_round(number, first):
-        valid, (found,) = compact(counts[...], [locals_[...]], number * SLOTS)
-        high[...] = jnp.where(valid, found >> 8, -1).astype(F32)
+    def one_round(number, found, first):
+        high[...] = (found >> 8).astype(F32)
         low[...] = (found & (NKEYS - 1)).astype(F32)
 
         def some_tokens(step, carried):
@@ -371,8 +380,9 @@
             return carried
 
         lax.fori_loop(0, rows // (8 * unroll), some_tokens, 0)
-        slot = counts[...].astype(jnp.int32) - (1 + number * SLOTS)
-        inside = (locals_[...] >= 0) & (locals_[...] < total)
+        slot = count_ref[...].astype(jnp.int32) - (1 + number * SLOTS)
+        local = picks_ref[...] - base_ref[0]
+        inside = (local >= 0) & (local < total)
         here = (slot >= 0) & (slot < SLOTS) & inside
         token = lax.broadcasted_iota(jnp.int32, slot.shape, 0) & (LANES // SLOTS - 1)
         lane = token * SLOTS + jnp.clip(slot, 0, SLOTS - 1)
@@ -381,14 +391,15 @@
         out_ref[...] = jnp.where(here, value, before).astype(out_ref.dtype)
 
     def more(number, carried):
-        one_round(number, False)
+        local = picks_ref[...] - base_ref[0]
+        one_round(number, place_of(count_ref[...], local, number)[1], False)
         return carried
 
-    one_round(0, True)
-    lax.fori_loop(1, rounds_of(counts[...]), more, 0)
-
-
-def picked_products(base, picks, grads, table, rows=256, unroll=16):
+    one_round(0, found_ref[...], True)
+    lax.fori_loop(1, rounds_of(count_ref[...]), more, 0)
+
+
+def picked_products(base, picks, located, grads, table, rows=256, unroll=32):
     amount, width = grads.shape
     total = table.shape[1]
     return pl.pallas_call(
@@ -397,14 +408,14 @@
         in_specs=[
             pl.BlockSpec(memory_space=pltpu.SMEM),
             pl.BlockSpec((rows, PICKS), lambda i: (i, 0)),
+            pl.BlockSpec((rows, PICKS), lambda i: (i, 0)),
+            pl.BlockSpec((rows, PICKS), lambda i: (i, 0)),
             pl.BlockSpec((rows, width), lambda i: (i, 0)),
             pl.BlockSpec((width, total), lambda i: (0, 0)),
         ],
         out_specs=pl.BlockSpec((rows, PICKS), lambda i: (i, 0)),
         out_shape=jax.ShapeDtypeStruct((amount, PICKS), BF16),
         scratch_shapes=[
-            pltpu.VMEM((rows, LANES), F32),
-            pltpu.VMEM((rows, LANES), jnp.int32),
             pltpu.VMEM((rows, LANES), F32),
             pltpu.VMEM((rows, LANES), F32),
             pltpu.VMEM((rows, LANES), F32),
@@ -415,7 +426,211 @@
             flops=7 * amount * total * width, bytes_accessed=amount * width * 4, transcendentals=0
         ),
         name="picked_products",
-    )(base, picks, grads, table)
+    )(base, picks, located[0], located[2], grads, table)
+
+
+def gather_lanes(block, index):
+    return jnp.take_along_axis(block, index, axis=1)
+
+
+def over_head(block, merge):
+    lanes = lane_numbers(block.shape)
+    step = 1
+    while step < TOPK:
+        block = merge(block, gather_lanes(block, lanes ^ step))
+        step *= 2
+    return block
+
+
+def softmax_body(score_ref, prob_ref, weight_ref):
+    scores = score_ref[...]
+    raised = jnp.exp(scores - over_head(scores, jnp.maximum))
+    probs = raised / over_head(raised, jnp.add)
+    prob_ref[...] = probs
+    weight_ref[...] = probs.astype(BF16)
+
+
+def pick_softmax(scores, rows=256):
+    block = pl.BlockSpec((rows, PICKS), lambda i: (i, 0))
+    amount = scores.shape[0]
+    return pl.pallas_call(
+        softmax_body,
+        grid=(amount // rows,),
+        in_specs=[block],
+        out_specs=[block] * 2,
+        out_shape=[
+            jax.ShapeDtypeStruct((amount, PICKS), F32),
+            jax.ShapeDtypeStruct((amount, PICKS), BF16),
+        ],
+        compiler_params=params(32),
+        name="pick_softmax",
+    )(scores)
+
+
+def store_lanes(out_ref, lead, row, block):
+    rows, columns = block.shape
+    for start in range(0, columns, LANES):
+        out_ref[(*lead, slice(row, row + rows), slice(None))] = block[:, start : start + LANES]
+        row += rows
+    return row
+
+
+def load_lanes(ref, lead, row, rows, columns):
+    parts = []
+    for _ in range(columns // LANES):
+        parts.append(ref[(*lead, slice(row, row + rows), slice(None))])
+        row += rows
+    return jnp.concatenate(parts, axis=1), row
+
+
+def pack_body(qkv_ref, out_ref, mixer_ref, gate_ref, query_ref, keys_ref, gain_ref, packed_ref):
+    row = 0
+    for j in range(3):
+        row = store_lanes(packed_ref, (), row, qkv_ref[j])
+    row = store_lanes(packed_ref, (), row, out_ref[...].T)
+    row = store_lanes(packed_ref, (), row, mixer_ref[...].T)
+    row = store_lanes(packed_ref, (), row, gate_ref[...])
+    for unit in range(query_ref.shape[0]):
+        row = store_lanes(packed_ref, (), row, query_ref[unit])
+    for unit in range(keys_ref.shape[0]):
+        row = store_lanes(packed_ref, (), row, keys_ref[unit])
+    store_lanes(packed_ref, (), row, gain_ref[...])
+
+
+def pack_weights(blocks):
+    amount = sum(block.size for block in blocks) // LANES
+    return pl.pallas_call(
+        pack_body,
+        out_shape=jax.ShapeDtypeStruct((amount, LANES), BF16),
+        compiler_params=params(32),
+        name="pack_weights",
+    )(*blocks)
+
+
+def unpack_body(
+    packed_ref, q_ref, k_ref, v_ref, out_ref, mixer_ref, gate_ref, query_ref, keys_ref, gain_ref
+):
+    row = 0
+    for target in (q_ref, k_ref, v_ref, out_ref, mixer_ref, gate_ref):
+        target[...], row = load_lanes(packed_ref, (0,), row, *target.shape)
+    for unit in range(query_ref.shape[1] // NKEYS):
+        span = slice(unit * NKEYS, (unit + 1) * NKEYS)
+        query_ref[:, span], row = load_lanes(packed_ref, (0,), row, query_ref.shape[0], NKEYS)
+    for unit in range(keys_ref.shape[0]):
+        keys_ref[unit], row = load_lanes(packed_ref, (0,), row, keys_ref.shape[1], NKEYS)
+    gain_ref[0] = packed_ref[0, row : row + gain_ref.shape[1], :]
+
+
+def unpack_weights(packed, part, width, units, key_part):
+    shards, amount, _ = packed.shape
+    model = shards * part
+
+    def rows_of(columns):
+        return pl.BlockSpec((part, columns), lambda i: (i, 0))
+
+    return pl.pallas_call(
+        unpack_body,
+        grid=(shards,),
+        in_specs=[pl.BlockSpec((1, amount, LANES), lambda i: (i, 0, 0))],
+        out_specs=[rows_of(width)] * 6
+        + [
+            rows_of(units * NKEYS),
+            pl.BlockSpec((units, key_part, NKEYS), lambda i: (0, i, 0)),
+            pl.BlockSpec((1, GAIN_ROWS, LANES), lambda i: (i, 0, 0)),
+        ],
+        out_shape=[jax.ShapeDtypeStruct((model, width), BF16)] * 6
+        + [
+            jax.ShapeDtypeStruct((model, units * NKEYS), BF16),
+            jax.ShapeDtypeStruct((units, shards * key_part, NKEYS), BF16),
+            jax.ShapeDtypeStruct((shards, GAIN_ROWS, LANES), BF16),
+        ],
+        compiler_params=params(32),
+        name="unpack_weights",
+    )(packed)
+
+
+def grads_body(*refs, pairs, part, units):
+    lefts, rights, rest = refs[:pairs], refs[pairs : 2 * pairs], refs[2 * pairs :]
+    packed_ref = rest[-1]
+    per = LANES // part
+    rows = [0] * per
+    for left, right in zip(lefts, rights):
+        grad = lax.dot_general(left[...], right[...], TN, preferred_element_type=F32).astype(BF16)
+        for number in range(per):
+            own = grad[number * part : (number + 1) * part]
+            rows[number] = store_lanes(packed_ref, (number,), rows[number], own)
+    if units:
+        key_ref = rest[0]
+        key_part = key_ref.shape[1] // per
+        for number in range(per):
+            for unit in range(units):
+                own = key_ref[unit, number * key_part : (number + 1) * key_part, :].astype(BF16)
+                rows[number] = store_lanes(packed_ref, (number,), rows[number], own)
+
+
+def pack_grads(lefts, rights, part, key_grad=None):
+    length, model = lefts[0].shape
+    shards = model // part
+    per = LANES // part
+    amount = part * sum(right.shape[1] for right in rights) // LANES
+    units = 0
+    extra, extra_specs = [], []
+    if key_grad is not None:
+        units, keys, _ = key_grad.shape
+        amount += key_grad.size // shards // LANES
+        extra = [key_grad]
+        extra_specs = [pl.BlockSpec((units, keys // shards * per, NKEYS), lambda i: (0, i, 0))]
+    return pl.pallas_call(
+        functools.partial(grads_body, pairs=len(lefts), part=part, units=units),
+        grid=(shards // per,),
+        in_specs=[pl.BlockSpec((length, LANES), lambda i: (0, i))] * len(lefts)
+        + [pl.BlockSpec(right.shape, lambda i: (0, 0)) for right in rights]
+        + extra_specs,
+        out_specs=pl.BlockSpec((per, amount, LANES), lambda i: (i, 0, 0)),
+        out_shape=jax.ShapeDtypeStruct((shards, amount, LANES), BF16),
+        compiler_params=params(48),
+        name="pack_grads",
+    )(*lefts, *rights, *extra)
+
+
+def unpack_grads_body(
+    early_ref, late_ref, qkv_ref, out_ref, mixer_ref, gate_ref, query_ref, keys_ref
+):
+    part, width = gate_ref.shape
+    row = 0
+    for j in range(3):
+        block, row = load_lanes(late_ref, (), row, part, width)
+        qkv_ref[j] = block.astype(F32)
+    block, row = load_lanes(late_ref, (), row, part, width)
+    out_ref[...] = block.astype(F32).T
+    row = 0
+    block, row = load_lanes(early_ref, (), row, part, width)
+    mixer_ref[...] = block.astype(F32).T
+    block, row = load_lanes(early_ref, (), row, part, width)
+    gate_ref[...] = block.astype(F32)
+    for unit in range(query_ref.shape[0]):
+        block, row = load_lanes(early_ref, (), row, part, NKEYS)
+        query_ref[unit] = block.astype(F32)
+    for unit in range(keys_ref.shape[0]):
+        block, row = load_lanes(early_ref, (), row, keys_ref.shape[1], NKEYS)
+        keys_ref[unit] = block.astype(F32)
+
+
+def unpack_grads(early, late, part, width, units, key_part):
+    shapes = [
+        (3, part, width),
+        (width, part),
+        (width, part),
+        (part, width),
+        (units, part, NKEYS),
+        (units, key_part, NKEYS),
+    ]
+    return pl.pallas_call(
+        unpack_grads_body,
+        out_shape=[jax.ShapeDtypeStruct(shape, F32) for shape in shapes],
+        compiler_params=params(32),
+        name="unpack_grads",
+    )(early, late)
 
 
 def unit_indices(picks, number):
@@ -463,11 +678,14 @@
 
 
 def spread_body(
-    column_ref, picks_ref, grad_ref, query_ref, keys_ref, out_ref, sum_ref, held_index, held_grad,
-    *, units
+    column_ref, picks_ref, prob_ref, grad_ref, query_ref, keys_ref, out_ref, sum_ref, held_index,
+    held_grad, *, units
 ):
     rows = picks_ref.shape[0]
-    held_grad[...] = grad_ref[...].astype(F32).T
+    probs = prob_ref[...]
+    pick_grad = grad_ref[...]
+    centre = over_head(probs * pick_grad, jnp.add)
+    held_grad[...] = (probs * (pick_grad - centre)).astype(BF16).astype(F32).T
 
     @pl.when(pl.program_id(0) == 0)
     def clear():
@@ -491,7 +709,7 @@
         sum_ref[unit] += jnp.dot(table, query_ref[:, span], preferred_element_type=F32)
 
 
-def spread_grads(column, picks, grads, queries, keys, rows=128):
+def spread_grads(column, picks, probs, grads, queries, keys, rows=128):
     amount = picks.shape[0]
     units = keys.shape[0]
     return pl.pallas_call(
@@ -501,6 +719,7 @@
             pl.BlockSpec(memory_space=pltpu.SMEM),
             pl.BlockSpec((rows, PICKS), lambda i: (i, 0)),
             pl.BlockSpec((rows, PICKS), lambda i: (i, 0)),
+            pl.BlockSpec((rows, PICKS), lambda i: (i, 0)),
             pl.BlockSpec((rows, units * NKEYS), lambda i: (i, 0)),
             pl.BlockSpec(keys.shape, lambda i: (0, 0, 0)),
         ],
@@ -515,7 +734,7 @@
         scratch_shapes=[pltpu.VMEM((PICKS, rows), jnp.int32), pltpu.VMEM((PICKS, rows), F32)],
         compiler_params=params(32),
         name="spread_grads",
-    )(column, picks, grads, queries, keys)
+    )(column, picks, probs, grads, queries, keys)
 
 
 def swap_narrow(block, bit):
@@ -586,33 +805,6 @@
 
 def sum_wide(block):
     return lax.psum_scatter(block, "wide", scatter_dimension=0)
-
-
-def lane_blocks(block):
-    return jnp.concatenate(
-        [block[..., start : start + LANES] for start in range(0, block.shape[-1], LANES)], axis=-2
-    )
-
-
-def join_lanes(blocks, rows):
-    count = blocks.shape[-2] // rows
-    return jnp.concatenate(
-        [blocks[..., part * rows : (part + 1) * rows, :] for part in range(count)], axis=-1
-    )
-
-
-def pack(blocks):
-    return jnp.concatenate([lane_blocks(block) for block in blocks], axis=-2)
-
-
-def unpack(packed, shapes):
-    result = []
-    start = 0
-    for rows, columns in shapes:
-        stop = start + rows * columns // LANES
-        result.append(join_lanes(packed[..., start:stop, :], rows))
-        start = stop
-    return result
 
 
 def per_device(
@@ -642,59 +834,41 @@
     key_part = sub_keys.shape[1]
 
     rows_one = gather_narrow(inputs).astype(F32)
-    first_shapes = [(3 * part, width), (part, width), (2 * part // LANES, LANES)]
-    first_pack = pack(
-        [
-            jnp.transpose(qkv_weight, (1, 0, 2)).reshape(3 * part, width),
-            out_weight.T,
-            jnp.concatenate([attn_gain, memory_gain]).reshape(-1, LANES),
-        ]
-    )
-    qkv_parts, out_turned, gains = unpack(gather_wide(first_pack), first_shapes)
-    qkv_full = [
-        qkv_parts[:, j * part : (j + 1) * part].reshape(model, width) for j in range(3)
-    ]
-    gains = gains.reshape(shards, 2, part).astype(F32)
+    gains = jnp.concatenate([attn_gain, memory_gain]).reshape(-1, LANES)
+    gains = jnp.pad(gains, ((0, GAIN_ROWS - gains.shape[0]), (0, 0)))
+    packed = gather_wide(
+        pack_weights(
+            [
+                jnp.transpose(qkv_weight, (1, 0, 2)),
+                out_weight,
+                memory_out,
+                gate_weight,
+                jnp.transpose(query_weight, (1, 0, 2)),
+                sub_keys,
+                gains,
+            ]
+        )
+    )
+    (
+        query_matrix, key_matrix, value_matrix, out_turned, mixer_turned, gate_full, query_full,
+        keys_full, gains,
+    ) = unpack_weights(packed, part, width, units, key_part)
+    qkv_full = [query_matrix, key_matrix, value_matrix]
+    gains = gains.reshape(shards, -1)[:, : 2 * part].reshape(shards, 2, part).astype(F32)
     gain_one = gains[:, 0].reshape(model)
     gain_two = gains[:, 1].reshape(model)
-    second_shapes = [
-        (part, width),
-        (part, width),
-        (part, units * NKEYS),
-        (units * key_part, NKEYS),
-    ]
-    second_pack = pack(
-        [
-            memory_out.T,
-            gate_weight,
-            query_weight.reshape(part, units * NKEYS),
-            sub_keys.reshape(units * key_part, NKEYS),
-        ]
-    )
-    second_pack, first_pack = lax.optimization_barrier((second_pack, first_pack))
-    mixer_turned, gate_full, query_full, keys_full = unpack(
-        gather_wide(second_pack), second_shapes
-    )
-    out_turned = out_turned.reshape(model, width)
-    mixer_turned = mixer_turned.reshape(model, width)
-    gate_full = gate_full.reshape(model, width)
-    query_full = query_full.reshape(model, units * NKEYS)
-    keys_full = jnp.transpose(
-        keys_full.reshape(shards, units, key_part, NKEYS), (1, 0, 2, 3)
-    ).reshape(units, NKEYS, NKEYS)
     out_all = gather_narrow(out_turned)
     upstream = gather_narrow(cotangent)
-    moving = {0: picks.astype(jnp.uint16)}
-    bits = bits_down(shards)
-    moving = swap_all(moving, "wide", bits[0])
-    rows_one, moving = lax.optimization_barrier((rows_one, moving))
-    for bit in bits[1:-1]:
-        moving = swap_all(moving, "wide", bit)
+    half = length // 2
+    pairs = picks[:half] | (picks[half:] << 16)
+    pairs, packed = lax.optimization_barrier((pairs, packed))
+    pairs = gather_wide(pairs)
+    all_picks = jnp.concatenate([pairs & 0xFFFF, (pairs >> 16) & 0xFFFF], axis=1)
+    all_picks = all_picks.reshape(shards * length, PICKS)
+    located = locate(base, all_picks, shard_rows)
 
     factor_one, normed = norm_rows(rows_one, gain_one)
     normed = normed.astype(BF16)
-    normed, moving = lax.optimization_barrier((normed, moving))
-    moving = swap_all(moving, "wide", bits[-1])
     queries, key_rows, value_rows = [
         jnp.dot(normed, qkv_full[j], preferred_element_type=F32).astype(BF16) for j in range(3)
     ]
@@ -704,8 +878,6 @@
     hidden = rows_one + lax.dot_general(head_all, out_all, NT, preferred_element_type=F32)
     factor_two, second = norm_rows(hidden, gain_two)
     second = second.astype(BF16)
-    second, moving = lax.optimization_barrier((second, moving))
-    all_picks = jnp.concatenate(in_order(moving, "wide"), axis=0).astype(jnp.int32)
 
     gate_value = jnp.dot(second, gate_full, preferred_element_type=F32)
     gate_act = jax.nn.silu(gate_value)
@@ -715,34 +887,23 @@
 
     memory_query = jnp.dot(second, query_full, preferred_element_type=F32).astype(BF16)
     own_scores = pick_scores(column_ref, picks, memory_query, keys_full)
-    mem_scores = sum_by_swaps(own_scores, "narrow").reshape(length, PKH, TOPK)
-    score_peak = jnp.max(mem_scores, axis=-1, keepdims=True)
-    raised = jnp.exp(mem_scores - score_peak)
-    mem_probs = raised / jnp.sum(raised, axis=-1, keepdims=True)
-    pick_weights = mem_probs.astype(BF16).reshape(length, PICKS)
+    mem_probs, pick_weights = pick_softmax(sum_by_swaps(own_scores, "narrow"))
     pick_weights, memory_grad = lax.optimization_barrier((pick_weights, memory_grad))
     all_weights = gather_wide(pick_weights).reshape(shards * length, PICKS)
 
-    pick_part = picked_products(base, all_picks, all_grads, memory_values.T)
+    pick_part = picked_products(base, all_picks, located, all_grads, memory_values.T)
     all_weights, pick_part = lax.optimization_barrier((all_weights, pick_part))
     pick_own = sum_wide(pick_part.reshape(shards, length, PICKS)).astype(F32)
-    tables = None
-    memory_parts = []
-    for number in range(PARTS):
-        part_sums, tables = bag_sums(
-            base, all_picks, all_weights, memory_values, tables, number, PARTS, shards
-        )
-        part_sums, pick_own = lax.optimization_barrier((part_sums, pick_own))
-        memory_parts.append(sum_wide(part_sums.reshape(shards, length // PARTS, width)))
+    memory_part, tables = bag_sums(base, all_picks, located, all_weights, memory_values)
+    memory_part, pick_own = lax.optimization_barrier((memory_part, pick_own))
+    memory_own = sum_wide(memory_part.reshape(shards, length, width))
     values_grad = lax.dot_general(tables, all_grads, TN, preferred_element_type=F32)
-    memory_parts, values_grad = lax.optimization_barrier((memory_parts, values_grad))
-    memory = jnp.concatenate(memory_parts, axis=0).astype(F32)
-
-    pick_grad = sum_by_swaps(pick_own, "narrow").reshape(length, PKH, TOPK)
-    centre = jnp.sum(mem_probs * pick_grad, axis=-1, keepdims=True)
-    score_grad = (mem_probs * (pick_grad - centre)).astype(BF16).reshape(length, PICKS)
+    memory_own, values_grad = lax.optimization_barrier((memory_own, values_grad))
+    memory = memory_own.astype(F32)
+
+    pick_grad = sum_by_swaps(pick_own, "narrow")
     memory_query_grad, key_grad = spread_grads(
-        column_ref, picks, score_grad, memory_query, keys_full
+        column_ref, picks, mem_probs, pick_grad, memory_query, keys_full
     )
 
     product = (gate_act * memory).astype(BF16)
@@ -750,6 +911,14 @@
     gate_rows_grad = (
         product_grad * memory * sigmoid * (1.0 + gate_value * (1.0 - sigmoid))
     ).astype(BF16)
+    early_pack = pack_grads(
+        [upstream, second, second],
+        [product, gate_rows_grad, memory_query_grad],
+        part,
+        key_grad,
+    )
+    early_pack, gate_rows_grad = lax.optimization_barrier((early_pack, gate_rows_grad))
+    early_sums = sum_wide(early_pack)
     second_part = lax.dot_general(gate_rows_grad, gate_full, NT, preferred_element_type=F32)
     second_part = second_part + lax.dot_general(
         memory_query_grad, query_full, NT, preferred_element_type=F32
@@ -780,25 +949,16 @@
     heads_grad = jnp.dot(branch_grad, out_turned, preferred_element_type=F32)
     heads_grad = heads_grad.astype(BF16)
 
-    mixer_grad = lax.dot_general(upstream, product, TN, preferred_element_type=F32)
-    query_grad = lax.dot_general(second, memory_query_grad, TN, preferred_element_type=F32)
-    gate_grad = lax.dot_general(second, gate_rows_grad, TN, preferred_element_type=F32)
-    key_grad = jnp.transpose(
-        key_grad.astype(BF16).reshape(units, shards, key_part, NKEYS), (1, 0, 2, 3)
-    ).reshape(shards, units * key_part, NKEYS)
-
-    def by_shard(block):
-        return block.astype(BF16).reshape(shards, part, block.shape[1])
-
     mixed_grad = attend_backward(starts, queries, key_rows, value_rows, heads_grad)
     normed_part = sum(
         lax.dot_general(mixed_grad[j], qkv_full[j], NT, preferred_element_type=F32)
         for j in range(3)
     )
-    out_grad = lax.dot_general(branch_grad, head_rows, TN, preferred_element_type=F32)
-    qkv_grad = [
-        lax.dot_general(normed, mixed_grad[j], TN, preferred_element_type=F32) for j in range(3)
-    ]
+    late_pack = pack_grads(
+        [normed, normed, normed, branch_grad], [*mixed_grad, head_rows], part
+    )
+    late_pack, early_sums = lax.optimization_barrier((late_pack, early_sums))
+    late_sums = sum_wide(late_pack)
     inner_part = jnp.sum(normed_part * gain_one * rows_one, axis=-1)
     gain_one_part = jnp.sum(normed_part * rows_one * factor_one, axis=0)
     tiny = sum_by_swaps(jnp.concatenate([inner_part, gain_one_part]), "narrow")
@@ -810,32 +970,23 @@
         + factor_one * own_columns(gain_one) * own_normed_grad
         - inputs.astype(F32) * (factor_one * factor_one * factor_one) * inner_one
     )
-    gain_parts = jnp.concatenate(
-        [gain_one_part.reshape(shards, 1, part), gain_two_part.reshape(shards, 1, part)], axis=1
-    ).astype(BF16).reshape(shards, -1, LANES)
-    all_grads_pack = pack(
-        [by_shard(block) for block in qkv_grad + [out_grad, mixer_grad, gate_grad, query_grad]]
-        + [key_grad, gain_parts]
-    )
-    sums = sum_wide(all_grads_pack).astype(F32)
-    sum_shapes = [(part, width)] * 4 + second_shapes + [(2 * part // LANES, LANES)]
-    (
-        query_sum, key_sum, value_sum, out_sum, mixer_sums, gate_sums, query_sums, key_sums,
-        gain_sums,
-    ) = unpack(sums, sum_shapes)
-    gain_sums = gain_sums.reshape(2, part)
+    gain_sums = sum_by_swaps(jnp.stack([gain_one_part, gain_two_part]), "wide")
+    gain_sums = lax.dynamic_slice_in_dim(gain_sums, lax.axis_index("wide") * part, part, 1)
+    qkv_sum, out_sum, mixer_sum, gate_sum, query_sum, key_sum = unpack_grads(
+        early_sums, late_sums, part, width, units, key_part
+    )
     return (
         outputs,
         input_grad,
         gain_sums[0],
-        jnp.stack([query_sum, key_sum, value_sum], axis=1),
-        out_sum.T,
+        jnp.transpose(qkv_sum, (1, 0, 2)),
+        out_sum,
         gain_sums[1],
-        query_sums.reshape(part, units, NKEYS),
-        key_sums.reshape(units, key_part, NKEYS),
-        gate_sums,
+        jnp.transpose(query_sum, (1, 0, 2)),
+        key_sum,
+        gate_sum,
         values_grad,
-        mixer_sums.T,
+        mixer_sum,
     )
 
 

time: 774 us -> 655 us (0.85)
  local copies, waits for them, and re-layouts: 103 us -> 43.5 us
  waiting for transfers between devices: 230 us -> 177 us
  Pallas kernels: 270 us -> 259 us
    pallas_call x0 -> x7, Pallas kernels: none -> 49.1 us  [the longest x1 25.9 us: locate(): pl.pallas_call(functools.partial(locate_body, total=total), grid=(amount...]
    pallas_call x2 -> x1, Pallas kernels: 134 us -> 87.5 us  [bag_sums(): pl.pallas_call(functools.partial(bag_body, chunk=chunk, unroll=unroll), g...]
    all_gather x4, waiting for transfers between devices: 100 us -> 57.4 us  [gather_wide(): return lax.all_gather(block, 'wide')]
    reduce_scatter x4, waiting for transfers between devices: 50.2 us -> 16.3 us  [sum_wide(): return lax.psum_scatter(block, 'wide', scatter_dimension=0)]
    ppermute x8 -> x11, waiting for transfers between devices: 17.8 us -> 44.2 us  [sum_by_swaps(): lax.ppermute(block, axis, [(i, i ^ bit) for i in range(lax.axis_size(axis...]
    unnamed x276 -> x178, local copies, waits for them, and re-layouts: 60.8 us -> 37.6 us
    pallas_call x1, Pallas kernels: 99.7 us -> 84.1 us  [picked_products(): pl.pallas_call(functools.partial(picked_body, unroll=unroll), grid=(amoun...]
    ppermute x9, waiting for transfers between devices: 30.8 us -> 18 us  [swap_narrow(): return lax.ppermute(block, 'narrow', [(i, i ^ bit) for i in range(size)])]
  transfers between devices with their start and end apart: 47 -> 43, of which waited for: 17 -> 19; matrix products, arithmetic and copies ran while one was open for 21% -> 19% of each run, Pallas kernels for 34% -> 39%
where the time goes in v5:
time: 655 us; the launch traced here: 645 us
  Pallas kernels  259 us (40%)
  waiting for transfers between devices  177 us (27%)
  matrix products  80.6 us (12%)
  local copies, waits for them, and re-layouts  43.5 us (7%)
  other arithmetic  36.6 us (6%)
  starting transfers between devices  32.2 us (5%)
  between operations  15.6 us (2%)
    pallas_call x1, Pallas kernels, bag_sums(): pl.pallas_call(functools.partial(bag_body, chunk=chunk, unroll=unroll), g...  87.5 us
    pallas_call x1, Pallas kernels, picked_products(): pl.pallas_call(functools.partial(picked_body, unroll=unroll), grid=(amoun...  84.1 us
    all_gather x4, waiting for transfers between devices, gather_wide(): return lax.all_gather(block, 'wide')  57.4 us
    dot_general x1, matrix products, per_device(): lax.dot_general(tables, all_grads, TN, preferred_element_type=F32)  53.6 us
    ppermute x11, waiting for transfers between devices, sum_by_swaps(): lax.ppermute(block, axis, [(i, i ^ bit) for i in range(lax.axis_size(axis...  44.2 us
    ppermute x15, waiting for transfers between devices, swap_all(): lax.ppermute(part, axis, pairs)  40.5 us
    unnamed x178, local copies, waits for them, and re-layouts  37.6 us
    pallas_call x1, Pallas kernels, locate(): pl.pallas_call(functools.partial(locate_body, total=total), grid=(amount...  25.9 us
  transfers between devices with their start and end apart: 43, of which 19 were waited for; matrix products, arithmetic and copies ran while one was open for 19% of the time, Pallas kernels for 39%

profile of v5, /device:TPU:0, one launch (start us, length us, event | category | flops | bytes accessed | tf_op | source)
XLA Modules:
  0.0 644.5 jit_solution(7604810066018540023)
XLA Ops:
  14.0 3.0 collective-permute-start.1
  17.6 12.4 %collective-permute-done.1 = bf16[1024,256]{1,0:T(8,128)(2,1)S(1)} collective-permute-done((bf16[1024,256]{1,0:T(8,128)(2,1)}, bf16[1024,256]{1,0:T(8,128)(2,1)S(1)}, u32[]{:S(2)}, u32[]{:S(2)}) %collective-permute-start.1) | collective-permute-done | bytes 524320 | tf_op jit(solution)/shard_map/ppermute | solution.py:747
  31.3 2.0 fusion.50.start_ref
  33.3 1.8 shift-left_or_fusion
  35.1 5.4 collective-permute-done.12
  44.0 49.9 %all-gather.9.cloned.1.call-done = bf16[17536,128]{1,0:T(8,128)(2,1)} async-done(((bf16[2192,128]{1,0:T(8,128)(2,1)}), bf16[17536,128]{1,0:T(8,128)(2,1)}) %all-gather.9.cloned.1.call-update) | async-done | bytes 4489232 | tf_op jit(solution)/shard_map/all_gather | solution.py:803
  93.9 2.3 copy-done.4
  98.6 1.5 collective-permute-start.7
  100.1 2.0 fusion.2.refs_0_.refs_1_.refs_2_
  104.5 9.4 %attend_forward.1.refs_7_ = bf16[1024,256]{1,0:T(8,128)(2,1)S(1)} custom-call(s32[1,1024]{1,0:T(1,128)S(1)} %fusion.50.start_ref, bf16[1024,256]{1,0:T(8,128)(2,1)S(1)} %convolution_convert_fusion.4.query_ref, bf16[1024,256]{1,0:T(8,128)(2,1)S(1)} %convolution_convert_fusion.3.key_ref, bf16[1024,256]{1,0:T(8,128)(2,1)S(1)} %convolution_convert_fusion.2.value_ref), custom_call_target="tpu_custom_call" | custom-call | flops 4294967296 | bytes 2097152 | tf_op jit(solution)/shard_map/attend_forward/pallas_call | solution.py:85
  115.7 1.6 pad_maximum_fusion.7
  117.4 8.7 %collective-permute-done.4 = bf16[1024,256]{1,0:T(8,128)(2,1)S(1)} collective-permute-done((bf16[1024,256]{1,0:T(8,128)(2,1)S(1)}, bf16[1024,256]{1,0:T(8,128)(2,1)S(1)}, u32[]{:S(2)}, u32[]{:S(2)}) %collective-permute-start.4) | collective-permute-done | bytes 524320 | tf_op jit(solution)/shard_map/ppermute | solution.py:747
  129.8 2.5 multiply_reduce_fusion.2
  135.1 1.9 multiply_convert_fusion.1
  137.0 9.6 %all-gather.13.cloned.1.call-start = ((), (), s32[]{:S(2)}) async-start(), calls=%async_computation.10 | async-start | bytes 2359296 | tf_op jit(solution)/shard_map/all_gather | solution.py:803
  146.6 2.9 convolution_convert_fusion.query_ref
  149.6 2.3 pick_scores.1
  151.9 1.5 collective-permute-start.9
  153.4 12.5 %collective-permute-done.9 = f32[1024,128]{1,0:T(8,128)S(1)} collective-permute-done((f32[1024,128]{1,0:T(8,128)S(1)}, f32[1024,128]{1,0:T(8,128)S(1)}, u32[]{:S(2)}, u32[]{:S(2)}) %collective-permute-start.9) | collective-permute-done | bytes 524320 | tf_op jit(solution)/shard_map/ppermute | solution.py:767
  166.1 6.4 copy.26
  172.5 3.6 pick_softmax.1
  177.1 1.9 broadcast_and_fusion
  179.2 25.9 %locate.1 = (f32[8192,128]{1,0:T(8,128)S(1)}, s32[8192,128]{1,0:T(8,128)S(1)}, s32[8192,128]{1,0:T(8,128)S(1)}) custom-call(s32[1]{0:T(128)} %bitcast.32.base_ref, s32[8192,128]{1,0:T(8,128)S(1)} %bitcast.208), custom_call_target="tpu_custom_call" | custom-call | flops 20971520000 | bytes 16777216 | tf_op jit(solution)/shard_map/locate/pallas_call | solution.py:212
  205.1 2.0 copy-done.7
  207.1 2.0 copy-done.47
  209.1 2.0 copy-done.48
  211.1 2.0 copy-done.49
  213.1 7.5 %all-gather.15.cloned.1.call-done.grad_ref = bf16[8192,256]{1,0:T(8,128)(2,1)} async-done(((bf16[1024,256]{1,0:T(8,128)(2,1)}), bf16[8192,256]{1,0:T(8,128)(2,1)}) %all-gather.15.cloned.1.call-update) | async-done | bytes 4194320 | tf_op jit(solution)/shard_map/all_gather | solution.py:803
  220.6 84.1 %picked_products.1 = bf16[8192,128]{1,0:T(8,128)(2,1)} custom-call(s32[1]{0:T(128)} %bitcast.32.base_ref, s32[8192,128]{1,0:T(8,128)} %bitcast.209, f32[8192,128]{1,0:T(8,128)} %copy-done.47, s32[8192,128]{1,0:T(8,128)} %copy-done.49, bf16[8192,256]{1,0:T(8,128)(2,1)} %all-gather.15.cloned.1.call-done.grad_ref, bf16[256,8192]{1,0:T(8,128)(2,1)} %bitcast.222), custom_call_target="tpu_custom_call" | custom-call | flops 120259084288 | bytes 8388608 | tf_op jit(solution)/shard_map/picked_products/pallas_call | solution.py:405
  304.8 87.5 %bag_sums.1 = (bf16[8192,256]{1,0:T(8,128)(2,1)}, bf16[8192,8192]{1,0:T(8,128)(2,1)}) custom-call(s32[1]{0:T(128)} %bitcast.32.base_ref, s32[8192,128]{1,0:T(8,128)} %bitcast.210, f32[8192,128]{1,0:T(8,128)} %copy-done.47, s32[8192,128]{1,0:T(8,128)} %copy-done.48, s32[8192,128]{1,0:T(8,128)} %copy-done.49, ...), custom_call_target="tpu_custom_call" | custom-call | flops 154618822656 | bytes 134217728 | tf_op jit(solution)/shard_map/bag_sums/pallas_call | solution.py:319
  393.3 1.4 collective-permute-start.14
  395.0 11.0 %collective-permute-done.14 = f32[1024,128]{1,0:T(8,128)S(1)} collective-permute-done((f32[1024,128]{1,0:T(8,128)S(1)}, f32[1024,128]{1,0:T(8,128)S(1)}, u32[]{:S(2)}, u32[]{:S(2)}) %collective-permute-start.14) | collective-permute-done | bytes 524320 | tf_op jit(solution)/shard_map/ppermute | solution.py:767
  406.9 53.6 %fusion.64 = f32[8192,256]{1,0:T(8,128)} fusion(bf16[8192,8192]{1,0:T(8,128)(2,1)} %get-tuple-element.71, bf16[8192,256]{1,0:T(8,128)(2,1)} %all-gather.15.cloned.1.call-done.grad_ref), kind=kOutput, calls=%fused_computation.162 | convolution fusion | flops 34359738368 | bytes 146800640 | tf_op jit(solution)/shard_map/dot_general | solution.py:900
  460.4 1.4 add.188.grad_ref
  464.1 14.7 %spread_grads.1 = (bf16[1024,512]{1,0:T(8,128)(2,1)S(1)}, f32[2,256,256]{2,1,0:T(8,128)S(1)}) custom-call(s32[1]{0:T(128)} %bitcast.36.column_ref, s32[1024,128]{1,0:T(8,128)S(1)} %copy-done.3, f32[1024,128]{1,0:T(8,128)S(1)} %copy-done.33, f32[1024,128]{1,0:T(8,128)S(1)} %add.188.grad_ref, bf16[1024,512]{1,0:T(8,128)(2,1)S(1)} %copy-done.6, ...), custom_call_target="tpu_custom_call" | custom-call | tf_op jit(solution)/shard_map/spread_grads/pallas_call | solution.py:715
  480.7 2.3 fusion.28
  484.1 8.1 %pack_grads.2 = bf16[8,1152,128]{2,1,0:T(8,128)(2,1)} custom-call(bf16[1024,1024]{1,0:T(8,128)(2,1)S(1)} %copy-done.1, bf16[1024,1024]{1,0:T(8,128)(2,1)} %copy-done.53, bf16[1024,1024]{1,0:T(8,128)(2,1)} %copy-done.53, bf16[1024,256]{1,0:T(8,128)(2,1)S(1)} %get-tuple-element.153.refs_3_, bf16[1024,256]{1,0:T(8,128)(2,1)S(1)} %get-tuple-element.77.refs_4_, ...), custom_call_target="tpu_custom_call" | custom-call | tf_op jit(solution)/shard_map/pack_grads/pallas_call | solution.py:583
  492.7 1.9 fusion.66
  495.4 1.9 multiply_reduce_fusion.1
  499.0 1.5 collective-permute-done.17
  502.7 12.4 %collective-permute-done.19 = f32[2048]{0:T(1024)S(1)} collective-permute-done((f32[2048]{0:T(1024)S(1)}, f32[2048]{0:T(1024)S(1)}, u32[]{:S(2)}, u32[]{:S(2)}) %collective-permute-start.19) | collective-permute-done | bytes 8224 | tf_op jit(solution)/shard_map/ppermute | solution.py:767
  516.3 3.3 fusion.59
  520.7 12.9 %collective-permute-done.22 = bf16[1024,256]{1,0:T(8,128)(2,1)S(1)} collective-permute-done((bf16[1024,256]{1,0:T(8,128)(2,1)S(1)}, bf16[1024,256]{1,0:T(8,128)(2,1)S(1)}, u32[]{:S(2)}, u32[]{:S(2)}) %collective-permute-start.22) | collective-permute-done | bytes 524320 | tf_op jit(solution)/shard_map/ppermute | solution.py:747
  533.6 2.8 fusion.65
  538.4 12.3 %attend_backward.1 = (bf16[1024,256]{1,0:T(8,128)(2,1)S(1)}, bf16[1024,256]{1,0:T(8,128)(2,1)S(1)}, bf16[1024,256]{1,0:T(8,128)(2,1)S(1)}) custom-call(s32[1,1024]{1,0:T(1,128)S(1)} %fusion.50.start_ref, bf16[1024,256]{1,0:T(8,128)(2,1)S(1)} %copy-done.31, bf16[1024,256]{1,0:T(8,128)(2,1)S(1)} %copy-done.29, bf16[1024,256]{1,0:T(8,128)(2,1)S(1)} %copy-done.27, ...), custom_call_target="tpu_custom_call" | custom-call | flops 268435456 | bytes 3670016 | tf_op jit(solution)/shard_map/attend_backward/pallas_call | solution.py:140
  550.7 9.0 %pack_grads.3 = bf16[8,1024,128]{2,1,0:T(8,128)(2,1)} custom-call(bf16[1024,1024]{1,0:T(8,128)(2,1)} %copy-done.50, bf16[1024,1024]{1,0:T(8,128)(2,1)} %copy-done.50, bf16[1024,1024]{1,0:T(8,128)(2,1)} %copy-done.50, bf16[1024,1024]{1,0:T(8,128)(2,1)} %copy-done.58, bf16[1024,256]{1,0:T(8,128)(2,1)S(1)} %get-tuple-element.80.refs_4_, ...), custom_call_target="tpu_custom_call" | custom-call | tf_op jit(solution)/shard_map/pack_grads/pallas_call | solution.py:583
  559.8 2.9 fusion.68
  562.6 2.8 fusion.67
  565.4 1.7 slice_bitcast_fusion.11
  567.3 2.2 pad_maximum_fusion.1
  569.5 2.0 copy-done.55
  572.9 4.0 fusion.3
  578.3 2.3 collective-permute-done.30
  581.8 2.0 collective-permute-start.32
  585.0 1.5 collective-permute-done.32
  587.9 2.6 collective-permute-done.33
  591.1 1.4 fusion.34
  592.5 1.6 collective-permute-start.26
  594.1 1.4 fusion.29
  596.6 10.9 %collective-permute-done.26 = bf16[1024,256]{1,0:T(8,128)(2,1)S(1)} collective-permute-done((bf16[1024,256]{1,0:T(8,128)(2,1)S(1)}, bf16[1024,256]{1,0:T(8,128)(2,1)S(1)}, u32[]{:S(2)}, u32[]{:S(2)}) %collective-permute-start.26) | collective-permute-done | bytes 524320 | tf_op jit(solution)/shard_map/ppermute | solution.py:742
  607.4 2.6 fusion.37
  610.0 5.7 collective-permute-done.29
  615.7 2.7 fusion.33
  618.4 16.3 %reduce-scatter.11.cloned.1.call-done = bf16[1,1024,128]{2,1,0:T(8,128)(2,1)} async-done(((bf16[8,1024,128]{2,1,0:T(8,128)(2,1)}), bf16[1,1024,128]{2,1,0:T(8,128)(2,1)}) %reduce-scatter.11.cloned.1.call-update) | async-done | bytes 262160 | tf_op jit(solution)/shard_map/reduce_scatter | solution.py:807
  (297 shorter events, 53.9 us)
Async XLA Ops:
  7.2 86.7 %all-gather.9.cloned.1.call-start = ((), (), s32[]{:S(2)}) async-start(), calls=%async_computation.8 | async-start | bytes 5050368 | tf_op jit(solution)/shard_map/all_gather | solution.py:803
  14.0 163.1 %all-gather.11.cloned.1.call-start = ((), (), s32[]{:S(2)}) async-start(), calls=%async_computation.9 | async-start | bytes 2359296 | tf_op jit(solution)/shard_map/all_gather | solution.py:803
  14.0 16.0 %collective-permute-start.1 = (bf16[1024,256]{1,0:T(8,128)(2,1)}, bf16[1024,256]{1,0:T(8,128)(2,1)S(1)}, u32[]{:S(2)}, u32[]{:S(2)}) collective-permute-start(bf16[1024,256]{1,0:T(8,128)(2,1)} %param.13), channel_id=1, source_target_pairs={{0,2},{1,3},{2,0},{3,1},{4,6},{5,7},{6,4},{7,5},{8,10},{9,11},{10,... | collective-permute-start | bytes 1572872 | tf_op jit(solution)/shard_map/ppermute | solution.py:747
  17.0 23.5 %collective-permute-start = (bf16[1024,256]{1,0:T(8,128)(2,1)}, bf16[1024,256]{1,0:T(8,128)(2,1)S(1)}, u32[]{:S(2)}, u32[]{:S(2)}) collective-permute-start(bf16[1024,256]{1,0:T(8,128)(2,1)} %param.13), channel_id=1, source_target_pairs={{0,1},{1,0},{2,3},{3,2},{4,5},{5,4},{6,7},{7,6},{8,9},{9,8},{10,11... | collective-permute-start | bytes 1572872 | tf_op jit(solution)/shard_map/ppermute | solution.py:747
  17.0 98.6 %collective-permute-start.11 = (bf16[1024,256]{1,0:T(8,128)(2,1)}, bf16[1024,256]{1,0:T(8,128)(2,1)}, u32[]{:S(2)}, u32[]{:S(2)}) collective-permute-start(bf16[1024,256]{1,0:T(8,128)(2,1)} %param.25), channel_id=1, source_target_pairs={{0,1},{1,0},{2,3},{3,2},{4,5},{5,4},{6,7},{7,6},{8,9},{9,8},{10,11... | collective-permute-start | bytes 1572872 | tf_op jit(solution)/shard_map/ppermute | solution.py:747
  17.5 23.0 %collective-permute-start.12 = (bf16[1024,256]{1,0:T(8,128)(2,1)}, bf16[1024,256]{1,0:T(8,128)(2,1)}, u32[]{:S(2)}, u32[]{:S(2)}) collective-permute-start(bf16[1024,256]{1,0:T(8,128)(2,1)} %param.25), channel_id=1, source_target_pairs={{0,2},{1,3},{2,0},{3,1},{4,6},{5,7},{6,4},{7,5},{8,10},{9,11},{10,... | collective-permute-start | bytes 1572872 | tf_op jit(solution)/shard_map/ppermute | solution.py:747
  30.0 10.5 %collective-permute-start.2 = (bf16[1024,256]{1,0:T(8,128)(2,1)S(1)}, bf16[1024,256]{1,0:T(8,128)(2,1)S(1)}, u32[]{:S(2)}, u32[]{:S(2)}) collective-permute-start(bf16[1024,256]{1,0:T(8,128)(2,1)S(1)} %collective-permute-done.1), channel_id=1, source_target_pairs={{0,1},{1,0},{2,3},{3,2},{4,5},{5,4},{6,7},{7,6},{8,9},{9,8},{10,11... | collective-permute-start | bytes 1572872 | tf_op jit(solution)/shard_map/ppermute | solution.py:747
  40.5 75.2 %collective-permute-start.13 = (bf16[1024,256]{1,0:T(8,128)(2,1)}, bf16[1024,256]{1,0:T(8,128)(2,1)}, u32[]{:S(2)}, u32[]{:S(2)}) collective-permute-start(bf16[1024,256]{1,0:T(8,128)(2,1)} %collective-permute-done.12), channel_id=1, source_target_pairs={{0,1},{1,0},{2,3},{3,2},{4,5},{5,4},{6,7},{7,6},{8,9},{9,8},{10,11... | collective-permute-start | bytes 1572872 | tf_op jit(solution)/shard_map/ppermute | solution.py:747
  44.0 58.2 %copy-start.81 = (f32[1024]{0:T(1024)}, f32[1024]{0:T(1024)S(1)}, u32[]{:S(2)}) copy-start(f32[1024]{0:T(1024)S(1)} %get-tuple-element.161) | copy-start | bytes 12292
  98.4 35.9 %copy-start.23 = (bf16[1024,256]{1,0:T(8,128)(2,1)}, bf16[1024,256]{1,0:T(8,128)(2,1)S(1)}, u32[]{:S(2)}) copy-start(bf16[1024,256]{1,0:T(8,128)(2,1)S(1)} %get-tuple-element.57) | copy-start | bytes 1572868
  98.4 36.6 %copy-start.21 = (bf16[1024,256]{1,0:T(8,128)(2,1)}, bf16[1024,256]{1,0:T(8,128)(2,1)S(1)}, u32[]{:S(2)}) copy-start(bf16[1024,256]{1,0:T(8,128)(2,1)S(1)} %get-tuple-element.65) | copy-start | bytes 1572868
  98.4 48.2 %copy-start.13 = (bf16[1024,512]{1,0:T(8,128)(2,1)}, bf16[1024,512]{1,0:T(8,128)(2,1)S(1)}, u32[]{:S(2)}) copy-start(bf16[1024,512]{1,0:T(8,128)(2,1)S(1)} %get-tuple-element.62) | copy-start | bytes 3145732
  98.5 51.1 %copy-start.15 = (bf16[2,256,256]{2,1,0:T(8,128)(2,1)}, bf16[2,256,256]{2,1,0:T(8,128)(2,1)S(1)}, u32[]{:S(2)}) copy-start(bf16[2,256,256]{2,1,0:T(8,128)(2,1)S(1)} %get-tuple-element.63.keys_ref) | copy-start | bytes 786436
  98.5 122.1 %all-gather.15.cloned.1.call-start = ((), (), s32[]{:S(2)}) async-start(), calls=%async_computation.11 | async-start | bytes 4718592 | tf_op jit(solution)/shard_map/all_gather | solution.py:803
  98.6 34.4 %copy-start.79 = (f32[1024]{0:T(1024)}, f32[1024]{0:T(1024)S(1)}, u32[]{:S(2)}) copy-start(f32[1024]{0:T(1024)S(1)} %get-tuple-element.158) | copy-start | bytes 12292
  98.6 16.5 %collective-permute-start.7 = (bf16[1024,256]{1,0:T(8,128)(2,1)}, bf16[1024,256]{1,0:T(8,128)(2,1)S(1)}, u32[]{:S(2)}, u32[]{:S(2)}) collective-permute-start(bf16[1024,256]{1,0:T(8,128)(2,1)} %copy-done.34), channel_id=1, source_target_pairs={{0,2},{1,3},{2,0},{3,1},{4,6},{5,7},{6,4},{7,5},{8,10},{9,11},{10,... | collective-permute-start | bytes 1572872 | tf_op jit(solution)/shard_map/ppermute | solution.py:747
  104.4 10.7 %copy-start.35 = (bf16[1024,256]{1,0:T(8,128)(2,1)S(1)}, bf16[1024,256]{1,0:T(8,128)(2,1)}, u32[]{:S(2)}) copy-start(bf16[1024,256]{1,0:T(8,128)(2,1)} %copy-done.34) | copy-start | bytes 1572868
  104.4 11.2 %copy-start.74 = (bf16[1024,256]{1,0:T(8,128)(2,1)S(1)}, bf16[1024,256]{1,0:T(8,128)(2,1)}, u32[]{:S(2)}) copy-start(bf16[1024,256]{1,0:T(8,128)(2,1)} %param.25) | copy-start | bytes 1572868
  113.9 14.1 %copy-start.11 = (bf16[1024,256]{1,0:T(8,128)(2,1)}, bf16[1024,256]{1,0:T(8,128)(2,1)S(1)}, u32[]{:S(2)}) copy-start(bf16[1024,256]{1,0:T(8,128)(2,1)S(1)} %attend_forward.1.refs_7_) | copy-start | bytes 1572868
  113.9 12.2 %collective-permute-start.4 = (bf16[1024,256]{1,0:T(8,128)(2,1)S(1)}, bf16[1024,256]{1,0:T(8,128)(2,1)S(1)}, u32[]{:S(2)}, u32[]{:S(2)}) collective-permute-start(bf16[1024,256]{1,0:T(8,128)(2,1)S(1)} %attend_forward.1.refs_7_), channel_id=1, source_target_pairs={{0,2},{1,3},{2,0},{3,1},{4,6},{5,7},{6,4},{7,5},{8,10},{9,11},{10,... | collective-permute-start | bytes 1572872 | tf_op jit(solution)/shard_map/ppermute | solution.py:747
  115.1 11.4 %collective-permute-start.6 = (bf16[1024,256]{1,0:T(8,128)(2,1)S(1)}, bf16[1024,256]{1,0:T(8,128)(2,1)S(1)}, u32[]{:S(2)}, u32[]{:S(2)}) collective-permute-start(bf16[1024,256]{1,0:T(8,128)(2,1)S(1)} %copy-done.35), channel_id=1, source_target_pairs={{0,1},{1,0},{2,3},{3,2},{4,5},{5,4},{6,7},{7,6},{8,9},{9,8},{10,11... | collective-permute-start | bytes 1572872 | tf_op jit(solution)/shard_map/ppermute | solution.py:747
  115.2 11.4 %collective-permute-start.8 = (bf16[1024,256]{1,0:T(8,128)(2,1)S(1)}, bf16[1024,256]{1,0:T(8,128)(2,1)S(1)}, u32[]{:S(2)}, u32[]{:S(2)}) collective-permute-start(bf16[1024,256]{1,0:T(8,128)(2,1)S(1)} %collective-permute-done.7), channel_id=1, source_target_pairs={{0,1},{1,0},{2,3},{3,2},{4,5},{5,4},{6,7},{7,6},{8,9},{9,8},{10,11... | collective-permute-start | bytes 1572872 | tf_op jit(solution)/shard_map/ppermute | solution.py:747
  117.3 9.6 %collective-permute-start.3 = (bf16[1024,256]{1,0:T(8,128)(2,1)S(1)}, bf16[1024,256]{1,0:T(8,128)(2,1)S(1)}, u32[]{:S(2)}, u32[]{:S(2)}) collective-permute-start(bf16[1024,256]{1,0:T(8,128)(2,1)S(1)} %attend_forward.1.refs_7_), channel_id=1, source_target_pairs={{0,1},{1,0},{2,3},{3,2},{4,5},{5,4},{6,7},{7,6},{8,9},{9,8},{10,11... | collective-permute-start | bytes 1572872 | tf_op jit(solution)/shard_map/ppermute | solution.py:747
  126.1 1.9 collective-permute-start.5
  137.0 167.7 %all-gather.13.cloned.1.call-start = ((), (), s32[]{:S(2)}) async-start(), calls=%async_computation.10 | async-start | bytes 2359296 | tf_op jit(solution)/shard_map/all_gather | solution.py:803
  151.9 14.0 %collective-permute-start.9 = (f32[1024,128]{1,0:T(8,128)S(1)}, f32[1024,128]{1,0:T(8,128)S(1)}, u32[]{:S(2)}, u32[]{:S(2)}) collective-permute-start(f32[1024,128]{1,0:T(8,128)S(1)} %pick_scores.1), channel_id=1, source_target_pairs={{0,2},{1,3},{2,0},{3,1},{4,6},{5,7},{6,4},{7,5},{8,10},{9,11},{10,... | collective-permute-start | bytes 1572872 | tf_op jit(solution)/shard_map/ppermute | solution.py:767
  166.0 6.5 %collective-permute-start.10 = (f32[1024,128]{1,0:T(8,128)S(1)}, f32[1024,128]{1,0:T(8,128)S(1)}, u32[]{:S(2)}, u32[]{:S(2)}) collective-permute-start(f32[1024,128]{1,0:T(8,128)S(1)} %add.184), channel_id=1, source_target_pairs={{0,1},{1,0},{2,3},{3,2},{4,5},{5,4},{6,7},{7,6},{8,9},{9,8},{10,11... | collective-permute-start | bytes 1572872 | tf_op jit(solution)/shard_map/ppermute | solution.py:767
  177.0 215.3 %reduce-scatter.5.cloned.1.call-start = ((), (), s32[]{:S(2)}) async-start(), calls=%async_computation.4 | async-start | bytes 2359296 | tf_op jit(solution)/shard_map/reduce_scatter | solution.py:807
  304.7 176.0 %reduce-scatter.7.cloned.1.call-start = ((), (), s32[]{:S(2)}) async-start(), calls=%async_computation.5 | async-start | bytes 4718592 | tf_op jit(solution)/shard_map/reduce_scatter | solution.py:807
  393.3 12.6 %collective-permute-start.14 = (f32[1024,128]{1,0:T(8,128)S(1)}, f32[1024,128]{1,0:T(8,128)S(1)}, u32[]{:S(2)}, u32[]{:S(2)}) collective-permute-start(f32[1024,128]{1,0:T(8,128)S(1)} %bitcast_convert_fusion), channel_id=1, source_target_pairs={{0,2},{1,3},{2,0},{3,1},{4,6},{5,7},{6,4},{7,5},{8,10},{9,11},{10,... | collective-permute-start | bytes 1572872 | tf_op jit(solution)/shard_map/ppermute | solution.py:767
  394.7 172.4 %reduce-scatter.9.cloned.1.call-start = ((), (), s32[]{:S(2)}) async-start(), calls=%async_computation.6 | async-start | bytes 2654208 | tf_op jit(solution)/shard_map/reduce_scatter | solution.py:807
  406.8 53.6 %collective-permute-start.15 = (f32[1024,128]{1,0:T(8,128)}, f32[1024,128]{1,0:T(8,128)}, u32[]{:S(2)}, u32[]{:S(2)}) collective-permute-start(f32[1024,128]{1,0:T(8,128)} %add.187), channel_id=1, source_target_pairs={{0,1},{1,0},{2,3},{3,2},{4,5},{5,4},{6,7},{7,6},{8,9},{9,8},{10,11... | collective-permute-start | bytes 1572872 | tf_op jit(solution)/shard_map/ppermute | solution.py:767
  406.9 55.0 %copy-start.3 = (s32[1024,128]{1,0:T(8,128)S(1)}, s32[1024,128]{1,0:T(8,128)}, u32[]{:S(2)}) copy-start(s32[1024,128]{1,0:T(8,128)} %picks_ref.3) | copy-start | bytes 1572868
  406.9 55.0 %copy-start.16 = (bf16[2,256,256]{2,1,0:T(8,128)(2,1)S(1)}, bf16[2,256,256]{2,1,0:T(8,128)(2,1)}, u32[]{:S(2)}) copy-start(bf16[2,256,256]{2,1,0:T(8,128)(2,1)} %copy-done.15) | copy-start | bytes 786436
  460.4 22.6 %copy-start.1 = (bf16[1024,1024]{1,0:T(8,128)(2,1)S(1)}, bf16[1024,1024]{1,0:T(8,128)(2,1)}, u32[]{:S(2)}) copy-start(bf16[1024,1024]{1,0:T(8,128)(2,1)} %copy-done) | copy-start | bytes 6291460
  492.2 142.4 %reduce-scatter.11.cloned.1.call-start = ((), (), s32[]{:S(2)}) async-start(), calls=%async_computation.7 | async-start | bytes 2359296 | tf_op jit(solution)/shard_map/reduce_scatter | solution.py:807
  498.0 18.2 %copy-start.75 = (bf16[1024,256]{1,0:T(8,128)(2,1)S(1)}, bf16[1024,256]{1,0:T(8,128)(2,1)}, u32[]{:S(2)}) copy-start(bf16[1024,256]{1,0:T(8,128)(2,1)} %param.25) | copy-start | bytes 1572868
  498.0 18.2 %copy-start.86 = (f32[1024]{0:T(1024)S(1)}, f32[1024]{0:T(1024)}, u32[]{:S(2)}) copy-start(f32[1024]{0:T(1024)} %get-tuple-element.162) | copy-start | bytes 12292
  498.2 35.4 %copy-start.22 = (bf16[1024,256]{1,0:T(8,128)(2,1)S(1)}, bf16[1024,256]{1,0:T(8,128)(2,1)}, u32[]{:S(2)}) copy-start(bf16[1024,256]{1,0:T(8,128)(2,1)} %copy-done.21) | copy-start | bytes 1572868
  498.2 2.3 collective-permute-start.17
  498.9 17.3 %collective-permute-start.16 = (bf16[1024,256]{1,0:T(8,128)(2,1)S(1)}, bf16[1024,256]{1,0:T(8,128)(2,1)S(1)}, u32[]{:S(2)}, u32[]{:S(2)}) collective-permute-start(bf16[1024,256]{1,0:T(8,128)(2,1)S(1)} %get-tuple-element.124), channel_id=1, source_target_pairs={{0,1},{1,0},{2,3},{3,2},{4,5},{5,4},{6,7},{7,6},{8,9},{9,8},{10,11... | collective-permute-start | bytes 1572872 | tf_op jit(solution)/shard_map/ppermute | solution.py:742
  500.6 15.7 %collective-permute-start.18 = (bf16[1024,256]{1,0:T(8,128)(2,1)S(1)}, bf16[1024,256]{1,0:T(8,128)(2,1)}, u32[]{:S(2)}, u32[]{:S(2)}) collective-permute-start(bf16[1024,256]{1,0:T(8,128)(2,1)S(1)} %fusion.38), channel_id=1, source_target_pairs={{0,2},{1,3},{2,0},{3,1},{4,6},{5,7},{6,4},{7,5},{8,10},{9,11},{10,... | collective-permute-start | bytes 1572872 | tf_op jit(solution)/shard_map/ppermute | solution.py:742
  501.8 13.2 %collective-permute-start.19 = (f32[2048]{0:T(1024)S(1)}, f32[2048]{0:T(1024)S(1)}, u32[]{:S(2)}, u32[]{:S(2)}) collective-permute-start(f32[2048]{0:T(1024)S(1)} %pad_maximum_fusion.11), channel_id=1, source_target_pairs={{0,2},{1,3},{2,0},{3,1},{4,6},{5,7},{6,4},{7,5},{8,10},{9,11},{10,... | collective-permute-start | bytes 24584 | tf_op jit(solution)/shard_map/ppermute | solution.py:767
  515.1 1.2 collective-permute-start.20
  519.6 14.0 %collective-permute-start.22 = (bf16[1024,256]{1,0:T(8,128)(2,1)S(1)}, bf16[1024,256]{1,0:T(8,128)(2,1)S(1)}, u32[]{:S(2)}, u32[]{:S(2)}) collective-permute-start(bf16[1024,256]{1,0:T(8,128)(2,1)S(1)} %get-tuple-element.110), channel_id=1, source_target_pairs={{0,2},{1,3},{2,0},{3,1},{4,6},{5,7},{6,4},{7,5},{8,10},{9,11},{10,... | collective-permute-start | bytes 1572872 | tf_op jit(solution)/shard_map/ppermute | solution.py:747
  520.7 15.6 %collective-permute-start.21 = (bf16[1024,256]{1,0:T(8,128)(2,1)S(1)}, bf16[1024,256]{1,0:T(8,128)(2,1)S(1)}, u32[]{:S(2)}, u32[]{:S(2)}) collective-permute-start(bf16[1024,256]{1,0:T(8,128)(2,1)S(1)} %get-tuple-element.110), channel_id=1, source_target_pairs={{0,1},{1,0},{2,3},{3,2},{4,5},{5,4},{6,7},{7,6},{8,9},{9,8},{10,11... | collective-permute-start | bytes 1572872 | tf_op jit(solution)/shard_map/ppermute | solution.py:747
  533.6 2.8 collective-permute-start.23
  537.7 13.0 %copy-start.58 = (bf16[1024,1024]{1,0:T(8,128)(2,1)}, bf16[1024,1024]{1,0:T(8,128)(2,1)S(1)}, u32[]{:S(2)}) copy-start(bf16[1024,1024]{1,0:T(8,128)(2,1)S(1)} %pad_maximum_fusion.10.refs_3_) | copy-start | bytes 6291460
  537.7 13.0 %copy-start.12 = (bf16[1024,256]{1,0:T(8,128)(2,1)S(1)}, bf16[1024,256]{1,0:T(8,128)(2,1)}, u32[]{:S(2)}) copy-start(bf16[1024,256]{1,0:T(8,128)(2,1)} %copy-done.11) | copy-start | bytes 1572868
  572.4 18.7 %collective-permute-start.25 = (bf16[1024,256]{1,0:T(8,128)(2,1)}, bf16[1024,256]{1,0:T(8,128)(2,1)S(1)}, u32[]{:S(2)}, u32[]{:S(2)}) collective-permute-start(bf16[1024,256]{1,0:T(8,128)(2,1)} %get-tuple-element.119), channel_id=1, source_target_pairs={{0,1},{1,0},{2,3},{3,2},{4,5},{5,4},{6,7},{7,6},{8,9},{9,8},{10,11... | collective-permute-start | bytes 1572872 | tf_op jit(solution)/shard_map/ppermute | solution.py:742
  576.9 3.7 collective-permute-start.30
  580.6 1.2 collective-permute-start.31
  581.8 4.7 collective-permute-start.32
  584.9 30.7 %copy-start.72 = (f32[1024,256]{1,0:T(8,128)S(1)}, f32[1024,256]{1,0:T(8,128)}, u32[]{:S(2)}) copy-start(f32[1024,256]{1,0:T(8,128)} %get-tuple-element.111) | copy-start | bytes 3145732
  584.9 30.7 %copy-start.73 = (bf16[1024,256]{1,0:T(8,128)(2,1)S(1)}, bf16[1024,256]{1,0:T(8,128)(2,1)}, u32[]{:S(2)}) copy-start(bf16[1024,256]{1,0:T(8,128)(2,1)} %param.13) | copy-start | bytes 1572868
  584.9 30.7 %copy-start.85 = (f32[1024]{0:T(1024)S(1)}, f32[1024]{0:T(1024)}, u32[]{:S(2)}) copy-start(f32[1024]{0:T(1024)} %get-tuple-element.160) | copy-start | bytes 12292
  584.9 9.2 %collective-permute-start.28 = (bf16[1024,256]{1,0:T(8,128)(2,1)}, bf16[1024,256]{1,0:T(8,128)(2,1)S(1)}, u32[]{:S(2)}, u32[]{:S(2)}) collective-permute-start(bf16[1024,256]{1,0:T(8,128)(2,1)} %get-tuple-element.113), channel_id=1, source_target_pairs={{0,1},{1,0},{2,3},{3,2},{4,5},{5,4},{6,7},{7,6},{8,9},{9,8},{10,11... | collective-permute-start | bytes 1572872 | tf_op jit(solution)/shard_map/ppermute | solution.py:742
  586.5 3.9 collective-permute-start.33
  587.4 9.2 %collective-permute-start.24 = (bf16[1024,256]{1,0:T(8,128)(2,1)S(1)}, bf16[1024,256]{1,0:T(8,128)(2,1)S(1)}, u32[]{:S(2)}, u32[]{:S(2)}) collective-permute-start(bf16[1024,256]{1,0:T(8,128)(2,1)S(1)} %get-tuple-element.118), channel_id=1, source_target_pairs={{0,1},{1,0},{2,3},{3,2},{4,5},{5,4},{6,7},{7,6},{8,9},{9,8},{10,11... | collective-permute-start | bytes 1572872 | tf_op jit(solution)/shard_map/ppermute | solution.py:742
  587.4 22.6 %collective-permute-start.27 = (bf16[1024,256]{1,0:T(8,128)(2,1)}, bf16[1024,256]{1,0:T(8,128)(2,1)S(1)}, u32[]{:S(2)}, u32[]{:S(2)}) collective-permute-start(bf16[1024,256]{1,0:T(8,128)(2,1)} %get-tuple-element.112), channel_id=1, source_target_pairs={{0,1},{1,0},{2,3},{3,2},{4,5},{5,4},{6,7},{7,6},{8,9},{9,8},{10,11... | collective-permute-start | bytes 1572872 | tf_op jit(solution)/shard_map/ppermute | solution.py:742
  590.5 5.6 collective-permute-start.34
  592.5 14.9 %collective-permute-start.26 = (bf16[1024,256]{1,0:T(8,128)(2,1)S(1)}, bf16[1024,256]{1,0:T(8,128)(2,1)S(1)}, u32[]{:S(2)}, u32[]{:S(2)}) collective-permute-start(bf16[1024,256]{1,0:T(8,128)(2,1)S(1)} %fusion.34), channel_id=1, source_target_pairs={{0,2},{1,3},{2,0},{3,1},{4,6},{5,7},{6,4},{7,5},{8,10},{9,11},{10,... | collective-permute-start | bytes 1572872 | tf_op jit(solution)/shard_map/ppermute | solution.py:742
  595.5 20.2 %collective-permute-start.29 = (bf16[1024,256]{1,0:T(8,128)(2,1)S(1)}, bf16[1024,256]{1,0:T(8,128)(2,1)S(1)}, u32[]{:S(2)}, u32[]{:S(2)}) collective-permute-start(bf16[1024,256]{1,0:T(8,128)(2,1)S(1)} %fusion.29), channel_id=1, source_target_pairs={{0,2},{1,3},{2,0},{3,1},{4,6},{5,7},{6,4},{7,5},{8,10},{9,11},{10,... | collective-permute-start | bytes 1572872 | tf_op jit(solution)/shard_map/ppermute | solution.py:742
  596.6 38.1 %copy-start.37 = (bf16[1,1152,128]{2,1,0:T(8,128)(2,1)S(1)}, bf16[1,1152,128]{2,1,0:T(8,128)(2,1)}, u32[]{:S(2)}) copy-start(bf16[1,1152,128]{2,1,0:T(8,128)(2,1)} %reduce-scatter.9.cloned.1.call-done) | copy-start | bytes 884740
  (66 other events, 186.9 us)
Sparse Core Ops, SparseCore 0:
  14.1 79.7 all-gather.8
  98.6 47.6 all-gather.10
  148.4 72.1 all-gather.14
  223.2 47.6 all-gather.12
  304.8 66.0 reduce-scatter.4
  394.8 85.5 reduce-scatter.6
  492.4 68.7 reduce-scatter.8
  567.3 67.3 reduce-scatter.10

commit v6 on v5

--- a/solution.py
+++ b/solution.py
@@ -15,6 +15,7 @@
 DOCS = 3
 DOC_MOST = 512
 LANES = 128
+ROWS = 512
 GAIN_ROWS = 16
 COVER = 1
 
@@ -197,13 +198,25 @@
     return place, jnp.where(valid, jnp.take_along_axis(local, place, axis=1), -1)
 
 
-def locate_body(base_ref, picks_ref, count_ref, place_ref, found_ref, *, total):
+def locate_body(base_ref, picks_ref, out_ref, *, total):
     local = picks_ref[...] - base_ref[0]
     counts = count_local(local, total)
     valid, place = search(counts, 0)
-    count_ref[...] = counts
-    place_ref[...] = place
-    found_ref[...] = jnp.where(valid, jnp.take_along_axis(local, place, axis=1), -1)
+    found = jnp.where(valid, jnp.take_along_axis(local, place, axis=1) + 1, 0)
+    inside = jnp.where((local >= 0) & (local < total), 1, 0)
+    out_ref[...] = found | (place << 16) | (counts.astype(jnp.int32) << 23) | (inside << 31)
+
+
+def found_in(located):
+    return (located & 0xFFFF) - 1
+
+
+def place_in(located):
+    return (located >> 16) & (LANES - 1)
+
+
+def count_in(located):
+    return (located >> 23) & (2 * LANES - 1)
 
 
 def locate(base, picks, total, rows=512):
@@ -213,12 +226,8 @@
         functools.partial(locate_body, total=total),
         grid=(amount // rows,),
         in_specs=[pl.BlockSpec(memory_space=pltpu.SMEM), block],
-        out_specs=[block] * 3,
-        out_shape=[
-            jax.ShapeDtypeStruct((amount, PICKS), F32),
-            jax.ShapeDtypeStruct((amount, PICKS), jnp.int32),
-            jax.ShapeDtypeStruct((amount, PICKS), jnp.int32),
-        ],
+        out_specs=block,
+        out_shape=pltpu.HBM((amount, PICKS), jnp.int32),
         compiler_params=params(32),
         cost_estimate=pl.CostEstimate(
             flops=amount * PICKS * 20000, bytes_accessed=amount * PICKS * 16, transcendentals=0
@@ -245,9 +254,22 @@
     return jnp.concatenate(parts, axis=1)
 
 
+def token_places(picks, shards, before):
+    own = before is None
+    length = picks.shape[0] if own else picks.shape[0] // shards
+    blocks = length // ROWS
+
+    def place(i, where):
+        shard = where[1] if own else lax.rem(where[1] + 1 + i // blocks, shards)
+        return (shard * blocks + i % blocks, 0)
+
+    block = pl.BlockSpec((ROWS, PICKS), (lambda i, where: (i, 0)) if own else place)
+    return (blocks if own else (shards - 1) * blocks), block, place, length
+
+
 def bag_body(
-    base_ref, picks_ref, count_ref, place_ref, found_ref, weight_ref, table_ref, out_ref, keep_ref,
-    high, low, weights, *, chunk, unroll
+    base_ref, picks_ref, located_ref, weight_ref, table_ref, out_ref, keep_ref, high, low, weights,
+    *, chunk, unroll
 ):
     rows = picks_ref.shape[0]
     total = table_ref.shape[0]
@@ -297,11 +319,13 @@
 
     def more(number, carried):
         local = picks_ref[...] - base_ref[0]
-        one_round(*place_of(count_ref[...], local, number), False)
+        one_round(*place_of(counts, local, number), False)
         return carried
 
-    one_round(place_ref[...], found_ref[...], True)
-    lax.fori_loop(1, rounds_of(count_ref[...]), more, 0)
+    located = located_ref[...]
+    counts = count_in(located).astype(F32)
+    one_round(place_in(located), found_in(located), True)
+    lax.fori_loop(1, rounds_of(counts), more, 0)
     result = jnp.zeros(out_ref.shape, F32)
     for start in range(0, total, chunk):
         result = result + jnp.dot(
@@ -312,41 +336,42 @@
     out_ref[...] = result.astype(out_ref.dtype)
 
 
-def bag_sums(base, picks, located, weights, table, rows=256, chunk=1024, unroll=16):
+def bag_sums(base, picks, located, weights, table, chunk=1024, unroll=32):
     amount = picks.shape[0]
     total, width = table.shape
-    block = pl.BlockSpec((rows, PICKS), lambda i: (i, 0))
+    block = pl.BlockSpec((ROWS, PICKS), lambda i: (i, 0))
     return pl.pallas_call(
         functools.partial(bag_body, chunk=chunk, unroll=unroll),
-        grid=(amount // rows,),
+        grid=(amount // ROWS,),
         in_specs=[pl.BlockSpec(memory_space=pltpu.SMEM)]
-        + [block] * 5
+        + [block] * 3
         + [pl.BlockSpec((total, width), lambda i: (0, 0))],
         out_specs=[
-            pl.BlockSpec((rows, width), lambda i: (i, 0)),
-            pl.BlockSpec((rows, total), lambda i: (i, 0)),
+            pl.BlockSpec((ROWS, width), lambda i: (i, 0)),
+            pl.BlockSpec((ROWS, total), lambda i: (i, 0)),
         ],
         out_shape=[
             jax.ShapeDtypeStruct((amount, width), BF16),
             jax.ShapeDtypeStruct((amount, total), BF16),
         ],
-        scratch_shapes=[pltpu.VMEM((rows, LANES), F32)] * 3,
+        scratch_shapes=[pltpu.VMEM((ROWS, LANES), F32)] * 3,
         compiler_params=params(56),
         cost_estimate=pl.CostEstimate(
             flops=9 * amount * total * width, bytes_accessed=amount * total * 2, transcendentals=0
         ),
         name="bag_sums",
-    )(base, picks, *located, weights, table)
+    )(base, picks, located, weights, table)
 
 
 def picked_body(
-    base_ref, picks_ref, count_ref, found_ref, grad_ref, table_ref, out_ref, high, low, found_at,
-    held, *, unroll
+    base_ref, picks_ref, located_ref, grad_ref, table_ref, *rest, unroll
 ):
+    out_ref, high, low, found_at, held = rest[-5:]
     rows = picks_ref.shape[0]
     total = table_ref.shape[1]
     groups = total // NKEYS
     masks = group_masks()
+    located = located_ref[...]
     grads = grad_ref[...]
     for group in range(groups):
         held[group] = jnp.dot(
@@ -380,10 +405,8 @@
             return carried
 
         lax.fori_loop(0, rows // (8 * unroll), some_tokens, 0)
-        slot = count_ref[...].astype(jnp.int32) - (1 + number * SLOTS)
-        local = picks_ref[...] - base_ref[0]
-        inside = (local >= 0) & (local < total)
-        here = (slot >= 0) & (slot < SLOTS) & inside
+        slot = count_in(located) - (1 + number * SLOTS)
+        here = (slot >= 0) & (slot < SLOTS) & (located < 0)
         token = lax.broadcasted_iota(jnp.int32, slot.shape, 0) & (LANES // SLOTS - 1)
         lane = token * SLOTS + jnp.clip(slot, 0, SLOTS - 1)
         value = jnp.take_along_axis(found_at[...], lane, axis=1)
@@ -392,41 +415,43 @@
 
     def more(number, carried):
         local = picks_ref[...] - base_ref[0]
-        one_round(number, place_of(count_ref[...], local, number)[1], False)
+        one_round(number, place_of(counts, local, number)[1], False)
         return carried
 
-    one_round(0, found_ref[...], True)
-    lax.fori_loop(1, rounds_of(count_ref[...]), more, 0)
-
-
-def picked_products(base, picks, located, grads, table, rows=256, unroll=32):
-    amount, width = grads.shape
-    total = table.shape[1]
+    counts = count_in(located).astype(F32)
+    one_round(0, found_in(located), True)
+    lax.fori_loop(1, rounds_of(counts), more, 0)
+
+
+def picked_products(where, picks, located, grads, table, shards, before=None, unroll=64):
+    width, total = table.shape
+    count, block, place, length = token_places(picks, shards, before)
+    grad_map = block.index_map
     return pl.pallas_call(
         functools.partial(picked_body, unroll=unroll),
-        grid=(amount // rows,),
-        in_specs=[
-            pl.BlockSpec(memory_space=pltpu.SMEM),
-            pl.BlockSpec((rows, PICKS), lambda i: (i, 0)),
-            pl.BlockSpec((rows, PICKS), lambda i: (i, 0)),
-            pl.BlockSpec((rows, PICKS), lambda i: (i, 0)),
-            pl.BlockSpec((rows, width), lambda i: (i, 0)),
-            pl.BlockSpec((width, total), lambda i: (0, 0)),
-        ],
-        out_specs=pl.BlockSpec((rows, PICKS), lambda i: (i, 0)),
-        out_shape=jax.ShapeDtypeStruct((amount, PICKS), BF16),
-        scratch_shapes=[
-            pltpu.VMEM((rows, LANES), F32),
-            pltpu.VMEM((rows, LANES), F32),
-            pltpu.VMEM((rows, LANES), F32),
-            pltpu.VMEM((total // NKEYS, rows, NKEYS), F32),
-        ],
+        grid_spec=pltpu.PrefetchScalarGridSpec(
+            num_scalar_prefetch=1,
+            grid=(count,),
+            in_specs=[block] * 2
+            + [
+                pl.BlockSpec((ROWS, width), grad_map),
+                pl.BlockSpec((width, total), lambda i, where: (0, 0)),
+            ]
+            + [pl.BlockSpec(memory_space=pl.ANY)] * (0 if before is None else 1),
+            out_specs=pl.BlockSpec((ROWS, PICKS), place),
+            scratch_shapes=[pltpu.VMEM((ROWS, LANES), F32)] * 3
+            + [pltpu.VMEM((total // NKEYS, ROWS, NKEYS), F32)],
+        ),
+        out_shape=jax.ShapeDtypeStruct((length * shards, PICKS), BF16),
+        input_output_aliases={} if before is None else {5: 0},
         compiler_params=params(56),
         cost_estimate=pl.CostEstimate(
-            flops=7 * amount * total * width, bytes_accessed=amount * width * 4, transcendentals=0
+            flops=7 * count * ROWS * total * width,
+            bytes_accessed=count * ROWS * width * 4,
+            transcendentals=0,
         ),
         name="picked_products",
-    )(base, picks, located[0], located[2], grads, table)
+    )(where, picks, located, grads, table, *(() if before is None else (before,)))
 
 
 def gather_lanes(block, index):
@@ -483,92 +508,112 @@
     return jnp.concatenate(parts, axis=1), row
 
 
-def pack_body(qkv_ref, out_ref, mixer_ref, gate_ref, query_ref, keys_ref, gain_ref, packed_ref):
+def pack_body(
+    qkv_ref, out_ref, mixer_ref, gate_ref, query_ref, keys_ref, gain_ref, packed_ref, scores_ref
+):
     row = 0
     for j in range(3):
         row = store_lanes(packed_ref, (), row, qkv_ref[j])
     row = store_lanes(packed_ref, (), row, out_ref[...].T)
     row = store_lanes(packed_ref, (), row, mixer_ref[...].T)
     row = store_lanes(packed_ref, (), row, gate_ref[...])
+    store_lanes(packed_ref, (), row, gain_ref[...])
+    row = 0
     for unit in range(query_ref.shape[0]):
-        row = store_lanes(packed_ref, (), row, query_ref[unit])
+        row = store_lanes(scores_ref, (), row, query_ref[unit])
     for unit in range(keys_ref.shape[0]):
-        row = store_lanes(packed_ref, (), row, keys_ref[unit])
-    store_lanes(packed_ref, (), row, gain_ref[...])
-
-
-def pack_weights(blocks):
-    amount = sum(block.size for block in blocks) // LANES
+        row = store_lanes(scores_ref, (), row, keys_ref[unit])
+
+
+def pack_weights(blocks, query, keys, gains):
+    first = sum(block.size for block in [*blocks, gains]) // LANES
+    second = (query.size + keys.size) // LANES
     return pl.pallas_call(
         pack_body,
-        out_shape=jax.ShapeDtypeStruct((amount, LANES), BF16),
+        out_shape=[
+            jax.ShapeDtypeStruct((first, LANES), BF16),
+            jax.ShapeDtypeStruct((second, LANES), BF16),
+        ],
         compiler_params=params(32),
         name="pack_weights",
-    )(*blocks)
-
-
-def unpack_body(
-    packed_ref, q_ref, k_ref, v_ref, out_ref, mixer_ref, gate_ref, query_ref, keys_ref, gain_ref
-):
+    )(*blocks, query, keys, gains)
+
+
+def unpack_body(packed_ref, q_ref, k_ref, v_ref, out_ref, mixer_ref, gate_ref, gain_ref):
     row = 0
     for target in (q_ref, k_ref, v_ref, out_ref, mixer_ref, gate_ref):
         target[...], row = load_lanes(packed_ref, (0,), row, *target.shape)
+    gain_ref[0] = packed_ref[0, row : row + gain_ref.shape[1], :]
+
+
+def unpack_weights(packed, part, width):
+    shards, amount, _ = packed.shape
+    model = shards * part
+    return pl.pallas_call(
+        unpack_body,
+        grid=(shards,),
+        in_specs=[pl.BlockSpec((1, amount, LANES), lambda i: (i, 0, 0))],
+        out_specs=[pl.BlockSpec((part, width), lambda i: (i, 0))] * 6
+        + [pl.BlockSpec((1, GAIN_ROWS, LANES), lambda i: (i, 0, 0))],
+        out_shape=[jax.ShapeDtypeStruct((model, width), BF16)] * 6
+        + [jax.ShapeDtypeStruct((shards, GAIN_ROWS, LANES), BF16)],
+        compiler_params=params(32),
+        name="unpack_weights",
+    )(packed)
+
+
+def unpack_scores_body(me_ref, packed_ref, query_ref, keys_ref):
+    row = 0
     for unit in range(query_ref.shape[1] // NKEYS):
         span = slice(unit * NKEYS, (unit + 1) * NKEYS)
         query_ref[:, span], row = load_lanes(packed_ref, (0,), row, query_ref.shape[0], NKEYS)
     for unit in range(keys_ref.shape[0]):
         keys_ref[unit], row = load_lanes(packed_ref, (0,), row, keys_ref.shape[1], NKEYS)
-    gain_ref[0] = packed_ref[0, row : row + gain_ref.shape[1], :]
-
-
-def unpack_weights(packed, part, width, units, key_part):
+
+
+def unpack_scores(me, packed, part, units, key_part):
     shards, amount, _ = packed.shape
-    model = shards * part
-
-    def rows_of(columns):
-        return pl.BlockSpec((part, columns), lambda i: (i, 0))
-
-    return pl.pallas_call(
-        unpack_body,
-        grid=(shards,),
-        in_specs=[pl.BlockSpec((1, amount, LANES), lambda i: (i, 0, 0))],
-        out_specs=[rows_of(width)] * 6
-        + [
-            rows_of(units * NKEYS),
-            pl.BlockSpec((units, key_part, NKEYS), lambda i: (0, i, 0)),
-            pl.BlockSpec((1, GAIN_ROWS, LANES), lambda i: (i, 0, 0)),
-        ],
-        out_shape=[jax.ShapeDtypeStruct((model, width), BF16)] * 6
-        + [
-            jax.ShapeDtypeStruct((model, units * NKEYS), BF16),
+    return pl.pallas_call(
+        unpack_scores_body,
+        grid_spec=pltpu.PrefetchScalarGridSpec(
+            num_scalar_prefetch=1,
+            grid=(shards,),
+            in_specs=[pl.BlockSpec((1, amount, LANES), lambda i, me: (i ^ me[0], 0, 0))],
+            out_specs=[
+                pl.BlockSpec((part, units * NKEYS), lambda i, me: (i, 0)),
+                pl.BlockSpec((units, key_part, NKEYS), lambda i, me: (0, i, 0)),
+            ],
+        ),
+        out_shape=[
+            jax.ShapeDtypeStruct((shards * part, units * NKEYS), BF16),
             jax.ShapeDtypeStruct((units, shards * key_part, NKEYS), BF16),
-            jax.ShapeDtypeStruct((shards, GAIN_ROWS, LANES), BF16),
         ],
         compiler_params=params(32),
-        name="unpack_weights",
-    )(packed)
-
-
-def grads_body(*refs, pairs, part, units):
+        name="unpack_scores",
+    )(me, packed)
+
+
+def grads_body(me_ref, *refs, pairs, part, units):
     lefts, rights, rest = refs[:pairs], refs[pairs : 2 * pairs], refs[2 * pairs :]
     packed_ref = rest[-1]
     per = LANES // part
     rows = [0] * per
+    places = [number ^ (me_ref[0] & (per - 1)) for number in range(per)]
     for left, right in zip(lefts, rights):
         grad = lax.dot_general(left[...], right[...], TN, preferred_element_type=F32).astype(BF16)
         for number in range(per):
             own = grad[number * part : (number + 1) * part]
-            rows[number] = store_lanes(packed_ref, (number,), rows[number], own)
+            rows[number] = store_lanes(packed_ref, (places[number],), rows[number], own)
     if units:
         key_ref = rest[0]
         key_part = key_ref.shape[1] // per
         for number in range(per):
             for unit in range(units):
                 own = key_ref[unit, number * key_part : (number + 1) * key_part, :].astype(BF16)
-                rows[number] = store_lanes(packed_ref, (number,), rows[number], own)
-
-
-def pack_grads(lefts, rights, part, key_grad=None):
+                rows[number] = store_lanes(packed_ref, (places[number],), rows[number], own)
+
+
+def pack_grads(me, lefts, rights, part, key_grad=None):
     length, model = lefts[0].shape
     shards = model // part
     per = LANES // part
@@ -579,18 +624,26 @@
         units, keys, _ = key_grad.shape
         amount += key_grad.size // shards // LANES
         extra = [key_grad]
-        extra_specs = [pl.BlockSpec((units, keys // shards * per, NKEYS), lambda i: (0, i, 0))]
+        extra_specs = [pl.BlockSpec((units, keys // shards * per, NKEYS), lambda i, me: (0, i, 0))]
     return pl.pallas_call(
         functools.partial(grads_body, pairs=len(lefts), part=part, units=units),
-        grid=(shards // per,),
-        in_specs=[pl.BlockSpec((length, LANES), lambda i: (0, i))] * len(lefts)
-        + [pl.BlockSpec(right.shape, lambda i: (0, 0)) for right in rights]
-        + extra_specs,
-        out_specs=pl.BlockSpec((per, amount, LANES), lambda i: (i, 0, 0)),
+        grid_spec=pltpu.PrefetchScalarGridSpec(
+            num_scalar_prefetch=1,
+            grid=(shards // per,),
+            in_specs=[pl.BlockSpec((length, LANES), lambda i, me: (0, i))] * len(lefts)
+            + [pl.BlockSpec(right.shape, lambda i, me: (0, 0)) for right in rights]
+            + extra_specs,
+            out_specs=pl.BlockSpec((per, amount, LANES), lambda i, me: (i ^ (me[0] // per), 0, 0)),
+        ),
         out_shape=jax.ShapeDtypeStruct((shards, amount, LANES), BF16),
         compiler_params=params(48),
+        cost_estimate=pl.CostEstimate(
+            flops=2 * length * model * sum(right.shape[1] for right in rights),
+            bytes_accessed=2 * length * model * len(lefts),
+            transcendentals=0,
+        ),
         name="pack_grads",
-    )(*lefts, *rights, *extra)
+    )(me, *lefts, *rights, *extra)
 
 
 def unpack_grads_body(
@@ -791,6 +844,22 @@
 
 def bits_down(size):
     return [1 << level for level in reversed(range(size.bit_length() - 1))]
+
+
+def scatter_by_swaps(blocks, axis, bits, other=None):
+    size = lax.axis_size(axis)
+    held = {offset: blocks[offset] for offset in range(size)}
+    for bit in bits:
+        if bit == bits[-1] and other is not None:
+            held, other = lax.optimization_barrier((held, other))
+        sent = jnp.stack([held[offset] for offset in sorted(held) if offset & bit])
+        kept = [offset for offset in sorted(held) if not offset & bit]
+        arrived = lax.ppermute(sent.astype(BF16), axis, [(i, i ^ bit) for i in range(size)])
+        held = {
+            offset: held[offset].astype(F32) + arrived[place].astype(F32)
+            for place, offset in enumerate(kept)
+        }
+    return held[0], other
 
 
 def gather_narrow(block):
@@ -836,23 +905,32 @@
     rows_one = gather_narrow(inputs).astype(F32)
     gains = jnp.concatenate([attn_gain, memory_gain]).reshape(-1, LANES)
     gains = jnp.pad(gains, ((0, GAIN_ROWS - gains.shape[0]), (0, 0)))
-    packed = gather_wide(
-        pack_weights(
-            [
-                jnp.transpose(qkv_weight, (1, 0, 2)),
-                out_weight,
-                memory_out,
-                gate_weight,
-                jnp.transpose(query_weight, (1, 0, 2)),
-                sub_keys,
-                gains,
-            ]
-        )
+    packed, scores_packed = pack_weights(
+        [
+            jnp.transpose(qkv_weight, (1, 0, 2)),
+            out_weight,
+            memory_out,
+            gate_weight,
+        ],
+        jnp.transpose(query_weight, (1, 0, 2)),
+        sub_keys,
+        gains,
+    )
+    packed = gather_wide(packed)
+    moving = {0: scores_packed}
+    for bit in bits_down(shards):
+        moving = swap_all(moving, "wide", bit)
+    moving = jnp.stack([moving[offset] for offset in range(shards)])
+    table_turned = memory_values.T
+    located_own = locate(base, picks, shard_rows)
+    packed, moving, table_turned, located_own = lax.optimization_barrier(
+        (packed, moving, table_turned, located_own)
     )
     (
-        query_matrix, key_matrix, value_matrix, out_turned, mixer_turned, gate_full, query_full,
-        keys_full, gains,
-    ) = unpack_weights(packed, part, width, units, key_part)
+        query_matrix, key_matrix, value_matrix, out_turned, mixer_turned, gate_full, gains
+    ) = unpack_weights(packed, part, width)
+    me_wide = lax.axis_index("wide").astype(jnp.int32).reshape(1)
+    query_full, keys_full = unpack_scores(me_wide, moving, part, units, key_part)
     qkv_full = [query_matrix, key_matrix, value_matrix]
     gains = gains.reshape(shards, -1)[:, : 2 * part].reshape(shards, 2, part).astype(F32)
     gain_one = gains[:, 0].reshape(model)
@@ -866,6 +944,7 @@
     all_picks = jnp.concatenate([pairs & 0xFFFF, (pairs >> 16) & 0xFFFF], axis=1)
     all_picks = all_picks.reshape(shards * length, PICKS)
     located = locate(base, all_picks, shard_rows)
+    where = jnp.concatenate([base, me_wide])
 
     factor_one, normed = norm_rows(rows_one, gain_one)
     normed = normed.astype(BF16)
@@ -891,7 +970,10 @@
     pick_weights, memory_grad = lax.optimization_barrier((pick_weights, memory_grad))
     all_weights = gather_wide(pick_weights).reshape(shards * length, PICKS)
 
-    pick_part = picked_products(base, all_picks, located, all_grads, memory_values.T)
+    pick_part = picked_products(where, picks, located_own, memory_grad, table_turned, shards)
+    pick_part = picked_products(
+        where, all_picks, located, all_grads, table_turned, shards, pick_part
+    )
     all_weights, pick_part = lax.optimization_barrier((all_weights, pick_part))
     pick_own = sum_wide(pick_part.reshape(shards, length, PICKS)).astype(F32)
     memory_part, tables = bag_sums(base, all_picks, located, all_weights, memory_values)
@@ -912,12 +994,12 @@
         product_grad * memory * sigmoid * (1.0 + gate_value * (1.0 - sigmoid))
     ).astype(BF16)
     early_pack = pack_grads(
+        column_ref * 0,
         [upstream, second, second],
         [product, gate_rows_grad, memory_query_grad],
         part,
         key_grad,
     )
-    early_pack, gate_rows_grad = lax.optimization_barrier((early_pack, gate_rows_grad))
     early_sums = sum_wide(early_pack)
     second_part = lax.dot_general(gate_rows_grad, gate_full, NT, preferred_element_type=F32)
     second_part = second_part + lax.dot_general(
@@ -940,7 +1022,9 @@
         + factor_two * own_columns(gain_two) * own_second_grad
         - own_hidden * (factor_two * factor_two * factor_two) * inner_two
     )
-    branch_grad = gather_narrow(own_hidden_grad.astype(BF16))
+    branch_grad = own_hidden_grad.astype(BF16)
+    branch_grad, early_pack = lax.optimization_barrier((branch_grad, early_pack))
+    branch_grad = gather_narrow(branch_grad)
 
     mixer_part = lax.dot_general(product, mixer_turned, NT, preferred_element_type=F32)
     mixer_part, branch_grad = lax.optimization_barrier((mixer_part, branch_grad))
@@ -955,10 +1039,13 @@
         for j in range(3)
     )
     late_pack = pack_grads(
-        [normed, normed, normed, branch_grad], [*mixed_grad, head_rows], part
-    )
-    late_pack, early_sums = lax.optimization_barrier((late_pack, early_sums))
-    late_sums = sum_wide(late_pack)
+        me_wide, [normed, normed, normed, branch_grad], [*mixed_grad, head_rows], part
+    )
+    bits = bits_down(shards)
+    cut = late_pack.shape[1] * 5 // 8 // 16 * 16
+    upper_sums, early_sums = scatter_by_swaps(late_pack[:, :cut], "wide", bits[::-1], early_sums)
+    lower_sums, _ = scatter_by_swaps(late_pack[:, cut:], "wide", bits)
+    late_sums = jnp.concatenate([upper_sums, lower_sums], axis=0)
     inner_part = jnp.sum(normed_part * gain_one * rows_one, axis=-1)
     gain_one_part = jnp.sum(normed_part * rows_one * factor_one, axis=0)
     tiny = sum_by_swaps(jnp.concatenate([inner_part, gain_one_part]), "narrow")

time: 655 us -> 608 us (0.928)
  waiting for transfers between devices: 177 us -> 155 us
  local copies, waits for them, and re-layouts: 43.5 us -> 33.5 us
  matrix products: 80.6 us -> 71.6 us
    all_gather x4, waiting for transfers between devices: 57.4 us -> 32.6 us  [gather_wide(): return lax.all_gather(block, 'wide')]
    ppermute x0 -> x6, waiting for transfers between devices: none -> 24.4 us  [scatter_by_swaps(): lax.ppermute(sent.astype(BF16), axis, [(i, i ^ bit) for i in range(size)])]
    reduce_scatter x4 -> x3, waiting for transfers between devices: 16.3 us -> 2.89 us  [sum_wide(): return lax.psum_scatter(block, 'wide', scatter_dimension=0)]
    all_gather x4, starting transfers between devices: 9.73 us -> 0.55 us  [gather_wide(): return lax.all_gather(block, 'wide')]
    ppermute x9, waiting for transfers between devices: 18 us -> 9.09 us  [swap_narrow(): return lax.ppermute(block, 'narrow', [(i, i ^ bit) for i in range(size)])]
    unnamed x178 -> x169, local copies, waits for them, and re-layouts: 37.6 us -> 28.8 us
    ppermute x15 -> x22, starting transfers between devices: 8.15 us -> 16.7 us  [swap_all(): lax.ppermute(part, axis, pairs)]
    pallas_call x1, Pallas kernels: 87.5 us -> 80.2 us  [bag_sums(): pl.pallas_call(functools.partial(bag_body, chunk=chunk, unroll=unroll), g...]
  transfers between devices with their start and end apart: 43 -> 55, of which waited for: 19 -> 26; matrix products, arithmetic and copies ran while one was open for 19% -> 17% of each run, Pallas kernels for 39% -> 43%
where the time goes in v6:
time: 608 us; the launch traced here: 603 us
  Pallas kernels  259 us (43%)
  waiting for transfers between devices  155 us (25%)
  matrix products  71.6 us (12%)
  starting transfers between devices  36.9 us (6%)
  local copies, waits for them, and re-layouts  33.5 us (6%)
  other arithmetic  30.5 us (5%)
  between operations  15.7 us (3%)
    pallas_call x2, Pallas kernels, picked_products(): pl.pallas_call(functools.partial(picked_body, unroll=unroll), grid_spec=p...  86.8 us
    pallas_call x1, Pallas kernels, bag_sums(): pl.pallas_call(functools.partial(bag_body, chunk=chunk, unroll=unroll), g...  80.2 us
    dot_general x1, matrix products, per_device(): lax.dot_general(tables, all_grads, TN, preferred_element_type=F32)  53.8 us
    ppermute x22, waiting for transfers between devices, swap_all(): lax.ppermute(part, axis, pairs)  43.4 us
    ppermute x11, waiting for transfers between devices, sum_by_swaps(): lax.ppermute(block, axis, [(i, i ^ bit) for i in range(lax.axis_size(axis...  42.8 us
    all_gather x4, waiting for transfers between devices, gather_wide(): return lax.all_gather(block, 'wide')  32.6 us
    pallas_call x2, Pallas kernels, locate(): pl.pallas_call(functools.partial(locate_body, total=total), grid=(amount...  30.6 us
    unnamed x169, local copies, waits for them, and re-layouts  28.8 us
  transfers between devices with their start and end apart: 55, of which 26 were waited for; matrix products, arithmetic and copies ran while one was open for 17% of the time, Pallas kernels for 43%

profile of v6, /device:TPU:0, one launch (start us, length us, event | category | flops | bytes accessed | tf_op | source)
XLA Modules:
  0.0 602.8 jit_solution(9455579374580700040)
XLA Ops:
  14.0 4.1 collective-permute-start.6
  18.1 1.6 collective-permute-start.4
  19.6 1.5 collective-permute-start.3
  21.2 1.5 collective-permute-start.1
  22.7 6.5 %copy.26 = bf16[8192,256]{0,1:T(8,128)(2,1)} copy(bf16[8192,256]{1,0:T(8,128)(2,1)} %table_ref.1) | data formatting | bytes 8388608 | tf_op args[9]
  30.6 3.9 locate.2.located_ref
  37.1 5.6 collective-permute-done.5
  45.9 2.1 collective-permute-done.7
  48.6 7.7 %collective-permute-done.9 = bf16[640,128]{1,0:T(8,128)(2,1)S(1)} collective-permute-done((bf16[640,128]{1,0:T(8,128)(2,1)S(1)}, bf16[640,128]{1,0:T(8,128)(2,1)S(1)}, u32[]{:S(2)}, u32[]{:S(2)}) %collective-permute-start.9) | collective-permute-done | bytes 163872 | tf_op jit(solution)/shard_map/ppermute | solution.py:800
  56.3 2.2 collective-permute-done.19
  60.9 20.5 %all-gather.9.cloned.1.call-done = bf16[12416,128]{1,0:T(8,128)(2,1)} async-done(((bf16[1552,128]{1,0:T(8,128)(2,1)}), bf16[12416,128]{1,0:T(8,128)(2,1)}) %all-gather.9.cloned.1.call-update) | async-done | bytes 3178512 | tf_op jit(solution)/shard_map/all_gather | solution.py:872
  81.5 1.9 copy-done.10
  86.5 1.5 collective-permute-start.14
  88.0 2.0 fusion.2.refs_0_.refs_1_.refs_2_
  92.3 9.4 %attend_forward.1.refs_7_ = bf16[1024,256]{1,0:T(8,128)(2,1)S(1)} custom-call(s32[1,1024]{1,0:T(1,128)S(1)} %fusion.50.start_ref, bf16[1024,256]{1,0:T(8,128)(2,1)S(1)} %convolution_convert_fusion.4.query_ref, bf16[1024,256]{1,0:T(8,128)(2,1)S(1)} %convolution_convert_fusion.3.key_ref, bf16[1024,256]{1,0:T(8,128)(2,1)S(1)} %convolution_convert_fusion.2.value_ref), custom_call_target="tpu_custom_call" | custom-call | flops 4294967296 | bytes 2097152 | tf_op jit(solution)/shard_map/attend_forward/pallas_call | solution.py:86
  103.0 1.8 pad_maximum_fusion.7
  104.9 10.6 %collective-permute-done.11 = bf16[1024,256]{1,0:T(8,128)(2,1)S(1)} collective-permute-done((bf16[1024,256]{1,0:T(8,128)(2,1)S(1)}, bf16[1024,256]{1,0:T(8,128)(2,1)S(1)}, u32[]{:S(2)}, u32[]{:S(2)}) %collective-permute-start.11) | collective-permute-done | bytes 524320 | tf_op jit(solution)/shard_map/ppermute | solution.py:800
  119.1 2.5 multiply_reduce_fusion.2
  123.8 1.9 multiply_convert_fusion.1
  126.4 3.3 convolution_convert_fusion.query_ref
  129.7 2.3 pick_scores.1
  132.8 13.3 %collective-permute-done.16 = f32[1024,128]{1,0:T(8,128)S(1)} collective-permute-done((f32[1024,128]{1,0:T(8,128)S(1)}, f32[1024,128]{1,0:T(8,128)S(1)}, u32[]{:S(2)}, u32[]{:S(2)}) %collective-permute-start.16) | collective-permute-done | bytes 524320 | tf_op jit(solution)/shard_map/ppermute | solution.py:820
  148.2 3.6 pick_softmax.1
  151.9 13.7 %picked_products.2.rest_0_ = bf16[8192,128]{1,0:T(8,128)(2,1)} custom-call(s32[2]{0:T(128)} %pad_add_fusion.1.base_ref, s32[1024,128]{1,0:T(8,128)} %picks_ref.7, s32[1024,128]{1,0:T(8,128)} %locate.2.located_ref, bf16[1024,256]{1,0:T(8,128)(2,1)} %get-tuple-element.74.grad_ref, bf16[256,8192]{1,0:T(8,128)(2,1)} %bitcast.248), custom_call_target="tpu_custom_call" | custom-call | flops 15032385536 | bytes 1048576 | tf_op jit(solution)/shard_map/picked_products/pallas_call | solution.py:430
  165.7 1.9 broadcast_and_fusion
  167.8 26.7 %locate.3.located_ref = s32[8192,128]{1,0:T(8,128)} custom-call(s32[1]{0:T(128)} %bitcast.21.base_ref, s32[8192,128]{1,0:T(8,128)S(1)} %bitcast.235), custom_call_target="tpu_custom_call" | custom-call | flops 20971520000 | bytes 16777216 | tf_op jit(solution)/shard_map/locate/pallas_call | solution.py:225
  194.5 2.0 copy-done.6
  196.5 12.1 %all-gather.15.cloned.1.call-done.grad_ref = bf16[8192,256]{1,0:T(8,128)(2,1)} async-done(((bf16[1024,256]{1,0:T(8,128)(2,1)}), bf16[8192,256]{1,0:T(8,128)(2,1)}) %all-gather.15.cloned.1.call-update) | async-done | bytes 4194320 | tf_op jit(solution)/shard_map/all_gather | solution.py:872
  208.6 73.1 %picked_products.3 = bf16[8192,128]{1,0:T(8,128)(2,1)} custom-call(s32[2]{0:T(128)} %pad_add_fusion.1.base_ref, s32[8192,128]{1,0:T(8,128)} %bitcast.236, s32[8192,128]{1,0:T(8,128)} %locate.3.located_ref, bf16[8192,256]{1,0:T(8,128)(2,1)} %all-gather.15.cloned.1.call-done.grad_ref, bf16[256,8192]{1,0:T(8,128)(2,1)} %bitcast.249, ...), custom_call_target="tpu_custom_call", output_to_operand_aliasing={{}: (5, {})} | custom-call | flops 105226698752 | bytes 7340032 | tf_op jit(solution)/shard_map/picked_products/pallas_call | solution.py:430
  281.8 80.2 %bag_sums.1 = (bf16[8192,256]{1,0:T(8,128)(2,1)}, bf16[8192,8192]{1,0:T(8,128)(2,1)}) custom-call(s32[1]{0:T(128)} %bitcast.21.base_ref, s32[8192,128]{1,0:T(8,128)} %bitcast.237, s32[8192,128]{1,0:T(8,128)} %locate.3.located_ref, bf16[8192,128]{1,0:T(8,128)(2,1)} %all-gather.13.cloned.1.call-done.weight_ref, bf16[8192,256]{1,0:T(8,128)(2,1)} %table_ref.1), custom_call_target="tpu_custom_call" | custom-call | flops 154618822656 | bytes 134217728 | tf_op jit(solution)/shard_map/bag_sums/pallas_call | solution.py:343
  363.0 1.5 collective-permute-start.21
  364.5 10.9 %collective-permute-done.21 = f32[1024,128]{1,0:T(8,128)S(1)} collective-permute-done((f32[1024,128]{1,0:T(8,128)S(1)}, f32[1024,128]{1,0:T(8,128)S(1)}, u32[]{:S(2)}, u32[]{:S(2)}) %collective-permute-start.21) | collective-permute-done | bytes 524320 | tf_op jit(solution)/shard_map/ppermute | solution.py:820
  375.7 53.8 %fusion.65 = f32[8192,256]{1,0:T(8,128)} fusion(bf16[8192,8192]{1,0:T(8,128)(2,1)} %get-tuple-element.79, bf16[8192,256]{1,0:T(8,128)(2,1)} %all-gather.15.cloned.1.call-done.grad_ref), kind=kOutput, calls=%fused_computation.186 | convolution fusion | flops 34359738368 | bytes 146800640 | tf_op jit(solution)/shard_map/dot_general | solution.py:982
  430.7 14.7 %spread_grads.1 = (bf16[1024,512]{1,0:T(8,128)(2,1)S(1)}, f32[2,256,256]{2,1,0:T(8,128)S(1)}) custom-call(s32[1]{0:T(128)} %bitcast.45.column_ref, s32[1024,128]{1,0:T(8,128)S(1)} %copy-done.3, f32[1024,128]{1,0:T(8,128)S(1)} %get-tuple-element.81.prob_ref, f32[1024,128]{1,0:T(8,128)S(1)} %add.247.grad_ref, bf16[1024,512]{1,0:T(8,128)(2,1)S(1)} %copy-done.5, ...), custom_call_target="tpu_custom_call" | custom-call | tf_op jit(solution)/shard_map/spread_grads/pallas_call | solution.py:768
  447.2 2.9 reduce-scatter.6.cloned.1.call-done
  450.1 2.4 fusion.28
  453.7 1.7 multiply_reduce_fusion.1
  456.2 2.0 copy-done.51
  459.4 1.5 collective-permute-start.26
  461.6 2.3 fusion.38
  463.9 1.5 collective-permute-start.25
  467.7 8.5 %pack_grads.2 = bf16[8,1152,128]{2,1,0:T(8,128)(2,1)} custom-call(s32[1]{0:T(128)} %constant.118.clone.1.me_ref, bf16[1024,1024]{1,0:T(8,128)(2,1)S(1)} %copy-done.1, bf16[1024,1024]{1,0:T(8,128)(2,1)} %copy-done.49, bf16[1024,1024]{1,0:T(8,128)(2,1)} %copy-done.49, bf16[1024,256]{1,0:T(8,128)(2,1)S(1)} %get-tuple-element.169.refs_3_, ...), custom_call_target="tpu_custom_call" | custom-call | flops 2147483648 | bytes 6291456 | tf_op jit(solution)/shard_map/pack_grads/pallas_call | solution.py:628
  476.2 2.0 collective-permute-done.25
  478.2 2.5 fusion.59
  480.7 1.5 collective-permute-start.29
  482.2 11.7 %collective-permute-done.29 = bf16[1024,256]{1,0:T(8,128)(2,1)S(1)} collective-permute-done((bf16[1024,256]{1,0:T(8,128)(2,1)S(1)}, bf16[1024,256]{1,0:T(8,128)(2,1)S(1)}, u32[]{:S(2)}, u32[]{:S(2)}) %collective-permute-start.29) | collective-permute-done | bytes 524320 | tf_op jit(solution)/shard_map/ppermute | solution.py:800
  499.2 12.1 %attend_backward.1 = (bf16[1024,256]{1,0:T(8,128)(2,1)S(1)}, bf16[1024,256]{1,0:T(8,128)(2,1)S(1)}, bf16[1024,256]{1,0:T(8,128)(2,1)S(1)}) custom-call(s32[1,1024]{1,0:T(1,128)S(1)} %fusion.50.start_ref, bf16[1024,256]{1,0:T(8,128)(2,1)S(1)} %copy-done.33, bf16[1024,256]{1,0:T(8,128)(2,1)S(1)} %copy-done.31, bf16[1024,256]{1,0:T(8,128)(2,1)S(1)} %copy-done.29, ...), custom_call_target="tpu_custom_call" | custom-call | flops 268435456 | bytes 3670016 | tf_op jit(solution)/shard_map/attend_backward/pallas_call | solution.py:141
  511.3 8.4 %pack_grads.3 = bf16[8,1024,128]{2,1,0:T(8,128)(2,1)S(1)} custom-call(s32[1]{0:T(128)} %bitcast.46.me_ref, bf16[1024,1024]{1,0:T(8,128)(2,1)} %copy-done.46, bf16[1024,1024]{1,0:T(8,128)(2,1)} %copy-done.46, bf16[1024,1024]{1,0:T(8,128)(2,1)} %copy-done.46, bf16[1024,1024]{1,0:T(8,128)(2,1)} %copy-done.52, bf16[1024,256]{1,0:T(8,128)(2,1)S(1)} %get-tuple-element.88.refs_4_, ...), custom_call_target="tpu_custom_call" | custom-call | flops 2147483648 | bytes 8388608 | tf_op jit(solution)/shard_map/pack_grads/pallas_call | solution.py:628
  522.0 2.2 collective-permute-start.45
  524.3 1.5 collective-permute-start.42
  525.9 1.8 fusion.3
  527.7 1.5 collective-permute-start.37
  529.6 1.9 collective-permute-done.37
  534.0 9.8 %collective-permute-done.39 = f32[2,1024]{1,0:T(2,128)S(1)} collective-permute-done((f32[2,1024]{1,0:T(2,128)S(1)}, f32[2,1024]{1,0:T(2,128)S(1)}, u32[]{:S(2)}, u32[]{:S(2)}) %collective-permute-start.39) | collective-permute-done | bytes 8224 | tf_op jit(solution)/shard_map/ppermute | solution.py:820
  544.3 3.3 collective-permute-done.40
  549.1 2.3 collective-permute-done.41
  552.7 6.7 %collective-permute-done.46 = bf16[2,384,128]{2,1,0:T(8,128)(2,1)S(1)} collective-permute-done((bf16[2,384,128]{2,1,0:T(8,128)(2,1)S(1)}, bf16[2,384,128]{2,1,0:T(8,128)(2,1)S(1)}, u32[]{:S(2)}, u32[]{:S(2)}) %collective-permute-start.46) | collective-permute-done | bytes 196640 | tf_op jit(solution)/shard_map/ppermute | solution.py:857
  559.4 1.5 collective-permute-start.33
  562.7 2.9 collective-permute-done.47
  566.7 10.1 %collective-permute-done.43 = bf16[2,640,128]{2,1,0:T(8,128)(2,1)S(1)} collective-permute-done((bf16[2,640,128]{2,1,0:T(8,128)(2,1)S(1)}, bf16[2,640,128]{2,1,0:T(8,128)(2,1)S(1)}, u32[]{:S(2)}, u32[]{:S(2)}) %collective-permute-start.43) | collective-permute-done | bytes 327712 | tf_op jit(solution)/shard_map/ppermute | solution.py:857
  577.0 6.6 %collective-permute-done.36 = bf16[1024,256]{1,0:T(8,128)(2,1)S(1)} collective-permute-done((bf16[1024,256]{1,0:T(8,128)(2,1)S(1)}, bf16[1024,256]{1,0:T(8,128)(2,1)S(1)}, u32[]{:S(2)}, u32[]{:S(2)}) %collective-permute-start.36) | collective-permute-done | bytes 524320 | tf_op jit(solution)/shard_map/ppermute | solution.py:795
  583.6 1.5 fusion.33
  586.4 2.8 fusion.37
  589.1 4.7 collective-permute-done.44
  (329 shorter events, 63.1 us)
Async XLA Ops:
  7.2 74.3 %all-gather.9.cloned.1.call-start = ((), (), s32[]{:S(2)}) async-start(), calls=%async_computation.6 | async-start | bytes 3575808 | tf_op jit(solution)/shard_map/all_gather | solution.py:872
  13.9 151.7 %all-gather.11.cloned.1.call-start = ((), (), s32[]{:S(2)}) async-start(), calls=%async_computation.7 | async-start | bytes 2359296 | tf_op jit(solution)/shard_map/all_gather | solution.py:872
  14.0 21.9 %collective-permute-start.6 = (bf16[640,128]{1,0:T(8,128)(2,1)S(1)}, bf16[640,128]{1,0:T(8,128)(2,1)S(1)}, u32[]{:S(2)}, u32[]{:S(2)}) collective-permute-start(bf16[640,128]{1,0:T(8,128)(2,1)S(1)} %get-tuple-element.57), channel_id=1, source_target_pairs={{0,16},{4,20},{8,24},{12,28},{16,0},{20,4},{24,8},{28,12},{1,17},{... | collective-permute-start | bytes 491528 | tf_op jit(solution)/shard_map/ppermute | solution.py:800
  18.1 18.0 %collective-permute-start.4 = (bf16[640,128]{1,0:T(8,128)(2,1)S(1)}, bf16[640,128]{1,0:T(8,128)(2,1)S(1)}, u32[]{:S(2)}, u32[]{:S(2)}) collective-permute-start(bf16[640,128]{1,0:T(8,128)(2,1)S(1)} %get-tuple-element.57), channel_id=1, source_target_pairs={{0,8},{4,12},{8,0},{12,4},{16,24},{20,28},{24,16},{28,20},{1,9},{5... | collective-permute-start | bytes 491528 | tf_op jit(solution)/shard_map/ppermute | solution.py:800
  19.6 16.9 %collective-permute-start.3 = (bf16[640,128]{1,0:T(8,128)(2,1)S(1)}, bf16[640,128]{1,0:T(8,128)(2,1)S(1)}, u32[]{:S(2)}, u32[]{:S(2)}) collective-permute-start(bf16[640,128]{1,0:T(8,128)(2,1)S(1)} %get-tuple-element.57), channel_id=1, source_target_pairs={{0,4},{4,0},{8,12},{12,8},{16,20},{20,16},{24,28},{28,24},{1,5},{5... | collective-permute-start | bytes 491528 | tf_op jit(solution)/shard_map/ppermute | solution.py:800
  21.2 37.4 %collective-permute-start = (bf16[1024,256]{1,0:T(8,128)(2,1)}, bf16[1024,256]{1,0:T(8,128)(2,1)S(1)}, u32[]{:S(2)}, u32[]{:S(2)}) collective-permute-start(bf16[1024,256]{1,0:T(8,128)(2,1)} %param.13), channel_id=1, source_target_pairs={{0,1},{1,0},{2,3},{3,2},{4,5},{5,4},{6,7},{7,6},{8,9},{9,8},{10,11... | collective-permute-start | bytes 1572872 | tf_op jit(solution)/shard_map/ppermute | solution.py:800
  21.2 27.4 %collective-permute-start.1 = (bf16[1024,256]{1,0:T(8,128)(2,1)}, bf16[1024,256]{1,0:T(8,128)(2,1)S(1)}, u32[]{:S(2)}, u32[]{:S(2)}) collective-permute-start(bf16[1024,256]{1,0:T(8,128)(2,1)} %param.13), channel_id=1, source_target_pairs={{0,2},{1,3},{2,0},{3,1},{4,6},{5,7},{6,4},{7,5},{8,10},{9,11},{10,... | collective-permute-start | bytes 1572872 | tf_op jit(solution)/shard_map/ppermute | solution.py:800
  30.6 28.0 %copy-start.65 = (bf16[1024,256]{1,0:T(8,128)(2,1)S(1)}, bf16[1024,256]{1,0:T(8,128)(2,1)}, u32[]{:S(2)}) copy-start(bf16[1024,256]{1,0:T(8,128)(2,1)} %param.13) | copy-start | bytes 1572868
  35.8 67.1 %collective-permute-start.18 = (bf16[1024,256]{1,0:T(8,128)(2,1)}, bf16[1024,256]{1,0:T(8,128)(2,1)}, u32[]{:S(2)}, u32[]{:S(2)}) collective-permute-start(bf16[1024,256]{1,0:T(8,128)(2,1)} %param.25), channel_id=1, source_target_pairs={{0,1},{1,0},{2,3},{3,2},{4,5},{5,4},{6,7},{7,6},{8,9},{9,8},{10,11... | collective-permute-start | bytes 1572872 | tf_op jit(solution)/shard_map/ppermute | solution.py:800
  36.1 8.4 %collective-permute-start.8 = (bf16[640,128]{1,0:T(8,128)(2,1)S(1)}, bf16[640,128]{1,0:T(8,128)(2,1)S(1)}, u32[]{:S(2)}, u32[]{:S(2)}) collective-permute-start(bf16[640,128]{1,0:T(8,128)(2,1)S(1)} %collective-permute-done.6), channel_id=1, source_target_pairs={{0,8},{4,12},{8,0},{12,4},{16,24},{20,28},{24,16},{28,20},{1,9},{5... | collective-permute-start | bytes 491528 | tf_op jit(solution)/shard_map/ppermute | solution.py:800
  36.6 6.1 %collective-permute-start.5 = (bf16[640,128]{1,0:T(8,128)(2,1)S(1)}, bf16[640,128]{1,0:T(8,128)(2,1)S(1)}, u32[]{:S(2)}, u32[]{:S(2)}) collective-permute-start(bf16[640,128]{1,0:T(8,128)(2,1)S(1)} %collective-permute-done.4), channel_id=1, source_target_pairs={{0,4},{4,0},{8,12},{12,8},{16,20},{20,16},{24,28},{28,24},{1,5},{5... | collective-permute-start | bytes 491528 | tf_op jit(solution)/shard_map/ppermute | solution.py:800
  42.7 5.3 collective-permute-start.7
  44.5 14.1 %collective-permute-start.19 = (bf16[1024,256]{1,0:T(8,128)(2,1)}, bf16[1024,256]{1,0:T(8,128)(2,1)}, u32[]{:S(2)}, u32[]{:S(2)}) collective-permute-start(bf16[1024,256]{1,0:T(8,128)(2,1)} %param.25), channel_id=1, source_target_pairs={{0,2},{1,3},{2,0},{3,1},{4,6},{5,7},{6,4},{7,5},{8,10},{9,11},{10,... | collective-permute-start | bytes 1572872 | tf_op jit(solution)/shard_map/ppermute | solution.py:800
  48.0 8.3 %collective-permute-start.9 = (bf16[640,128]{1,0:T(8,128)(2,1)S(1)}, bf16[640,128]{1,0:T(8,128)(2,1)S(1)}, u32[]{:S(2)}, u32[]{:S(2)}) collective-permute-start(bf16[640,128]{1,0:T(8,128)(2,1)S(1)} %collective-permute-done.8), channel_id=1, source_target_pairs={{0,4},{4,0},{8,12},{12,8},{16,20},{20,16},{24,28},{28,24},{1,5},{5... | collective-permute-start | bytes 491528 | tf_op jit(solution)/shard_map/ppermute | solution.py:800
  48.5 10.0 %collective-permute-start.2 = (bf16[1024,256]{1,0:T(8,128)(2,1)S(1)}, bf16[1024,256]{1,0:T(8,128)(2,1)S(1)}, u32[]{:S(2)}, u32[]{:S(2)}) collective-permute-start(bf16[1024,256]{1,0:T(8,128)(2,1)S(1)} %collective-permute-done.1), channel_id=1, source_target_pairs={{0,1},{1,0},{2,3},{3,2},{4,5},{5,4},{6,7},{7,6},{8,9},{9,8},{10,11... | collective-permute-start | bytes 1572872 | tf_op jit(solution)/shard_map/ppermute | solution.py:800
  58.5 44.4 %collective-permute-start.20 = (bf16[1024,256]{1,0:T(8,128)(2,1)}, bf16[1024,256]{1,0:T(8,128)(2,1)}, u32[]{:S(2)}, u32[]{:S(2)}) collective-permute-start(bf16[1024,256]{1,0:T(8,128)(2,1)} %collective-permute-done.19), channel_id=1, source_target_pairs={{0,1},{1,0},{2,3},{3,2},{4,5},{5,4},{6,7},{7,6},{8,9},{9,8},{10,11... | collective-permute-start | bytes 1572872 | tf_op jit(solution)/shard_map/ppermute | solution.py:800
  60.9 29.8 %copy-start.72 = (f32[1024]{0:T(1024)}, f32[1024]{0:T(1024)S(1)}, u32[]{:S(2)}) copy-start(f32[1024]{0:T(1024)S(1)} %get-tuple-element.177) | copy-start | bytes 12292
  86.2 37.6 %copy-start.21 = (bf16[1024,256]{1,0:T(8,128)(2,1)}, bf16[1024,256]{1,0:T(8,128)(2,1)S(1)}, u32[]{:S(2)}) copy-start(bf16[1024,256]{1,0:T(8,128)(2,1)S(1)} %get-tuple-element.70) | copy-start | bytes 1572868
  86.2 122.3 %all-gather.15.cloned.1.call-start = ((), (), s32[]{:S(2)}) async-start(), calls=%async_computation.9 | async-start | bytes 4718592 | tf_op jit(solution)/shard_map/all_gather | solution.py:872
  86.5 35.8 %copy-start.70 = (f32[1024]{0:T(1024)}, f32[1024]{0:T(1024)S(1)}, u32[]{:S(2)}) copy-start(f32[1024]{0:T(1024)S(1)} %get-tuple-element.174) | copy-start | bytes 12292
  86.5 15.9 %collective-permute-start.14 = (bf16[1024,256]{1,0:T(8,128)(2,1)}, bf16[1024,256]{1,0:T(8,128)(2,1)S(1)}, u32[]{:S(2)}, u32[]{:S(2)}) collective-permute-start(bf16[1024,256]{1,0:T(8,128)(2,1)} %copy-done.34), channel_id=1, source_target_pairs={{0,2},{1,3},{2,0},{3,1},{4,6},{5,7},{6,4},{7,5},{8,10},{9,11},{10,... | collective-permute-start | bytes 1572872 | tf_op jit(solution)/shard_map/ppermute | solution.py:800
  101.8 13.7 %collective-permute-start.11 = (bf16[1024,256]{1,0:T(8,128)(2,1)S(1)}, bf16[1024,256]{1,0:T(8,128)(2,1)S(1)}, u32[]{:S(2)}, u32[]{:S(2)}) collective-permute-start(bf16[1024,256]{1,0:T(8,128)(2,1)S(1)} %attend_forward.1.refs_7_), channel_id=1, source_target_pairs={{0,2},{1,3},{2,0},{3,1},{4,6},{5,7},{6,4},{7,5},{8,10},{9,11},{10,... | collective-permute-start | bytes 1572872 | tf_op jit(solution)/shard_map/ppermute | solution.py:800
  102.4 13.4 %collective-permute-start.13 = (bf16[1024,256]{1,0:T(8,128)(2,1)S(1)}, bf16[1024,256]{1,0:T(8,128)(2,1)S(1)}, u32[]{:S(2)}, u32[]{:S(2)}) collective-permute-start(bf16[1024,256]{1,0:T(8,128)(2,1)S(1)} %copy-done.35), channel_id=1, source_target_pairs={{0,1},{1,0},{2,3},{3,2},{4,5},{5,4},{6,7},{7,6},{8,9},{9,8},{10,11... | collective-permute-start | bytes 1572872 | tf_op jit(solution)/shard_map/ppermute | solution.py:800
  102.4 13.4 %collective-permute-start.15 = (bf16[1024,256]{1,0:T(8,128)(2,1)S(1)}, bf16[1024,256]{1,0:T(8,128)(2,1)S(1)}, u32[]{:S(2)}, u32[]{:S(2)}) collective-permute-start(bf16[1024,256]{1,0:T(8,128)(2,1)S(1)} %collective-permute-done.14), channel_id=1, source_target_pairs={{0,1},{1,0},{2,3},{3,2},{4,5},{5,4},{6,7},{7,6},{8,9},{9,8},{10,11... | collective-permute-start | bytes 1572872 | tf_op jit(solution)/shard_map/ppermute | solution.py:800
  104.7 11.4 %collective-permute-start.10 = (bf16[1024,256]{1,0:T(8,128)(2,1)S(1)}, bf16[1024,256]{1,0:T(8,128)(2,1)S(1)}, u32[]{:S(2)}, u32[]{:S(2)}) collective-permute-start(bf16[1024,256]{1,0:T(8,128)(2,1)S(1)} %attend_forward.1.refs_7_), channel_id=1, source_target_pairs={{0,1},{1,0},{2,3},{3,2},{4,5},{5,4},{6,7},{7,6},{8,9},{9,8},{10,11... | collective-permute-start | bytes 1572872 | tf_op jit(solution)/shard_map/ppermute | solution.py:800
  115.4 1.9 collective-permute-start.12
  125.8 155.9 %all-gather.13.cloned.1.call-start = ((), (), s32[]{:S(2)}) async-start(), calls=%async_computation.8 | async-start | bytes 2359296 | tf_op jit(solution)/shard_map/all_gather | solution.py:872
  132.1 14.0 %collective-permute-start.16 = (f32[1024,128]{1,0:T(8,128)S(1)}, f32[1024,128]{1,0:T(8,128)S(1)}, u32[]{:S(2)}, u32[]{:S(2)}) collective-permute-start(f32[1024,128]{1,0:T(8,128)S(1)} %pick_scores.1), channel_id=1, source_target_pairs={{0,2},{1,3},{2,0},{3,1},{4,6},{5,7},{6,4},{7,5},{8,10},{9,11},{10,... | collective-permute-start | bytes 1572872 | tf_op jit(solution)/shard_map/ppermute | solution.py:820
  146.2 2.0 collective-permute-start.17
  151.9 210.1 %reduce-scatter.4.cloned.1.call-start = ((), (), s32[]{:S(2)}) async-start(), calls=%async_computation.3 | async-start | bytes 2359296 | tf_op jit(solution)/shard_map/reduce_scatter | solution.py:876
  281.7 168.4 %reduce-scatter.6.cloned.1.call-start = ((), (), s32[]{:S(2)}) async-start(), calls=%async_computation.4 | async-start | bytes 4718592 | tf_op jit(solution)/shard_map/reduce_scatter | solution.py:876
  363.0 12.5 %collective-permute-start.21 = (f32[1024,128]{1,0:T(8,128)S(1)}, f32[1024,128]{1,0:T(8,128)S(1)}, u32[]{:S(2)}, u32[]{:S(2)}) collective-permute-start(f32[1024,128]{1,0:T(8,128)S(1)} %bitcast_convert_fusion), channel_id=1, source_target_pairs={{0,2},{1,3},{2,0},{3,1},{4,6},{5,7},{6,4},{7,5},{8,10},{9,11},{10,... | collective-permute-start | bytes 1572872 | tf_op jit(solution)/shard_map/ppermute | solution.py:820
  364.5 220.6 %reduce-scatter.8.cloned.1.call-start = ((), (), s32[]{:S(2)}) async-start(), calls=%async_computation.5 | async-start | bytes 2654208 | tf_op jit(solution)/shard_map/reduce_scatter | solution.py:876
  375.6 53.9 %collective-permute-start.22 = (f32[1024,128]{1,0:T(8,128)S(1)}, f32[1024,128]{1,0:T(8,128)}, u32[]{:S(2)}, u32[]{:S(2)}) collective-permute-start(f32[1024,128]{1,0:T(8,128)S(1)} %add.246), channel_id=1, source_target_pairs={{0,1},{1,0},{2,3},{3,2},{4,5},{5,4},{6,7},{7,6},{8,9},{9,8},{10,11... | collective-permute-start | bytes 1572872 | tf_op jit(solution)/shard_map/ppermute | solution.py:820
  375.6 55.0 %copy-start.3 = (s32[1024,128]{1,0:T(8,128)S(1)}, s32[1024,128]{1,0:T(8,128)}, u32[]{:S(2)}) copy-start(s32[1024,128]{1,0:T(8,128)} %picks_ref.7) | copy-start | bytes 1572868
  375.6 55.0 %copy-start.5 = (bf16[1024,512]{1,0:T(8,128)(2,1)S(1)}, bf16[1024,512]{1,0:T(8,128)(2,1)}, u32[]{:S(2)}) copy-start(bf16[1024,512]{1,0:T(8,128)(2,1)} %copy-done.4) | copy-start | bytes 3145732
  375.7 55.0 %copy-start.16 = (bf16[2,256,256]{2,1,0:T(8,128)(2,1)S(1)}, bf16[2,256,256]{2,1,0:T(8,128)(2,1)}, u32[]{:S(2)}) copy-start(bf16[2,256,256]{2,1,0:T(8,128)(2,1)} %copy-done.15) | copy-start | bytes 786436
  459.3 2.3 collective-permute-start.24
  459.4 6.0 collective-permute-start.26
  460.9 15.3 %collective-permute-start.23 = (bf16[1024,256]{1,0:T(8,128)(2,1)}, bf16[1024,256]{1,0:T(8,128)(2,1)}, u32[]{:S(2)}, u32[]{:S(2)}) collective-permute-start(bf16[1024,256]{1,0:T(8,128)(2,1)} %get-tuple-element.132), channel_id=1, source_target_pairs={{0,1},{1,0},{2,3},{3,2},{4,5},{5,4},{6,7},{7,6},{8,9},{9,8},{10,11... | collective-permute-start | bytes 1572872 | tf_op jit(solution)/shard_map/ppermute | solution.py:795
  463.9 14.3 %collective-permute-start.25 = (bf16[1024,256]{1,0:T(8,128)(2,1)}, bf16[1024,256]{1,0:T(8,128)(2,1)}, u32[]{:S(2)}, u32[]{:S(2)}) collective-permute-start(bf16[1024,256]{1,0:T(8,128)(2,1)} %fusion.38), channel_id=1, source_target_pairs={{0,2},{1,3},{2,0},{3,1},{4,6},{5,7},{6,4},{7,5},{8,10},{9,11},{10,... | collective-permute-start | bytes 1572872 | tf_op jit(solution)/shard_map/ppermute | solution.py:795
  465.4 10.8 %collective-permute-start.27 = (f32[2048]{0:T(1024)S(1)}, f32[2048]{0:T(1024)S(1)}, u32[]{:S(2)}, u32[]{:S(2)}) collective-permute-start(f32[2048]{0:T(1024)S(1)} %fusion.57), channel_id=1, source_target_pairs={{0,1},{1,0},{2,3},{3,2},{4,5},{5,4},{6,7},{7,6},{8,9},{9,8},{10,11... | collective-permute-start | bytes 24584 | tf_op jit(solution)/shard_map/ppermute | solution.py:820
  480.7 13.2 %collective-permute-start.29 = (bf16[1024,256]{1,0:T(8,128)(2,1)S(1)}, bf16[1024,256]{1,0:T(8,128)(2,1)S(1)}, u32[]{:S(2)}, u32[]{:S(2)}) collective-permute-start(bf16[1024,256]{1,0:T(8,128)(2,1)S(1)} %get-tuple-element.85), channel_id=1, source_target_pairs={{0,2},{1,3},{2,0},{3,1},{4,6},{5,7},{6,4},{7,5},{8,10},{9,11},{10,... | collective-permute-start | bytes 1572872 | tf_op jit(solution)/shard_map/ppermute | solution.py:800
  482.2 12.5 %collective-permute-start.28 = (bf16[1024,256]{1,0:T(8,128)(2,1)S(1)}, bf16[1024,256]{1,0:T(8,128)(2,1)}, u32[]{:S(2)}, u32[]{:S(2)}) collective-permute-start(bf16[1024,256]{1,0:T(8,128)(2,1)S(1)} %get-tuple-element.85), channel_id=1, source_target_pairs={{0,1},{1,0},{2,3},{3,2},{4,5},{5,4},{6,7},{7,6},{8,9},{9,8},{10,11... | collective-permute-start | bytes 1572872 | tf_op jit(solution)/shard_map/ppermute | solution.py:800
  493.9 2.0 collective-permute-start.30
  522.0 29.9 %collective-permute-start.45 = (bf16[4,384,128]{2,1,0:T(8,128)(2,1)S(1)}, bf16[4,384,128]{2,1,0:T(8,128)(2,1)S(1)}, u32[]{:S(2)}, u32[]{:S(2)}) collective-permute-start(bf16[4,384,128]{2,1,0:T(8,128)(2,1)S(1)} %slice.244), channel_id=1, source_target_pairs={{0,16},{4,20},{8,24},{12,28},{16,0},{20,4},{24,8},{28,12},{1,17},{... | collective-permute-start | bytes 1179656 | tf_op jit(solution)/shard_map/ppermute | solution.py:857
  524.3 36.6 %collective-permute-start.42 = (bf16[4,640,128]{2,1,0:T(8,128)(2,1)S(1)}, bf16[4,640,128]{2,1,0:T(8,128)(2,1)S(1)}, u32[]{:S(2)}, u32[]{:S(2)}) collective-permute-start(bf16[4,640,128]{2,1,0:T(8,128)(2,1)S(1)} %pad_maximum_fusion.11), channel_id=1, source_target_pairs={{0,4},{4,0},{8,12},{12,8},{16,20},{20,16},{24,28},{28,24},{1,5},{5... | collective-permute-start | bytes 1966088 | tf_op jit(solution)/shard_map/ppermute | solution.py:857
  527.7 3.7 collective-permute-start.37
  531.5 1.4 collective-permute-start.38
  532.4 54.0 %collective-permute-start.31 = (bf16[1024,256]{1,0:T(8,128)(2,1)}, bf16[1024,256]{1,0:T(8,128)(2,1)S(1)}, u32[]{:S(2)}, u32[]{:S(2)}) collective-permute-start(bf16[1024,256]{1,0:T(8,128)(2,1)} %get-tuple-element.126), channel_id=1, source_target_pairs={{0,1},{1,0},{2,3},{3,2},{4,5},{5,4},{6,7},{7,6},{8,9},{9,8},{10,11... | collective-permute-start | bytes 1572872 | tf_op jit(solution)/shard_map/ppermute | solution.py:795
  532.9 19.6 %collective-permute-start.32 = (bf16[1024,256]{1,0:T(8,128)(2,1)S(1)}, bf16[1024,256]{1,0:T(8,128)(2,1)S(1)}, u32[]{:S(2)}, u32[]{:S(2)}) collective-permute-start(bf16[1024,256]{1,0:T(8,128)(2,1)S(1)} %get-tuple-element.127), channel_id=1, source_target_pairs={{0,1},{1,0},{2,3},{3,2},{4,5},{5,4},{6,7},{7,6},{8,9},{9,8},{10,11... | collective-permute-start | bytes 1572872 | tf_op jit(solution)/shard_map/ppermute | solution.py:795
  532.9 11.0 %collective-permute-start.39 = (f32[2,1024]{1,0:T(2,128)S(1)}, f32[2,1024]{1,0:T(2,128)S(1)}, u32[]{:S(2)}, u32[]{:S(2)}) collective-permute-start(f32[2,1024]{1,0:T(2,128)S(1)} %pad_maximum_fusion.17), channel_id=1, source_target_pairs={{0,16},{4,20},{8,24},{12,28},{16,0},{20,4},{24,8},{28,12},{1,17},{... | collective-permute-start | bytes 24584 | tf_op jit(solution)/shard_map/ppermute | solution.py:820
  543.9 3.7 collective-permute-start.40
  547.6 3.7 collective-permute-start.41
  551.4 25.6 %collective-permute-start.34 = (bf16[1024,256]{1,0:T(8,128)(2,1)S(1)}, bf16[1024,256]{1,0:T(8,128)(2,1)S(1)}, u32[]{:S(2)}, u32[]{:S(2)}) collective-permute-start(bf16[1024,256]{1,0:T(8,128)(2,1)S(1)} %get-tuple-element.120), channel_id=1, source_target_pairs={{0,1},{1,0},{2,3},{3,2},{4,5},{5,4},{6,7},{7,6},{8,9},{9,8},{10,11... | collective-permute-start | bytes 1572872 | tf_op jit(solution)/shard_map/ppermute | solution.py:795
  551.9 10.4 %collective-permute-start.35 = (bf16[1024,256]{1,0:T(8,128)(2,1)S(1)}, bf16[1024,256]{1,0:T(8,128)(2,1)S(1)}, u32[]{:S(2)}, u32[]{:S(2)}) collective-permute-start(bf16[1024,256]{1,0:T(8,128)(2,1)S(1)} %get-tuple-element.121), channel_id=1, source_target_pairs={{0,1},{1,0},{2,3},{3,2},{4,5},{5,4},{6,7},{7,6},{8,9},{9,8},{10,11... | collective-permute-start | bytes 1572872 | tf_op jit(solution)/shard_map/ppermute | solution.py:795
  552.5 31.1 %copy-start.66 = (bf16[1024,256]{1,0:T(8,128)(2,1)S(1)}, bf16[1024,256]{1,0:T(8,128)(2,1)}, u32[]{:S(2)}) copy-start(bf16[1024,256]{1,0:T(8,128)(2,1)} %param.13) | copy-start | bytes 1572868
  552.5 31.1 %copy-start.76 = (f32[1024]{0:T(1024)S(1)}, f32[1024]{0:T(1024)}, u32[]{:S(2)}) copy-start(f32[1024]{0:T(1024)} %get-tuple-element.176) | copy-start | bytes 12292
  552.5 6.9 %collective-permute-start.46 = (bf16[2,384,128]{2,1,0:T(8,128)(2,1)S(1)}, bf16[2,384,128]{2,1,0:T(8,128)(2,1)S(1)}, u32[]{:S(2)}, u32[]{:S(2)}) collective-permute-start(bf16[2,384,128]{2,1,0:T(8,128)(2,1)S(1)} %pad_maximum_fusion.14), channel_id=1, source_target_pairs={{0,8},{4,12},{8,0},{12,4},{16,24},{20,28},{24,16},{28,20},{1,9},{5... | collective-permute-start | bytes 589832 | tf_op jit(solution)/shard_map/ppermute | solution.py:857
  559.4 27.0 %collective-permute-start.33 = (bf16[1024,256]{1,0:T(8,128)(2,1)S(1)}, bf16[1024,256]{1,0:T(8,128)(2,1)}, u32[]{:S(2)}, u32[]{:S(2)}) collective-permute-start(bf16[1024,256]{1,0:T(8,128)(2,1)S(1)} %fusion.34), channel_id=1, source_target_pairs={{0,2},{1,3},{2,0},{3,1},{4,6},{5,7},{6,4},{7,5},{8,10},{9,11},{10,... | collective-permute-start | bytes 1572872 | tf_op jit(solution)/shard_map/ppermute | solution.py:795
  560.9 4.7 collective-permute-start.47
  562.2 14.6 %collective-permute-start.43 = (bf16[2,640,128]{2,1,0:T(8,128)(2,1)S(1)}, bf16[2,640,128]{2,1,0:T(8,128)(2,1)S(1)}, u32[]{:S(2)}, u32[]{:S(2)}) collective-permute-start(bf16[2,640,128]{2,1,0:T(8,128)(2,1)S(1)} %pad_maximum_fusion.13), channel_id=1, source_target_pairs={{0,8},{4,12},{8,0},{12,4},{16,24},{20,28},{24,16},{28,20},{1,9},{5... | collective-permute-start | bytes 983048 | tf_op jit(solution)/shard_map/ppermute | solution.py:857
  565.6 18.0 %collective-permute-start.36 = (bf16[1024,256]{1,0:T(8,128)(2,1)S(1)}, bf16[1024,256]{1,0:T(8,128)(2,1)S(1)}, u32[]{:S(2)}, u32[]{:S(2)}) collective-permute-start(bf16[1024,256]{1,0:T(8,128)(2,1)S(1)} %fusion.29), channel_id=1, source_target_pairs={{0,2},{1,3},{2,0},{3,1},{4,6},{5,7},{6,4},{7,5},{8,10},{9,11},{10,... | collective-permute-start | bytes 1572872 | tf_op jit(solution)/shard_map/ppermute | solution.py:795
  585.1 8.7 %collective-permute-start.44 = (bf16[1,640,128]{2,1,0:T(8,128)(2,1)S(1)}, bf16[1,640,128]{2,1,0:T(8,128)(2,1)S(1)}, u32[]{:S(2)}, u32[]{:S(2)}) collective-permute-start(bf16[1,640,128]{2,1,0:T(8,128)(2,1)S(1)} %bitcast.265), channel_id=1, source_target_pairs={{0,16},{4,20},{8,24},{12,28},{16,0},{20,4},{24,8},{28,12},{1,17},{... | collective-permute-start | bytes 491528 | tf_op jit(solution)/shard_map/ppermute | solution.py:857
  (70 other events, 324.5 us)
Sparse Core Ops, SparseCore 0:
  14.0 67.3 all-gather.8
  86.3 48.1 all-gather.10
  136.6 71.8 all-gather.14
  211.1 47.6 all-gather.12
  281.8 66.0 reduce-scatter.3
  364.6 85.3 reduce-scatter.5
  494.1 81.9 reduce-scatter.7

commit v7 on v6

--- a/solution.py
+++ b/solution.py
@@ -823,7 +823,7 @@
     return block
 
 
-def scatter_narrow(block):
+def scatter_narrow(block, after=None):
     size = lax.axis_size("narrow")
     me = lax.axis_index("narrow")
     width = block.shape[1] // size
@@ -835,6 +835,8 @@
             for offset in range(size)
             if not offset & (2 * bit - 1)
         }
+        if len(arrived) == 1 and after is not None:
+            held[0], _ = lax.optimization_barrier((held[0], after))
         held = {
             offset: held[offset].astype(F32) + value.astype(F32)
             for offset, value in arrived.items()
@@ -846,20 +848,34 @@
     return [1 << level for level in reversed(range(size.bit_length() - 1))]
 
 
-def scatter_by_swaps(blocks, axis, bits, other=None):
+def send_half(held, axis, bit):
+    pairs = [(i, i ^ bit) for i in range(lax.axis_size(axis))]
+    sent = jnp.stack([held[offset] for offset in sorted(held) if offset & bit])
+    return lax.ppermute(sent.astype(BF16), axis, pairs)
+
+
+def add_half(held, arrived, bit):
+    kept = [offset for offset in sorted(held) if not offset & bit]
+    return {
+        offset: held[offset].astype(F32) + arrived[place].astype(F32)
+        for place, offset in enumerate(kept)
+    }
+
+
+def scatter_both(blocks, cut, axis, other):
     size = lax.axis_size(axis)
-    held = {offset: blocks[offset] for offset in range(size)}
-    for bit in bits:
-        if bit == bits[-1] and other is not None:
-            held, other = lax.optimization_barrier((held, other))
-        sent = jnp.stack([held[offset] for offset in sorted(held) if offset & bit])
-        kept = [offset for offset in sorted(held) if not offset & bit]
-        arrived = lax.ppermute(sent.astype(BF16), axis, [(i, i ^ bit) for i in range(size)])
-        held = {
-            offset: held[offset].astype(F32) + arrived[place].astype(F32)
-            for place, offset in enumerate(kept)
-        }
-    return held[0], other
+    upper = {offset: blocks[offset, :cut] for offset in range(size)}
+    lower = {offset: blocks[offset, cut:] for offset in range(size)}
+    bits = bits_down(size)
+    for step, bit in enumerate(bits):
+        back = bits[len(bits) - 1 - step]
+        upper_arrived = send_half(upper, axis, back)
+        lower_arrived = send_half(lower, axis, bit)
+        upper = add_half(upper, upper_arrived, back)
+        lower = add_half(lower, lower_arrived, bit)
+        if step == 0:
+            upper, lower, other = lax.optimization_barrier((upper, lower, other))
+    return jnp.concatenate([upper[0], lower[0]], axis=0), other
 
 
 def gather_narrow(block):
@@ -1026,10 +1042,6 @@
     branch_grad, early_pack = lax.optimization_barrier((branch_grad, early_pack))
     branch_grad = gather_narrow(branch_grad)
 
-    mixer_part = lax.dot_general(product, mixer_turned, NT, preferred_element_type=F32)
-    mixer_part, branch_grad = lax.optimization_barrier((mixer_part, branch_grad))
-    outputs = (own_hidden + scatter_narrow(mixer_part)).astype(BF16)
-
     heads_grad = jnp.dot(branch_grad, out_turned, preferred_element_type=F32)
     heads_grad = heads_grad.astype(BF16)
 
@@ -1041,23 +1053,24 @@
     late_pack = pack_grads(
         me_wide, [normed, normed, normed, branch_grad], [*mixed_grad, head_rows], part
     )
-    bits = bits_down(shards)
-    cut = late_pack.shape[1] * 5 // 8 // 16 * 16
-    upper_sums, early_sums = scatter_by_swaps(late_pack[:, :cut], "wide", bits[::-1], early_sums)
-    lower_sums, _ = scatter_by_swaps(late_pack[:, cut:], "wide", bits)
-    late_sums = jnp.concatenate([upper_sums, lower_sums], axis=0)
     inner_part = jnp.sum(normed_part * gain_one * rows_one, axis=-1)
     gain_one_part = jnp.sum(normed_part * rows_one * factor_one, axis=0)
     tiny = sum_by_swaps(jnp.concatenate([inner_part, gain_one_part]), "narrow")
     inner_one = tiny[:length, None] / model
     gain_one_part = tiny[length:]
-    own_normed_grad = scatter_narrow(normed_part)
+    late_sums, gain_parts = scatter_both(
+        late_pack, late_pack.shape[1] * 5 // 8 // 16 * 16, "wide", (gain_one_part, gain_two_part)
+    )
+    gain_sums = sum_by_swaps(jnp.stack(gain_parts), "wide")
+    mixer_part = lax.dot_general(product, mixer_turned, NT, preferred_element_type=F32)
+    mixer_part, _ = lax.optimization_barrier((mixer_part, branch_grad))
+    outputs = (own_hidden + scatter_narrow(mixer_part, late_sums)).astype(BF16)
+    own_normed_grad = scatter_narrow(normed_part, late_sums)
     input_grad = (
         own_hidden_grad
         + factor_one * own_columns(gain_one) * own_normed_grad
         - inputs.astype(F32) * (factor_one * factor_one * factor_one) * inner_one
     )
-    gain_sums = sum_by_swaps(jnp.stack([gain_one_part, gain_two_part]), "wide")
     gain_sums = lax.dynamic_slice_in_dim(gain_sums, lax.axis_index("wide") * part, part, 1)
     qkv_sum, out_sum, mixer_sum, gate_sum, query_sum, key_sum = unpack_grads(
         early_sums, late_sums, part, width, units, key_part

time: 608 us -> 599 us (0.985)
  waiting for transfers between devices: 155 us -> 147 us
    ppermute x11, waiting for transfers between devices: 42.8 us -> 34.2 us  [sum_by_swaps(): lax.ppermute(block, axis, [(i, i ^ bit) for i in range(lax.axis_size(axis...]
    ppermute x9, waiting for transfers between devices: 9.09 us -> 2.4 us  [swap_narrow(): return lax.ppermute(block, 'narrow', [(i, i ^ bit) for i in range(size)])]
    ppermute x6, waiting for transfers between devices: 24.4 us -> 31 us  [send_half(): return lax.ppermute(sent.astype(BF16), axis, pairs)]
    unnamed x169 -> x167, local copies, waits for them, and re-layouts: 28.8 us -> 29.7 us
  transfers between devices with their start and end apart: 55 -> 55, of which waited for: 26 -> 25; matrix products, arithmetic and copies ran while one was open for 17% -> 17% of each run, Pallas kernels for 43% -> 43%
where the time goes in v7:
time: 599 us; the launch traced here: 594 us
  Pallas kernels  259 us (43%)
  waiting for transfers between devices  147 us (25%)
  matrix products  71.7 us (12%)
  starting transfers between devices  36.4 us (6%)
  local copies, waits for them, and re-layouts  33.6 us (6%)
  other arithmetic  30.2 us (5%)
  between operations  15.7 us (3%)
    pallas_call x2, Pallas kernels, picked_products(): pl.pallas_call(functools.partial(picked_body, unroll=unroll), grid_spec=p...  86.8 us
    pallas_call x1, Pallas kernels, bag_sums(): pl.pallas_call(functools.partial(bag_body, chunk=chunk, unroll=unroll), g...  80.2 us
    dot_general x1, matrix products, per_device(): lax.dot_general(tables, all_grads, TN, preferred_element_type=F32)  53.8 us
    ppermute x22, waiting for transfers between devices, swap_all(): lax.ppermute(part, axis, pairs)  43.4 us
    ppermute x11, waiting for transfers between devices, sum_by_swaps(): lax.ppermute(block, axis, [(i, i ^ bit) for i in range(lax.axis_size(axis...  34.2 us
    all_gather x4, waiting for transfers between devices, gather_wide(): return lax.all_gather(block, 'wide')  32.8 us
    ppermute x6, waiting for transfers between devices, send_half(): return lax.ppermute(sent.astype(BF16), axis, pairs)  31 us
    pallas_call x2, Pallas kernels, locate(): pl.pallas_call(functools.partial(locate_body, total=total), grid=(amount...  30.6 us
  transfers between devices with their start and end apart: 55, of which 25 were waited for; matrix products, arithmetic and copies ran while one was open for 17% of the time, Pallas kernels for 43%

profile of v7, /device:TPU:0, one launch (start us, length us, event | category | flops | bytes accessed | tf_op | source)
XLA Modules:
  0.0 593.5 jit_solution(14637413118973238133)
XLA Ops:
  14.0 4.1 collective-permute-start.6
  18.1 1.6 collective-permute-start.4
  19.6 1.5 collective-permute-start.3
  21.2 1.5 collective-permute-start.1
  22.7 6.5 %copy.26 = bf16[8192,256]{0,1:T(8,128)(2,1)} copy(bf16[8192,256]{1,0:T(8,128)(2,1)} %table_ref.1) | data formatting | bytes 8388608 | tf_op args[9]
  30.6 3.9 locate.2.located_ref
  37.1 5.6 collective-permute-done.5
  44.5 1.5 collective-permute-start.19
  45.9 2.0 collective-permute-done.7
  48.6 7.7 %collective-permute-done.9 = bf16[640,128]{1,0:T(8,128)(2,1)S(1)} collective-permute-done((bf16[640,128]{1,0:T(8,128)(2,1)S(1)}, bf16[640,128]{1,0:T(8,128)(2,1)S(1)}, u32[]{:S(2)}, u32[]{:S(2)}) %collective-permute-start.9) | collective-permute-done | bytes 163872 | tf_op jit(solution)/shard_map/ppermute | solution.py:800
  56.3 2.3 collective-permute-done.19
  60.9 20.5 %all-gather.9.cloned.1.call-done = bf16[12416,128]{1,0:T(8,128)(2,1)} async-done(((bf16[1552,128]{1,0:T(8,128)(2,1)}), bf16[12416,128]{1,0:T(8,128)(2,1)}) %all-gather.9.cloned.1.call-update) | async-done | bytes 3178512 | tf_op jit(solution)/shard_map/all_gather | solution.py:888
  81.4 1.9 copy-done.10
  86.5 1.5 collective-permute-start.14
  88.0 2.0 fusion.2.refs_0_.refs_1_.refs_2_
  92.3 9.4 %attend_forward.1.refs_7_ = bf16[1024,256]{1,0:T(8,128)(2,1)S(1)} custom-call(s32[1,1024]{1,0:T(1,128)S(1)} %fusion.47.start_ref, bf16[1024,256]{1,0:T(8,128)(2,1)S(1)} %convolution_convert_fusion.4.query_ref, bf16[1024,256]{1,0:T(8,128)(2,1)S(1)} %convolution_convert_fusion.3.key_ref, bf16[1024,256]{1,0:T(8,128)(2,1)S(1)} %convolution_convert_fusion.2.value_ref), custom_call_target="tpu_custom_call" | custom-call | flops 4294967296 | bytes 2097152 | tf_op jit(solution)/shard_map/attend_forward/pallas_call | solution.py:86
  103.0 1.8 pad_maximum_fusion.7
  104.9 10.5 %collective-permute-done.11 = bf16[1024,256]{1,0:T(8,128)(2,1)S(1)} collective-permute-done((bf16[1024,256]{1,0:T(8,128)(2,1)S(1)}, bf16[1024,256]{1,0:T(8,128)(2,1)S(1)}, u32[]{:S(2)}, u32[]{:S(2)}) %collective-permute-start.11) | collective-permute-done | bytes 524320 | tf_op jit(solution)/shard_map/ppermute | solution.py:800
  119.2 2.5 multiply_reduce_fusion.2
  123.8 1.9 multiply_convert_fusion.1
  126.4 3.3 convolution_convert_fusion.query_ref
  129.8 2.3 pick_scores.1
  132.8 13.3 %collective-permute-done.16 = f32[1024,128]{1,0:T(8,128)S(1)} collective-permute-done((f32[1024,128]{1,0:T(8,128)S(1)}, f32[1024,128]{1,0:T(8,128)S(1)}, u32[]{:S(2)}, u32[]{:S(2)}) %collective-permute-start.16) | collective-permute-done | bytes 524320 | tf_op jit(solution)/shard_map/ppermute | solution.py:820
  148.3 3.6 pick_softmax.1
  152.0 13.7 %picked_products.2.rest_0_ = bf16[8192,128]{1,0:T(8,128)(2,1)} custom-call(s32[2]{0:T(128)} %pad_add_fusion.1.base_ref, s32[1024,128]{1,0:T(8,128)} %picks_ref.7, s32[1024,128]{1,0:T(8,128)} %locate.2.located_ref, bf16[1024,256]{1,0:T(8,128)(2,1)} %get-tuple-element.82.grad_ref, bf16[256,8192]{1,0:T(8,128)(2,1)} %bitcast.280), custom_call_target="tpu_custom_call" | custom-call | flops 15032385536 | bytes 1048576 | tf_op jit(solution)/shard_map/picked_products/pallas_call | solution.py:430
  165.7 1.9 broadcast_and_fusion
  167.8 26.7 %locate.3.located_ref = s32[8192,128]{1,0:T(8,128)} custom-call(s32[1]{0:T(128)} %bitcast.21.base_ref, s32[8192,128]{1,0:T(8,128)S(1)} %bitcast.267), custom_call_target="tpu_custom_call" | custom-call | flops 20971520000 | bytes 16777216 | tf_op jit(solution)/shard_map/locate/pallas_call | solution.py:225
  194.5 2.0 copy-done.6
  196.5 12.3 %all-gather.15.cloned.1.call-done.grad_ref = bf16[8192,256]{1,0:T(8,128)(2,1)} async-done(((bf16[1024,256]{1,0:T(8,128)(2,1)}), bf16[8192,256]{1,0:T(8,128)(2,1)}) %all-gather.15.cloned.1.call-update) | async-done | bytes 4194320 | tf_op jit(solution)/shard_map/all_gather | solution.py:888
  208.8 73.1 %picked_products.3 = bf16[8192,128]{1,0:T(8,128)(2,1)} custom-call(s32[2]{0:T(128)} %pad_add_fusion.1.base_ref, s32[8192,128]{1,0:T(8,128)} %bitcast.268, s32[8192,128]{1,0:T(8,128)} %locate.3.located_ref, bf16[8192,256]{1,0:T(8,128)(2,1)} %all-gather.15.cloned.1.call-done.grad_ref, bf16[256,8192]{1,0:T(8,128)(2,1)} %bitcast.281, ...), custom_call_target="tpu_custom_call", output_to_operand_aliasing={{}: (5, {})} | custom-call | flops 105226698752 | bytes 7340032 | tf_op jit(solution)/shard_map/picked_products/pallas_call | solution.py:430
  282.0 80.2 %bag_sums.1 = (bf16[8192,256]{1,0:T(8,128)(2,1)}, bf16[8192,8192]{1,0:T(8,128)(2,1)}) custom-call(s32[1]{0:T(128)} %bitcast.21.base_ref, s32[8192,128]{1,0:T(8,128)} %bitcast.269, s32[8192,128]{1,0:T(8,128)} %locate.3.located_ref, bf16[8192,128]{1,0:T(8,128)(2,1)} %all-gather.13.cloned.1.call-done.weight_ref, bf16[8192,256]{1,0:T(8,128)(2,1)} %table_ref.1), custom_call_target="tpu_custom_call" | custom-call | flops 154618822656 | bytes 134217728 | tf_op jit(solution)/shard_map/bag_sums/pallas_call | solution.py:343
  363.2 1.5 collective-permute-start.21
  364.7 11.1 %collective-permute-done.21 = f32[1024,128]{1,0:T(8,128)S(1)} collective-permute-done((f32[1024,128]{1,0:T(8,128)S(1)}, f32[1024,128]{1,0:T(8,128)S(1)}, u32[]{:S(2)}, u32[]{:S(2)}) %collective-permute-start.21) | collective-permute-done | bytes 524320 | tf_op jit(solution)/shard_map/ppermute | solution.py:820
  376.0 53.8 %fusion.61 = f32[8192,256]{1,0:T(8,128)} fusion(bf16[8192,8192]{1,0:T(8,128)(2,1)} %get-tuple-element.87, bf16[8192,256]{1,0:T(8,128)(2,1)} %all-gather.15.cloned.1.call-done.grad_ref), kind=kOutput, calls=%fused_computation.196 | convolution fusion | flops 34359738368 | bytes 146800640 | tf_op jit(solution)/shard_map/dot_general | solution.py:998
  431.0 14.7 %spread_grads.1 = (bf16[1024,512]{1,0:T(8,128)(2,1)S(1)}, f32[2,256,256]{2,1,0:T(8,128)S(1)}) custom-call(s32[1]{0:T(128)} %bitcast.45.column_ref, s32[1024,128]{1,0:T(8,128)S(1)} %copy-done.3, f32[1024,128]{1,0:T(8,128)S(1)} %get-tuple-element.89.prob_ref, f32[1024,128]{1,0:T(8,128)S(1)} %add.252.grad_ref, bf16[1024,512]{1,0:T(8,128)(2,1)S(1)} %copy-done.5, ...), custom_call_target="tpu_custom_call" | custom-call | tf_op jit(solution)/shard_map/spread_grads/pallas_call | solution.py:768
  447.5 2.6 reduce-scatter.6.cloned.1.call-done
  450.1 2.4 fusion.28
  453.7 1.9 multiply_reduce_fusion.1
  456.4 2.0 copy-done.50
  459.6 1.5 collective-permute-start.26
  461.7 2.3 fusion.31
  464.0 1.5 collective-permute-start.25
  467.8 8.6 %pack_grads.2 = bf16[8,1152,128]{2,1,0:T(8,128)(2,1)} custom-call(s32[1]{0:T(128)} %constant.118.clone.1.me_ref, bf16[1024,1024]{1,0:T(8,128)(2,1)S(1)} %copy-done.1, bf16[1024,1024]{1,0:T(8,128)(2,1)} %copy-done.49, bf16[1024,1024]{1,0:T(8,128)(2,1)} %copy-done.49, bf16[1024,256]{1,0:T(8,128)(2,1)S(1)} %get-tuple-element.193.refs_3_, ...), custom_call_target="tpu_custom_call" | custom-call | flops 2147483648 | bytes 6291456 | tf_op jit(solution)/shard_map/pack_grads/pallas_call | solution.py:628
  476.4 1.9 collective-permute-done.25
  478.3 2.5 fusion.56
  480.8 1.6 collective-permute-start.29
  482.4 11.7 %collective-permute-done.29 = bf16[1024,256]{1,0:T(8,128)(2,1)S(1)} collective-permute-done((bf16[1024,256]{1,0:T(8,128)(2,1)S(1)}, bf16[1024,256]{1,0:T(8,128)(2,1)S(1)}, u32[]{:S(2)}, u32[]{:S(2)}) %collective-permute-start.29) | collective-permute-done | bytes 524320 | tf_op jit(solution)/shard_map/ppermute | solution.py:800
  496.1 1.5 pad_maximum_fusion.9
  499.3 12.1 %attend_backward.1 = (bf16[1024,256]{1,0:T(8,128)(2,1)S(1)}, bf16[1024,256]{1,0:T(8,128)(2,1)S(1)}, bf16[1024,256]{1,0:T(8,128)(2,1)S(1)}) custom-call(s32[1,1024]{1,0:T(1,128)S(1)} %fusion.47.start_ref, bf16[1024,256]{1,0:T(8,128)(2,1)S(1)} %copy-done.33, bf16[1024,256]{1,0:T(8,128)(2,1)S(1)} %copy-done.31, bf16[1024,256]{1,0:T(8,128)(2,1)S(1)} %copy-done.29, ...), custom_call_target="tpu_custom_call" | custom-call | flops 268435456 | bytes 3670016 | tf_op jit(solution)/shard_map/attend_backward/pallas_call | solution.py:141
  511.5 8.4 %pack_grads.3 = bf16[8,1024,128]{2,1,0:T(8,128)(2,1)S(1)} custom-call(s32[1]{0:T(128)} %bitcast.46.me_ref, bf16[1024,1024]{1,0:T(8,128)(2,1)} %copy-done.46, bf16[1024,1024]{1,0:T(8,128)(2,1)} %copy-done.46, bf16[1024,1024]{1,0:T(8,128)(2,1)} %copy-done.46, bf16[1024,1024]{1,0:T(8,128)(2,1)} %copy-done.51, bf16[1024,256]{1,0:T(8,128)(2,1)S(1)} %get-tuple-element.95.refs_4_, ...), custom_call_target="tpu_custom_call" | custom-call | flops 2147483648 | bytes 8388608 | tf_op jit(solution)/shard_map/pack_grads/pallas_call | solution.py:628
  521.7 2.2 collective-permute-start.33
  524.0 1.5 collective-permute-start.32
  525.5 1.7 fusion.3
  527.6 1.5 collective-permute-start.34
  532.7 10.7 %collective-permute-done.33 = bf16[4,384,128]{2,1,0:T(8,128)(2,1)S(1)} collective-permute-done((bf16[4,384,128]{2,1,0:T(8,128)(2,1)S(1)}, bf16[4,384,128]{2,1,0:T(8,128)(2,1)S(1)}, u32[]{:S(2)}, u32[]{:S(2)}) %collective-permute-start.33) | collective-permute-done | bytes 393248 | tf_op jit(solution)/shard_map/ppermute | solution.py:854
  543.8 1.5 collective-permute-start.44
  547.3 2.9 collective-permute-done.45
  550.3 2.1 collective-permute-start.38
  552.3 1.7 collective-permute-done.46
  555.3 2.5 collective-permute-done.47
  559.4 12.4 %collective-permute-done.36 = bf16[2,640,128]{2,1,0:T(8,128)(2,1)S(1)} collective-permute-done((bf16[2,640,128]{2,1,0:T(8,128)(2,1)S(1)}, bf16[2,640,128]{2,1,0:T(8,128)(2,1)S(1)}, u32[]{:S(2)}, u32[]{:S(2)}) %collective-permute-start.36) | collective-permute-done | bytes 327712 | tf_op jit(solution)/shard_map/ppermute | solution.py:854
  572.0 7.9 %collective-permute-done.37 = bf16[1,640,128]{2,1,0:T(8,128)(2,1)S(1)} collective-permute-done((bf16[1,640,128]{2,1,0:T(8,128)(2,1)S(1)}, bf16[1,640,128]{2,1,0:T(8,128)(2,1)S(1)}, u32[]{:S(2)}, u32[]{:S(2)}) %collective-permute-start.37) | collective-permute-done | bytes 163872 | tf_op jit(solution)/shard_map/ppermute | solution.py:854
  580.0 2.2 add_convert_fusion
  582.2 1.5 multiply_subtract_fusion
  (328 shorter events, 59.5 us)
Async XLA Ops:
  7.2 74.3 %all-gather.9.cloned.1.call-start = ((), (), s32[]{:S(2)}) async-start(), calls=%async_computation.6 | async-start | bytes 3575808 | tf_op jit(solution)/shard_map/all_gather | solution.py:888
  13.9 151.8 %all-gather.11.cloned.1.call-start = ((), (), s32[]{:S(2)}) async-start(), calls=%async_computation.7 | async-start | bytes 2359296 | tf_op jit(solution)/shard_map/all_gather | solution.py:888
  14.0 21.8 %collective-permute-start.6 = (bf16[640,128]{1,0:T(8,128)(2,1)S(1)}, bf16[640,128]{1,0:T(8,128)(2,1)S(1)}, u32[]{:S(2)}, u32[]{:S(2)}) collective-permute-start(bf16[640,128]{1,0:T(8,128)(2,1)S(1)} %get-tuple-element.65), channel_id=1, source_target_pairs={{0,16},{4,20},{8,24},{12,28},{16,0},{20,4},{24,8},{28,12},{1,17},{... | collective-permute-start | bytes 491528 | tf_op jit(solution)/shard_map/ppermute | solution.py:800
  18.1 18.0 %collective-permute-start.4 = (bf16[640,128]{1,0:T(8,128)(2,1)S(1)}, bf16[640,128]{1,0:T(8,128)(2,1)S(1)}, u32[]{:S(2)}, u32[]{:S(2)}) collective-permute-start(bf16[640,128]{1,0:T(8,128)(2,1)S(1)} %get-tuple-element.65), channel_id=1, source_target_pairs={{0,8},{4,12},{8,0},{12,4},{16,24},{20,28},{24,16},{28,20},{1,9},{5... | collective-permute-start | bytes 491528 | tf_op jit(solution)/shard_map/ppermute | solution.py:800
  19.6 16.9 %collective-permute-start.3 = (bf16[640,128]{1,0:T(8,128)(2,1)S(1)}, bf16[640,128]{1,0:T(8,128)(2,1)S(1)}, u32[]{:S(2)}, u32[]{:S(2)}) collective-permute-start(bf16[640,128]{1,0:T(8,128)(2,1)S(1)} %get-tuple-element.65), channel_id=1, source_target_pairs={{0,4},{4,0},{8,12},{12,8},{16,20},{20,16},{24,28},{28,24},{1,5},{5... | collective-permute-start | bytes 491528 | tf_op jit(solution)/shard_map/ppermute | solution.py:800
  21.2 37.4 %collective-permute-start = (bf16[1024,256]{1,0:T(8,128)(2,1)}, bf16[1024,256]{1,0:T(8,128)(2,1)S(1)}, u32[]{:S(2)}, u32[]{:S(2)}) collective-permute-start(bf16[1024,256]{1,0:T(8,128)(2,1)} %param.13), channel_id=1, source_target_pairs={{0,1},{1,0},{2,3},{3,2},{4,5},{5,4},{6,7},{7,6},{8,9},{9,8},{10,11... | collective-permute-start | bytes 1572872 | tf_op jit(solution)/shard_map/ppermute | solution.py:800
  21.2 27.3 %collective-permute-start.1 = (bf16[1024,256]{1,0:T(8,128)(2,1)}, bf16[1024,256]{1,0:T(8,128)(2,1)S(1)}, u32[]{:S(2)}, u32[]{:S(2)}) collective-permute-start(bf16[1024,256]{1,0:T(8,128)(2,1)} %param.13), channel_id=1, source_target_pairs={{0,2},{1,3},{2,0},{3,1},{4,6},{5,7},{6,4},{7,5},{8,10},{9,11},{10,... | collective-permute-start | bytes 1572872 | tf_op jit(solution)/shard_map/ppermute | solution.py:800
  30.5 28.0 %copy-start.64 = (bf16[1024,256]{1,0:T(8,128)(2,1)S(1)}, bf16[1024,256]{1,0:T(8,128)(2,1)}, u32[]{:S(2)}) copy-start(bf16[1024,256]{1,0:T(8,128)(2,1)} %param.13) | copy-start | bytes 1572868
  35.8 67.2 %collective-permute-start.18 = (bf16[1024,256]{1,0:T(8,128)(2,1)}, bf16[1024,256]{1,0:T(8,128)(2,1)}, u32[]{:S(2)}, u32[]{:S(2)}) collective-permute-start(bf16[1024,256]{1,0:T(8,128)(2,1)} %param.25), channel_id=1, source_target_pairs={{0,1},{1,0},{2,3},{3,2},{4,5},{5,4},{6,7},{7,6},{8,9},{9,8},{10,11... | collective-permute-start | bytes 1572872 | tf_op jit(solution)/shard_map/ppermute | solution.py:800
  36.1 8.4 %collective-permute-start.8 = (bf16[640,128]{1,0:T(8,128)(2,1)S(1)}, bf16[640,128]{1,0:T(8,128)(2,1)S(1)}, u32[]{:S(2)}, u32[]{:S(2)}) collective-permute-start(bf16[640,128]{1,0:T(8,128)(2,1)S(1)} %collective-permute-done.6), channel_id=1, source_target_pairs={{0,8},{4,12},{8,0},{12,4},{16,24},{20,28},{24,16},{28,20},{1,9},{5... | collective-permute-start | bytes 491528 | tf_op jit(solution)/shard_map/ppermute | solution.py:800
  36.6 6.1 %collective-permute-start.5 = (bf16[640,128]{1,0:T(8,128)(2,1)S(1)}, bf16[640,128]{1,0:T(8,128)(2,1)S(1)}, u32[]{:S(2)}, u32[]{:S(2)}) collective-permute-start(bf16[640,128]{1,0:T(8,128)(2,1)S(1)} %collective-permute-done.4), channel_id=1, source_target_pairs={{0,4},{4,0},{8,12},{12,8},{16,20},{20,16},{24,28},{28,24},{1,5},{5... | collective-permute-start | bytes 491528 | tf_op jit(solution)/shard_map/ppermute | solution.py:800
  42.6 5.3 collective-permute-start.7
  44.5 14.1 %collective-permute-start.19 = (bf16[1024,256]{1,0:T(8,128)(2,1)}, bf16[1024,256]{1,0:T(8,128)(2,1)}, u32[]{:S(2)}, u32[]{:S(2)}) collective-permute-start(bf16[1024,256]{1,0:T(8,128)(2,1)} %param.25), channel_id=1, source_target_pairs={{0,2},{1,3},{2,0},{3,1},{4,6},{5,7},{6,4},{7,5},{8,10},{9,11},{10,... | collective-permute-start | bytes 1572872 | tf_op jit(solution)/shard_map/ppermute | solution.py:800
  48.0 8.2 %collective-permute-start.9 = (bf16[640,128]{1,0:T(8,128)(2,1)S(1)}, bf16[640,128]{1,0:T(8,128)(2,1)S(1)}, u32[]{:S(2)}, u32[]{:S(2)}) collective-permute-start(bf16[640,128]{1,0:T(8,128)(2,1)S(1)} %collective-permute-done.8), channel_id=1, source_target_pairs={{0,4},{4,0},{8,12},{12,8},{16,20},{20,16},{24,28},{28,24},{1,5},{5... | collective-permute-start | bytes 491528 | tf_op jit(solution)/shard_map/ppermute | solution.py:800
  48.5 10.0 %collective-permute-start.2 = (bf16[1024,256]{1,0:T(8,128)(2,1)S(1)}, bf16[1024,256]{1,0:T(8,128)(2,1)S(1)}, u32[]{:S(2)}, u32[]{:S(2)}) collective-permute-start(bf16[1024,256]{1,0:T(8,128)(2,1)S(1)} %collective-permute-done.1), channel_id=1, source_target_pairs={{0,1},{1,0},{2,3},{3,2},{4,5},{5,4},{6,7},{7,6},{8,9},{9,8},{10,11... | collective-permute-start | bytes 1572872 | tf_op jit(solution)/shard_map/ppermute | solution.py:800
  58.6 44.4 %collective-permute-start.20 = (bf16[1024,256]{1,0:T(8,128)(2,1)}, bf16[1024,256]{1,0:T(8,128)(2,1)}, u32[]{:S(2)}, u32[]{:S(2)}) collective-permute-start(bf16[1024,256]{1,0:T(8,128)(2,1)} %collective-permute-done.19), channel_id=1, source_target_pairs={{0,1},{1,0},{2,3},{3,2},{4,5},{5,4},{6,7},{7,6},{8,9},{9,8},{10,11... | collective-permute-start | bytes 1572872 | tf_op jit(solution)/shard_map/ppermute | solution.py:800
  60.9 29.8 %copy-start.71 = (f32[1024]{0:T(1024)}, f32[1024]{0:T(1024)S(1)}, u32[]{:S(2)}) copy-start(f32[1024]{0:T(1024)S(1)} %get-tuple-element.201) | copy-start | bytes 12292
  86.2 37.6 %copy-start.21 = (bf16[1024,256]{1,0:T(8,128)(2,1)}, bf16[1024,256]{1,0:T(8,128)(2,1)S(1)}, u32[]{:S(2)}) copy-start(bf16[1024,256]{1,0:T(8,128)(2,1)S(1)} %get-tuple-element.78) | copy-start | bytes 1572868
  86.2 122.6 %all-gather.15.cloned.1.call-start = ((), (), s32[]{:S(2)}) async-start(), calls=%async_computation.9 | async-start | bytes 4718592 | tf_op jit(solution)/shard_map/all_gather | solution.py:888
  86.5 35.8 %copy-start.69 = (f32[1024]{0:T(1024)}, f32[1024]{0:T(1024)S(1)}, u32[]{:S(2)}) copy-start(f32[1024]{0:T(1024)S(1)} %get-tuple-element.198) | copy-start | bytes 12292
  86.5 15.9 %collective-permute-start.14 = (bf16[1024,256]{1,0:T(8,128)(2,1)}, bf16[1024,256]{1,0:T(8,128)(2,1)S(1)}, u32[]{:S(2)}, u32[]{:S(2)}) collective-permute-start(bf16[1024,256]{1,0:T(8,128)(2,1)} %copy-done.34), channel_id=1, source_target_pairs={{0,2},{1,3},{2,0},{3,1},{4,6},{5,7},{6,4},{7,5},{8,10},{9,11},{10,... | collective-permute-start | bytes 1572872 | tf_op jit(solution)/shard_map/ppermute | solution.py:800
  101.8 13.7 %collective-permute-start.11 = (bf16[1024,256]{1,0:T(8,128)(2,1)S(1)}, bf16[1024,256]{1,0:T(8,128)(2,1)S(1)}, u32[]{:S(2)}, u32[]{:S(2)}) collective-permute-start(bf16[1024,256]{1,0:T(8,128)(2,1)S(1)} %attend_forward.1.refs_7_), channel_id=1, source_target_pairs={{0,2},{1,3},{2,0},{3,1},{4,6},{5,7},{6,4},{7,5},{8,10},{9,11},{10,... | collective-permute-start | bytes 1572872 | tf_op jit(solution)/shard_map/ppermute | solution.py:800
  102.5 13.4 %collective-permute-start.13 = (bf16[1024,256]{1,0:T(8,128)(2,1)S(1)}, bf16[1024,256]{1,0:T(8,128)(2,1)S(1)}, u32[]{:S(2)}, u32[]{:S(2)}) collective-permute-start(bf16[1024,256]{1,0:T(8,128)(2,1)S(1)} %copy-done.35), channel_id=1, source_target_pairs={{0,1},{1,0},{2,3},{3,2},{4,5},{5,4},{6,7},{7,6},{8,9},{9,8},{10,11... | collective-permute-start | bytes 1572872 | tf_op jit(solution)/shard_map/ppermute | solution.py:800
  102.5 13.4 %collective-permute-start.15 = (bf16[1024,256]{1,0:T(8,128)(2,1)S(1)}, bf16[1024,256]{1,0:T(8,128)(2,1)S(1)}, u32[]{:S(2)}, u32[]{:S(2)}) collective-permute-start(bf16[1024,256]{1,0:T(8,128)(2,1)S(1)} %collective-permute-done.14), channel_id=1, source_target_pairs={{0,1},{1,0},{2,3},{3,2},{4,5},{5,4},{6,7},{7,6},{8,9},{9,8},{10,11... | collective-permute-start | bytes 1572872 | tf_op jit(solution)/shard_map/ppermute | solution.py:800
  104.8 11.4 %collective-permute-start.10 = (bf16[1024,256]{1,0:T(8,128)(2,1)S(1)}, bf16[1024,256]{1,0:T(8,128)(2,1)S(1)}, u32[]{:S(2)}, u32[]{:S(2)}) collective-permute-start(bf16[1024,256]{1,0:T(8,128)(2,1)S(1)} %attend_forward.1.refs_7_), channel_id=1, source_target_pairs={{0,1},{1,0},{2,3},{3,2},{4,5},{5,4},{6,7},{7,6},{8,9},{9,8},{10,11... | collective-permute-start | bytes 1572872 | tf_op jit(solution)/shard_map/ppermute | solution.py:800
  115.4 1.9 collective-permute-start.12
  125.8 156.2 %all-gather.13.cloned.1.call-start = ((), (), s32[]{:S(2)}) async-start(), calls=%async_computation.8 | async-start | bytes 2359296 | tf_op jit(solution)/shard_map/all_gather | solution.py:888
  132.1 14.0 %collective-permute-start.16 = (f32[1024,128]{1,0:T(8,128)S(1)}, f32[1024,128]{1,0:T(8,128)S(1)}, u32[]{:S(2)}, u32[]{:S(2)}) collective-permute-start(f32[1024,128]{1,0:T(8,128)S(1)} %pick_scores.1), channel_id=1, source_target_pairs={{0,2},{1,3},{2,0},{3,1},{4,6},{5,7},{6,4},{7,5},{8,10},{9,11},{10,... | collective-permute-start | bytes 1572872 | tf_op jit(solution)/shard_map/ppermute | solution.py:820
  146.2 2.0 collective-permute-start.17
  151.9 210.3 %reduce-scatter.4.cloned.1.call-start = ((), (), s32[]{:S(2)}) async-start(), calls=%async_computation.3 | async-start | bytes 2359296 | tf_op jit(solution)/shard_map/reduce_scatter | solution.py:892
  282.0 168.1 %reduce-scatter.6.cloned.1.call-start = ((), (), s32[]{:S(2)}) async-start(), calls=%async_computation.4 | async-start | bytes 4718592 | tf_op jit(solution)/shard_map/reduce_scatter | solution.py:892
  363.2 12.6 %collective-permute-start.21 = (f32[1024,128]{1,0:T(8,128)S(1)}, f32[1024,128]{1,0:T(8,128)S(1)}, u32[]{:S(2)}, u32[]{:S(2)}) collective-permute-start(f32[1024,128]{1,0:T(8,128)S(1)} %bitcast_convert_fusion), channel_id=1, source_target_pairs={{0,2},{1,3},{2,0},{3,1},{4,6},{5,7},{6,4},{7,5},{8,10},{9,11},{10,... | collective-permute-start | bytes 1572872 | tf_op jit(solution)/shard_map/ppermute | solution.py:820
  364.7 219.0 %reduce-scatter.8.cloned.1.call-start = ((), (), s32[]{:S(2)}) async-start(), calls=%async_computation.5 | async-start | bytes 2654208 | tf_op jit(solution)/shard_map/reduce_scatter | solution.py:892
  375.9 53.9 %collective-permute-start.22 = (f32[1024,128]{1,0:T(8,128)S(1)}, f32[1024,128]{1,0:T(8,128)}, u32[]{:S(2)}, u32[]{:S(2)}) collective-permute-start(f32[1024,128]{1,0:T(8,128)S(1)} %add.251), channel_id=1, source_target_pairs={{0,1},{1,0},{2,3},{3,2},{4,5},{5,4},{6,7},{7,6},{8,9},{9,8},{10,11... | collective-permute-start | bytes 1572872 | tf_op jit(solution)/shard_map/ppermute | solution.py:820
  375.9 55.0 %copy-start.3 = (s32[1024,128]{1,0:T(8,128)S(1)}, s32[1024,128]{1,0:T(8,128)}, u32[]{:S(2)}) copy-start(s32[1024,128]{1,0:T(8,128)} %picks_ref.7) | copy-start | bytes 1572868
  375.9 55.0 %copy-start.5 = (bf16[1024,512]{1,0:T(8,128)(2,1)S(1)}, bf16[1024,512]{1,0:T(8,128)(2,1)}, u32[]{:S(2)}) copy-start(bf16[1024,512]{1,0:T(8,128)(2,1)} %copy-done.4) | copy-start | bytes 3145732
  376.0 55.0 %copy-start.16 = (bf16[2,256,256]{2,1,0:T(8,128)(2,1)S(1)}, bf16[2,256,256]{2,1,0:T(8,128)(2,1)}, u32[]{:S(2)}) copy-start(bf16[2,256,256]{2,1,0:T(8,128)(2,1)} %copy-done.15) | copy-start | bytes 786436
  459.5 2.3 collective-permute-start.24
  459.6 6.0 %collective-permute-start.26 = (f32[2048]{0:T(1024)S(1)}, f32[2048]{0:T(1024)S(1)}, u32[]{:S(2)}, u32[]{:S(2)}) collective-permute-start(f32[2048]{0:T(1024)S(1)} %pad_maximum_fusion.15), channel_id=1, source_target_pairs={{0,2},{1,3},{2,0},{3,1},{4,6},{5,7},{6,4},{7,5},{8,10},{9,11},{10,... | collective-permute-start | bytes 24584 | tf_op jit(solution)/shard_map/ppermute | solution.py:820
  461.0 15.4 %collective-permute-start.23 = (bf16[1024,256]{1,0:T(8,128)(2,1)}, bf16[1024,256]{1,0:T(8,128)(2,1)}, u32[]{:S(2)}, u32[]{:S(2)}) collective-permute-start(bf16[1024,256]{1,0:T(8,128)(2,1)} %get-tuple-element.152), channel_id=1, source_target_pairs={{0,1},{1,0},{2,3},{3,2},{4,5},{5,4},{6,7},{7,6},{8,9},{9,8},{10,11... | collective-permute-start | bytes 1572872 | tf_op jit(solution)/shard_map/ppermute | solution.py:795
  464.0 14.3 %collective-permute-start.25 = (bf16[1024,256]{1,0:T(8,128)(2,1)}, bf16[1024,256]{1,0:T(8,128)(2,1)}, u32[]{:S(2)}, u32[]{:S(2)}) collective-permute-start(bf16[1024,256]{1,0:T(8,128)(2,1)} %fusion.31), channel_id=1, source_target_pairs={{0,2},{1,3},{2,0},{3,1},{4,6},{5,7},{6,4},{7,5},{8,10},{9,11},{10,... | collective-permute-start | bytes 1572872 | tf_op jit(solution)/shard_map/ppermute | solution.py:795
  465.5 10.9 %collective-permute-start.27 = (f32[2048]{0:T(1024)S(1)}, f32[2048]{0:T(1024)S(1)}, u32[]{:S(2)}, u32[]{:S(2)}) collective-permute-start(f32[2048]{0:T(1024)S(1)} %fusion.54), channel_id=1, source_target_pairs={{0,1},{1,0},{2,3},{3,2},{4,5},{5,4},{6,7},{7,6},{8,9},{9,8},{10,11... | collective-permute-start | bytes 24584 | tf_op jit(solution)/shard_map/ppermute | solution.py:820
  480.8 13.2 %collective-permute-start.29 = (bf16[1024,256]{1,0:T(8,128)(2,1)S(1)}, bf16[1024,256]{1,0:T(8,128)(2,1)S(1)}, u32[]{:S(2)}, u32[]{:S(2)}) collective-permute-start(bf16[1024,256]{1,0:T(8,128)(2,1)S(1)} %get-tuple-element.93), channel_id=1, source_target_pairs={{0,2},{1,3},{2,0},{3,1},{4,6},{5,7},{6,4},{7,5},{8,10},{9,11},{10,... | collective-permute-start | bytes 1572872 | tf_op jit(solution)/shard_map/ppermute | solution.py:800
  482.4 12.5 %collective-permute-start.28 = (bf16[1024,256]{1,0:T(8,128)(2,1)S(1)}, bf16[1024,256]{1,0:T(8,128)(2,1)}, u32[]{:S(2)}, u32[]{:S(2)}) collective-permute-start(bf16[1024,256]{1,0:T(8,128)(2,1)S(1)} %get-tuple-element.93), channel_id=1, source_target_pairs={{0,1},{1,0},{2,3},{3,2},{4,5},{5,4},{6,7},{7,6},{8,9},{9,8},{10,11... | collective-permute-start | bytes 1572872 | tf_op jit(solution)/shard_map/ppermute | solution.py:800
  494.0 2.0 collective-permute-start.30
  521.7 21.7 %collective-permute-start.33 = (bf16[4,384,128]{2,1,0:T(8,128)(2,1)S(1)}, bf16[4,384,128]{2,1,0:T(8,128)(2,1)S(1)}, u32[]{:S(2)}, u32[]{:S(2)}) collective-permute-start(bf16[4,384,128]{2,1,0:T(8,128)(2,1)S(1)} %slice.217), channel_id=1, source_target_pairs={{0,16},{4,20},{8,24},{12,28},{16,0},{20,4},{24,8},{28,12},{1,17},{... | collective-permute-start | bytes 1179656 | tf_op jit(solution)/shard_map/ppermute | solution.py:854
  524.0 21.4 %collective-permute-start.32 = (bf16[4,640,128]{2,1,0:T(8,128)(2,1)S(1)}, bf16[4,640,128]{2,1,0:T(8,128)(2,1)S(1)}, u32[]{:S(2)}, u32[]{:S(2)}) collective-permute-start(bf16[4,640,128]{2,1,0:T(8,128)(2,1)S(1)} %pad_maximum_fusion.11), channel_id=1, source_target_pairs={{0,4},{4,0},{8,12},{12,8},{16,20},{20,16},{24,28},{28,24},{1,5},{5... | collective-permute-start | bytes 1966088 | tf_op jit(solution)/shard_map/ppermute | solution.py:854
  527.6 3.7 collective-permute-start.34
  529.7 13.9 %collective-permute-start.43 = (bf16[1024,256]{1,0:T(8,128)(2,1)S(1)}, bf16[1024,256]{1,0:T(8,128)(2,1)S(1)}, u32[]{:S(2)}, u32[]{:S(2)}) collective-permute-start(bf16[1024,256]{1,0:T(8,128)(2,1)S(1)} %get-tuple-element.138), channel_id=1, source_target_pairs={{0,1},{1,0},{2,3},{3,2},{4,5},{5,4},{6,7},{7,6},{8,9},{9,8},{10,11... | collective-permute-start | bytes 1572872 | tf_op jit(solution)/shard_map/ppermute | solution.py:795
  529.7 13.8 %collective-permute-start.42 = (bf16[1024,256]{1,0:T(8,128)(2,1)S(1)}, bf16[1024,256]{1,0:T(8,128)(2,1)S(1)}, u32[]{:S(2)}, u32[]{:S(2)}) collective-permute-start(bf16[1024,256]{1,0:T(8,128)(2,1)S(1)} %get-tuple-element.139), channel_id=1, source_target_pairs={{0,1},{1,0},{2,3},{3,2},{4,5},{5,4},{6,7},{7,6},{8,9},{9,8},{10,11... | collective-permute-start | bytes 1572872 | tf_op jit(solution)/shard_map/ppermute | solution.py:795
  531.3 1.2 collective-permute-start.35
  532.5 13.1 %collective-permute-start.40 = (bf16[1024,256]{1,0:T(8,128)(2,1)S(1)}, bf16[1024,256]{1,0:T(8,128)(2,1)S(1)}, u32[]{:S(2)}, u32[]{:S(2)}) collective-permute-start(bf16[1024,256]{1,0:T(8,128)(2,1)S(1)} %get-tuple-element.146), channel_id=1, source_target_pairs={{0,1},{1,0},{2,3},{3,2},{4,5},{5,4},{6,7},{7,6},{8,9},{9,8},{10,11... | collective-permute-start | bytes 1572872 | tf_op jit(solution)/shard_map/ppermute | solution.py:795
  543.4 2.2 collective-permute-start.31
  543.8 38.4 %collective-permute-start.44 = (bf16[1024,256]{1,0:T(8,128)(2,1)S(1)}, bf16[1024,256]{1,0:T(8,128)(2,1)S(1)}, u32[]{:S(2)}, u32[]{:S(2)}) collective-permute-start(bf16[1024,256]{1,0:T(8,128)(2,1)S(1)} %get-tuple-element.136), channel_id=1, source_target_pairs={{0,2},{1,3},{2,0},{3,1},{4,6},{5,7},{6,4},{7,5},{8,10},{9,11},{10,... | collective-permute-start | bytes 1572872 | tf_op jit(solution)/shard_map/ppermute | solution.py:795
  545.5 4.6 collective-permute-start.45
  545.9 36.3 %copy-start.65 = (bf16[1024,256]{1,0:T(8,128)(2,1)S(1)}, bf16[1024,256]{1,0:T(8,128)(2,1)}, u32[]{:S(2)}) copy-start(bf16[1024,256]{1,0:T(8,128)(2,1)} %param.13) | copy-start | bytes 1572868
  545.9 36.3 %copy-start.76 = (f32[1024]{0:T(1024)S(1)}, f32[1024]{0:T(1024)}, u32[]{:S(2)}) copy-start(f32[1024]{0:T(1024)} %get-tuple-element.200) | copy-start | bytes 12292
  545.9 34.1 %collective-permute-start.41 = (bf16[1024,256]{1,0:T(8,128)(2,1)S(1)}, bf16[1024,256]{1,0:T(8,128)(2,1)S(1)}, u32[]{:S(2)}, u32[]{:S(2)}) collective-permute-start(bf16[1024,256]{1,0:T(8,128)(2,1)S(1)} %get-tuple-element.144), channel_id=1, source_target_pairs={{0,2},{1,3},{2,0},{3,1},{4,6},{5,7},{6,4},{7,5},{8,10},{9,11},{10,... | collective-permute-start | bytes 1572872 | tf_op jit(solution)/shard_map/ppermute | solution.py:795
  550.2 3.9 collective-permute-start.46
  550.3 8.0 %collective-permute-start.38 = (bf16[2,384,128]{2,1,0:T(8,128)(2,1)S(1)}, bf16[2,384,128]{2,1,0:T(8,128)(2,1)S(1)}, u32[]{:S(2)}, u32[]{:S(2)}) collective-permute-start(bf16[2,384,128]{2,1,0:T(8,128)(2,1)S(1)} %pad_maximum_fusion.14), channel_id=1, source_target_pairs={{0,8},{4,12},{8,0},{12,4},{16,24},{20,28},{24,16},{28,20},{1,9},{5... | collective-permute-start | bytes 589832 | tf_op jit(solution)/shard_map/ppermute | solution.py:854
  554.0 3.7 collective-permute-start.47
  555.2 16.7 %collective-permute-start.36 = (bf16[2,640,128]{2,1,0:T(8,128)(2,1)S(1)}, bf16[2,640,128]{2,1,0:T(8,128)(2,1)S(1)}, u32[]{:S(2)}, u32[]{:S(2)}) collective-permute-start(bf16[2,640,128]{2,1,0:T(8,128)(2,1)S(1)} %pad_maximum_fusion.13), channel_id=1, source_target_pairs={{0,8},{4,12},{8,0},{12,4},{16,24},{20,28},{24,16},{28,20},{1,9},{5... | collective-permute-start | bytes 983048 | tf_op jit(solution)/shard_map/ppermute | solution.py:854
  558.3 13.6 %collective-permute-start.39 = (bf16[1,384,128]{2,1,0:T(8,128)(2,1)S(1)}, bf16[1,384,128]{2,1,0:T(8,128)(2,1)S(1)}, u32[]{:S(2)}, u32[]{:S(2)}) collective-permute-start(bf16[1,384,128]{2,1,0:T(8,128)(2,1)S(1)} %fusion.46), channel_id=1, source_target_pairs={{0,4},{4,0},{8,12},{12,8},{16,20},{20,16},{24,28},{28,24},{1,5},{5... | collective-permute-start | bytes 294920 | tf_op jit(solution)/shard_map/ppermute | solution.py:854
  571.9 8.0 %collective-permute-start.37 = (bf16[1,640,128]{2,1,0:T(8,128)(2,1)S(1)}, bf16[1,640,128]{2,1,0:T(8,128)(2,1)S(1)}, u32[]{:S(2)}, u32[]{:S(2)}) collective-permute-start(bf16[1,640,128]{2,1,0:T(8,128)(2,1)S(1)} %fusion.45), channel_id=1, source_target_pairs={{0,16},{4,20},{8,24},{12,28},{16,0},{20,4},{24,8},{28,12},{1,17},{... | collective-permute-start | bytes 491528 | tf_op jit(solution)/shard_map/ppermute | solution.py:854
  (69 other events, 295.0 us)
Sparse Core Ops, SparseCore 0:
  14.0 67.3 all-gather.8
  86.3 48.2 all-gather.10
  136.8 71.9 all-gather.14
  211.4 47.4 all-gather.12
  282.1 66.0 reduce-scatter.3
  364.8 85.2 reduce-scatter.5
  494.3 82.8 reduce-scatter.7

commit v8 on v7

--- a/solution.py
+++ b/solution.py
@@ -827,6 +827,7 @@
     size = lax.axis_size("narrow")
     me = lax.axis_index("narrow")
     width = block.shape[1] // size
+    block = block.astype(BF16)
     parts = jnp.stack([block[:, n * width : (n + 1) * width] for n in range(size)])
     held = [lax.dynamic_index_in_dim(parts, me ^ offset, 0, False) for offset in range(size)]
     for bit in bits_down(size)[::-1]:

time: 599 us -> 604 us (level)
    unnamed x167 -> x165, local copies, waits for them, and re-layouts: 29.7 us -> 34.3 us
  transfers between devices with their start and end apart: 55 -> 55, of which waited for: 25 -> 27; matrix products, arithmetic and copies ran while one was open for 17% -> 17% of each run, Pallas kernels for 43% -> 43%
where the time goes in v8:
time: 604 us; the launch traced here: 598 us
  Pallas kernels  259 us (43%)
  waiting for transfers between devices  145 us (24%)
  matrix products  72.5 us (12%)
  starting transfers between devices  39.8 us (7%)
  local copies, waits for them, and re-layouts  37.4 us (6%)
  other arithmetic  28.6 us (5%)
  between operations  15.9 us (3%)
    pallas_call x2, Pallas kernels, picked_products(): pl.pallas_call(functools.partial(picked_body, unroll=unroll), grid_spec=p...  86.8 us
    pallas_call x1, Pallas kernels, bag_sums(): pl.pallas_call(functools.partial(bag_body, chunk=chunk, unroll=unroll), g...  80.2 us
    dot_general x1, matrix products, per_device(): lax.dot_general(tables, all_grads, TN, preferred_element_type=F32)  53.6 us
    ppermute x22, waiting for transfers between devices, swap_all(): lax.ppermute(part, axis, pairs)  43.3 us
    ppermute x11, waiting for transfers between devices, sum_by_swaps(): lax.ppermute(block, axis, [(i, i ^ bit) for i in range(lax.axis_size(axis...  35 us
    unnamed x165, local copies, waits for them, and re-layouts  34.3 us
    all_gather x4, waiting for transfers between devices, gather_wide(): return lax.all_gather(block, 'wide')  31.3 us
    pallas_call x2, Pallas kernels, locate(): pl.pallas_call(functools.partial(locate_body, total=total), grid=(amount...  30.6 us
  transfers between devices with their start and end apart: 55, of which 27 were waited for; matrix products, arithmetic and copies ran while one was open for 17% of the time, Pallas kernels for 43%

profile of v8, /device:TPU:0, one launch (start us, length us, event | category | flops | bytes accessed | tf_op | source)
XLA Modules:
  0.0 598.3 jit_solution(12410073057961444626)
XLA Ops:
  14.0 4.1 collective-permute-start.6
  18.1 1.6 collective-permute-start.4
  19.6 1.5 collective-permute-start.3
  21.2 1.5 collective-permute-start.1
  22.7 6.5 %copy.26 = bf16[8192,256]{0,1:T(8,128)(2,1)} copy(bf16[8192,256]{1,0:T(8,128)(2,1)} %table_ref.1) | data formatting | bytes 8388608 | tf_op args[9]
  30.6 3.9 locate.2.located_ref
  37.2 5.6 collective-permute-done.5
  45.9 2.2 collective-permute-done.7
  48.7 7.9 %collective-permute-done.9 = bf16[640,128]{1,0:T(8,128)(2,1)S(1)} collective-permute-done((bf16[640,128]{1,0:T(8,128)(2,1)S(1)}, bf16[640,128]{1,0:T(8,128)(2,1)S(1)}, u32[]{:S(2)}, u32[]{:S(2)}) %collective-permute-start.9) | collective-permute-done | bytes 163872 | tf_op jit(solution)/shard_map/ppermute | solution.py:800
  56.6 2.0 collective-permute-done.19
  60.9 20.6 %all-gather.9.cloned.1.call-done = bf16[12416,128]{1,0:T(8,128)(2,1)} async-done(((bf16[1552,128]{1,0:T(8,128)(2,1)}), bf16[12416,128]{1,0:T(8,128)(2,1)}) %all-gather.9.cloned.1.call-update) | async-done | bytes 3178512 | tf_op jit(solution)/shard_map/all_gather | solution.py:889
  81.5 1.9 copy-done.9
  86.5 1.5 collective-permute-start.14
  88.1 2.1 fusion.2.refs_0_.refs_1_.refs_2_
  92.5 9.4 %attend_forward.1.refs_7_ = bf16[1024,256]{1,0:T(8,128)(2,1)S(1)} custom-call(s32[1,1024]{1,0:T(1,128)S(1)} %fusion.41.start_ref, bf16[1024,256]{1,0:T(8,128)(2,1)S(1)} %convolution_convert_fusion.4.query_ref, bf16[1024,256]{1,0:T(8,128)(2,1)S(1)} %convolution_convert_fusion.3.key_ref, bf16[1024,256]{1,0:T(8,128)(2,1)S(1)} %convolution_convert_fusion.2.value_ref), custom_call_target="tpu_custom_call" | custom-call | flops 4294967296 | bytes 2097152 | tf_op jit(solution)/shard_map/attend_forward/pallas_call | solution.py:86
  103.1 1.8 pad_maximum_fusion.4
  105.0 10.6 %collective-permute-done.11 = bf16[1024,256]{1,0:T(8,128)(2,1)S(1)} collective-permute-done((bf16[1024,256]{1,0:T(8,128)(2,1)S(1)}, bf16[1024,256]{1,0:T(8,128)(2,1)S(1)}, u32[]{:S(2)}, u32[]{:S(2)}) %collective-permute-start.11) | collective-permute-done | bytes 524320 | tf_op jit(solution)/shard_map/ppermute | solution.py:800
  119.3 2.5 multiply_reduce_fusion.2
  125.2 2.0 multiply_convert_fusion.1
  127.9 3.3 convolution_convert_fusion.query_ref
  131.2 2.3 pick_scores.1
  134.0 13.5 %collective-permute-done.16 = f32[1024,128]{1,0:T(8,128)S(1)} collective-permute-done((f32[1024,128]{1,0:T(8,128)S(1)}, f32[1024,128]{1,0:T(8,128)S(1)}, u32[]{:S(2)}, u32[]{:S(2)}) %collective-permute-start.16) | collective-permute-done | bytes 524320 | tf_op jit(solution)/shard_map/ppermute | solution.py:820
  149.7 3.6 pick_softmax.1
  153.4 13.7 %picked_products.2.rest_0_ = bf16[8192,128]{1,0:T(8,128)(2,1)} custom-call(s32[2]{0:T(128)} %pad_add_fusion.1.base_ref, s32[1024,128]{1,0:T(8,128)} %picks_ref.7, s32[1024,128]{1,0:T(8,128)} %locate.2.located_ref, bf16[1024,256]{1,0:T(8,128)(2,1)} %get-tuple-element.82.grad_ref, bf16[256,8192]{1,0:T(8,128)(2,1)} %bitcast.272), custom_call_target="tpu_custom_call" | custom-call | flops 15032385536 | bytes 1048576 | tf_op jit(solution)/shard_map/picked_products/pallas_call | solution.py:430
  167.1 1.9 broadcast_and_fusion
  169.3 26.7 %locate.3.located_ref = s32[8192,128]{1,0:T(8,128)} custom-call(s32[1]{0:T(128)} %bitcast.21.base_ref, s32[8192,128]{1,0:T(8,128)S(1)} %bitcast.259), custom_call_target="tpu_custom_call" | custom-call | flops 20971520000 | bytes 16777216 | tf_op jit(solution)/shard_map/locate/pallas_call | solution.py:225
  195.9 2.0 copy-done.6
  198.0 10.7 %all-gather.15.cloned.1.call-done.grad_ref = bf16[8192,256]{1,0:T(8,128)(2,1)} async-done(((bf16[1024,256]{1,0:T(8,128)(2,1)}), bf16[8192,256]{1,0:T(8,128)(2,1)}) %all-gather.15.cloned.1.call-update) | async-done | bytes 4194320 | tf_op jit(solution)/shard_map/all_gather | solution.py:889
  208.7 73.1 %picked_products.3 = bf16[8192,128]{1,0:T(8,128)(2,1)} custom-call(s32[2]{0:T(128)} %pad_add_fusion.1.base_ref, s32[8192,128]{1,0:T(8,128)} %bitcast.260, s32[8192,128]{1,0:T(8,128)} %locate.3.located_ref, bf16[8192,256]{1,0:T(8,128)(2,1)} %all-gather.15.cloned.1.call-done.grad_ref, bf16[256,8192]{1,0:T(8,128)(2,1)} %bitcast.273, ...), custom_call_target="tpu_custom_call", output_to_operand_aliasing={{}: (5, {})} | custom-call | flops 105226698752 | bytes 7340032 | tf_op jit(solution)/shard_map/picked_products/pallas_call | solution.py:430
  281.9 80.2 %bag_sums.1 = (bf16[8192,256]{1,0:T(8,128)(2,1)}, bf16[8192,8192]{1,0:T(8,128)(2,1)}) custom-call(s32[1]{0:T(128)} %bitcast.21.base_ref, s32[8192,128]{1,0:T(8,128)} %bitcast.261, s32[8192,128]{1,0:T(8,128)} %locate.3.located_ref, bf16[8192,128]{1,0:T(8,128)(2,1)} %all-gather.13.cloned.1.call-done.weight_ref, bf16[8192,256]{1,0:T(8,128)(2,1)} %table_ref.1), custom_call_target="tpu_custom_call" | custom-call | flops 154618822656 | bytes 134217728 | tf_op jit(solution)/shard_map/bag_sums/pallas_call | solution.py:343
  363.0 1.5 collective-permute-start.21
  364.6 10.9 %collective-permute-done.21 = f32[1024,128]{1,0:T(8,128)S(1)} collective-permute-done((f32[1024,128]{1,0:T(8,128)S(1)}, f32[1024,128]{1,0:T(8,128)S(1)}, u32[]{:S(2)}, u32[]{:S(2)}) %collective-permute-start.21) | collective-permute-done | bytes 524320 | tf_op jit(solution)/shard_map/ppermute | solution.py:820
  375.7 53.6 %fusion.55 = f32[8192,256]{1,0:T(8,128)} fusion(bf16[8192,8192]{1,0:T(8,128)(2,1)} %get-tuple-element.87, bf16[8192,256]{1,0:T(8,128)(2,1)} %all-gather.15.cloned.1.call-done.grad_ref), kind=kOutput, calls=%fused_computation.190 | convolution fusion | flops 34359738368 | bytes 146800640 | tf_op jit(solution)/shard_map/dot_general | solution.py:999
  430.8 14.7 %spread_grads.1 = (bf16[1024,512]{1,0:T(8,128)(2,1)S(1)}, f32[2,256,256]{2,1,0:T(8,128)S(1)}) custom-call(s32[1]{0:T(128)} %bitcast.45.column_ref, s32[1024,128]{1,0:T(8,128)S(1)} %copy-done.3, f32[1024,128]{1,0:T(8,128)S(1)} %get-tuple-element.89.prob_ref, f32[1024,128]{1,0:T(8,128)S(1)} %add.251.grad_ref, bf16[1024,512]{1,0:T(8,128)(2,1)S(1)} %copy-done.5, ...), custom_call_target="tpu_custom_call" | custom-call | tf_op jit(solution)/shard_map/spread_grads/pallas_call | solution.py:768
  446.3 3.9 reduce-scatter.6.cloned.1.call-done
  450.2 2.3 fusion.28
  455.0 2.1 multiply_reduce_fusion.1
  460.1 1.5 collective-permute-start.26
  462.2 2.1 fusion.31
  466.9 8.4 %pack_grads.2 = bf16[8,1152,128]{2,1,0:T(8,128)(2,1)} custom-call(s32[1]{0:T(128)} %constant.116.clone.1.me_ref, bf16[1024,1024]{1,0:T(8,128)(2,1)S(1)} %copy-done.1, bf16[1024,1024]{1,0:T(8,128)(2,1)} %copy-done.48, bf16[1024,1024]{1,0:T(8,128)(2,1)} %copy-done.48, bf16[1024,256]{1,0:T(8,128)(2,1)S(1)} %get-tuple-element.195.refs_3_, ...), custom_call_target="tpu_custom_call" | custom-call | flops 2147483648 | bytes 6291456 | tf_op jit(solution)/shard_map/pack_grads/pallas_call | solution.py:628
  475.4 3.3 collective-permute-done.25
  478.7 2.3 fusion.50
  481.0 1.5 collective-permute-start.29
  482.5 11.7 %collective-permute-done.29 = bf16[1024,256]{1,0:T(8,128)(2,1)S(1)} collective-permute-done((bf16[1024,256]{1,0:T(8,128)(2,1)S(1)}, bf16[1024,256]{1,0:T(8,128)(2,1)S(1)}, u32[]{:S(2)}, u32[]{:S(2)}) %collective-permute-start.29) | collective-permute-done | bytes 524320 | tf_op jit(solution)/shard_map/ppermute | solution.py:800
  501.0 12.1 %attend_backward.1 = (bf16[1024,256]{1,0:T(8,128)(2,1)S(1)}, bf16[1024,256]{1,0:T(8,128)(2,1)S(1)}, bf16[1024,256]{1,0:T(8,128)(2,1)S(1)}) custom-call(s32[1,1024]{1,0:T(1,128)S(1)} %fusion.41.start_ref, bf16[1024,256]{1,0:T(8,128)(2,1)S(1)} %copy-done.29, bf16[1024,256]{1,0:T(8,128)(2,1)S(1)} %copy-done.27, bf16[1024,256]{1,0:T(8,128)(2,1)S(1)} %copy-done.25, ...), custom_call_target="tpu_custom_call" | custom-call | flops 268435456 | bytes 3670016 | tf_op jit(solution)/shard_map/attend_backward/pallas_call | solution.py:141
  513.1 8.3 %pack_grads.3 = bf16[8,1024,128]{2,1,0:T(8,128)(2,1)S(1)} custom-call(s32[1]{0:T(128)} %bitcast.46.me_ref, bf16[1024,1024]{1,0:T(8,128)(2,1)} %copy-done.45, bf16[1024,1024]{1,0:T(8,128)(2,1)} %copy-done.45, bf16[1024,1024]{1,0:T(8,128)(2,1)} %copy-done.45, bf16[1024,1024]{1,0:T(8,128)(2,1)} %copy-done.49, bf16[1024,256]{1,0:T(8,128)(2,1)S(1)} %get-tuple-element.95.refs_4_, ...), custom_call_target="tpu_custom_call" | custom-call | flops 2147483648 | bytes 8388608 | tf_op jit(solution)/shard_map/pack_grads/pallas_call | solution.py:628
  524.4 2.2 collective-permute-start.33
  526.7 1.5 collective-permute-start.32
  530.1 2.4 fusion.3
  532.6 1.5 collective-permute-start.34
  534.4 1.9 collective-permute-done.34
  537.7 7.3 %collective-permute-done.33 = bf16[4,384,128]{2,1,0:T(8,128)(2,1)S(1)} collective-permute-done((bf16[4,384,128]{2,1,0:T(8,128)(2,1)S(1)}, bf16[4,384,128]{2,1,0:T(8,128)(2,1)S(1)}, u32[]{:S(2)}, u32[]{:S(2)}) %collective-permute-start.33) | collective-permute-done | bytes 393248 | tf_op jit(solution)/shard_map/ppermute | solution.py:855
  545.4 1.5 collective-permute-start.41
  548.9 1.5 collective-permute-start.44
  550.4 2.0 collective-permute-done.45
  553.0 1.7 collective-permute-start.38
  554.6 2.1 collective-permute-done.46
  558.3 2.1 collective-permute-done.47
  561.0 5.0 collective-permute-done.38
  567.1 7.4 %collective-permute-done.36 = bf16[2,640,128]{2,1,0:T(8,128)(2,1)S(1)} collective-permute-done((bf16[2,640,128]{2,1,0:T(8,128)(2,1)S(1)}, bf16[2,640,128]{2,1,0:T(8,128)(2,1)S(1)}, u32[]{:S(2)}, u32[]{:S(2)}) %collective-permute-start.36) | collective-permute-done | bytes 327712 | tf_op jit(solution)/shard_map/ppermute | solution.py:855
  574.6 2.3 collective-permute-start.37
  577.0 7.3 %collective-permute-done.37 = bf16[1,640,128]{2,1,0:T(8,128)(2,1)S(1)} collective-permute-done((bf16[1,640,128]{2,1,0:T(8,128)(2,1)S(1)}, bf16[1,640,128]{2,1,0:T(8,128)(2,1)S(1)}, u32[]{:S(2)}, u32[]{:S(2)}) %collective-permute-start.37) | collective-permute-done | bytes 163872 | tf_op jit(solution)/shard_map/ppermute | solution.py:855
  584.4 2.2 add_convert_fusion
  586.6 1.5 multiply_subtract_fusion
  (326 shorter events, 68.5 us)
Async XLA Ops:
  7.2 74.3 %all-gather.9.cloned.1.call-start = ((), (), s32[]{:S(2)}) async-start(), calls=%async_computation.6 | async-start | bytes 3575808 | tf_op jit(solution)/shard_map/all_gather | solution.py:889
  13.9 153.2 %all-gather.11.cloned.1.call-start = ((), (), s32[]{:S(2)}) async-start(), calls=%async_computation.7 | async-start | bytes 2359296 | tf_op jit(solution)/shard_map/all_gather | solution.py:889
  14.0 21.9 %collective-permute-start.6 = (bf16[640,128]{1,0:T(8,128)(2,1)S(1)}, bf16[640,128]{1,0:T(8,128)(2,1)S(1)}, u32[]{:S(2)}, u32[]{:S(2)}) collective-permute-start(bf16[640,128]{1,0:T(8,128)(2,1)S(1)} %get-tuple-element.65), channel_id=1, source_target_pairs={{0,16},{4,20},{8,24},{12,28},{16,0},{20,4},{24,8},{28,12},{1,17},{... | collective-permute-start | bytes 491528 | tf_op jit(solution)/shard_map/ppermute | solution.py:800
  18.1 18.1 %collective-permute-start.4 = (bf16[640,128]{1,0:T(8,128)(2,1)S(1)}, bf16[640,128]{1,0:T(8,128)(2,1)S(1)}, u32[]{:S(2)}, u32[]{:S(2)}) collective-permute-start(bf16[640,128]{1,0:T(8,128)(2,1)S(1)} %get-tuple-element.65), channel_id=1, source_target_pairs={{0,8},{4,12},{8,0},{12,4},{16,24},{20,28},{24,16},{28,20},{1,9},{5... | collective-permute-start | bytes 491528 | tf_op jit(solution)/shard_map/ppermute | solution.py:800
  19.6 17.0 %collective-permute-start.3 = (bf16[640,128]{1,0:T(8,128)(2,1)S(1)}, bf16[640,128]{1,0:T(8,128)(2,1)S(1)}, u32[]{:S(2)}, u32[]{:S(2)}) collective-permute-start(bf16[640,128]{1,0:T(8,128)(2,1)S(1)} %get-tuple-element.65), channel_id=1, source_target_pairs={{0,4},{4,0},{8,12},{12,8},{16,20},{20,16},{24,28},{28,24},{1,5},{5... | collective-permute-start | bytes 491528 | tf_op jit(solution)/shard_map/ppermute | solution.py:800
  21.2 37.4 %collective-permute-start = (bf16[1024,256]{1,0:T(8,128)(2,1)}, bf16[1024,256]{1,0:T(8,128)(2,1)S(1)}, u32[]{:S(2)}, u32[]{:S(2)}) collective-permute-start(bf16[1024,256]{1,0:T(8,128)(2,1)} %param.13), channel_id=1, source_target_pairs={{0,1},{1,0},{2,3},{3,2},{4,5},{5,4},{6,7},{7,6},{8,9},{9,8},{10,11... | collective-permute-start | bytes 1572872 | tf_op jit(solution)/shard_map/ppermute | solution.py:800
  21.2 27.4 %collective-permute-start.1 = (bf16[1024,256]{1,0:T(8,128)(2,1)}, bf16[1024,256]{1,0:T(8,128)(2,1)S(1)}, u32[]{:S(2)}, u32[]{:S(2)}) collective-permute-start(bf16[1024,256]{1,0:T(8,128)(2,1)} %param.13), channel_id=1, source_target_pairs={{0,2},{1,3},{2,0},{3,1},{4,6},{5,7},{6,4},{7,5},{8,10},{9,11},{10,... | collective-permute-start | bytes 1572872 | tf_op jit(solution)/shard_map/ppermute | solution.py:800
  34.5 24.0 %copy-start.63 = (bf16[1024,256]{1,0:T(8,128)(2,1)S(1)}, bf16[1024,256]{1,0:T(8,128)(2,1)}, u32[]{:S(2)}) copy-start(bf16[1024,256]{1,0:T(8,128)(2,1)} %param.13) | copy-start | bytes 1572868
  35.9 67.2 %collective-permute-start.18 = (bf16[1024,256]{1,0:T(8,128)(2,1)}, bf16[1024,256]{1,0:T(8,128)(2,1)}, u32[]{:S(2)}, u32[]{:S(2)}) collective-permute-start(bf16[1024,256]{1,0:T(8,128)(2,1)} %param.25), channel_id=1, source_target_pairs={{0,1},{1,0},{2,3},{3,2},{4,5},{5,4},{6,7},{7,6},{8,9},{9,8},{10,11... | collective-permute-start | bytes 1572872 | tf_op jit(solution)/shard_map/ppermute | solution.py:800
  36.2 8.3 %collective-permute-start.8 = (bf16[640,128]{1,0:T(8,128)(2,1)S(1)}, bf16[640,128]{1,0:T(8,128)(2,1)S(1)}, u32[]{:S(2)}, u32[]{:S(2)}) collective-permute-start(bf16[640,128]{1,0:T(8,128)(2,1)S(1)} %collective-permute-done.6), channel_id=1, source_target_pairs={{0,8},{4,12},{8,0},{12,4},{16,24},{20,28},{24,16},{28,20},{1,9},{5... | collective-permute-start | bytes 491528 | tf_op jit(solution)/shard_map/ppermute | solution.py:800
  36.7 6.1 %collective-permute-start.5 = (bf16[640,128]{1,0:T(8,128)(2,1)S(1)}, bf16[640,128]{1,0:T(8,128)(2,1)S(1)}, u32[]{:S(2)}, u32[]{:S(2)}) collective-permute-start(bf16[640,128]{1,0:T(8,128)(2,1)S(1)} %collective-permute-done.4), channel_id=1, source_target_pairs={{0,4},{4,0},{8,12},{12,8},{16,20},{20,16},{24,28},{28,24},{1,5},{5... | collective-permute-start | bytes 491528 | tf_op jit(solution)/shard_map/ppermute | solution.py:800
  42.7 5.3 collective-permute-start.7
  44.5 14.1 %collective-permute-start.19 = (bf16[1024,256]{1,0:T(8,128)(2,1)}, bf16[1024,256]{1,0:T(8,128)(2,1)}, u32[]{:S(2)}, u32[]{:S(2)}) collective-permute-start(bf16[1024,256]{1,0:T(8,128)(2,1)} %param.25), channel_id=1, source_target_pairs={{0,2},{1,3},{2,0},{3,1},{4,6},{5,7},{6,4},{7,5},{8,10},{9,11},{10,... | collective-permute-start | bytes 1572872 | tf_op jit(solution)/shard_map/ppermute | solution.py:800
  48.1 8.5 %collective-permute-start.9 = (bf16[640,128]{1,0:T(8,128)(2,1)S(1)}, bf16[640,128]{1,0:T(8,128)(2,1)S(1)}, u32[]{:S(2)}, u32[]{:S(2)}) collective-permute-start(bf16[640,128]{1,0:T(8,128)(2,1)S(1)} %collective-permute-done.8), channel_id=1, source_target_pairs={{0,4},{4,0},{8,12},{12,8},{16,20},{20,16},{24,28},{28,24},{1,5},{5... | collective-permute-start | bytes 491528 | tf_op jit(solution)/shard_map/ppermute | solution.py:800
  48.6 9.9 %collective-permute-start.2 = (bf16[1024,256]{1,0:T(8,128)(2,1)S(1)}, bf16[1024,256]{1,0:T(8,128)(2,1)S(1)}, u32[]{:S(2)}, u32[]{:S(2)}) collective-permute-start(bf16[1024,256]{1,0:T(8,128)(2,1)S(1)} %collective-permute-done.1), channel_id=1, source_target_pairs={{0,1},{1,0},{2,3},{3,2},{4,5},{5,4},{6,7},{7,6},{8,9},{9,8},{10,11... | collective-permute-start | bytes 1572872 | tf_op jit(solution)/shard_map/ppermute | solution.py:800
  58.5 44.5 %collective-permute-start.20 = (bf16[1024,256]{1,0:T(8,128)(2,1)}, bf16[1024,256]{1,0:T(8,128)(2,1)}, u32[]{:S(2)}, u32[]{:S(2)}) collective-permute-start(bf16[1024,256]{1,0:T(8,128)(2,1)} %collective-permute-done.19), channel_id=1, source_target_pairs={{0,1},{1,0},{2,3},{3,2},{4,5},{5,4},{6,7},{7,6},{8,9},{9,8},{10,11... | collective-permute-start | bytes 1572872 | tf_op jit(solution)/shard_map/ppermute | solution.py:800
  60.9 29.3 %copy-start.70 = (f32[1024]{0:T(1024)}, f32[1024]{0:T(1024)S(1)}, u32[]{:S(2)}) copy-start(f32[1024]{0:T(1024)S(1)} %get-tuple-element.203) | copy-start | bytes 12292
  86.2 37.6 %copy-start.20 = (bf16[1024,256]{1,0:T(8,128)(2,1)}, bf16[1024,256]{1,0:T(8,128)(2,1)S(1)}, u32[]{:S(2)}) copy-start(bf16[1024,256]{1,0:T(8,128)(2,1)S(1)} %get-tuple-element.72) | copy-start | bytes 1572868
  86.3 122.4 %all-gather.15.cloned.1.call-start = ((), (), s32[]{:S(2)}) async-start(), calls=%async_computation.9 | async-start | bytes 4718592 | tf_op jit(solution)/shard_map/all_gather | solution.py:889
  86.5 35.9 %copy-start.68 = (f32[1024]{0:T(1024)}, f32[1024]{0:T(1024)S(1)}, u32[]{:S(2)}) copy-start(f32[1024]{0:T(1024)S(1)} %get-tuple-element.200) | copy-start | bytes 12292
  86.5 16.0 %collective-permute-start.14 = (bf16[1024,256]{1,0:T(8,128)(2,1)}, bf16[1024,256]{1,0:T(8,128)(2,1)S(1)}, u32[]{:S(2)}, u32[]{:S(2)}) collective-permute-start(bf16[1024,256]{1,0:T(8,128)(2,1)} %copy-done.33), channel_id=1, source_target_pairs={{0,2},{1,3},{2,0},{3,1},{4,6},{5,7},{6,4},{7,5},{8,10},{9,11},{10,... | collective-permute-start | bytes 1572872 | tf_op jit(solution)/shard_map/ppermute | solution.py:800
  101.9 15.6 %copy-start.10 = (bf16[1024,256]{1,0:T(8,128)(2,1)}, bf16[1024,256]{1,0:T(8,128)(2,1)S(1)}, u32[]{:S(2)}) copy-start(bf16[1024,256]{1,0:T(8,128)(2,1)S(1)} %attend_forward.1.refs_7_) | copy-start | bytes 1572868
  101.9 13.7 %collective-permute-start.11 = (bf16[1024,256]{1,0:T(8,128)(2,1)S(1)}, bf16[1024,256]{1,0:T(8,128)(2,1)S(1)}, u32[]{:S(2)}, u32[]{:S(2)}) collective-permute-start(bf16[1024,256]{1,0:T(8,128)(2,1)S(1)} %attend_forward.1.refs_7_), channel_id=1, source_target_pairs={{0,2},{1,3},{2,0},{3,1},{4,6},{5,7},{6,4},{7,5},{8,10},{9,11},{10,... | collective-permute-start | bytes 1572872 | tf_op jit(solution)/shard_map/ppermute | solution.py:800
  102.6 13.5 %collective-permute-start.13 = (bf16[1024,256]{1,0:T(8,128)(2,1)S(1)}, bf16[1024,256]{1,0:T(8,128)(2,1)S(1)}, u32[]{:S(2)}, u32[]{:S(2)}) collective-permute-start(bf16[1024,256]{1,0:T(8,128)(2,1)S(1)} %copy-done.34), channel_id=1, source_target_pairs={{0,1},{1,0},{2,3},{3,2},{4,5},{5,4},{6,7},{7,6},{8,9},{9,8},{10,11... | collective-permute-start | bytes 1572872 | tf_op jit(solution)/shard_map/ppermute | solution.py:800
  102.6 13.5 %collective-permute-start.15 = (bf16[1024,256]{1,0:T(8,128)(2,1)S(1)}, bf16[1024,256]{1,0:T(8,128)(2,1)S(1)}, u32[]{:S(2)}, u32[]{:S(2)}) collective-permute-start(bf16[1024,256]{1,0:T(8,128)(2,1)S(1)} %collective-permute-done.14), channel_id=1, source_target_pairs={{0,1},{1,0},{2,3},{3,2},{4,5},{5,4},{6,7},{7,6},{8,9},{9,8},{10,11... | collective-permute-start | bytes 1572872 | tf_op jit(solution)/shard_map/ppermute | solution.py:800
  104.9 11.5 %collective-permute-start.10 = (bf16[1024,256]{1,0:T(8,128)(2,1)S(1)}, bf16[1024,256]{1,0:T(8,128)(2,1)S(1)}, u32[]{:S(2)}, u32[]{:S(2)}) collective-permute-start(bf16[1024,256]{1,0:T(8,128)(2,1)S(1)} %attend_forward.1.refs_7_), channel_id=1, source_target_pairs={{0,1},{1,0},{2,3},{3,2},{4,5},{5,4},{6,7},{7,6},{8,9},{9,8},{10,11... | collective-permute-start | bytes 1572872 | tf_op jit(solution)/shard_map/ppermute | solution.py:800
  115.6 1.9 collective-permute-start.12
  127.2 154.6 %all-gather.13.cloned.1.call-start = ((), (), s32[]{:S(2)}) async-start(), calls=%async_computation.8 | async-start | bytes 2359296 | tf_op jit(solution)/shard_map/all_gather | solution.py:889
  133.5 14.0 %collective-permute-start.16 = (f32[1024,128]{1,0:T(8,128)S(1)}, f32[1024,128]{1,0:T(8,128)S(1)}, u32[]{:S(2)}, u32[]{:S(2)}) collective-permute-start(f32[1024,128]{1,0:T(8,128)S(1)} %pick_scores.1), channel_id=1, source_target_pairs={{0,2},{1,3},{2,0},{3,1},{4,6},{5,7},{6,4},{7,5},{8,10},{9,11},{10,... | collective-permute-start | bytes 1572872 | tf_op jit(solution)/shard_map/ppermute | solution.py:820
  147.6 2.0 collective-permute-start.17
  153.4 208.7 %reduce-scatter.4.cloned.1.call-start = ((), (), s32[]{:S(2)}) async-start(), calls=%async_computation.3 | async-start | bytes 2359296 | tf_op jit(solution)/shard_map/reduce_scatter | solution.py:893
  281.8 168.4 %reduce-scatter.6.cloned.1.call-start = ((), (), s32[]{:S(2)}) async-start(), calls=%async_computation.4 | async-start | bytes 4718592 | tf_op jit(solution)/shard_map/reduce_scatter | solution.py:893
  363.0 12.5 %collective-permute-start.21 = (f32[1024,128]{1,0:T(8,128)S(1)}, f32[1024,128]{1,0:T(8,128)S(1)}, u32[]{:S(2)}, u32[]{:S(2)}) collective-permute-start(f32[1024,128]{1,0:T(8,128)S(1)} %bitcast_convert_fusion), channel_id=1, source_target_pairs={{0,2},{1,3},{2,0},{3,1},{4,6},{5,7},{6,4},{7,5},{8,10},{9,11},{10,... | collective-permute-start | bytes 1572872 | tf_op jit(solution)/shard_map/ppermute | solution.py:820
  364.6 223.5 %reduce-scatter.8.cloned.1.call-start = ((), (), s32[]{:S(2)}) async-start(), calls=%async_computation.5 | async-start | bytes 2654208 | tf_op jit(solution)/shard_map/reduce_scatter | solution.py:893
  375.6 53.7 %collective-permute-start.22 = (f32[1024,128]{1,0:T(8,128)S(1)}, f32[1024,128]{1,0:T(8,128)S(1)}, u32[]{:S(2)}, u32[]{:S(2)}) collective-permute-start(f32[1024,128]{1,0:T(8,128)S(1)} %add.250), channel_id=1, source_target_pairs={{0,1},{1,0},{2,3},{3,2},{4,5},{5,4},{6,7},{7,6},{8,9},{9,8},{10,11... | collective-permute-start | bytes 1572872 | tf_op jit(solution)/shard_map/ppermute | solution.py:820
  375.7 53.7 %copy-start.3 = (s32[1024,128]{1,0:T(8,128)S(1)}, s32[1024,128]{1,0:T(8,128)}, u32[]{:S(2)}) copy-start(s32[1024,128]{1,0:T(8,128)} %picks_ref.7) | copy-start | bytes 1572868
  375.7 53.7 %copy-start.15 = (bf16[2,256,256]{2,1,0:T(8,128)(2,1)S(1)}, bf16[2,256,256]{2,1,0:T(8,128)(2,1)}, u32[]{:S(2)}) copy-start(bf16[2,256,256]{2,1,0:T(8,128)(2,1)} %copy-done.14) | copy-start | bytes 786436
  460.0 2.3 collective-permute-start.24
  460.1 5.8 collective-permute-start.26
  461.5 13.8 %collective-permute-start.23 = (bf16[1024,256]{1,0:T(8,128)(2,1)}, bf16[1024,256]{1,0:T(8,128)(2,1)}, u32[]{:S(2)}, u32[]{:S(2)}) collective-permute-start(bf16[1024,256]{1,0:T(8,128)(2,1)} %get-tuple-element.170), channel_id=1, source_target_pairs={{0,1},{1,0},{2,3},{3,2},{4,5},{5,4},{6,7},{7,6},{8,9},{9,8},{10,11... | collective-permute-start | bytes 1572872 | tf_op jit(solution)/shard_map/ppermute | solution.py:795
  464.4 14.3 %collective-permute-start.25 = (bf16[1024,256]{1,0:T(8,128)(2,1)}, bf16[1024,256]{1,0:T(8,128)(2,1)}, u32[]{:S(2)}, u32[]{:S(2)}) collective-permute-start(bf16[1024,256]{1,0:T(8,128)(2,1)} %fusion.31), channel_id=1, source_target_pairs={{0,2},{1,3},{2,0},{3,1},{4,6},{5,7},{6,4},{7,5},{8,10},{9,11},{10,... | collective-permute-start | bytes 1572872 | tf_op jit(solution)/shard_map/ppermute | solution.py:795
  465.8 9.5 %collective-permute-start.27 = (f32[2048]{0:T(1024)S(1)}, f32[2048]{0:T(1024)S(1)}, u32[]{:S(2)}, u32[]{:S(2)}) collective-permute-start(f32[2048]{0:T(1024)S(1)} %fusion.48), channel_id=1, source_target_pairs={{0,1},{1,0},{2,3},{3,2},{4,5},{5,4},{6,7},{7,6},{8,9},{9,8},{10,11... | collective-permute-start | bytes 24584 | tf_op jit(solution)/shard_map/ppermute | solution.py:820
  478.7 15.5 %copy-start.73 = (f32[1024]{0:T(1024)S(1)}, f32[1024]{0:T(1024)}, u32[]{:S(2)}) copy-start(f32[1024]{0:T(1024)} %copy-done.72) | copy-start | bytes 12292
  481.0 13.3 %copy-start.32 = (bf16[1024,256]{1,0:T(8,128)(2,1)S(1)}, bf16[1024,256]{1,0:T(8,128)(2,1)}, u32[]{:S(2)}) copy-start(bf16[1024,256]{1,0:T(8,128)(2,1)} %copy-done.30) | copy-start | bytes 1572868
  481.0 13.2 %collective-permute-start.29 = (bf16[1024,256]{1,0:T(8,128)(2,1)S(1)}, bf16[1024,256]{1,0:T(8,128)(2,1)S(1)}, u32[]{:S(2)}, u32[]{:S(2)}) collective-permute-start(bf16[1024,256]{1,0:T(8,128)(2,1)S(1)} %get-tuple-element.93), channel_id=1, source_target_pairs={{0,2},{1,3},{2,0},{3,1},{4,6},{5,7},{6,4},{7,5},{8,10},{9,11},{10,... | collective-permute-start | bytes 1572872 | tf_op jit(solution)/shard_map/ppermute | solution.py:800
  482.5 12.5 %collective-permute-start.28 = (bf16[1024,256]{1,0:T(8,128)(2,1)S(1)}, bf16[1024,256]{1,0:T(8,128)(2,1)}, u32[]{:S(2)}, u32[]{:S(2)}) collective-permute-start(bf16[1024,256]{1,0:T(8,128)(2,1)S(1)} %get-tuple-element.93), channel_id=1, source_target_pairs={{0,1},{1,0},{2,3},{3,2},{4,5},{5,4},{6,7},{7,6},{8,9},{9,8},{10,11... | collective-permute-start | bytes 1572872 | tf_op jit(solution)/shard_map/ppermute | solution.py:800
  494.2 2.0 collective-permute-start.30
  524.4 20.6 %collective-permute-start.33 = (bf16[4,384,128]{2,1,0:T(8,128)(2,1)S(1)}, bf16[4,384,128]{2,1,0:T(8,128)(2,1)S(1)}, u32[]{:S(2)}, u32[]{:S(2)}) collective-permute-start(bf16[4,384,128]{2,1,0:T(8,128)(2,1)S(1)} %slice.221), channel_id=1, source_target_pairs={{0,16},{4,20},{8,24},{12,28},{16,0},{20,4},{24,8},{28,12},{1,17},{... | collective-permute-start | bytes 1179656 | tf_op jit(solution)/shard_map/ppermute | solution.py:855
  526.7 20.9 %collective-permute-start.32 = (bf16[4,640,128]{2,1,0:T(8,128)(2,1)S(1)}, bf16[4,640,128]{2,1,0:T(8,128)(2,1)S(1)}, u32[]{:S(2)}, u32[]{:S(2)}) collective-permute-start(bf16[4,640,128]{2,1,0:T(8,128)(2,1)S(1)} %pad_maximum_fusion.11), channel_id=1, source_target_pairs={{0,4},{4,0},{8,12},{12,8},{16,20},{20,16},{24,28},{28,24},{1,5},{5... | collective-permute-start | bytes 1966088 | tf_op jit(solution)/shard_map/ppermute | solution.py:855
  528.6 16.4 %collective-permute-start.40 = (bf16[1024,256]{1,0:T(8,128)(2,1)S(1)}, bf16[1024,256]{1,0:T(8,128)(2,1)S(1)}, u32[]{:S(2)}, u32[]{:S(2)}) collective-permute-start(bf16[1024,256]{1,0:T(8,128)(2,1)S(1)} %get-tuple-element.156), channel_id=1, source_target_pairs={{0,1},{1,0},{2,3},{3,2},{4,5},{5,4},{6,7},{7,6},{8,9},{9,8},{10,11... | collective-permute-start | bytes 1572872 | tf_op jit(solution)/shard_map/ppermute | solution.py:795
  528.7 16.4 %collective-permute-start.31 = (bf16[1024,256]{1,0:T(8,128)(2,1)S(1)}, bf16[1024,256]{1,0:T(8,128)(2,1)S(1)}, u32[]{:S(2)}, u32[]{:S(2)}) collective-permute-start(bf16[1024,256]{1,0:T(8,128)(2,1)S(1)} %get-tuple-element.157), channel_id=1, source_target_pairs={{0,1},{1,0},{2,3},{3,2},{4,5},{5,4},{6,7},{7,6},{8,9},{9,8},{10,11... | collective-permute-start | bytes 1572872 | tf_op jit(solution)/shard_map/ppermute | solution.py:795
  532.6 3.7 collective-permute-start.34
  536.3 1.2 collective-permute-start.35
  537.5 11.1 %collective-permute-start.43 = (bf16[1024,256]{1,0:T(8,128)(2,1)S(1)}, bf16[1024,256]{1,0:T(8,128)(2,1)S(1)}, u32[]{:S(2)}, u32[]{:S(2)}) collective-permute-start(bf16[1024,256]{1,0:T(8,128)(2,1)S(1)} %get-tuple-element.148), channel_id=1, source_target_pairs={{0,1},{1,0},{2,3},{3,2},{4,5},{5,4},{6,7},{7,6},{8,9},{9,8},{10,11... | collective-permute-start | bytes 1572872 | tf_op jit(solution)/shard_map/ppermute | solution.py:795
  545.0 3.6 collective-permute-start.42
  545.4 39.0 %collective-permute-start.41 = (bf16[1024,256]{1,0:T(8,128)(2,1)S(1)}, bf16[1024,256]{1,0:T(8,128)(2,1)S(1)}, u32[]{:S(2)}, u32[]{:S(2)}) collective-permute-start(bf16[1024,256]{1,0:T(8,128)(2,1)S(1)} %get-tuple-element.154), channel_id=1, source_target_pairs={{0,2},{1,3},{2,0},{3,1},{4,6},{5,7},{6,4},{7,5},{8,10},{9,11},{10,... | collective-permute-start | bytes 1572872 | tf_op jit(solution)/shard_map/ppermute | solution.py:795
  547.8 4.6 collective-permute-start.45
  548.9 37.8 %collective-permute-start.44 = (bf16[1024,256]{1,0:T(8,128)(2,1)S(1)}, bf16[1024,256]{1,0:T(8,128)(2,1)S(1)}, u32[]{:S(2)}, u32[]{:S(2)}) collective-permute-start(bf16[1024,256]{1,0:T(8,128)(2,1)S(1)} %get-tuple-element.146), channel_id=1, source_target_pairs={{0,2},{1,3},{2,0},{3,1},{4,6},{5,7},{6,4},{7,5},{8,10},{9,11},{10,... | collective-permute-start | bytes 1572872 | tf_op jit(solution)/shard_map/ppermute | solution.py:795
  552.4 4.3 collective-permute-start.46
  553.0 13.0 %collective-permute-start.38 = (bf16[2,384,128]{2,1,0:T(8,128)(2,1)S(1)}, bf16[2,384,128]{2,1,0:T(8,128)(2,1)S(1)}, u32[]{:S(2)}, u32[]{:S(2)}) collective-permute-start(bf16[2,384,128]{2,1,0:T(8,128)(2,1)S(1)} %pad_maximum_fusion.14), channel_id=1, source_target_pairs={{0,8},{4,12},{8,0},{12,4},{16,24},{20,28},{24,16},{28,20},{1,9},{5... | collective-permute-start | bytes 589832 | tf_op jit(solution)/shard_map/ppermute | solution.py:855
  556.7 3.7 collective-permute-start.47
  558.2 16.3 %collective-permute-start.36 = (bf16[2,640,128]{2,1,0:T(8,128)(2,1)S(1)}, bf16[2,640,128]{2,1,0:T(8,128)(2,1)S(1)}, u32[]{:S(2)}, u32[]{:S(2)}) collective-permute-start(bf16[2,640,128]{2,1,0:T(8,128)(2,1)S(1)} %pad_maximum_fusion.13), channel_id=1, source_target_pairs={{0,8},{4,12},{8,0},{12,4},{16,24},{20,28},{24,16},{28,20},{1,9},{5... | collective-permute-start | bytes 983048 | tf_op jit(solution)/shard_map/ppermute | solution.py:855
  566.0 10.9 %collective-permute-start.39 = (bf16[1,384,128]{2,1,0:T(8,128)(2,1)S(1)}, bf16[1,384,128]{2,1,0:T(8,128)(2,1)S(1)}, u32[]{:S(2)}, u32[]{:S(2)}) collective-permute-start(bf16[1,384,128]{2,1,0:T(8,128)(2,1)S(1)} %fusion.40), channel_id=1, source_target_pairs={{0,4},{4,0},{8,12},{12,8},{16,20},{20,16},{24,28},{28,24},{1,5},{5... | collective-permute-start | bytes 294920 | tf_op jit(solution)/shard_map/ppermute | solution.py:855
  574.6 9.7 %collective-permute-start.37 = (bf16[1,640,128]{2,1,0:T(8,128)(2,1)S(1)}, bf16[1,640,128]{2,1,0:T(8,128)(2,1)S(1)}, u32[]{:S(2)}, u32[]{:S(2)}) collective-permute-start(bf16[1,640,128]{2,1,0:T(8,128)(2,1)S(1)} %fusion.39), channel_id=1, source_target_pairs={{0,16},{4,20},{8,24},{12,28},{16,0},{20,4},{24,8},{28,12},{1,17},{... | collective-permute-start | bytes 491528 | tf_op jit(solution)/shard_map/ppermute | solution.py:855
  (68 other events, 187.1 us)
Sparse Core Ops, SparseCore 0:
  14.0 67.3 all-gather.8
  86.4 48.1 all-gather.10
  136.8 71.8 all-gather.14
  211.2 47.6 all-gather.12
  281.9 65.8 reduce-scatter.3
  364.7 85.4 reduce-scatter.5
  494.4 77.4 reduce-scatter.7
